TPU v7x, 256 devices: a whole 4x4x8 slice. The times are simulated.
256 devices in a mesh: space: 16 (over z_hi, y), chan: 16 (over x, z_lo, core).
Axes of the slice: x: 4, y: 4, z: 8 (z_hi: 4, z_lo: 2; z = z_hi * 2 + z_lo), core: 2. Of those that a mesh axis runs over, the one named last changes fastest.
Arguments:
- image: bfloat16 [3, 32, 8192], P(None, None, 'space'), may hold values from -6 to 6
- mask: int32 [32, 8192], P(None, 'space'), may hold values from 0 to 1, as said below
- anchors: bfloat16 [1024, 75], P('chan'), may hold values from -0.75 to 0.75
- whiten: bfloat16 [1024, 1024], P(None, 'chan'), may hold values from -0.1875 to 0.1875
- cotangent: bfloat16 [1024, 16, 4096], P('chan', None, 'space'), may hold values from -0.59765625 to 0.59765625
Outputs:
- grad_anchors: float32 [1024, 75], P('chan')
- grad_whiten: float32 [1024, 1024], P('space', 'chan')
- grad_image: float32 [3, 32, 8192], P(None, 'chan', 'space')
Inputs may be any that keep to these rules, and one draw needn't show every extreme that they name: `mask`: 1 where a pixel holds tissue.
All inputs are finite; a program needn't handle non-finite values.
Results may differ from a plain program's by a relative error of at most 0.011.
Values may be sent and summed in bfloat16 or wider, within the bound.
No kernel may reach another device: no remote copies, remote signals or barrier semaphores. Data moves between devices by JAX's collectives and lax.ppermute only.
A program may use at most 128 MiB of HBM per device.

v0:
```python
import functools
import math

import jax
import jax.numpy as jnp
from jax import lax
from jax.experimental import pallas as pl
from jax.experimental.pallas import tpu as pltpu
from jax.sharding import PartitionSpec as P

EPS = 1e-05
RIM = 6
LANES = 384
HALF = 128
ROWS = 32
GROUP = 16
OWN = 64
VMEM = 56 * 1024 * 1024

CHIPS = ((0, 0), (0, 1), (1, 0), (3, 0), (1, 1), (3, 1), (2, 0), (2, 1))

CORE = [(i, i ^ 1) for i in range(16)]
ZED = [(i, i ^ 2) for i in range(16)]
RIGHT = [(i, (i + 4) % 16) for i in range(16)]
LEFT = [(i, (i - 4) % 16) for i in range(16)]

f32 = jnp.float32
bf16 = jnp.bfloat16


def tap(distance):
    return math.exp(-distance * distance / 8.0)


def column_pool():
    lane = lax.broadcasted_iota(jnp.int32, (LANES, HALF), 0)
    target = lax.broadcasted_iota(jnp.int32, (LANES, HALF), 1)
    distance = (2 * target - lane + 4).astype(f32)
    return jnp.where(jnp.abs(distance) <= 4.0, jnp.exp(-distance * distance / 8.0), 0.0).astype(bf16)


def row_pool():
    a = lax.broadcasted_iota(jnp.int32, (ROWS // 2, ROWS), 0)
    i = lax.broadcasted_iota(jnp.int32, (ROWS // 2, ROWS), 1)
    distance = (2 * a - i).astype(f32)
    return jnp.where(jnp.abs(distance) <= 4.0, jnp.exp(-distance * distance / 8.0), 0.0)


def fold_rows():
    out = lax.broadcasted_iota(jnp.int32, (96, 36 * GROUP), 0)
    src = lax.broadcasted_iota(jnp.int32, (96, 36 * GROUP), 1)
    i = 2 * (out // 6) + out % 2
    colour = (out % 6) // 2
    hit = (src // GROUP == i + 2) & ((src % GROUP) // 5 == colour)
    return jnp.where(hit, 1.0, 0.0).astype(bf16)


def forward_kernel(
    blk, rep, mask, anch, pool, rows, wcat,
    patches, masked, whitened, inv_density, inv_square, wturned,
    scale, norm, columned,
):
    x = rep[...].astype(f32)
    offset = (lax.broadcasted_iota(jnp.int32, x.shape, 0) % GROUP) % 5
    s = x
    for b in range(1, 5):
        s = jnp.where(offset == b, pltpu.roll(x, LANES - b, 1), s)
    patches[...] = s.astype(bf16)
    square = jnp.sum((s * s).reshape(36, GROUP, LANES), axis=1)
    total = square[0:ROWS]
    for a in range(1, 5):
        total = total + square[a : a + ROWS]
    total = total + EPS
    root = lax.rsqrt(total)
    scale[...] = 4.0 * root
    norm[...] = total * root
    inv_square[...] = 1.0 / total
    counted = jnp.dot(mask[...].astype(bf16), pool[...], preferred_element_type=f32)
    density = jnp.dot(rows[...], counted, precision=lax.Precision.HIGHEST, preferred_element_type=f32)
    inv_density[...] = 1.0 / jnp.maximum(density, 1.0)

    @pl.loop(0, ROWS)
    def _(i):
        patch = patches[pl.ds(pl.multiple_of(i * GROUP, GROUP), 80), :]
        raw = jnp.dot(anch[...], patch, preferred_element_type=f32)
        value = jnp.exp(raw * scale[pl.ds(i, 1), :] - 4.0) * mask[pl.ds(i, 1), :]
        masked[i] = value.astype(bf16)
        lifted = (value * norm[pl.ds(i, 1), :]).astype(bf16)
        columned[i] = jnp.dot(lifted, pool[...], preferred_element_type=f32)

    for a in range(ROWS // 2):
        acc = None
        for i in range(max(0, 2 * a - 4), min(ROWS, 2 * a + 5)):
            term = tap(2 * a - i) * columned[i]
            acc = term if acc is None else acc + term
        whitened[:, a * HALF : (a + 1) * HALF] = (acc * inv_density[a : a + 1, :]).astype(bf16)

    ordered = jnp.concatenate(
        [wcat[pl.ds(pl.multiple_of(blk[p] * OWN, OWN), OWN), :] for p in range(16)], axis=0
    )
    wturned[...] = ordered.astype(f32).T.astype(bf16)


def fold(block, rows):
    top, low = block[:rows], block[rows:]
    left = lax.broadcasted_iota(jnp.int32, top.shape, 1) < OWN
    own = jnp.where(left, top, pltpu.roll(low, OWN, 1))
    partner = jnp.where(left, pltpu.roll(top, OWN, 1), low)
    return own.astype(bf16), partner.astype(bf16)


def backward_kernel(
    blk, b0, bz, br, bl, bzr, bzl, b2a, b2b, b2za, b2zb,
    wturned, whitened, inv_density, masked, patches, inv_square, anch_t, pool_t, folder,
    own_w, partner_w, own_a, partner_a, image,
    rowed, spread_grad, anchor_grad,
):
    refs = (b0, bz, br, bl, bzr, bzl, b2a, b2b, b2za, b2zb)
    grad_w = None
    pooled = []
    for n in range(8):
        cols = pl.ds(n * 256, 256)
        stack = jnp.concatenate([ref[:, cols] for ref in refs], axis=0)
        pooled.append(jnp.dot(wturned[...], stack, preferred_element_type=f32))
        term = lax.dot_general(
            stack, whitened[:, cols], (((1,), (1,)), ((), ())), preferred_element_type=f32
        )
        grad_w = term if grad_w is None else grad_w + term
    for p in range(16):
        own, partner = fold(grad_w[p * OWN : (p + 1) * OWN], OWN // 2)
        own_w[blk[p]] = own
        partner_w[blk[p]] = partner
    scaled = []
    for a in range(ROWS // 2):
        part = pooled[a // 2][:, (a % 2) * HALF : (a % 2 + 1) * HALF]
        scaled.append(part.astype(bf16).astype(f32) * inv_density[a : a + 1, :])
    for i in range(ROWS):
        acc = None
        for a in range(ROWS // 2):
            if abs(2 * a - i) <= 4:
                term = (4.0 * tap(2 * a - i)) * scaled[a]
                acc = term if acc is None else acc + term
        rowed[i] = acc.astype(bf16)
    spread_grad[...] = jnp.zeros_like(spread_grad)
    anchor_grad[...] = jnp.zeros_like(anchor_grad)

    @pl.loop(0, ROWS)
    def _(i):
        here = pl.ds(pl.multiple_of(i * GROUP, GROUP), 80)
        spread = jnp.dot(rowed[i], pool_t[...], preferred_element_type=f32)
        grad = (spread * masked[i].astype(f32)).astype(bf16)
        patch = patches[here, :]
        anchor_grad[...] += lax.dot_general(
            patch, grad, (((1,), (1,)), ((), ())), preferred_element_type=f32
        )
        unit = jnp.dot(anch_t[...], grad, preferred_element_type=f32)
        wide = patch.astype(f32)
        along = jnp.sum(wide * unit, axis=0, keepdims=True) * inv_square[pl.ds(i, 1), :]
        spread_grad[here, :] += unit - wide * along

    own, partner = fold(anchor_grad[...], 40)
    own_a[...] = own
    partner_a[...] = partner
    t = spread_grad[...]
    offset = (lax.broadcasted_iota(jnp.int32, t.shape, 0) % GROUP) % 5
    moved = t
    for b in range(1, 5):
        moved = jnp.where(offset == b, pltpu.roll(t, b, 1), moved)
    high = moved.astype(bf16)
    low = (moved - high.astype(f32)).astype(bf16)
    image[...] = (
        jnp.dot(folder[...], high, preferred_element_type=f32)
        + jnp.dot(folder[...], low, preferred_element_type=f32)
    ).astype(bf16)


def call(kernel, outs, scratch, flops, bytes_accessed, *args):
    specs = [pl.BlockSpec(memory_space=pltpu.SMEM)]
    specs += [pl.BlockSpec(memory_space=pltpu.VMEM)] * (len(args) - 1)
    return pl.pallas_call(
        kernel,
        out_shape=[jax.ShapeDtypeStruct(shape, dtype) for shape, dtype in outs],
        in_specs=specs,
        out_specs=[pl.BlockSpec(memory_space=pltpu.VMEM)] * len(outs),
        scratch_shapes=[pltpu.VMEM(shape, dtype) for shape, dtype in scratch],
        compiler_params=pltpu.CompilerParams(vmem_limit_bytes=VMEM),
        cost_estimate=pl.CostEstimate(
            flops=flops, bytes_accessed=bytes_accessed, transcendentals=ROWS * 128 * LANES
        ),
    )(*args)


def neighbours(first, last, axis):
    count = lax.axis_size(axis)
    up = [(i, i + 1) for i in range(count - 1)]
    down = [(i + 1, i) for i in range(count - 1)]
    return lax.ppermute(last, axis, up), lax.ppermute(first, axis, down)


def shards(image, mask, anchors, whiten, cotangent):
    chan = lax.axis_index("chan")
    core = chan % 2
    zed = (chan // 2) % 2
    ex = chan // 4
    blk = jnp.stack(
        [((ex + dx) % 4) * 4 + (zed ^ dz) * 2 + (core ^ o) for dx, dz in CHIPS for o in (0, 1)]
    ).astype(jnp.int32)

    left, right = cotangent[:, :, :HALF], cotangent[:, :, HALF:]
    own = jnp.where(core == 0, left, right).reshape(OWN, -1)
    away = jnp.where(core == 0, right, left).reshape(OWN, -1)
    b0 = jnp.concatenate([own, lax.ppermute(away, "chan", CORE)], axis=0)
    bz = lax.ppermute(b0, "chan", ZED)
    bl = lax.ppermute(b0, "chan", RIGHT)
    br = lax.ppermute(b0, "chan", LEFT)
    b2a = lax.ppermute(bl[:OWN], "chan", RIGHT)
    b2b = lax.ppermute(br[OWN:], "chan", LEFT)
    bzl = lax.ppermute(bz, "chan", RIGHT)
    bzr = lax.ppermute(bz, "chan", LEFT)
    b2za = lax.ppermute(b2a, "chan", ZED)
    b2zb = lax.ppermute(b2b, "chan", ZED)

    stacked = jnp.concatenate([image, mask.astype(bf16)[None]], axis=0)
    width = stacked.shape[2]
    before, after = neighbours(stacked[:, :, :RIM], stacked[:, :, width - RIM :], "space")
    first = jnp.concatenate([before, stacked[:, :, : 256 + RIM]], axis=2)
    second = jnp.concatenate([stacked[:, :, 256 - RIM :], after], axis=2)
    extended = jnp.where(core == 0, first, second)
    extended = jnp.pad(extended, ((0, 0), (0, 0), (0, LANES - 256 - 2 * RIM)))
    tissue = jnp.pad(extended[3, :, 2:], ((0, 0), (0, 2))).astype(f32)
    tall = jnp.pad(jnp.transpose(extended[:3], (1, 0, 2)), ((2, 2), (0, 0), (0, 0)))
    rep = jnp.broadcast_to(tall[:, :, None, :], (36, 3, 5, LANES)).reshape(36, 15, LANES)
    rep = jnp.pad(rep, ((0, 0), (0, 1), (0, 0))).reshape(36 * GROUP, LANES)

    turned = jnp.transpose(anchors.reshape(OWN, 3, 5, 5), (0, 2, 1, 3)).reshape(OWN, 5, 15)
    turned = jnp.pad(turned, ((0, 0), (0, 0), (0, 1))).reshape(OWN, 80)
    anch = jnp.concatenate([turned, lax.ppermute(turned, "chan", CORE)], axis=0)
    wcat = jnp.concatenate([whiten, lax.ppermute(whiten, "chan", CORE)], axis=1)

    pool = column_pool()
    patches, masked, whitened, inv_density, inv_square, wturned = call(
        forward_kernel,
        [
            ((36 * GROUP, LANES), bf16),
            ((ROWS, 128, LANES), bf16),
            ((128, 16 * HALF), bf16),
            ((16, HALF), f32),
            ((ROWS, LANES), f32),
            ((128, 1024), bf16),
        ],
        [((ROWS, LANES), f32), ((ROWS, LANES), f32), ((ROWS, 128, HALF), f32)],
        4_000_000_000,
        6_000_000,
        blk, rep, tissue, anch, pool, row_pool(), wcat,
    )
    own_w, partner_w, own_a, partner_a, image_part = call(
        backward_kernel,
        [
            ((16, 32, 128), bf16),
            ((16, 32, 128), bf16),
            ((40, 128), bf16),
            ((40, 128), bf16),
            ((96, LANES), bf16),
        ],
        [((ROWS, 128, HALF), bf16), ((36 * GROUP, LANES), f32), ((80, 128), f32)],
        4_000_000_000,
        9_000_000,
        blk, b0, bz, br, bl, bzr, bzl, b2a, b2b, b2za, b2zb,
        wturned, whitened, inv_density, masked, patches, inv_square,
        jnp.transpose(anch), jnp.transpose(pool), fold_rows(),
    )

    send_w = (own_w.astype(f32) + lax.ppermute(partner_w, "chan", CORE).astype(f32)).astype(bf16)
    send_a = (own_a.astype(f32) + lax.ppermute(partner_a, "chan", CORE).astype(f32)).astype(bf16)
    packed = jnp.concatenate([send_w, jnp.broadcast_to(send_a[None], (16, 40, 128))], axis=1)
    summed = jnp.sum(lax.all_to_all(packed, "space", 0, 0).astype(f32), axis=0)
    grad_whiten = jnp.concatenate([summed[:32, :OWN], summed[:32, OWN:]], axis=0)
    turned = jnp.concatenate([summed[32:, :OWN], summed[32:, OWN:]], axis=0)
    turned = turned.reshape(5, GROUP, OWN)[:, :15].reshape(5, 3, 5, OWN)
    grad_anchors = jnp.transpose(turned, (3, 1, 0, 2)).reshape(OWN, 75)

    parts = lax.all_to_all(image_part.reshape(16, 6, LANES), "chan", 0, 0)
    parts = jnp.sum(parts.astype(f32).reshape(8, 2, 6, LANES), axis=0)
    whole = jnp.pad(parts[0], ((0, 0), (0, 256))) + jnp.pad(parts[1], ((0, 0), (256, 0)))
    from_before, from_after = neighbours(
        whole[:, :RIM], whole[:, RIM + width : 2 * RIM + width], "space"
    )
    middle = jnp.zeros((6, width - 2 * RIM), f32)
    rims = jnp.concatenate([from_before, middle, from_after], axis=1)
    grad_image = (whole[:, RIM : RIM + width] + rims).reshape(3, 2, width)
    return (grad_anchors, grad_whiten, grad_image)


def solution(mesh):
    placed = (
        P(None, None, "space"),
        P(None, "space"),
        P("chan", None),
        P(None, "chan"),
        P("chan", None, "space"),
    )
    return jax.shard_map(
        shards,
        mesh=mesh,
        in_specs=placed,
        out_specs=(P("chan", None), P("space", "chan"), P(None, "chan", "space")),
        check_vma=False,
    )
```

profile of v0, /device:TPU:24, one launch (start us, length us, event | category | flops | bytes accessed | tf_op | source)
XLA Modules:
  0.0 117.1 jit_solution(1317846354566171782)
XLA Ops:
  0.7 0.9 convert_bitcast_fusion
  1.5 0.8 pad_maximum_fusion.3
  2.4 4.8 %collective-permute-start.10 = (bf16[4,32,6]{2,1,0:T(8,128)(2,1)S(1)}, bf16[4,32,6]{2,1,0:T(8,128)(2,1)S(1)}, u32[]{:S(2)}, u32[]{:S(2)}) collective-permute-start(bf16[4,32,6]{2,1,0:T(8,128)(2,1)S(1)} %get-tuple-element.36), channel_id=1, source_target_pairs={{0,16},{16,32},{32,48},{48,64},{64,80},{80,96},{96,112},{112,128},... | collective-permute-start | bytes 4616 | tf_op jit(solution)/shard_map/ppermute | solution.py:197
  7.2 1.9 %collective-permute-start.11 = (bf16[4,32,6]{2,1,0:T(8,128)(2,1)S(1)}, bf16[4,32,6]{2,1,0:T(8,128)(2,1)S(1)}, u32[]{:S(2)}, u32[]{:S(2)}) collective-permute-start(bf16[4,32,6]{2,1,0:T(8,128)(2,1)S(1)} %get-tuple-element.35), channel_id=1, source_target_pairs={{16,0},{32,16},{48,32},{64,48},{80,64},{96,80},{112,96},{128,112},... | collective-permute-start | bytes 4616 | tf_op jit(solution)/shard_map/ppermute | solution.py:197
  9.1 0.8 copy.23
  10.2 1.1 broadcast_select_fusion
  12.0 0.7 fusion.13.pool
  12.7 0.8 fusion.17.pool_t
  14.3 0.8 select_convert_fusion.folder
  15.2 1.6 %collective-permute-start.3 = (bf16[128,2048]{1,0:T(8,128)(2,1)S(1)}, bf16[128,2048]{1,0:T(8,128)(2,1)S(1)}, u32[]{:S(2)}, u32[]{:S(2)}) collective-permute-start(bf16[128,2048]{1,0:T(8,128)(2,1)S(1)} %constant_dynamic-update-slice_fusion.b0), channel_id=1, source_target_pairs={{0,4},{1,5},{2,6},{3,7},{4,8},{5,9},{6,10},{7,11},{8,12},{9,13},{1... | collective-permute-start | bytes 1572872 | tf_op jit(solution)/shard_map/ppermute | solution.py:214
  16.8 1.7 %collective-permute-start.2 = (bf16[128,2048]{1,0:T(8,128)(2,1)S(1)}, bf16[128,2048]{1,0:T(8,128)(2,1)S(1)}, u32[]{:S(2)}, u32[]{:S(2)}) collective-permute-start(bf16[128,2048]{1,0:T(8,128)(2,1)S(1)} %constant_dynamic-update-slice_fusion.b0), channel_id=1, source_target_pairs={{0,12},{1,13},{2,14},{3,15},{4,0},{5,1},{6,2},{7,3},{8,4},{9,5},{1... | collective-permute-start | bytes 1572872 | tf_op jit(solution)/shard_map/ppermute | solution.py:215
  19.5 2.0 %collective-permute-start.1 = (bf16[128,2048]{1,0:T(8,128)(2,1)S(1)}, bf16[128,2048]{1,0:T(8,128)(2,1)S(1)}, u32[]{:S(2)}, u32[]{:S(2)}) collective-permute-start(bf16[128,2048]{1,0:T(8,128)(2,1)S(1)} %constant_dynamic-update-slice_fusion.b0), channel_id=1, source_target_pairs={{0,2},{1,3},{2,0},{3,1},{4,6},{5,7},{6,4},{7,5},{8,10},{9,11},{10,... | collective-permute-start | bytes 1572872 | tf_op jit(solution)/shard_map/ppermute | solution.py:213
  22.5 0.8 pad.30.clone
  23.3 7.0 %collective-permute-done.3.bl = bf16[128,2048]{1,0:T(8,128)(2,1)S(1)} collective-permute-done((bf16[128,2048]{1,0:T(8,128)(2,1)S(1)}, bf16[128,2048]{1,0:T(8,128)(2,1)S(1)}, u32[]{:S(2)}, u32[]{:S(2)}) %collective-permute-start.3) | collective-permute-done | bytes 524320 | tf_op jit(solution)/shard_map/ppermute | solution.py:214
  30.8 3.0 %collective-permute-start.7 = (bf16[64,2048]{1,0:T(8,128)(2,1)S(1)}, bf16[64,2048]{1,0:T(8,128)(2,1)}, u32[]{:S(2)}, u32[]{:S(2)}) collective-permute-start(bf16[64,2048]{1,0:T(8,128)(2,1)S(1)} %slice.81), channel_id=1, source_target_pairs={{0,12},{1,13},{2,14},{3,15},{4,0},{5,1},{6,2},{7,3},{8,4},{9,5},{1... | collective-permute-start | bytes 786440 | tf_op jit(solution)/shard_map/ppermute | solution.py:217
  34.0 1.5 %collective-permute-start.4 = (bf16[128,2048]{1,0:T(8,128)(2,1)S(1)}, bf16[128,2048]{1,0:T(8,128)(2,1)}, u32[]{:S(2)}, u32[]{:S(2)}) collective-permute-start(bf16[128,2048]{1,0:T(8,128)(2,1)S(1)} %collective-permute-done.1.bz), channel_id=1, source_target_pairs={{0,12},{1,13},{2,14},{3,15},{4,0},{5,1},{6,2},{7,3},{8,4},{9,5},{1... | collective-permute-start | bytes 1572872 | tf_op jit(solution)/shard_map/ppermute | solution.py:219
  36.7 0.7 copy.27.anch
  37.5 0.9 pad_maximum_fusion.1.wcat
  38.3 1.0 collective-permute-done.6.b2a
  39.3 2.3 %collective-permute-start.8 = (bf16[64,2048]{1,0:T(8,128)(2,1)}, bf16[64,2048]{1,0:T(8,128)(2,1)S(1)}, u32[]{:S(2)}, u32[]{:S(2)}) collective-permute-start(bf16[64,2048]{1,0:T(8,128)(2,1)} %collective-permute-done.6.b2a), channel_id=1, source_target_pairs={{0,2},{1,3},{2,0},{3,1},{4,6},{5,7},{6,4},{7,5},{8,10},{9,11},{10,... | collective-permute-start | bytes 786440 | tf_op jit(solution)/shard_map/ppermute | solution.py:220
  41.6 0.9 collective-permute-start.9
  42.5 14.4 %shard_map.76 = (bf16[576,384]{1,0:T(8,128)(2,1)}, bf16[32,128,384]{2,1,0:T(8,128)(2,1)}, bf16[128,2048]{1,0:T(8,128)(2,1)}, f32[16,128]{1,0:T(8,128)}, f32[32,384]{1,0:T(8,128)}, /*index=5*/bf16[128,1024]{1,0:T(8,128)(2,1)}) custom-call(s32[16]{0:T(128)} %stack.67.blk, bf16[576,384]{1,0:T(8,128)(2,1)} %bitcast.53, f32[32,384]{1,0:T(8,128)} %pad_convert_fusion.mask, ...), custom_call_target="tpu_custom_call" | custom-call | flops 4000000000 | bytes 6000000 | tf_op jit(solution)/shard_map/pallas_call | solution.py:180
  57.8 19.4 %shard_map.77 = (bf16[16,32,128]{2,1,0:T(8,128)(2,1)}, bf16[16,32,128]{2,1,0:T(8,128)(2,1)}, bf16[40,128]{1,0:T(8,128)(2,1)}, bf16[40,128]{1,0:T(8,128)(2,1)}, bf16[96,384]{1,0:T(8,128)(2,1)}) custom-call(s32[16]{0:T(128)} %stack.67.blk, bf16[128,2048]{1,0:T(8,128)(2,1)} %copy-done.2, bf16[128,2048]{1,0:T(8,128)(2,1)} %copy-done.5, ...), custom_call_target="tpu_custom_call" | custom-call | flops 4000000000 | bytes 9000000 | tf_op jit(solution)/shard_map/pallas_call | solution.py:180
  77.2 1.5 %reshape.60 = bf16[16,6,384]{2,1,0:T(8,128)(2,1)} reshape(bf16[96,384]{1,0:T(8,128)(2,1)} %get-tuple-element.24) | data formatting | bytes 147456 | tf_op jit(solution)/shard_map/reshape | solution.py:282
  78.8 5.3 %all-to-all-start.1 = ((bf16[16,6,384]{2,1,0:T(8,128)(2,1)}), bf16[16,6,384]{2,1,0:T(8,128)(2,1)S(1)}, u32[]{:S(2)}, u32[]{:S(2)}) async-start(bf16[16,6,384]{2,1,0:T(8,128)(2,1)} %reshape.60), calls=%async_computation.1 | async-start | bytes 196608 | tf_op jit(solution)/shard_map/all_to_all | solution.py:282
  85.7 0.9 add_convert_fusion
  86.7 0.7 pad_maximum_fusion
  87.4 2.9 %all-to-all-done.1 = bf16[16,6,384]{2,1,0:T(8,128)(2,1)S(1)} async-done(((bf16[16,6,384]{2,1,0:T(8,128)(2,1)}), bf16[16,6,384]{2,1,0:T(8,128)(2,1)S(1)}, u32[]{:S(2)}, u32[]{:S(2)}) %all-to-all-start.1) | async-done | bytes 73760 | tf_op jit(solution)/shard_map/all_to_all | solution.py:282
  90.4 11.6 %all-to-all-start = ((bf16[16,72,128]{2,1,0:T(8,128)(2,1)}), bf16[16,72,128]{2,1,0:T(8,128)(2,1)S(1)}, u32[]{:S(2)}, u32[]{:S(2)}) async-start(bf16[16,72,128]{2,1,0:T(8,128)(2,1)} %pad_maximum_fusion), calls=%async_computation | async-start | bytes 589824 | tf_op jit(solution)/shard_map/all_to_all | solution.py:276
  102.0 4.3 %collective-permute-start.16 = (f32[6,6]{1,0:T(8,128)S(1)}, f32[6,6]{1,0:T(8,128)S(1)}, u32[]{:S(2)}, u32[]{:S(2)}) collective-permute-start(f32[6,6]{1,0:T(8,128)S(1)} %get-tuple-element.41), channel_id=1, source_target_pairs={{0,16},{16,32},{32,48},{48,64},{64,80},{80,96},{96,112},{112,128},... | collective-permute-start | bytes 440 | tf_op jit(solution)/shard_map/ppermute | solution.py:197
  106.3 1.9 %collective-permute-start.17 = (f32[6,6]{1,0:T(8,128)S(1)}, f32[6,6]{1,0:T(8,128)S(1)}, u32[]{:S(2)}, u32[]{:S(2)}) collective-permute-start(f32[6,6]{1,0:T(8,128)S(1)} %get-tuple-element.42), channel_id=1, source_target_pairs={{16,0},{32,16},{48,32},{64,48},{80,64},{96,80},{112,96},{128,112},... | collective-permute-start | bytes 440 | tf_op jit(solution)/shard_map/ppermute | solution.py:197
  108.3 6.5 %collective-permute-done.17 = f32[6,6]{1,0:T(8,128)S(1)} collective-permute-done((f32[6,6]{1,0:T(8,128)S(1)}, f32[6,6]{1,0:T(8,128)S(1)}, u32[]{:S(2)}, u32[]{:S(2)}) %collective-permute-start.17) | collective-permute-done | bytes 176 | tf_op jit(solution)/shard_map/ppermute | solution.py:197
  (89 shorter events, 10.1 us)
Async XLA Ops:
  0.6 17.9 %copy-start = (bf16[3,32,512]{2,1,0:T(8,128)(2,1)S(1)}, bf16[3,32,512]{2,1,0:T(8,128)(2,1)}, u32[]{:S(2)}) copy-start(bf16[3,32,512]{2,1,0:T(8,128)(2,1)} %param.5) | copy-start | bytes 294916
  0.6 18.0 %copy-start.1 = (bf16[1024,64]{0,1:T(8,128)(2,1)S(1)}, bf16[1024,64]{0,1:T(8,128)(2,1)}, u32[]{:S(2)}) copy-start(bf16[1024,64]{0,1:T(8,128)(2,1)} %param.8) | copy-start | bytes 393220
  2.4 17.1 %collective-permute-start.10 = (bf16[4,32,6]{2,1,0:T(8,128)(2,1)S(1)}, bf16[4,32,6]{2,1,0:T(8,128)(2,1)S(1)}, u32[]{:S(2)}, u32[]{:S(2)}) collective-permute-start(bf16[4,32,6]{2,1,0:T(8,128)(2,1)S(1)} %get-tuple-element.36), channel_id=1, source_target_pairs={{0,16},{16,32},{32,48},{48,64},{64,80},{80,96},{96,112},{112,128},... | collective-permute-start | bytes 4616 | tf_op jit(solution)/shard_map/ppermute | solution.py:197
  7.2 12.3 %collective-permute-start.11 = (bf16[4,32,6]{2,1,0:T(8,128)(2,1)S(1)}, bf16[4,32,6]{2,1,0:T(8,128)(2,1)S(1)}, u32[]{:S(2)}, u32[]{:S(2)}) collective-permute-start(bf16[4,32,6]{2,1,0:T(8,128)(2,1)S(1)} %get-tuple-element.35), channel_id=1, source_target_pairs={{16,0},{32,16},{48,32},{64,48},{80,64},{96,80},{112,96},{128,112},... | collective-permute-start | bytes 4616 | tf_op jit(solution)/shard_map/ppermute | solution.py:197
  10.0 23.8 %collective-permute-start.12 = (bf16[64,80]{0,1:T(8,128)(2,1)S(1)}, bf16[64,80]{0,1:T(8,128)(2,1)S(1)}, u32[]{:S(2)}, u32[]{:S(2)}) collective-permute-start(bf16[64,80]{0,1:T(8,128)(2,1)S(1)} %bitcast.57), channel_id=1, source_target_pairs={{0,1},{1,0},{2,3},{3,2},{4,5},{5,4},{6,7},{7,6},{8,9},{9,8},{10,11... | collective-permute-start | bytes 30728 | tf_op jit(solution)/shard_map/ppermute | solution.py:237
  11.3 3.9 %collective-permute-start = (bf16[64,2048]{1,0:T(8,128)(2,1)S(1)}, bf16[64,2048]{1,0:T(8,128)(2,1)S(1)}, u32[]{:S(2)}, u32[]{:S(2)}) collective-permute-start(bf16[64,2048]{1,0:T(8,128)(2,1)S(1)} %bitcast.55), channel_id=1, source_target_pairs={{0,1},{1,0},{2,3},{3,2},{4,5},{5,4},{6,7},{7,6},{8,9},{9,8},{10,11... | collective-permute-start | bytes 786440 | tf_op jit(solution)/shard_map/ppermute | solution.py:212
  15.2 41.7 %copy-start.2 = (bf16[128,2048]{1,0:T(8,128)(2,1)}, bf16[128,2048]{1,0:T(8,128)(2,1)S(1)}, u32[]{:S(2)}) copy-start(bf16[128,2048]{1,0:T(8,128)(2,1)S(1)} %constant_dynamic-update-slice_fusion.b0) | copy-start | bytes 1572868
  15.2 15.2 %collective-permute-start.3 = (bf16[128,2048]{1,0:T(8,128)(2,1)S(1)}, bf16[128,2048]{1,0:T(8,128)(2,1)S(1)}, u32[]{:S(2)}, u32[]{:S(2)}) collective-permute-start(bf16[128,2048]{1,0:T(8,128)(2,1)S(1)} %constant_dynamic-update-slice_fusion.b0), channel_id=1, source_target_pairs={{0,4},{1,5},{2,6},{3,7},{4,8},{5,9},{6,10},{7,11},{8,12},{9,13},{1... | collective-permute-start | bytes 1572872 | tf_op jit(solution)/shard_map/ppermute | solution.py:214
  16.8 14.0 %collective-permute-start.2 = (bf16[128,2048]{1,0:T(8,128)(2,1)S(1)}, bf16[128,2048]{1,0:T(8,128)(2,1)S(1)}, u32[]{:S(2)}, u32[]{:S(2)}) collective-permute-start(bf16[128,2048]{1,0:T(8,128)(2,1)S(1)} %constant_dynamic-update-slice_fusion.b0), channel_id=1, source_target_pairs={{0,12},{1,13},{2,14},{3,15},{4,0},{5,1},{6,2},{7,3},{8,4},{9,5},{1... | collective-permute-start | bytes 1572872 | tf_op jit(solution)/shard_map/ppermute | solution.py:215
  19.5 18.0 %collective-permute-start.13 = (bf16[1024,64]{1,0:T(8,128)(2,1)S(1)}, bf16[1024,64]{1,0:T(8,128)(2,1)S(1)}, u32[]{:S(2)}, u32[]{:S(2)}) collective-permute-start(bf16[1024,64]{1,0:T(8,128)(2,1)S(1)} %copy.26), channel_id=1, source_target_pairs={{0,1},{1,0},{2,3},{3,2},{4,5},{5,4},{6,7},{7,6},{8,9},{9,8},{10,11... | collective-permute-start | bytes 393224 | tf_op jit(solution)/shard_map/ppermute | solution.py:238
  19.5 14.5 %collective-permute-start.1 = (bf16[128,2048]{1,0:T(8,128)(2,1)S(1)}, bf16[128,2048]{1,0:T(8,128)(2,1)S(1)}, u32[]{:S(2)}, u32[]{:S(2)}) collective-permute-start(bf16[128,2048]{1,0:T(8,128)(2,1)S(1)} %constant_dynamic-update-slice_fusion.b0), channel_id=1, source_target_pairs={{0,2},{1,3},{2,0},{3,1},{4,6},{5,7},{6,4},{7,5},{8,10},{9,11},{10,... | collective-permute-start | bytes 1572872 | tf_op jit(solution)/shard_map/ppermute | solution.py:213
  30.4 26.6 %copy-start.3 = (bf16[128,2048]{1,0:T(8,128)(2,1)}, bf16[128,2048]{1,0:T(8,128)(2,1)S(1)}, u32[]{:S(2)}) copy-start(bf16[128,2048]{1,0:T(8,128)(2,1)S(1)} %collective-permute-done.3.bl) | copy-start | bytes 1572868
  30.4 8.9 %collective-permute-start.6 = (bf16[64,2048]{1,0:T(8,128)(2,1)S(1)}, bf16[64,2048]{1,0:T(8,128)(2,1)}, u32[]{:S(2)}, u32[]{:S(2)}) collective-permute-start(bf16[64,2048]{1,0:T(8,128)(2,1)S(1)} %slice.80), channel_id=1, source_target_pairs={{0,4},{1,5},{2,6},{3,7},{4,8},{5,9},{6,10},{7,11},{8,12},{9,13},{1... | collective-permute-start | bytes 786440 | tf_op jit(solution)/shard_map/ppermute | solution.py:216
  30.8 26.2 %copy-start.4 = (bf16[128,2048]{1,0:T(8,128)(2,1)}, bf16[128,2048]{1,0:T(8,128)(2,1)S(1)}, u32[]{:S(2)}) copy-start(bf16[128,2048]{1,0:T(8,128)(2,1)S(1)} %collective-permute-done.2.br) | copy-start | bytes 1572868
  30.8 10.8 %collective-permute-start.7 = (bf16[64,2048]{1,0:T(8,128)(2,1)S(1)}, bf16[64,2048]{1,0:T(8,128)(2,1)}, u32[]{:S(2)}, u32[]{:S(2)}) collective-permute-start(bf16[64,2048]{1,0:T(8,128)(2,1)S(1)} %slice.81), channel_id=1, source_target_pairs={{0,12},{1,13},{2,14},{3,15},{4,0},{5,1},{6,2},{7,3},{8,4},{9,5},{1... | collective-permute-start | bytes 786440 | tf_op jit(solution)/shard_map/ppermute | solution.py:217
  34.0 22.9 %copy-start.5 = (bf16[128,2048]{1,0:T(8,128)(2,1)}, bf16[128,2048]{1,0:T(8,128)(2,1)S(1)}, u32[]{:S(2)}) copy-start(bf16[128,2048]{1,0:T(8,128)(2,1)S(1)} %collective-permute-done.1.bz) | copy-start | bytes 1572868
  34.0 23.0 %collective-permute-start.4 = (bf16[128,2048]{1,0:T(8,128)(2,1)S(1)}, bf16[128,2048]{1,0:T(8,128)(2,1)}, u32[]{:S(2)}, u32[]{:S(2)}) collective-permute-start(bf16[128,2048]{1,0:T(8,128)(2,1)S(1)} %collective-permute-done.1.bz), channel_id=1, source_target_pairs={{0,12},{1,13},{2,14},{3,15},{4,0},{5,1},{6,2},{7,3},{8,4},{9,5},{1... | collective-permute-start | bytes 1572872 | tf_op jit(solution)/shard_map/ppermute | solution.py:219
  35.6 21.5 %collective-permute-start.5 = (bf16[128,2048]{1,0:T(8,128)(2,1)S(1)}, bf16[128,2048]{1,0:T(8,128)(2,1)}, u32[]{:S(2)}, u32[]{:S(2)}) collective-permute-start(bf16[128,2048]{1,0:T(8,128)(2,1)S(1)} %collective-permute-done.1.bz), channel_id=1, source_target_pairs={{0,4},{1,5},{2,6},{3,7},{4,8},{5,9},{6,10},{7,11},{8,12},{9,13},{1... | collective-permute-start | bytes 1572872 | tf_op jit(solution)/shard_map/ppermute | solution.py:218
  39.3 17.7 %collective-permute-start.8 = (bf16[64,2048]{1,0:T(8,128)(2,1)}, bf16[64,2048]{1,0:T(8,128)(2,1)S(1)}, u32[]{:S(2)}, u32[]{:S(2)}) collective-permute-start(bf16[64,2048]{1,0:T(8,128)(2,1)} %collective-permute-done.6.b2a), channel_id=1, source_target_pairs={{0,2},{1,3},{2,0},{3,1},{4,6},{5,7},{6,4},{7,5},{8,10},{9,11},{10,... | collective-permute-start | bytes 786440 | tf_op jit(solution)/shard_map/ppermute | solution.py:220
  41.6 15.4 %collective-permute-start.9 = (bf16[64,2048]{1,0:T(8,128)(2,1)}, bf16[64,2048]{1,0:T(8,128)(2,1)S(1)}, u32[]{:S(2)}, u32[]{:S(2)}) collective-permute-start(bf16[64,2048]{1,0:T(8,128)(2,1)} %collective-permute-done.7.b2b), channel_id=1, source_target_pairs={{0,2},{1,3},{2,0},{3,1},{4,6},{5,7},{6,4},{7,5},{8,10},{9,11},{10,... | collective-permute-start | bytes 786440 | tf_op jit(solution)/shard_map/ppermute | solution.py:221
  57.0 0.7 copy-start.6
  57.0 0.8 copy-start.7
  77.2 7.3 %collective-permute-start.15 = (bf16[40,128]{1,0:T(8,128)(2,1)}, bf16[40,128]{1,0:T(8,128)(2,1)S(1)}, u32[]{:S(2)}, u32[]{:S(2)}) collective-permute-start(bf16[40,128]{1,0:T(8,128)(2,1)} %get-tuple-element.23), channel_id=1, source_target_pairs={{0,1},{1,0},{2,3},{3,2},{4,5},{5,4},{6,7},{7,6},{8,9},{9,8},{10,11... | collective-permute-start | bytes 30728 | tf_op jit(solution)/shard_map/ppermute | solution.py:274
  78.8 11.6 %all-to-all-start.1 = ((bf16[16,6,384]{2,1,0:T(8,128)(2,1)}), bf16[16,6,384]{2,1,0:T(8,128)(2,1)S(1)}, u32[]{:S(2)}, u32[]{:S(2)}) async-start(bf16[16,6,384]{2,1,0:T(8,128)(2,1)} %reshape.60), calls=%async_computation.1 | async-start | bytes 196608 | tf_op jit(solution)/shard_map/all_to_all | solution.py:282
  84.0 1.6 %collective-permute-start.14 = (bf16[16,32,128]{2,1,0:T(8,128)(2,1)}, bf16[16,32,128]{2,1,0:T(8,128)(2,1)S(1)}, u32[]{:S(2)}, u32[]{:S(2)}) collective-permute-start(bf16[16,32,128]{2,1,0:T(8,128)(2,1)} %get-tuple-element.21), channel_id=1, source_target_pairs={{0,1},{1,0},{2,3},{3,2},{4,5},{5,4},{6,7},{7,6},{8,9},{9,8},{10,11... | collective-permute-start | bytes 393224 | tf_op jit(solution)/shard_map/ppermute | solution.py:273
  90.4 25.1 %all-to-all-start = ((bf16[16,72,128]{2,1,0:T(8,128)(2,1)}), bf16[16,72,128]{2,1,0:T(8,128)(2,1)S(1)}, u32[]{:S(2)}, u32[]{:S(2)}) async-start(bf16[16,72,128]{2,1,0:T(8,128)(2,1)} %pad_maximum_fusion), calls=%async_computation | async-start | bytes 589824 | tf_op jit(solution)/shard_map/all_to_all | solution.py:276
  102.0 6.3 %collective-permute-start.16 = (f32[6,6]{1,0:T(8,128)S(1)}, f32[6,6]{1,0:T(8,128)S(1)}, u32[]{:S(2)}, u32[]{:S(2)}) collective-permute-start(f32[6,6]{1,0:T(8,128)S(1)} %get-tuple-element.41), channel_id=1, source_target_pairs={{0,16},{16,32},{32,48},{48,64},{64,80},{80,96},{96,112},{112,128},... | collective-permute-start | bytes 440 | tf_op jit(solution)/shard_map/ppermute | solution.py:197
  106.3 8.5 %collective-permute-start.17 = (f32[6,6]{1,0:T(8,128)S(1)}, f32[6,6]{1,0:T(8,128)S(1)}, u32[]{:S(2)}, u32[]{:S(2)}) collective-permute-start(f32[6,6]{1,0:T(8,128)S(1)} %get-tuple-element.42), channel_id=1, source_target_pairs={{16,0},{32,16},{48,32},{64,48},{80,64},{96,80},{112,96},{128,112},... | collective-permute-start | bytes 440 | tf_op jit(solution)/shard_map/ppermute | solution.py:197
where the time goes:
time: 119 us; the launch traced here: 117 us
  starting transfers between devices  44.8 us (38%)
  Pallas kernels  33.9 us (28%)
  waiting for transfers between devices  18.2 us (15%)
  other arithmetic  11.6 us (10%)
  local copies, waits for them, and re-layouts  7.58 us (6%)
    pallas_call x2, Pallas kernels, call(): pl.pallas_call(kernel, out_shape=[jax.ShapeDtypeStruct(shape, dtype) for...  33.9 us
    ppermute x4, starting transfers between devices, neighbours(): return (lax.ppermute(last, axis, up), lax.ppermute(first, axis, down))  12.9 us
    all_to_all x1, starting transfers between devices, shards(): summed = jnp.sum(lax.all_to_all(packed, 'space', 0, 0).astype(f32), axis=0)  11.6 us
    ppermute x1, waiting for transfers between devices, shards(): bl = lax.ppermute(b0, 'chan', RIGHT)  7.05 us
    ppermute x4, waiting for transfers between devices, neighbours(): return (lax.ppermute(last, axis, up), lax.ppermute(first, axis, down))  6.51 us
    all_to_all x1, starting transfers between devices, shards(): parts = lax.all_to_all(image_part.reshape(16, 6, LANES), 'chan', 0, 0)  5.28 us
    ppermute x1, starting transfers between devices, shards(): b2b = lax.ppermute(br[OWN:], 'chan', LEFT)  3.03 us
    all_to_all x1, waiting for transfers between devices, shards(): parts = lax.all_to_all(image_part.reshape(16, 6, LANES), 'chan', 0, 0)  2.95 us
  transfers between devices with their start and end apart: 20, of which 6 were waited for; matrix products, arithmetic and copies ran while one was open for 13% of the time, Pallas kernels for 12%

commit v1 on v0

v1 whole, which is shorter than its diff:
```python
import math

import jax
import jax.numpy as jnp
import ml_dtypes
import numpy as np
from jax import lax
from jax.experimental import pallas as pl
from jax.experimental.pallas import tpu as pltpu
from jax.sharding import PartitionSpec as P

EPS = 1e-05
LANES = 384
HALF = 128
ROWS = 32
GROUP = 16
OWN = 64
STEP = 4
VMEM = 56 * 1024 * 1024

CHIPS = ((0, 0), (0, 1), (1, 0), (3, 0), (1, 1), (3, 1), (2, 0), (2, 1))


def route(dx, dz, core):
    return [(i, ((i // 4 + dx) % 4) * 4 + ((i // 2) % 2 ^ dz) * 2 + (i % 2 ^ core)) for i in range(16)]


f32 = jnp.float32
bf16 = jnp.bfloat16


def tap(distance):
    return math.exp(-distance * distance / 8.0) if abs(distance) <= 4 else 0.0


def as_bf16(array):
    return array.astype(ml_dtypes.bfloat16)


def column_pool():
    return np.array([[tap(2 * b - l + 4) for b in range(HALF)] for l in range(LANES)], np.float32)


def row_pool():
    return np.array([[tap(2 * a - i) for i in range(ROWS)] for a in range(ROWS // 2)], np.float32)


def replicate_rows():
    out = np.zeros((36, GROUP, 3, ROWS), np.float32)
    for i in range(ROWS):
        for q in range(15):
            out[i + 2, q, q // 5, i] = 1.0
    return out.reshape(36 * GROUP, 96)


def fold_rows():
    out = np.zeros((128, 36, GROUP), np.float32)
    for i in range(ROWS):
        for q in range(15):
            out[8 * (i // 2) + 2 * (q // 5) + i % 2, i + 2, q] = 1.0
    return out.reshape(128, 36 * GROUP)


def entry_order():
    out = np.zeros((75, 80), np.float32)
    for c in range(3):
        for a in range(5):
            for b in range(5):
                out[25 * c + 5 * a + b, GROUP * a + 5 * c + b] = 1.0
    return out


def block_of(p):
    chan = lax.axis_index("chan")
    dx, dz = CHIPS[p // 2]
    ex = lax.rem(chan // 4 + dx, 4)
    zed = lax.rem(chan // 2 + dz, 2)
    core = lax.rem(chan + p % 2, 2)
    return ex * 4 + zed * 2 + core


def dot(a, b):
    return jnp.dot(a, b, preferred_element_type=f32)


def dot_nt(a, b):
    return lax.dot_general(a, b, (((1,), (1,)), ((), ())), preferred_element_type=f32)


def forward_kernel(
    image, mask, before, after, anch_own, anch_partner, w_own, w_partner, pool, rows, repeat, order,
    patches, masked, whitened, inv_density, inv_square, wturned, anch_t,
    scale, norm, tissue, columned,
):
    second = lax.rem(lax.axis_index("chan"), 2) == 1

    def half(left, middle, right, shift):
        wide = jnp.concatenate([left, middle, right], axis=1)
        part = jnp.where(second, wide[:, 256:], wide[:, :512])
        return pltpu.roll(part, 512 - shift, 1)[:, :LANES]

    colours = [
        half(before[c].astype(f32), image[c].astype(f32), after[c].astype(f32), 122) for c in range(3)
    ]
    here = half(before[3].astype(f32), mask[...].astype(f32), after[3].astype(f32), 124)
    lane = lax.broadcasted_iota(jnp.int32, here.shape, 1)
    here = jnp.where(lane < 263, here, 0.0)
    tissue[...] = here
    x = dot(repeat[...], jnp.concatenate(colours, axis=0).astype(bf16))
    offset = (lax.broadcasted_iota(jnp.int32, x.shape, 0) % GROUP) % 5
    s = x
    for b in range(1, 5):
        s = jnp.where(offset == b, pltpu.roll(x, LANES - b, 1), s)
    patches[...] = s.astype(bf16)
    square = jnp.sum((s * s).reshape(36, GROUP, LANES), axis=1)
    total = square[0:ROWS]
    for a in range(1, 5):
        total = total + square[a : a + ROWS]
    total = total + EPS
    root = lax.rsqrt(total)
    scale[...] = 4.0 * root
    norm[...] = total * root
    inv_square[...] = 1.0 / total
    counted = dot(here.astype(bf16), pool[...])
    density = jnp.dot(rows[...], counted, precision=lax.Precision.HIGHEST, preferred_element_type=f32)
    inv_density[...] = 1.0 / jnp.maximum(density, 1.0)
    both = jnp.concatenate([anch_own[...], anch_partner[...]], axis=0)
    anch = dot(both, order[...]).astype(bf16)
    anch_t[...] = anch.astype(f32).T.astype(bf16)

    @pl.loop(0, ROWS // STEP)
    def _(t):
        lifted = []
        for r in range(STEP):
            i = t * STEP + r
            patch = patches[pl.ds(pl.multiple_of(i * GROUP, GROUP), 80), :]
            raw = dot(anch, patch)
            value = jnp.exp(raw * scale[pl.ds(i, 1), :] - 4.0) * tissue[pl.ds(i, 1), :]
            masked[i] = value.astype(bf16)
            lifted.append((value * norm[pl.ds(i, 1), :]).astype(bf16))
        result = dot(jnp.concatenate(lifted, axis=0), pool[...])
        columned[pl.ds(t * STEP, STEP)] = result.reshape(STEP, 128, HALF)

    for a in range(ROWS // 2):
        acc = None
        for i in range(max(0, 2 * a - 4), min(ROWS, 2 * a + 5)):
            term = tap(2 * a - i) * columned[i]
            acc = term if acc is None else acc + term
        whitened[:, a * HALF : (a + 1) * HALF] = (acc * inv_density[a : a + 1, :]).astype(bf16)

    blocks = [pl.ds(pl.multiple_of(block_of(p) * OWN, OWN), OWN) for p in range(16)]
    for at, weights in ((0, w_own), (OWN, w_partner)):
        ordered = jnp.concatenate([weights[block, :] for block in blocks], axis=0)
        wturned[at : at + OWN, :] = ordered.astype(f32).T.astype(bf16)


def fold(block, rows):
    top, low = block[:rows], block[rows:]
    left = lax.broadcasted_iota(jnp.int32, top.shape, 1) < OWN
    own = jnp.where(left, top, pltpu.roll(low, OWN, 1))
    partner = jnp.where(left, pltpu.roll(top, OWN, 1), low)
    return own.astype(bf16), partner.astype(bf16)


def backward_kernel(*refs):
    blocks = refs[:16]
    (
        wturned, whitened, inv_density, masked, patches, inv_square, anch_t, pool_t, folder,
        own, partner, image,
        rowed, spread_grad, anchor_grad,
    ) = refs[16:]
    grad_w = None
    pooled = []
    for n in range(8):
        cols = pl.ds(n * 256, 256)
        stack = jnp.concatenate([block[:, cols] for block in blocks], axis=0)
        pooled.append(dot(wturned[...], stack))
        term = dot_nt(stack, whitened[:, cols])
        grad_w = term if grad_w is None else grad_w + term
    for p in range(16):
        mine, theirs = fold(grad_w[p * OWN : (p + 1) * OWN], OWN // 2)
        rows = pl.ds(pl.multiple_of(block_of(p) * 32, 32), 32)
        own[rows, :] = mine
        partner[rows, :] = theirs
    scaled = []
    for a in range(ROWS // 2):
        part = pooled[a // 2][:, (a % 2) * HALF : (a % 2 + 1) * HALF]
        scaled.append(part.astype(bf16).astype(f32) * inv_density[a : a + 1, :])
    for i in range(ROWS):
        acc = None
        for a in range(ROWS // 2):
            if abs(2 * a - i) <= 4:
                term = (4.0 * tap(2 * a - i)) * scaled[a]
                acc = term if acc is None else acc + term
        rowed[i * 128 : (i + 1) * 128, :] = acc.astype(bf16)
    spread_grad[...] = jnp.zeros_like(spread_grad)
    anchor_grad[...] = jnp.zeros_like(anchor_grad)

    @pl.loop(0, ROWS // STEP)
    def _(t):
        start = pl.multiple_of(t * (STEP * 128), STEP * 128)
        spread = dot(rowed[pl.ds(start, STEP * 128), :], pool_t[...])
        grads, wides, units = [], [], []
        for r in range(STEP):
            i = t * STEP + r
            patch = patches[pl.ds(pl.multiple_of(i * GROUP, GROUP), 80), :]
            grad = (spread[r * 128 : (r + 1) * 128] * masked[i].astype(f32)).astype(bf16)
            unit = dot(anch_t[...], grad)
            wide = patch.astype(f32)
            along = jnp.sum(wide * unit, axis=0, keepdims=True) * inv_square[pl.ds(i, 1), :]
            units.append(unit - wide * along)
            grads.append(grad)
            wides.append(patch)
        anchor_grad[...] += dot_nt(jnp.concatenate(wides, axis=1), jnp.concatenate(grads, axis=1))
        sums = []
        for g in range(STEP + 4):
            acc = None
            for r in range(STEP):
                if 0 <= g - r < 5:
                    term = units[r][(g - r) * GROUP : (g - r + 1) * GROUP]
                    acc = term if acc is None else acc + term
            sums.append(acc)
        here = pl.ds(pl.multiple_of(t * (STEP * GROUP), STEP * GROUP), (STEP + 4) * GROUP)
        spread_grad[here, :] += jnp.concatenate(sums, axis=0)

    mine, theirs = fold(anchor_grad[...], 40)
    own[512:552, :] = mine
    partner[512:552, :] = theirs
    own[552:560, :] = jnp.zeros((8, 128), bf16)
    partner[552:560, :] = jnp.zeros((8, 128), bf16)
    t = spread_grad[...]
    offset = (lax.broadcasted_iota(jnp.int32, t.shape, 0) % GROUP) % 5
    moved = t
    for b in range(1, 5):
        moved = jnp.where(offset == b, pltpu.roll(t, b, 1), moved)
    high = moved.astype(bf16)
    low = (moved - high.astype(f32)).astype(bf16)
    image[...] = (dot(folder[...], high) + dot(folder[...], low)).astype(bf16)


def pack_kernel(own, partner, parts, packed, middle):
    space = lax.axis_index("space")
    total = (own[...].astype(f32) + partner[...].astype(f32)).astype(bf16)
    halves = []
    for k in range(2):
        acc = parts[k].astype(f32)
        for chip in range(1, 8):
            acc = acc + parts[2 * chip + k].astype(f32)
        halves.append(acc)
    gap = jnp.zeros((8, 256), f32)
    whole = jnp.concatenate([halves[0], gap], axis=1) + jnp.concatenate([gap, halves[1]], axis=1)
    turned = pltpu.roll(whole, 640 - 6, 1)
    middle[...] = turned[:, :512]
    rims = turned[:, 512:]
    lane = lax.broadcasted_iota(jnp.int32, rims.shape, 1)
    for strip in range(16):
        to_next = jnp.where(space + 1 == strip, jnp.where(lane < 6, rims, 0.0), 0.0)
        to_last = jnp.where(space - 1 == strip, jnp.where(lane >= 122, rims, 0.0), 0.0)
        tail = jnp.concatenate([total[512:552].astype(f32), to_next + to_last], axis=0)
        packed[strip, 0:32, :] = total[strip * 32 : (strip + 1) * 32]
        packed[strip, 32:80, :] = tail.astype(bf16)


def unpack_kernel(received, middle, order, grad_anchors, grad_whiten, grad_image):
    total = received[0].astype(f32)
    for strip in range(1, 16):
        total = total + received[strip].astype(f32)
    other = pltpu.roll(total, OWN, 1)
    grad_whiten[0:32, :] = total[0:32, :OWN]
    grad_whiten[32:64, :] = other[0:32, :OWN]
    turned = jnp.concatenate([total[32:72], other[32:72]], axis=0).T[:OWN]
    grad_anchors[...] = lax.dot_general(
        turned, order[...], (((1,), (1,)), ((), ())),
        precision=lax.Precision.HIGHEST, preferred_element_type=f32,
    )
    rims = total[72:80]
    lane = lax.broadcasted_iota(jnp.int32, rims.shape, 1)
    first = jnp.where(lane < 6, rims, 0.0)
    last = jnp.where(lane >= 122, rims, 0.0)
    gap = jnp.zeros((8, 256), f32)
    image = middle[...] + jnp.concatenate([first, gap, last], axis=1)
    for colour in range(3):
        grad_image[colour] = image[2 * colour : 2 * colour + 2]


def call(kernel, outs, scratch, flops, *args):
    size = lambda shape, dtype: math.prod(shape) * jnp.dtype(dtype).itemsize
    moved = sum(size(a.shape, a.dtype) for a in args) + sum(size(*out) for out in outs)
    return pl.pallas_call(
        kernel,
        out_shape=[jax.ShapeDtypeStruct(shape, dtype) for shape, dtype in outs],
        in_specs=[pl.BlockSpec(memory_space=pltpu.VMEM)] * len(args),
        out_specs=[pl.BlockSpec(memory_space=pltpu.VMEM)] * len(outs),
        scratch_shapes=[pltpu.VMEM(shape, dtype) for shape, dtype in scratch],
        compiler_params=pltpu.CompilerParams(vmem_limit_bytes=VMEM),
        cost_estimate=pl.CostEstimate(flops=flops, bytes_accessed=moved, transcendentals=0),
    )(*args)


def shards(image, mask, anchors, whiten, cotangent):
    core = lax.axis_index("chan") % 2

    def send(value, dx, dz, other):
        return lax.ppermute(value, "chan", route(dx, dz, other))

    left, right = cotangent[:, :, :HALF], cotangent[:, :, HALF:]
    own = jnp.where(core == 0, left, right).reshape(OWN, -1)
    away = jnp.where(core == 0, right, left).reshape(OWN, -1)
    held = {(0, 0): (own, send(away, 0, 0, 1))}
    for dx, dz in ((1, 0), (3, 0), (0, 1)):
        held[(4 - dx) % 4, dz] = (send(own, dx, dz, 0), send(away, dx, dz, 1))
    far_own = send(held[0, 1][0], 1, 0, 0)
    far_partner = send(held[0, 1][1], 3, 0, 0)
    held[3, 1] = (far_own, send(held[3, 0][1], 0, 1, 0))
    held[1, 1] = (send(held[1, 0][0], 0, 1, 0), far_partner)
    held[2, 0] = (send(held[3, 0][0], 1, 0, 0), send(held[1, 0][1], 3, 0, 0))
    held[2, 1] = (send(far_own, 1, 0, 0), send(far_partner, 3, 0, 0))
    blocks = [block for chip in CHIPS for block in held[chip]]

    width = mask.shape[1]
    tiles = [
        jnp.concatenate([image[:, :, part], mask[None, :, part].astype(bf16)], axis=0)
        for part in (slice(0, 128), slice(width - 128, width))
    ]
    count = lax.axis_size("space")
    before = lax.ppermute(tiles[1], "space", [(i, i + 1) for i in range(count - 1)])
    after = lax.ppermute(tiles[0], "space", [(i + 1, i) for i in range(count - 1)])

    pool = as_bf16(column_pool())
    order = entry_order()
    patches, masked, whitened, inv_density, inv_square, wturned, anch_t = call(
        forward_kernel,
        [
            ((36 * GROUP, LANES), bf16),
            ((ROWS, 128, LANES), bf16),
            ((128, 16 * HALF), bf16),
            ((16, HALF), f32),
            ((ROWS, LANES), f32),
            ((128, 1024), bf16),
            ((80, 128), bf16),
        ],
        [
            ((ROWS, LANES), f32),
            ((ROWS, LANES), f32),
            ((ROWS, LANES), f32),
            ((ROWS, 128, HALF), f32),
        ],
        6_000_000_000,
        image, mask, before, after, anchors, send(anchors, 0, 0, 1), whiten, send(whiten, 0, 0, 1),
        jnp.asarray(pool), jnp.asarray(row_pool()),
        jnp.asarray(as_bf16(replicate_rows())), jnp.asarray(as_bf16(order)),
    )
    mine, theirs, image_part = call(
        backward_kernel,
        [((560, 128), bf16), ((560, 128), bf16), ((128, LANES), bf16)],
        [((ROWS * 128, HALF), bf16), ((36 * GROUP, LANES), f32), ((80, 128), f32)],
        6_000_000_000,
        *blocks,
        wturned, whitened, inv_density, masked, patches, inv_square, anch_t,
        jnp.asarray(pool.T.copy()), jnp.asarray(as_bf16(fold_rows())),
    )

    parts = lax.all_to_all(image_part.reshape(16, 8, LANES), "chan", 0, 0)
    packed, middle = call(
        pack_kernel,
        [((16, 80, 128), bf16), ((8, 512), f32)],
        [],
        1_000_000,
        mine, send(theirs, 0, 0, 1), parts,
    )
    received = lax.all_to_all(packed, "space", 0, 0)
    return call(
        unpack_kernel,
        [((OWN, 75), f32), ((OWN, OWN), f32), ((3, 2, 512), f32)],
        [],
        1_000_000,
        received, middle, jnp.asarray(order),
    )


def solution(mesh):
    placed = (
        P(None, None, "space"),
        P(None, "space"),
        P("chan", None),
        P(None, "chan"),
        P("chan", None, "space"),
    )
    return jax.shard_map(
        lambda *args: tuple(shards(*args)),
        mesh=mesh,
        in_specs=placed,
        out_specs=(P("chan", None), P("space", "chan"), P(None, "chan", "space")),
        check_vma=False,
    )
```

time: 119 us -> 104 us (0.87)
  blocking collectives: 0 us -> 23.7 us
  starting transfers between devices: 44.8 us -> 28.4 us
  other arithmetic: 11.6 us -> 1.93 us
  Pallas kernels: 33.9 us -> 24.9 us
  local copies, waits for them, and re-layouts: 7.58 us -> 3.73 us
    all_to_all x0 -> x1, blocking collectives: none -> 23.7 us  [shards(): received = lax.all_to_all(packed, 'space', 0, 0)]
    all_to_all x2 -> x1, starting transfers between devices: 16.8 us -> 3.51 us  [shards(): parts = lax.all_to_all(image_part.reshape(16, 8, LANES), 'chan', 0, 0)]
    pallas_call x2 -> x4, Pallas kernels: 33.9 us -> 24.9 us  [call(): pl.pallas_call(kernel, out_shape=[jax.ShapeDtypeStruct(shape, dtype) for...]
    convert_element_type x6 -> x0, other arithmetic: 4.63 us -> none  [the longest x2 1.51 us: column_pool(): jnp.where(jnp.abs(distance) <= 4.0, jnp.exp(-distance * distance / 8.0),...]
    concatenate x7 -> x2, other arithmetic: 3.23 us -> 0.01 us  [shards(): jnp.concatenate([image[:, :, part], mask[None, :, part].astype(bf16)], ax...]
    ppermute x18 -> x20, starting transfers between devices: 27.9 us -> 24.9 us  [the longest x18 18.2 us: send(): return lax.ppermute(value, 'chan', route(dx, dz, other))]
    reshape x6 -> x0, local copies, waits for them, and re-layouts: 2.23 us -> none  [the longest x1 1.55 us: shards(): parts = lax.all_to_all(image_part.reshape(16, 6, LANES), 'chan', 0, 0)]
    all_to_all x2 -> x1, waiting for transfers between devices: 2.95 us -> 4.61 us  [shards(): parts = lax.all_to_all(image_part.reshape(16, 8, LANES), 'chan', 0, 0)]
  transfers between devices with their start and end apart: 20 -> 21, of which waited for: 6 -> 8; matrix products, arithmetic and copies ran while one was open for 13% -> 4% of each run, Pallas kernels for 12% -> 9%
where the time goes in v1:
time: 104 us; the launch traced here: 102 us
  starting transfers between devices  28.4 us (27%)
  Pallas kernels  24.9 us (24%)
  blocking collectives  23.7 us (23%)
  waiting for transfers between devices  18.8 us (18%)
  local copies, waits for them, and re-layouts  3.73 us (4%)
  other arithmetic  1.93 us (2%)
    pallas_call x4, Pallas kernels, call(): pl.pallas_call(kernel, out_shape=[jax.ShapeDtypeStruct(shape, dtype) for...  24.9 us
    all_to_all x1, blocking collectives, shards(): received = lax.all_to_all(packed, 'space', 0, 0)  23.7 us
    ppermute x18, starting transfers between devices, send(): return lax.ppermute(value, 'chan', route(dx, dz, other))  18.2 us
    ppermute x18, waiting for transfers between devices, send(): return lax.ppermute(value, 'chan', route(dx, dz, other))  14.2 us
    ppermute x1, starting transfers between devices, shards(): lax.ppermute(tiles[1], 'space', [(i, i + 1) for i in range(count - 1)])  4.84 us
    all_to_all x1, waiting for transfers between devices, shards(): parts = lax.all_to_all(image_part.reshape(16, 8, LANES), 'chan', 0, 0)  4.61 us
    all_to_all x1, starting transfers between devices, shards(): parts = lax.all_to_all(image_part.reshape(16, 8, LANES), 'chan', 0, 0)  3.51 us
    unnamed x49, local copies, waits for them, and re-layouts  2.96 us
  transfers between devices with their start and end apart: 21, of which 8 were waited for; matrix products, arithmetic and copies ran while one was open for 4% of the time, Pallas kernels for 9%

profile of v1, /device:TPU:24, one launch (start us, length us, event | category | flops | bytes accessed | tf_op | source)
XLA Modules:
  0.0 102.4 jit_solution(10522143691222140980)
XLA Ops:
  0.7 0.8 convert.4
  1.6 0.8 fusion
  2.4 4.8 %collective-permute-start.15 = (bf16[4,32,128]{2,1,0:T(8,128)(2,1)S(1)}, bf16[4,32,128]{2,1,0:T(8,128)(2,1)S(1)}, u32[]{:S(2)}, u32[]{:S(2)}) collective-permute-start(bf16[4,32,128]{2,1,0:T(8,128)(2,1)S(1)} %pad_maximum_fusion), channel_id=1, source_target_pairs={{0,16},{16,32},{32,48},{48,64},{64,80},{80,96},{96,112},{112,128},... | collective-permute-start | bytes 98312 | tf_op jit(solution)/shard_map/ppermute | solution.py:326
  7.2 1.9 %collective-permute-start.16 = (bf16[4,32,128]{2,1,0:T(8,128)(2,1)S(1)}, bf16[4,32,128]{2,1,0:T(8,128)(2,1)S(1)}, u32[]{:S(2)}, u32[]{:S(2)}) collective-permute-start(bf16[4,32,128]{2,1,0:T(8,128)(2,1)S(1)} %pad_maximum_fusion.1), channel_id=1, source_target_pairs={{16,0},{32,16},{48,32},{64,48},{80,64},{96,80},{112,96},{128,112},... | collective-permute-start | bytes 98312 | tf_op jit(solution)/shard_map/ppermute | solution.py:327
  9.1 1.1 %copy.16.w_own = bf16[1024,64]{1,0:T(8,128)(2,1)S(1)} copy(bf16[1024,64]{0,1:T(8,128)(2,1)} %param.15) | data formatting | bytes 262144 | tf_op args[3]
  10.5 1.1 %broadcast_select_fusion = (bf16[64,16,128]{2,1,0:T(8,128)(2,1)S(1)}, bf16[64,16,128]{2,1,0:T(8,128)(2,1)S(1)}) fusion(pred[]{:T(512)S(6)} %eq.6, bf16[64,16,256]{2,1,0:T(8,128)(2,1)} %param.16), kind=kLoop, calls=%fused_computation.2 | loop fusion | flops 262144 | bytes 1048577 | tf_op jit(solution)/shard_map/jit(_where)/select_n | solution.py:308
  11.7 1.6 %collective-permute-start.5 = (bf16[64,2048]{1,0:T(8,128)(2,1)S(1)}, bf16[64,2048]{1,0:T(8,128)(2,1)S(1)}, u32[]{:S(2)}, u32[]{:S(2)}) collective-permute-start(bf16[64,2048]{1,0:T(8,128)(2,1)S(1)} %bitcast.15), channel_id=1, source_target_pairs={{0,4},{1,5},{2,6},{3,7},{4,8},{5,9},{6,10},{7,11},{8,12},{9,13},{1... | collective-permute-start | bytes 786440 | tf_op jit(solution)/shard_map/ppermute | solution.py:304
  13.4 1.8 %collective-permute-start.3 = (bf16[64,2048]{1,0:T(8,128)(2,1)S(1)}, bf16[64,2048]{1,0:T(8,128)(2,1)S(1)}, u32[]{:S(2)}, u32[]{:S(2)}) collective-permute-start(bf16[64,2048]{1,0:T(8,128)(2,1)S(1)} %bitcast.16), channel_id=1, source_target_pairs={{0,12},{1,13},{2,14},{3,15},{4,0},{5,1},{6,2},{7,3},{8,4},{9,5},{1... | collective-permute-start | bytes 786440 | tf_op jit(solution)/shard_map/ppermute | solution.py:304
  15.2 1.9 %collective-permute-start.1 = (bf16[64,2048]{1,0:T(8,128)(2,1)S(1)}, bf16[64,2048]{1,0:T(8,128)(2,1)S(1)}, u32[]{:S(2)}, u32[]{:S(2)}) collective-permute-start(bf16[64,2048]{1,0:T(8,128)(2,1)S(1)} %bitcast.17), channel_id=1, source_target_pairs={{0,2},{1,3},{2,0},{3,1},{4,6},{5,7},{6,4},{7,5},{8,10},{9,11},{10,... | collective-permute-start | bytes 786440 | tf_op jit(solution)/shard_map/ppermute | solution.py:304
  17.1 2.0 %collective-permute-start.2 = (bf16[64,2048]{1,0:T(8,128)(2,1)S(1)}, bf16[64,2048]{1,0:T(8,128)(2,1)S(1)}, u32[]{:S(2)}, u32[]{:S(2)}) collective-permute-start(bf16[64,2048]{1,0:T(8,128)(2,1)S(1)} %bitcast.20), channel_id=1, source_target_pairs={{0,3},{1,2},{2,1},{3,0},{4,7},{5,6},{6,5},{7,4},{8,11},{9,10},{10,... | collective-permute-start | bytes 786440 | tf_op jit(solution)/shard_map/ppermute | solution.py:304
  19.2 2.4 %collective-permute-done.5.refs_6_ = bf16[64,2048]{1,0:T(8,128)(2,1)S(1)} collective-permute-done((bf16[64,2048]{1,0:T(8,128)(2,1)S(1)}, bf16[64,2048]{1,0:T(8,128)(2,1)S(1)}, u32[]{:S(2)}, u32[]{:S(2)}) %collective-permute-start.5) | collective-permute-done | bytes 262176 | tf_op jit(solution)/shard_map/ppermute | solution.py:304
  21.6 0.5 collective-permute-start.4
  22.1 1.6 %collective-permute-start = (bf16[64,2048]{1,0:T(8,128)(2,1)S(1)}, bf16[64,2048]{1,0:T(8,128)(2,1)S(1)}, u32[]{:S(2)}, u32[]{:S(2)}) collective-permute-start(bf16[64,2048]{1,0:T(8,128)(2,1)S(1)} %bitcast.22), channel_id=1, source_target_pairs={{0,1},{1,0},{2,3},{3,2},{4,5},{5,4},{6,7},{7,6},{8,9},{9,8},{10,11... | collective-permute-start | bytes 786440 | tf_op jit(solution)/shard_map/ppermute | solution.py:304
  23.8 0.6 collective-permute-done.1.refs_2_
  24.6 2.3 %collective-permute-done.6.refs_7_ = bf16[64,2048]{1,0:T(8,128)(2,1)S(1)} collective-permute-done((bf16[64,2048]{1,0:T(8,128)(2,1)S(1)}, bf16[64,2048]{1,0:T(8,128)(2,1)S(1)}, u32[]{:S(2)}, u32[]{:S(2)}) %collective-permute-start.6) | collective-permute-done | bytes 262176 | tf_op jit(solution)/shard_map/ppermute | solution.py:304
  27.0 1.2 %collective-permute-done.2.refs_3_ = bf16[64,2048]{1,0:T(8,128)(2,1)S(1)} collective-permute-done((bf16[64,2048]{1,0:T(8,128)(2,1)S(1)}, bf16[64,2048]{1,0:T(8,128)(2,1)S(1)}, u32[]{:S(2)}, u32[]{:S(2)}) %collective-permute-start.2) | collective-permute-done | bytes 262176 | tf_op jit(solution)/shard_map/ppermute | solution.py:304
  28.2 2.1 %collective-permute-start.8 = (bf16[64,2048]{1,0:T(8,128)(2,1)S(1)}, bf16[64,2048]{1,0:T(8,128)(2,1)S(1)}, u32[]{:S(2)}, u32[]{:S(2)}) collective-permute-start(bf16[64,2048]{1,0:T(8,128)(2,1)S(1)} %collective-permute-done.2.refs_3_), channel_id=1, source_target_pairs={{0,12},{1,13},{2,14},{3,15},{4,0},{5,1},{6,2},{7,3},{8,4},{9,5},{1... | collective-permute-start | bytes 786440 | tf_op jit(solution)/shard_map/ppermute | solution.py:304
  30.3 1.4 %collective-permute-start.7 = (bf16[64,2048]{1,0:T(8,128)(2,1)S(1)}, bf16[64,2048]{1,0:T(8,128)(2,1)S(1)}, u32[]{:S(2)}, u32[]{:S(2)}) collective-permute-start(bf16[64,2048]{1,0:T(8,128)(2,1)S(1)} %collective-permute-done.3.refs_4_), channel_id=1, source_target_pairs={{0,2},{1,3},{2,0},{3,1},{4,6},{5,7},{6,4},{7,5},{8,10},{9,11},{10,... | collective-permute-start | bytes 786440 | tf_op jit(solution)/shard_map/ppermute | solution.py:304
  31.7 0.6 collective-permute-start.10
  32.3 2.5 %collective-permute-done.11.refs_12_ = bf16[64,2048]{1,0:T(8,128)(2,1)S(1)} collective-permute-done((bf16[64,2048]{1,0:T(8,128)(2,1)S(1)}, bf16[64,2048]{1,0:T(8,128)(2,1)S(1)}, u32[]{:S(2)}, u32[]{:S(2)}) %collective-permute-start.11) | collective-permute-done | bytes 262176 | tf_op jit(solution)/shard_map/ppermute | solution.py:304
  35.2 3.8 %collective-permute-done.9.refs_10_ = bf16[64,2048]{1,0:T(8,128)(2,1)S(1)} collective-permute-done((bf16[64,2048]{1,0:T(8,128)(2,1)S(1)}, bf16[64,2048]{1,0:T(8,128)(2,1)S(1)}, u32[]{:S(2)}, u32[]{:S(2)}) %collective-permute-start.9) | collective-permute-done | bytes 262176 | tf_op jit(solution)/shard_map/ppermute | solution.py:304
  38.9 3.2 %collective-permute-start.14 = (bf16[64,2048]{1,0:T(8,128)(2,1)S(1)}, bf16[64,2048]{1,0:T(8,128)(2,1)S(1)}, u32[]{:S(2)}, u32[]{:S(2)}) collective-permute-start(bf16[64,2048]{1,0:T(8,128)(2,1)S(1)} %collective-permute-done.8.refs_9_), channel_id=1, source_target_pairs={{0,12},{1,13},{2,14},{3,15},{4,0},{5,1},{6,2},{7,3},{8,4},{9,5},{1... | collective-permute-start | bytes 786440 | tf_op jit(solution)/shard_map/ppermute | solution.py:304
  42.2 8.9 %shard_map.139 = (bf16[576,384]{1,0:T(8,128)(2,1)}, bf16[32,128,384]{2,1,0:T(8,128)(2,1)}, bf16[128,2048]{1,0:T(8,128)(2,1)}, f32[16,128]{1,0:T(8,128)}, f32[32,...) custom-call(bf16[3,32,512]{2,1,0:T(8,128)(2,1)} %image.1, s32[32,512]{1,0:T(8,128)} %mask.1, ...), custom_call_target="tpu_custom_call" | custom-call | flops 6000000000 | bytes 5186016 | tf_op jit(solution)/shard_map/pallas_call | solution.py:289
  51.3 0.6 copy-done.15
  52.4 12.2 %shard_map.140 = (bf16[560,128]{1,0:T(8,128)(2,1)}, bf16[560,128]{1,0:T(8,128)(2,1)}, bf16[128,384]{1,0:T(8,128)(2,1)}) custom-call(bf16[64,2048]{1,0:T(8,128)(2,1)} %bitcast.18, bf16[64,2048]{1,0:T(8,128)(2,1)} %copy-done.11, bf16[64,2048]{1,0:T(8,128)(2,1)} %copy-done.7, bf16[64,2048]{1,0:T(8,128)(2,1)} %copy-done.9, bf16[64,2048]{1,0:T(8,128)(2,1)} %copy-done.6, ...), custom_call_target="tpu_custom_call" | custom-call | flops 6000000000 | bytes 9277440 | tf_op jit(solution)/shard_map/pallas_call | solution.py:289
  64.5 3.5 %all-to-all-start = ((bf16[16,8,384]{2,1,0:T(8,128)(2,1)}), bf16[16,8,384]{2,1,0:T(8,128)(2,1)S(1)}, u32[]{:S(2)}, u32[]{:S(2)}) async-start(bf16[16,8,384]{2,1,0:T(8,128)(2,1)} %bitcast.23), calls=%async_computation | async-start | bytes 196608 | tf_op jit(solution)/shard_map/all_to_all | solution.py:363
  68.3 1.4 %collective-permute-done.19.partner = bf16[560,128]{1,0:T(8,128)(2,1)S(1)} collective-permute-done((bf16[560,128]{1,0:T(8,128)(2,1)}, bf16[560,128]{1,0:T(8,128)(2,1)S(1)}, u32[]{:S(2)}, u32[]{:S(2)}) %collective-permute-start.19) | collective-permute-done | bytes 143392 | tf_op jit(solution)/shard_map/ppermute | solution.py:304
  69.7 4.6 %all-to-all-done.parts = bf16[16,8,384]{2,1,0:T(8,128)(2,1)S(1)} async-done(((bf16[16,8,384]{2,1,0:T(8,128)(2,1)}), bf16[16,8,384]{2,1,0:T(8,128)(2,1)S(1)}, u32[]{:S(2)}, u32[]{:S(2)}) %all-to-all-start) | async-done | bytes 98336 | tf_op jit(solution)/shard_map/all_to_all | solution.py:363
  74.3 0.6 copy-done
  74.9 1.9 %shard_map.141 = (bf16[16,80,128]{2,1,0:T(8,128)(2,1)}, f32[8,512]{1,0:T(8,128)}) custom-call(bf16[560,128]{1,0:T(8,128)(2,1)} %get-tuple-element.22.own, bf16[560,128]{1,0:T(8,128)(2,1)} %copy-done.3, bf16[16,8,384]{2,1,0:T(8,128)(2,1)} %copy-done), custom_call_target="tpu_custom_call" | custom-call | flops 1000000 | bytes 729088 | tf_op jit(solution)/shard_map/pallas_call | solution.py:289
  76.8 23.7 %all_to_all.10.received = bf16[16,80,128]{2,1,0:T(8,128)(2,1)} all-to-all(bf16[16,80,128]{2,1,0:T(8,128)(2,1)} %get-tuple-element.25), channel_id=1, replica_groups=mesh['space'=16,'chan'=16] {'space'}, dimensions={0} | all-to-all | bytes 655360 | tf_op jit(solution)/shard_map/all_to_all | solution.py:371
  100.5 1.9 %shard_map.142 = (f32[64,75]{1,0:T(8,128)}, f32[64,64]{1,0:T(8,128)}, f32[3,2,512]{2,1,0:T(2,128)}) custom-call(bf16[16,80,128]{2,1,0:T(8,128)(2,1)} %all_to_all.10.received, f32[8,512]{1,0:T(8,128)} %get-tuple-element.26.middle, f32[75,80]{1,0:T(8,128)} %constant.38.clone.order), custom_call_target="tpu_custom_call" | custom-call | flops 1000000 | bytes 415936 | tf_op jit(solution)/shard_map/pallas_call | solution.py:289
  (70 shorter events, 2.1 us)
Async XLA Ops:
  0.6 12.7 %collective-permute-start.17 = (bf16[64,75]{1,0:T(8,128)(2,1)}, bf16[64,75]{1,0:T(8,128)(2,1)S(1)}, u32[]{:S(2)}, u32[]{:S(2)}) collective-permute-start(bf16[64,75]{1,0:T(8,128)(2,1)} %anch_own.1), channel_id=1, source_target_pairs={{0,1},{1,0},{2,3},{3,2},{4,5},{5,4},{6,7},{7,6},{8,9},{9,8},{10,11... | collective-permute-start | bytes 28808 | tf_op jit(solution)/shard_map/ppermute | solution.py:304
  2.4 12.8 %collective-permute-start.15 = (bf16[4,32,128]{2,1,0:T(8,128)(2,1)S(1)}, bf16[4,32,128]{2,1,0:T(8,128)(2,1)S(1)}, u32[]{:S(2)}, u32[]{:S(2)}) collective-permute-start(bf16[4,32,128]{2,1,0:T(8,128)(2,1)S(1)} %pad_maximum_fusion), channel_id=1, source_target_pairs={{0,16},{16,32},{32,48},{48,64},{64,80},{80,96},{96,112},{112,128},... | collective-permute-start | bytes 98312 | tf_op jit(solution)/shard_map/ppermute | solution.py:326
  7.2 9.9 %collective-permute-start.16 = (bf16[4,32,128]{2,1,0:T(8,128)(2,1)S(1)}, bf16[4,32,128]{2,1,0:T(8,128)(2,1)S(1)}, u32[]{:S(2)}, u32[]{:S(2)}) collective-permute-start(bf16[4,32,128]{2,1,0:T(8,128)(2,1)S(1)} %pad_maximum_fusion.1), channel_id=1, source_target_pairs={{16,0},{32,16},{48,32},{64,48},{80,64},{96,80},{112,96},{128,112},... | collective-permute-start | bytes 98312 | tf_op jit(solution)/shard_map/ppermute | solution.py:327
  10.2 31.9 %copy-start.1 = (bf16[1024,64]{1,0:T(8,128)(2,1)}, bf16[1024,64]{1,0:T(8,128)(2,1)S(1)}, u32[]{:S(2)}) copy-start(bf16[1024,64]{1,0:T(8,128)(2,1)S(1)} %copy.16.w_own) | copy-start | bytes 393220
  10.2 6.9 %collective-permute-start.18 = (bf16[1024,64]{1,0:T(8,128)(2,1)S(1)}, bf16[1024,64]{1,0:T(8,128)(2,1)S(1)}, u32[]{:S(2)}, u32[]{:S(2)}) collective-permute-start(bf16[1024,64]{1,0:T(8,128)(2,1)S(1)} %copy.16.w_own), channel_id=1, source_target_pairs={{0,1},{1,0},{2,3},{3,2},{4,5},{5,4},{6,7},{7,6},{8,9},{9,8},{10,11... | collective-permute-start | bytes 393224 | tf_op jit(solution)/shard_map/ppermute | solution.py:304
  11.7 39.4 %copy-start.2 = (bf16[8,8,16,128]{3,1,2,0:T(8,128)(2,1)}, bf16[8,8,16,128]{3,1,2,0:T(8,128)(2,1)S(1)}, u32[]{:S(2)}) copy-start(bf16[8,8,16,128]{3,1,2,0:T(8,128)(2,1)S(1)} %copy.22) | copy-start | bytes 786436
  11.7 9.9 %collective-permute-start.5 = (bf16[64,2048]{1,0:T(8,128)(2,1)S(1)}, bf16[64,2048]{1,0:T(8,128)(2,1)S(1)}, u32[]{:S(2)}, u32[]{:S(2)}) collective-permute-start(bf16[64,2048]{1,0:T(8,128)(2,1)S(1)} %bitcast.15), channel_id=1, source_target_pairs={{0,4},{1,5},{2,6},{3,7},{4,8},{5,9},{6,10},{7,11},{8,12},{9,13},{1... | collective-permute-start | bytes 786440 | tf_op jit(solution)/shard_map/ppermute | solution.py:304
  13.3 28.8 %copy-start.22 = (bf16[64,75]{1,0:T(8,128)(2,1)}, bf16[64,75]{1,0:T(8,128)(2,1)S(1)}, u32[]{:S(2)}) copy-start(bf16[64,75]{1,0:T(8,128)(2,1)S(1)} %collective-permute-done.17.anch_partner) | copy-start | bytes 28804
  13.4 8.8 %collective-permute-start.3 = (bf16[64,2048]{1,0:T(8,128)(2,1)S(1)}, bf16[64,2048]{1,0:T(8,128)(2,1)S(1)}, u32[]{:S(2)}, u32[]{:S(2)}) collective-permute-start(bf16[64,2048]{1,0:T(8,128)(2,1)S(1)} %bitcast.16), channel_id=1, source_target_pairs={{0,12},{1,13},{2,14},{3,15},{4,0},{5,1},{6,2},{7,3},{8,4},{9,5},{1... | collective-permute-start | bytes 786440 | tf_op jit(solution)/shard_map/ppermute | solution.py:304
  15.2 27.0 %copy-start.20 = (bf16[4,32,128]{2,1,0:T(8,128)(2,1)}, bf16[4,32,128]{2,1,0:T(8,128)(2,1)S(1)}, u32[]{:S(2)}) copy-start(bf16[4,32,128]{2,1,0:T(8,128)(2,1)S(1)} %collective-permute-done.15.before) | copy-start | bytes 98308
  15.2 9.2 %collective-permute-start.1 = (bf16[64,2048]{1,0:T(8,128)(2,1)S(1)}, bf16[64,2048]{1,0:T(8,128)(2,1)S(1)}, u32[]{:S(2)}, u32[]{:S(2)}) collective-permute-start(bf16[64,2048]{1,0:T(8,128)(2,1)S(1)} %bitcast.17), channel_id=1, source_target_pairs={{0,2},{1,3},{2,0},{3,1},{4,6},{5,7},{6,4},{7,5},{8,10},{9,11},{10,... | collective-permute-start | bytes 786440 | tf_op jit(solution)/shard_map/ppermute | solution.py:304
  17.1 25.1 %copy-start.21 = (bf16[4,32,128]{2,1,0:T(8,128)(2,1)}, bf16[4,32,128]{2,1,0:T(8,128)(2,1)S(1)}, u32[]{:S(2)}) copy-start(bf16[4,32,128]{2,1,0:T(8,128)(2,1)S(1)} %collective-permute-done.16.after) | copy-start | bytes 98308
  17.1 9.9 %collective-permute-start.6 = (bf16[64,2048]{1,0:T(8,128)(2,1)S(1)}, bf16[64,2048]{1,0:T(8,128)(2,1)S(1)}, u32[]{:S(2)}, u32[]{:S(2)}) collective-permute-start(bf16[64,2048]{1,0:T(8,128)(2,1)S(1)} %bitcast.19), channel_id=1, source_target_pairs={{0,5},{1,4},{2,7},{3,6},{4,9},{5,8},{6,11},{7,10},{8,13},{9,12},{1... | collective-permute-start | bytes 786440 | tf_op jit(solution)/shard_map/ppermute | solution.py:304
  17.1 25.1 %copy-start.4 = (bf16[1024,64]{1,0:T(8,128)(2,1)}, bf16[1024,64]{1,0:T(8,128)(2,1)S(1)}, u32[]{:S(2)}) copy-start(bf16[1024,64]{1,0:T(8,128)(2,1)S(1)} %collective-permute-done.18.w_partner) | copy-start | bytes 393220
  17.1 11.1 %collective-permute-start.2 = (bf16[64,2048]{1,0:T(8,128)(2,1)S(1)}, bf16[64,2048]{1,0:T(8,128)(2,1)S(1)}, u32[]{:S(2)}, u32[]{:S(2)}) collective-permute-start(bf16[64,2048]{1,0:T(8,128)(2,1)S(1)} %bitcast.20), channel_id=1, source_target_pairs={{0,3},{1,2},{2,1},{3,0},{4,7},{5,6},{6,5},{7,4},{8,11},{9,10},{10,... | collective-permute-start | bytes 786440 | tf_op jit(solution)/shard_map/ppermute | solution.py:304
  21.6 29.5 %copy-start.5 = (bf16[64,2048]{1,0:T(8,128)(2,1)}, bf16[64,2048]{1,0:T(8,128)(2,1)S(1)}, u32[]{:S(2)}) copy-start(bf16[64,2048]{1,0:T(8,128)(2,1)S(1)} %collective-permute-done.5.refs_6_) | copy-start | bytes 786436
  21.6 8.6 %collective-permute-start.4 = (bf16[64,2048]{1,0:T(8,128)(2,1)S(1)}, bf16[64,2048]{1,0:T(8,128)(2,1)S(1)}, u32[]{:S(2)}, u32[]{:S(2)}) collective-permute-start(bf16[64,2048]{1,0:T(8,128)(2,1)S(1)} %bitcast.21), channel_id=1, source_target_pairs={{0,13},{1,12},{2,15},{3,14},{4,1},{5,0},{6,3},{7,2},{8,5},{9,4},{1... | collective-permute-start | bytes 786440 | tf_op jit(solution)/shard_map/ppermute | solution.py:304
  22.1 29.0 %copy-start.6 = (bf16[64,2048]{1,0:T(8,128)(2,1)}, bf16[64,2048]{1,0:T(8,128)(2,1)S(1)}, u32[]{:S(2)}) copy-start(bf16[64,2048]{1,0:T(8,128)(2,1)S(1)} %collective-permute-done.3.refs_4_) | copy-start | bytes 786436
  22.1 9.6 %collective-permute-start = (bf16[64,2048]{1,0:T(8,128)(2,1)S(1)}, bf16[64,2048]{1,0:T(8,128)(2,1)S(1)}, u32[]{:S(2)}, u32[]{:S(2)}) collective-permute-start(bf16[64,2048]{1,0:T(8,128)(2,1)S(1)} %bitcast.22), channel_id=1, source_target_pairs={{0,1},{1,0},{2,3},{3,2},{4,5},{5,4},{6,7},{7,6},{8,9},{9,8},{10,11... | collective-permute-start | bytes 786440 | tf_op jit(solution)/shard_map/ppermute | solution.py:304
  24.4 26.8 %copy-start.7 = (bf16[64,2048]{1,0:T(8,128)(2,1)}, bf16[64,2048]{1,0:T(8,128)(2,1)S(1)}, u32[]{:S(2)}) copy-start(bf16[64,2048]{1,0:T(8,128)(2,1)S(1)} %collective-permute-done.1.refs_2_) | copy-start | bytes 786436
  24.4 10.4 %collective-permute-start.11 = (bf16[64,2048]{1,0:T(8,128)(2,1)S(1)}, bf16[64,2048]{1,0:T(8,128)(2,1)S(1)}, u32[]{:S(2)}, u32[]{:S(2)}) collective-permute-start(bf16[64,2048]{1,0:T(8,128)(2,1)S(1)} %collective-permute-done.5.refs_6_), channel_id=1, source_target_pairs={{0,4},{1,5},{2,6},{3,7},{4,8},{5,9},{6,10},{7,11},{8,12},{9,13},{1... | collective-permute-start | bytes 786440 | tf_op jit(solution)/shard_map/ppermute | solution.py:304
  27.0 24.2 %copy-start.8 = (bf16[64,2048]{1,0:T(8,128)(2,1)}, bf16[64,2048]{1,0:T(8,128)(2,1)S(1)}, u32[]{:S(2)}) copy-start(bf16[64,2048]{1,0:T(8,128)(2,1)S(1)} %collective-permute-done.6.refs_7_) | copy-start | bytes 786436
  27.0 11.9 %collective-permute-start.9 = (bf16[64,2048]{1,0:T(8,128)(2,1)S(1)}, bf16[64,2048]{1,0:T(8,128)(2,1)S(1)}, u32[]{:S(2)}, u32[]{:S(2)}) collective-permute-start(bf16[64,2048]{1,0:T(8,128)(2,1)S(1)} %collective-permute-done.1.refs_2_), channel_id=1, source_target_pairs={{0,4},{1,5},{2,6},{3,7},{4,8},{5,9},{6,10},{7,11},{8,12},{9,13},{1... | collective-permute-start | bytes 786440 | tf_op jit(solution)/shard_map/ppermute | solution.py:304
  28.2 23.0 %copy-start.9 = (bf16[64,2048]{1,0:T(8,128)(2,1)}, bf16[64,2048]{1,0:T(8,128)(2,1)S(1)}, u32[]{:S(2)}) copy-start(bf16[64,2048]{1,0:T(8,128)(2,1)S(1)} %collective-permute-done.2.refs_3_) | copy-start | bytes 786436
  28.2 10.7 %collective-permute-start.8 = (bf16[64,2048]{1,0:T(8,128)(2,1)S(1)}, bf16[64,2048]{1,0:T(8,128)(2,1)S(1)}, u32[]{:S(2)}, u32[]{:S(2)}) collective-permute-start(bf16[64,2048]{1,0:T(8,128)(2,1)S(1)} %collective-permute-done.2.refs_3_), channel_id=1, source_target_pairs={{0,12},{1,13},{2,14},{3,15},{4,0},{5,1},{6,2},{7,3},{8,4},{9,5},{1... | collective-permute-start | bytes 786440 | tf_op jit(solution)/shard_map/ppermute | solution.py:304
  30.3 21.0 %collective-permute-start.7 = (bf16[64,2048]{1,0:T(8,128)(2,1)S(1)}, bf16[64,2048]{1,0:T(8,128)(2,1)S(1)}, u32[]{:S(2)}, u32[]{:S(2)}) collective-permute-start(bf16[64,2048]{1,0:T(8,128)(2,1)S(1)} %collective-permute-done.3.refs_4_), channel_id=1, source_target_pairs={{0,2},{1,3},{2,0},{3,1},{4,6},{5,7},{6,4},{7,5},{8,10},{9,11},{10,... | collective-permute-start | bytes 786440 | tf_op jit(solution)/shard_map/ppermute | solution.py:304
  31.7 19.5 %collective-permute-start.10 = (bf16[64,2048]{1,0:T(8,128)(2,1)S(1)}, bf16[64,2048]{1,0:T(8,128)(2,1)S(1)}, u32[]{:S(2)}, u32[]{:S(2)}) collective-permute-start(bf16[64,2048]{1,0:T(8,128)(2,1)S(1)} %collective-permute-done.6.refs_7_), channel_id=1, source_target_pairs={{0,2},{1,3},{2,0},{3,1},{4,6},{5,7},{6,4},{7,5},{8,10},{9,11},{10,... | collective-permute-start | bytes 786440 | tf_op jit(solution)/shard_map/ppermute | solution.py:304
  34.8 16.4 %collective-permute-start.12 = (bf16[64,2048]{1,0:T(8,128)(2,1)S(1)}, bf16[64,2048]{1,0:T(8,128)(2,1)S(1)}, u32[]{:S(2)}, u32[]{:S(2)}) collective-permute-start(bf16[64,2048]{1,0:T(8,128)(2,1)S(1)} %collective-permute-done.4.refs_5_), channel_id=1, source_target_pairs={{0,12},{1,13},{2,14},{3,15},{4,0},{5,1},{6,2},{7,3},{8,4},{9,5},{1... | collective-permute-start | bytes 786440 | tf_op jit(solution)/shard_map/ppermute | solution.py:304
  38.9 12.3 %collective-permute-start.13 = (bf16[64,2048]{1,0:T(8,128)(2,1)S(1)}, bf16[64,2048]{1,0:T(8,128)(2,1)S(1)}, u32[]{:S(2)}, u32[]{:S(2)}) collective-permute-start(bf16[64,2048]{1,0:T(8,128)(2,1)S(1)} %collective-permute-done.9.refs_10_), channel_id=1, source_target_pairs={{0,4},{1,5},{2,6},{3,7},{4,8},{5,9},{6,10},{7,11},{8,12},{9,13},{1... | collective-permute-start | bytes 786440 | tf_op jit(solution)/shard_map/ppermute | solution.py:304
  38.9 12.3 %collective-permute-start.14 = (bf16[64,2048]{1,0:T(8,128)(2,1)S(1)}, bf16[64,2048]{1,0:T(8,128)(2,1)S(1)}, u32[]{:S(2)}, u32[]{:S(2)}) collective-permute-start(bf16[64,2048]{1,0:T(8,128)(2,1)S(1)} %collective-permute-done.8.refs_9_), channel_id=1, source_target_pairs={{0,12},{1,13},{2,14},{3,15},{4,0},{5,1},{6,2},{7,3},{8,4},{9,5},{1... | collective-permute-start | bytes 786440 | tf_op jit(solution)/shard_map/ppermute | solution.py:304
  64.5 9.8 %all-to-all-start = ((bf16[16,8,384]{2,1,0:T(8,128)(2,1)}), bf16[16,8,384]{2,1,0:T(8,128)(2,1)S(1)}, u32[]{:S(2)}, u32[]{:S(2)}) async-start(bf16[16,8,384]{2,1,0:T(8,128)(2,1)} %bitcast.23), calls=%async_computation | async-start | bytes 196608 | tf_op jit(solution)/shard_map/all_to_all | solution.py:363
  68.0 1.7 %collective-permute-start.19 = (bf16[560,128]{1,0:T(8,128)(2,1)}, bf16[560,128]{1,0:T(8,128)(2,1)S(1)}, u32[]{:S(2)}, u32[]{:S(2)}) collective-permute-start(bf16[560,128]{1,0:T(8,128)(2,1)} %get-tuple-element.23), channel_id=1, source_target_pairs={{0,1},{1,0},{2,3},{3,2},{4,5},{5,4},{6,7},{7,6},{8,9},{9,8},{10,11... | collective-permute-start | bytes 430088 | tf_op jit(solution)/shard_map/ppermute | solution.py:304
  (12 other events, 91.0 us)

commit v2 on v1

v2 whole, which is shorter than its diff:
```python
import math

import jax
import jax.numpy as jnp
import ml_dtypes
import numpy as np
from jax import lax
from jax.experimental import pallas as pl
from jax.experimental.pallas import tpu as pltpu
from jax.sharding import Mesh
from jax.sharding import PartitionSpec as P

EPS = 1e-05
LANES = 384
HALF = 128
ROWS = 32
GROUP = 16
OWN = 64
STEP = 4
MIB = 1024 * 1024

CHIPS = ((0, 0), (0, 1), (1, 0), (3, 0), (1, 1), (3, 1), (2, 0), (2, 1))


STRIPS = ("z_hi", "y")
CHAN = ("x", "z_lo", "core")


def route(dx, dz, core):
    return [(i, ((i // 4 + dx) % 4) * 4 + ((i // 2) % 2 ^ dz) * 2 + (i % 2 ^ core)) for i in range(16)]


def seams():
    pairs = [(16 * s + 2 * q, 16 * s - 16 + 2 * q + 1) for s in range(1, 16) for q in range(8)]
    return pairs + [(b, a) for a, b in pairs]


f32 = jnp.float32
bf16 = jnp.bfloat16


def tap(distance):
    return math.exp(-distance * distance / 8.0) if abs(distance) <= 4 else 0.0


def as_bf16(array):
    return array.astype(ml_dtypes.bfloat16)


def column_pool():
    return np.array([[tap(2 * b - l + 4) for b in range(HALF)] for l in range(LANES)], np.float32)


def row_pool():
    return np.array([[tap(2 * a - i) for i in range(ROWS)] for a in range(ROWS // 2)], np.float32)


def replicate_rows():
    out = np.zeros((36, GROUP, 3, ROWS), np.float32)
    for i in range(ROWS):
        for q in range(15):
            out[i + 2, q, q // 5, i] = 1.0
    return out.reshape(36 * GROUP, 96)


def fold_rows():
    out = np.zeros((128, 36, GROUP), np.float32)
    for i in range(ROWS):
        for q in range(15):
            out[8 * (i // 2) + 2 * (q // 5) + i % 2, i + 2, q] = 1.0
    return out.reshape(128, 36 * GROUP)


def entry_order():
    out = np.zeros((75, 80), np.float32)
    for c in range(3):
        for a in range(5):
            for b in range(5):
                out[25 * c + 5 * a + b, GROUP * a + 5 * c + b] = 1.0
    return out


def on_second():
    return lax.axis_index("core") == 1


def block_of(p):
    dx, dz = CHIPS[p // 2]
    ex = lax.rem(lax.axis_index("x") + dx, 4)
    zed = lax.rem(lax.axis_index("z_lo") + dz, 2)
    core = lax.rem(lax.axis_index("core") + p % 2, 2)
    return ex * 4 + zed * 2 + core


def dot(a, b):
    return jnp.dot(a, b, preferred_element_type=f32)


def dot_nt(a, b):
    return lax.dot_general(a, b, (((1,), (1,)), ((), ())), preferred_element_type=f32)


def rim_kernel(image, mask, after, tile):
    del after
    second = on_second()
    for c in range(4):
        value = (image[c] if c < 3 else mask[...]).astype(f32)
        tile[c] = jnp.where(second, value[:, 384:], value[:, :128]).astype(bf16)


def patch_kernel(
    image, mask, beyond, anch_own, anch_partner, w_own, w_partner, pool, rows, repeat, order,
    patches, tissue, scale, norm, inv_square, inv_density, anch, anch_t, wturned,
):
    second = on_second()

    def half(middle, rim, shift):
        wide = jnp.concatenate([rim, middle, rim], axis=1)
        part = jnp.where(second, wide[:, 256:], wide[:, :512])
        return pltpu.roll(part, 512 - shift, 1)[:, :LANES]

    colours = [half(image[c].astype(f32), beyond[c].astype(f32), 122) for c in range(3)]
    here = half(mask[...].astype(f32), beyond[3].astype(f32), 124)
    lane = lax.broadcasted_iota(jnp.int32, here.shape, 1)
    here = jnp.where(lane < 263, here, 0.0)
    tissue[...] = here
    x = dot(repeat[...], jnp.concatenate(colours, axis=0).astype(bf16))
    offset = (lax.broadcasted_iota(jnp.int32, x.shape, 0) % GROUP) % 5
    s = x
    for b in range(1, 5):
        s = jnp.where(offset == b, pltpu.roll(x, LANES - b, 1), s)
    patches[...] = s.astype(bf16)
    square = jnp.sum((s * s).reshape(36, GROUP, LANES), axis=1)
    total = square[0:ROWS]
    for a in range(1, 5):
        total = total + square[a : a + ROWS]
    total = total + EPS
    root = lax.rsqrt(total)
    scale[...] = 4.0 * root
    norm[...] = total * root
    inv_square[...] = 1.0 / total
    counted = dot(here.astype(bf16), pool[...])
    density = jnp.dot(rows[...], counted, precision=lax.Precision.HIGHEST, preferred_element_type=f32)
    inv_density[...] = 1.0 / jnp.maximum(density, 1.0)
    both = jnp.concatenate([anch_own[...], anch_partner[...]], axis=0)
    ordered = dot(both, order[...])
    anch[...] = ordered.astype(bf16)
    anch_t[...] = ordered.T.astype(bf16)
    blocks = [pl.ds(pl.multiple_of(block_of(p) * OWN, OWN), OWN) for p in range(16)]
    for at, weights in ((0, w_own), (OWN, w_partner)):
        ordered = jnp.concatenate([weights[block, :] for block in blocks], axis=0)
        wturned[at : at + OWN, :] = ordered.astype(f32).T.astype(bf16)


def forward_kernel(
    patches, tissue, scale, norm, inv_density, anch, pool,
    masked, whitened,
    columned,
):
    @pl.loop(0, ROWS // STEP)
    def _(t):
        lifted = []
        for r in range(STEP):
            i = t * STEP + r
            patch = patches[pl.ds(pl.multiple_of(i * GROUP, GROUP), 80), :]
            raw = dot(anch[...], patch)
            value = jnp.exp(raw * scale[pl.ds(i, 1), :] - 4.0) * tissue[pl.ds(i, 1), :]
            masked[i] = value.astype(bf16)
            lifted.append((value * norm[pl.ds(i, 1), :]).astype(bf16))
        result = dot(jnp.concatenate(lifted, axis=0), pool[...])
        columned[pl.ds(t * STEP, STEP)] = result.reshape(STEP, 128, HALF)

    for a in range(ROWS // 2):
        acc = None
        for i in range(max(0, 2 * a - 4), min(ROWS, 2 * a + 5)):
            term = tap(2 * a - i) * columned[i]
            acc = term if acc is None else acc + term
        whitened[:, a * HALF : (a + 1) * HALF] = (acc * inv_density[a : a + 1, :]).astype(bf16)


def fold(block, rows):
    top, low = block[:rows], block[rows:]
    left = lax.broadcasted_iota(jnp.int32, top.shape, 1) < OWN
    own = jnp.where(left, top, pltpu.roll(low, OWN, 1))
    partner = jnp.where(left, pltpu.roll(top, OWN, 1), low)
    return own.astype(bf16), partner.astype(bf16)


def backward_kernel(*refs):
    blocks = refs[:16]
    (
        wturned, inv_density, masked, patches, inv_square, anch_t, pool_t, folder,
        anchor_grad, image, rim,
        rowed, spread_grad,
    ) = refs[16:]
    pooled = []
    for n in range(8):
        cols = pl.ds(n * 256, 256)
        stack = jnp.concatenate([block[:, cols] for block in blocks], axis=0)
        pooled.append(dot(wturned[...], stack))
    scaled = []
    for a in range(ROWS // 2):
        part = pooled[a // 2][:, (a % 2) * HALF : (a % 2 + 1) * HALF]
        scaled.append(part.astype(bf16).astype(f32) * inv_density[a : a + 1, :])
    for i in range(ROWS):
        acc = None
        for a in range(ROWS // 2):
            if abs(2 * a - i) <= 4:
                term = (4.0 * tap(2 * a - i)) * scaled[a]
                acc = term if acc is None else acc + term
        rowed[i * 128 : (i + 1) * 128, :] = acc.astype(bf16)
    spread_grad[...] = jnp.zeros_like(spread_grad)
    anchor_grad[...] = jnp.zeros_like(anchor_grad)

    @pl.loop(0, ROWS // STEP)
    def _(t):
        start = pl.multiple_of(t * (STEP * 128), STEP * 128)
        spread = dot(rowed[pl.ds(start, STEP * 128), :], pool_t[...])
        grads, wides, units = [], [], []
        for r in range(STEP):
            i = t * STEP + r
            patch = patches[pl.ds(pl.multiple_of(i * GROUP, GROUP), 80), :]
            grad = (spread[r * 128 : (r + 1) * 128] * masked[i].astype(f32)).astype(bf16)
            unit = dot(anch_t[...], grad)
            wide = patch.astype(f32)
            along = jnp.sum(wide * unit, axis=0, keepdims=True) * inv_square[pl.ds(i, 1), :]
            units.append(unit - wide * along)
            grads.append(grad)
            wides.append(patch)
        anchor_grad[...] += dot_nt(jnp.concatenate(wides, axis=1), jnp.concatenate(grads, axis=1))
        sums = []
        for g in range(STEP + 4):
            acc = None
            for r in range(STEP):
                if 0 <= g - r < 5:
                    term = units[r][(g - r) * GROUP : (g - r + 1) * GROUP]
                    acc = term if acc is None else acc + term
            sums.append(acc)
        here = pl.ds(pl.multiple_of(t * (STEP * GROUP), STEP * GROUP), (STEP + 4) * GROUP)
        spread_grad[here, :] += jnp.concatenate(sums, axis=0)

    t = spread_grad[...]
    offset = (lax.broadcasted_iota(jnp.int32, t.shape, 0) % GROUP) % 5
    moved = t
    for b in range(1, 5):
        moved = jnp.where(offset == b, pltpu.roll(t, b, 1), moved)
    high = moved.astype(bf16)
    low = (moved - high.astype(f32)).astype(bf16)
    summed = dot(folder[...], high) + dot(folder[...], low)
    image[...] = summed.astype(bf16)
    first, last = summed[:, :128], summed[:, 256:]
    lane = lax.broadcasted_iota(jnp.int32, first.shape, 1)
    first, last = jnp.where(lane < 6, first, 0.0), jnp.where(lane < 6, 0.0, last)
    rim[...] = jnp.where(on_second(), last, first).astype(bf16)


def whiten_kernel(*refs):
    blocks = refs[:16]
    whitened, anchor_grad, packed = refs[16:]
    grad_w = None
    for n in range(8):
        cols = pl.ds(n * 256, 256)
        stack = jnp.concatenate([block[:, cols] for block in blocks], axis=0)
        term = dot_nt(stack, whitened[:, cols])
        grad_w = term if grad_w is None else grad_w + term
    core = lax.axis_index("core")
    for p in range(16):
        strip = block_of(p)
        rows = pl.ds(pl.multiple_of((strip // 4) * 32, 32), 32)
        y = lax.rem(strip, 4)
        mine, theirs = fold(grad_w[p * OWN : (p + 1) * OWN], OWN // 2)
        packed[y * 2 + core, rows, :] = mine
        packed[y * 2 + 1 - core, rows, :] = theirs
    mine, theirs = fold(anchor_grad[...], 40)
    pad = jnp.zeros((8, 128), bf16)
    mine = jnp.concatenate([mine, pad], axis=0)
    theirs = jnp.concatenate([theirs, pad], axis=0)
    for y in range(4):
        packed[y * 2 + core, 128:176, :] = mine
        packed[y * 2 + 1 - core, 128:176, :] = theirs


def seam_kernel(image, rim, joined):
    second = on_second()
    value = rim[...].astype(f32)
    first = image[:, :128].astype(f32) + jnp.where(second, 0.0, value)
    last = image[:, 256:].astype(f32) + jnp.where(second, value, 0.0)
    joined[:, :128] = first.astype(bf16)
    joined[:, 128:256] = image[:, 128:256]
    joined[:, 256:] = last.astype(bf16)


def add_up(ref, count):
    total = ref[0].astype(f32)
    for source in range(1, count):
        total = total + ref[source].astype(f32)
    return total


def pack_kernel(received, packed):
    total = add_up(received, 8).astype(bf16)
    for z in range(4):
        packed[z, 0:32, :] = total[z * 32 : (z + 1) * 32]
        packed[z, 32:80, :] = total[128:176]


def unpack_kernel(received, parts, order, grad_anchors, grad_whiten, grad_image):
    total = add_up(received, 4)
    other = pltpu.roll(total, OWN, 1)
    grad_whiten[0:32, :] = total[0:32, :OWN]
    grad_whiten[32:64, :] = other[0:32, :OWN]
    turned = jnp.concatenate([total[32:72], other[32:72]], axis=0).T[:OWN]
    grad_anchors[...] = lax.dot_general(
        turned, order[...], (((1,), (1,)), ((), ())),
        precision=lax.Precision.HIGHEST, preferred_element_type=f32,
    )
    halves = []
    for k in range(2):
        acc = parts[k].astype(f32)
        for chip in range(1, 8):
            acc = acc + parts[2 * chip + k].astype(f32)
        halves.append(acc)
    gap = jnp.zeros((8, 256), f32)
    whole = jnp.concatenate([halves[0], gap], axis=1) + jnp.concatenate([gap, halves[1]], axis=1)
    image = pltpu.roll(whole, 640 - 6, 1)[:, :512]
    for colour in range(3):
        grad_image[colour] = image[2 * colour : 2 * colour + 2]


def call(kernel, outs, scratch, flops, limit, *args, loose=()):
    size = lambda shape, dtype: math.prod(shape) * jnp.dtype(dtype).itemsize
    moved = sum(size(a.shape, a.dtype) for a in args) + sum(size(*out) for out in outs)
    return pl.pallas_call(
        kernel,
        out_shape=[jax.ShapeDtypeStruct(shape, dtype) for shape, dtype in outs],
        in_specs=[
            pl.BlockSpec(memory_space=pl.ANY if n in loose else pltpu.VMEM) for n in range(len(args))
        ],
        out_specs=[pl.BlockSpec(memory_space=pltpu.VMEM)] * len(outs),
        scratch_shapes=[pltpu.VMEM(shape, dtype) for shape, dtype in scratch],
        compiler_params=pltpu.CompilerParams(vmem_limit_bytes=limit * MIB),
        cost_estimate=pl.CostEstimate(flops=flops, bytes_accessed=moved, transcendentals=0),
    )(*args)


def shards(image, mask, anchors, whiten, cotangent):
    second = on_second()

    def send(value, dx, dz, other):
        return lax.ppermute(value, CHAN, route(dx, dz, other))

    def cross(value):
        return lax.ppermute(value, STRIPS + CHAN, seams())

    left, right = cotangent[:, :, :HALF], cotangent[:, :, HALF:]
    own = jnp.where(second, right, left).reshape(OWN, -1)
    away = jnp.where(second, left, right).reshape(OWN, -1)
    held = {(0, 0): (own, send(away, 0, 0, 1))}
    for dx, dz in ((1, 0), (3, 0), (0, 1)):
        held[(4 - dx) % 4, dz] = (send(own, dx, dz, 0), send(away, dx, dz, 1))
    far_own = send(held[0, 1][0], 1, 0, 0)
    far_partner = send(held[0, 1][1], 3, 0, 0)
    held[3, 1] = (far_own, send(held[3, 0][1], 0, 1, 0))
    held[1, 1] = (send(held[1, 0][0], 0, 1, 0), far_partner)
    held[2, 0] = (send(held[3, 0][0], 1, 0, 0), send(held[1, 0][1], 3, 0, 0))
    held[2, 1] = (send(far_own, 1, 0, 0), send(far_partner, 3, 0, 0))
    blocks = [block for chip in CHIPS for block in held[chip]]

    (tile,) = call(
        rim_kernel, [((4, ROWS, 128), bf16)], [], 1_000_000, 4, image, mask, held[0, 0][1], loose=(2,)
    )
    pool = as_bf16(column_pool())
    order = entry_order()
    plane = ((ROWS, LANES), f32)
    patches, tissue, scale, norm, inv_square, inv_density, anch, anch_t, wturned = call(
        patch_kernel,
        [
            ((36 * GROUP, LANES), bf16),
            plane,
            plane,
            plane,
            plane,
            ((16, HALF), f32),
            ((128, 80), bf16),
            ((80, 128), bf16),
            ((128, 1024), bf16),
        ],
        [],
        1_000_000_000,
        12,
        image, mask, cross(tile), anchors, send(anchors, 0, 0, 1), whiten, send(whiten, 0, 0, 1),
        jnp.asarray(pool), jnp.asarray(row_pool()),
        jnp.asarray(as_bf16(replicate_rows())), jnp.asarray(as_bf16(order)),
    )
    masked, whitened = call(
        forward_kernel,
        [((ROWS, 128, LANES), bf16), ((128, 16 * HALF), bf16)],
        [((ROWS, 128, HALF), f32)],
        3_000_000_000,
        14,
        patches, tissue, scale, norm, inv_density, anch, jnp.asarray(pool),
    )
    anchor_grad, image_part, rim = call(
        backward_kernel,
        [((80, 128), f32), ((128, LANES), bf16), ((128, 128), bf16)],
        [((ROWS * 128, HALF), bf16), ((36 * GROUP, LANES), f32)],
        5_000_000_000,
        20,
        *blocks,
        wturned, inv_density, masked, patches, inv_square, anch_t,
        jnp.asarray(pool.T.copy()), jnp.asarray(as_bf16(fold_rows())),
    )
    rim = cross(rim)
    (packed,) = call(
        whiten_kernel, [((8, 176, 128), bf16)], [], 2_000_000_000, 12, *blocks, whitened, anchor_grad
    )
    (joined,) = call(seam_kernel, [((128, LANES), bf16)], [], 1_000_000, 4, image_part, rim)

    received = lax.all_to_all(packed, ("y", "core"), 0, 0)
    parts = lax.all_to_all(joined.reshape(16, 8, LANES), CHAN, 0, 0)
    (packed,) = call(pack_kernel, [((4, 80, 128), bf16)], [], 1_000_000, 4, received)
    received = lax.all_to_all(packed, "z_hi", 0, 0)
    return call(
        unpack_kernel,
        [((OWN, 75), f32), ((OWN, OWN), f32), ((3, 2, 512), f32)],
        [],
        1_000_000,
        8,
        received, parts, jnp.asarray(order),
    )


def solution(mesh):
    fine = Mesh(mesh.devices.reshape(4, 4, 4, 2, 2), STRIPS + CHAN)
    placed = (
        P(None, None, STRIPS),
        P(None, STRIPS),
        P(CHAN, None),
        P(None, CHAN),
        P(CHAN, None, STRIPS),
    )
    return jax.shard_map(
        lambda *args: tuple(shards(*args)),
        mesh=fine,
        in_specs=placed,
        out_specs=(P(CHAN, None), P(STRIPS, CHAN), P(None, CHAN, STRIPS)),
        check_vma=False,
    )
```

time: 104 us -> 97.8 us (0.940)
  starting transfers between devices: 28.4 us -> 40.9 us
  blocking collectives: 23.7 us -> 15.7 us
  Pallas kernels: 24.9 us -> 17 us
  waiting for transfers between devices: 18.8 us -> 12.3 us
  local copies, waits for them, and re-layouts: 3.73 us -> 8.63 us
    all_to_all x1 -> x2, starting transfers between devices: 3.51 us -> 12.3 us  [the longest x1 7.8 us: shards(): parts = lax.all_to_all(joined.reshape(16, 8, LANES), CHAN, 0, 0)]
    ppermute x20 -> x19, waiting for transfers between devices: 14.2 us -> 6.05 us  [the longest x2 3.64 us: cross(): return lax.ppermute(value, STRIPS + CHAN, seams())]
    all_to_all x1, blocking collectives: 23.7 us -> 15.7 us  [shards(): received = lax.all_to_all(packed, 'z_hi', 0, 0)]
    pallas_call x4 -> x8, Pallas kernels: 24.9 us -> 17 us  [call(): pl.pallas_call(kernel, out_shape=[jax.ShapeDtypeStruct(shape, dtype) for...]
    unnamed x49 -> x29, local copies, waits for them, and re-layouts: 2.96 us -> 8.63 us
    ppermute x20 -> x19, starting transfers between devices: 24.9 us -> 28.6 us  [the longest x17 23.4 us: send(): return lax.ppermute(value, CHAN, route(dx, dz, other))]
    all_to_all x1 -> x2, waiting for transfers between devices: 4.61 us -> 6.25 us  [the longest x1 6.25 us: shards(): parts = lax.all_to_all(joined.reshape(16, 8, LANES), CHAN, 0, 0)]
  transfers between devices with their start and end apart: 21 -> 21, of which waited for: 8 -> 4; matrix products, arithmetic and copies ran while one was open for 4% -> 1% of each run, Pallas kernels for 9% -> 7%
where the time goes in v2:
time: 97.8 us; the launch traced here: 96.5 us
  starting transfers between devices  40.9 us (42%)
  Pallas kernels  17 us (17%)
  blocking collectives  15.7 us (16%)
  waiting for transfers between devices  12.3 us (13%)
  local copies, waits for them, and re-layouts  8.63 us (9%)
  other arithmetic  1.1 us (1%)
    ppermute x17, starting transfers between devices, send(): return lax.ppermute(value, CHAN, route(dx, dz, other))  23.4 us
    pallas_call x8, Pallas kernels, call(): pl.pallas_call(kernel, out_shape=[jax.ShapeDtypeStruct(shape, dtype) for...  17 us
    all_to_all x1, blocking collectives, shards(): received = lax.all_to_all(packed, 'z_hi', 0, 0)  15.7 us
    unnamed x29, local copies, waits for them, and re-layouts  8.63 us
    all_to_all x1, starting transfers between devices, shards(): parts = lax.all_to_all(joined.reshape(16, 8, LANES), CHAN, 0, 0)  7.8 us
    all_to_all x1, waiting for transfers between devices, shards(): parts = lax.all_to_all(joined.reshape(16, 8, LANES), CHAN, 0, 0)  6.25 us
    ppermute x2, starting transfers between devices, cross(): return lax.ppermute(value, STRIPS + CHAN, seams())  5.26 us
    all_to_all x1, starting transfers between devices, shards(): received = lax.all_to_all(packed, ('y', 'core'), 0, 0)  4.51 us
  transfers between devices with their start and end apart: 21, of which 4 were waited for; matrix products, arithmetic and copies ran while one was open for 1% of the time, Pallas kernels for 7%

profile of v2, /device:TPU:24, one launch (start us, length us, event | category | flops | bytes accessed | tf_op | source)
XLA Modules:
  0.0 96.5 jit_solution(7680268196530647981)
XLA Ops:
  0.6 1.1 %broadcast_select_fusion = (bf16[64,16,128]{2,1,0:T(8,128)(2,1)S(1)}, bf16[64,16,128]{2,1,0:T(8,128)(2,1)S(1)}) fusion(pred[]{:T(512)S(6)} %eq.3, bf16[64,16,256]{2,1,0:T(8,128)(2,1)} %param.16), kind=kLoop, calls=%fused_computation.2 | loop fusion | flops 262144 | bytes 1048577 | tf_op jit(solution)/shard_map/jit(_where)/select_n | solution.py:357
  2.5 2.0 %collective-permute-start.1 = (bf16[64,2048]{1,0:T(8,128)(2,1)S(1)}, bf16[64,2048]{1,0:T(8,128)(2,1)S(1)}, u32[]{:S(2)}, u32[]{:S(2)}) collective-permute-start(bf16[64,2048]{1,0:T(8,128)(2,1)S(1)} %bitcast.9), channel_id=1, source_target_pairs={{0,2},{1,3},{2,0},{3,1},{4,6},{5,7},{6,4},{7,5},{8,10},{9,11},{10,... | collective-permute-start | bytes 786440 | tf_op jit(solution)/shard_map/ppermute | solution.py:350
  4.5 1.5 %collective-permute-start.5 = (bf16[64,2048]{1,0:T(8,128)(2,1)S(1)}, bf16[64,2048]{1,0:T(8,128)(2,1)S(1)}, u32[]{:S(2)}, u32[]{:S(2)}) collective-permute-start(bf16[64,2048]{1,0:T(8,128)(2,1)S(1)} %bitcast.10), channel_id=1, source_target_pairs={{0,4},{1,5},{2,6},{3,7},{4,8},{5,9},{6,10},{7,11},{8,12},{9,13},{1... | collective-permute-start | bytes 786440 | tf_op jit(solution)/shard_map/ppermute | solution.py:350
  6.0 1.7 %collective-permute-start.3 = (bf16[64,2048]{1,0:T(8,128)(2,1)S(1)}, bf16[64,2048]{1,0:T(8,128)(2,1)S(1)}, u32[]{:S(2)}, u32[]{:S(2)}) collective-permute-start(bf16[64,2048]{1,0:T(8,128)(2,1)S(1)} %bitcast.11), channel_id=1, source_target_pairs={{0,12},{1,13},{2,14},{3,15},{4,0},{5,1},{6,2},{7,3},{8,4},{9,5},{1... | collective-permute-start | bytes 786440 | tf_op jit(solution)/shard_map/ppermute | solution.py:350
  7.7 1.1 %copy.16.w_own = bf16[1024,64]{1,0:T(8,128)(2,1)S(1)} copy(bf16[1024,64]{0,1:T(8,128)(2,1)} %param.15) | data formatting | bytes 262144 | tf_op args[3]
  8.9 0.9 copy-done
  9.8 0.8 copy-done.2
  10.7 2.8 %collective-permute-start.15 = (bf16[4,32,128]{2,1,0:T(8,128)(2,1)S(1)}, bf16[4,32,128]{2,1,0:T(8,128)(2,1)S(1)}, u32[]{:S(2)}, u32[]{:S(2)}) collective-permute-start(bf16[4,32,128]{2,1,0:T(8,128)(2,1)S(1)} %shard_map.139), channel_id=1, source_target_pairs={{16,1},{18,3},{20,5},{22,7},{24,9},{26,11},{28,13},{30,15},{32,17}... | collective-permute-start | bytes 98312 | tf_op jit(solution)/shard_map/ppermute | solution.py:353
  13.5 2.2 %collective-permute-start.6 = (bf16[64,2048]{1,0:T(8,128)(2,1)S(1)}, bf16[64,2048]{1,0:T(8,128)(2,1)S(1)}, u32[]{:S(2)}, u32[]{:S(2)}) collective-permute-start(bf16[64,2048]{1,0:T(8,128)(2,1)S(1)} %bitcast.18), channel_id=1, source_target_pairs={{0,5},{1,4},{2,7},{3,6},{4,9},{5,8},{6,11},{7,10},{8,13},{9,12},{1... | collective-permute-start | bytes 786440 | tf_op jit(solution)/shard_map/ppermute | solution.py:350
  16.0 3.1 %collective-permute-start.4 = (bf16[64,2048]{1,0:T(8,128)(2,1)S(1)}, bf16[64,2048]{1,0:T(8,128)(2,1)S(1)}, u32[]{:S(2)}, u32[]{:S(2)}) collective-permute-start(bf16[64,2048]{1,0:T(8,128)(2,1)S(1)} %bitcast.19), channel_id=1, source_target_pairs={{0,13},{1,12},{2,15},{3,14},{4,1},{5,0},{6,3},{7,2},{8,5},{9,4},{1... | collective-permute-start | bytes 786440 | tf_op jit(solution)/shard_map/ppermute | solution.py:350
  19.2 3.2 %collective-permute-start.8 = (bf16[64,2048]{1,0:T(8,128)(2,1)S(1)}, bf16[64,2048]{1,0:T(8,128)(2,1)S(1)}, u32[]{:S(2)}, u32[]{:S(2)}) collective-permute-start(bf16[64,2048]{1,0:T(8,128)(2,1)S(1)} %collective-permute-done.2.refs_3_), channel_id=1, source_target_pairs={{0,12},{1,13},{2,14},{3,15},{4,0},{5,1},{6,2},{7,3},{8,4},{9,5},{1... | collective-permute-start | bytes 786440 | tf_op jit(solution)/shard_map/ppermute | solution.py:350
  22.4 0.9 copy-done.1
  23.3 0.8 copy-done.3
  24.2 0.7 copy-done.5
  24.9 0.9 copy-done.7
  25.8 0.9 copy-done.9
  26.7 0.7 copy-done.11
  28.1 1.8 %shard_map.140 = (bf16[576,384]{1,0:T(8,128)(2,1)S(1)}, f32[32,384]{1,0:T(8,128)S(1)}, f32[32,384]{1,0:T(8,128)S(1)}, f32[32,384]{1,0:T(8,128)S(1)}, f32[32,384]...) custom-call(bf16[3,32,512]{2,1,0:T(8,128)(2,1)S(1)} %copy-done.1, ...), custom_call_target="tpu_custom_call" | custom-call | flops 1000000000 | bytes 1651168 | tf_op jit(solution)/shard_map/pallas_call | solution.py:333
  29.9 2.2 %collective-permute-start.7 = (bf16[64,2048]{1,0:T(8,128)(2,1)S(1)}, bf16[64,2048]{1,0:T(8,128)(2,1)S(1)}, u32[]{:S(2)}, u32[]{:S(2)}) collective-permute-start(bf16[64,2048]{1,0:T(8,128)(2,1)S(1)} %collective-permute-done.3.refs_4_), channel_id=1, source_target_pairs={{0,2},{1,3},{2,0},{3,1},{4,6},{5,7},{6,4},{7,5},{8,10},{9,11},{10,... | collective-permute-start | bytes 786440 | tf_op jit(solution)/shard_map/ppermute | solution.py:350
  32.2 3.4 %collective-permute-start.12 = (bf16[64,2048]{1,0:T(8,128)(2,1)S(1)}, bf16[64,2048]{1,0:T(8,128)(2,1)S(1)}, u32[]{:S(2)}, u32[]{:S(2)}) collective-permute-start(bf16[64,2048]{1,0:T(8,128)(2,1)S(1)} %collective-permute-done.4.refs_5_), channel_id=1, source_target_pairs={{0,12},{1,13},{2,14},{3,15},{4,0},{5,1},{6,2},{7,3},{8,4},{9,5},{1... | collective-permute-start | bytes 786440 | tf_op jit(solution)/shard_map/ppermute | solution.py:350
  35.6 3.2 %collective-permute-start.14 = (bf16[64,2048]{1,0:T(8,128)(2,1)S(1)}, bf16[64,2048]{1,0:T(8,128)(2,1)S(1)}, u32[]{:S(2)}, u32[]{:S(2)}) collective-permute-start(bf16[64,2048]{1,0:T(8,128)(2,1)S(1)} %collective-permute-done.8.refs_9_), channel_id=1, source_target_pairs={{0,12},{1,13},{2,14},{3,15},{4,0},{5,1},{6,2},{7,3},{8,4},{9,5},{1... | collective-permute-start | bytes 786440 | tf_op jit(solution)/shard_map/ppermute | solution.py:350
  38.9 4.4 %shard_map.141 = (bf16[32,128,384]{2,1,0:T(8,128)(2,1)S(1)}, bf16[128,2048]{1,0:T(8,128)(2,1)S(1)}) custom-call(bf16[576,384]{1,0:T(8,128)(2,1)S(1)} %get-tuple-element.17.patches.refs_19_, f32[32,384]{1,0:T(8,128)S(1)} %get-tuple-element.18.tissue, f32[32,384]{1,0:T(8,128)S(1)} %get-tuple-element.19.scale, f32[32,384]{1,0:T(8,128)S(1)} %get-tuple-element.20.norm, ...), custom_call_target="tpu_custom_call" | custom-call | flops 3000000000 | bytes 4386816 | tf_op jit(solution)/shard_map/pallas_call | solution.py:333
  43.3 1.9 %collective-permute-done.14.refs_15_ = bf16[64,2048]{1,0:T(8,128)(2,1)S(1)} collective-permute-done((bf16[64,2048]{1,0:T(8,128)(2,1)S(1)}, bf16[64,2048]{1,0:T(8,128)(2,1)S(1)}, u32[]{:S(2)}, u32[]{:S(2)}) %collective-permute-start.14) | collective-permute-done | bytes 262176 | tf_op jit(solution)/shard_map/ppermute | solution.py:350
  45.2 7.1 %shard_map.142 = (f32[80,128]{1,0:T(8,128)S(1)}, bf16[128,384]{1,0:T(8,128)(2,1)S(1)}, bf16[128,128]{1,0:T(8,128)(2,1)S(1)}) custom-call(bf16[64,2048]{1,0:T(8,128)(2,1)S(1)} %bitcast.12, bf16[64,2048]{1,0:T(8,128)(2,1)S(1)} %collective-permute-done.after.refs_1_, bf16[64,2048]{1,0:T(8,128)(2,1)S(1)} %collective-permute-done.1.refs_2_, ...), custom_call_target="tpu_custom_call" | custom-call | flops 5000000000 | bytes 8540160 | tf_op jit(solution)/shard_map/pallas_call | solution.py:333
  52.4 2.1 %shard_map.143 = bf16[8,176,128]{2,1,0:T(8,128)(2,1)} custom-call(bf16[64,2048]{1,0:T(8,128)(2,1)S(1)} %bitcast.13, bf16[64,2048]{1,0:T(8,128)(2,1)S(1)} %collective-permute-done.after.refs_1_, bf16[64,2048]{1,0:T(8,128)(2,1)S(1)} %collective-permute-done.1.refs_2_, bf16[64,2048]{1,0:T(8,128)(2,1)S(1)} %collective-permute-done.2.refs_3_, ...), custom_call_target="tpu_custom_call" | custom-call | flops 2000000000 | bytes 5120000 | tf_op jit(solution)/shard_map/pallas_call | solution.py:333
  54.5 4.5 %all-to-all-start = ((bf16[8,176,128]{2,1,0:T(8,128)(2,1)}), bf16[8,176,128]{2,1,0:T(8,128)(2,1)S(1)}, u32[]{:S(2)}, u32[]{:S(2)}) async-start(bf16[8,176,128]{2,1,0:T(8,128)(2,1)} %shard_map.143), calls=%async_computation | async-start | bytes 720896 | tf_op jit(solution)/shard_map/all_to_all | solution.py:419
  59.0 2.5 %collective-permute-start.18 = (bf16[128,128]{1,0:T(8,128)(2,1)S(1)}, bf16[128,128]{1,0:T(8,128)(2,1)S(1)}, u32[]{:S(2)}, u32[]{:S(2)}) collective-permute-start(bf16[128,128]{1,0:T(8,128)(2,1)S(1)} %get-tuple-element.30), channel_id=1, source_target_pairs={{16,1},{18,3},{20,5},{22,7},{24,9},{26,11},{28,13},{30,15},{32,17}... | collective-permute-start | bytes 98312 | tf_op jit(solution)/shard_map/ppermute | solution.py:353
  61.5 3.6 %collective-permute-done.18.rim = bf16[128,128]{1,0:T(8,128)(2,1)S(1)} collective-permute-done((bf16[128,128]{1,0:T(8,128)(2,1)S(1)}, bf16[128,128]{1,0:T(8,128)(2,1)S(1)}, u32[]{:S(2)}, u32[]{:S(2)}) %collective-permute-start.18) | collective-permute-done | bytes 32800 | tf_op jit(solution)/shard_map/ppermute | solution.py:353
  65.8 7.8 %all-to-all-start.2 = ((bf16[16,8,384]{2,1,0:T(8,128)(2,1)}), bf16[16,8,384]{2,1,0:T(8,128)(2,1)S(1)}, u32[]{:S(2)}, u32[]{:S(2)}) async-start(bf16[16,8,384]{2,1,0:T(8,128)(2,1)} %bitcast), calls=%async_computation.2 | async-start | bytes 196608 | tf_op jit(solution)/shard_map/all_to_all | solution.py:420
  73.7 6.3 %all-to-all-done.2.parts = bf16[16,8,384]{2,1,0:T(8,128)(2,1)S(1)} async-done(((bf16[16,8,384]{2,1,0:T(8,128)(2,1)}), bf16[16,8,384]{2,1,0:T(8,128)(2,1)S(1)}, u32[]{:S(2)}, u32[]{:S(2)}) %all-to-all-start.2) | async-done | bytes 98336 | tf_op jit(solution)/shard_map/all_to_all | solution.py:420
  79.9 15.7 %all_to_all.15.received = bf16[4,80,128]{2,1,0:T(8,128)(2,1)S(1)} all-to-all(bf16[4,80,128]{2,1,0:T(8,128)(2,1)S(1)} %shard_map.144), channel_id=1, replica_groups=mesh['z_hi'=4,'y'=4,'x'=4,'z_lo'=2,'core'=2] {'z_hi'}, dimensions={0} | all-to-all | bytes 163840 | tf_op jit(solution)/shard_map/all_to_all | solution.py:422
  95.6 0.9 shard_map.146
  (49 shorter events, 2.9 us)
Async XLA Ops:
  0.6 38.2 %copy-start.10 = (bf16[384,128]{1,0:T(8,128)(2,1)S(1)}, bf16[384,128]{1,0:T(8,128)(2,1)}, u32[]{:S(2)}) copy-start(bf16[384,128]{1,0:T(8,128)(2,1)} %constant.20.clone.pool) | copy-start | bytes 294916
  1.8 7.0 %collective-permute-start = (bf16[64,2048]{1,0:T(8,128)(2,1)S(1)}, bf16[64,2048]{1,0:T(8,128)(2,1)S(1)}, u32[]{:S(2)}, u32[]{:S(2)}) collective-permute-start(bf16[64,2048]{1,0:T(8,128)(2,1)S(1)} %bitcast.16), channel_id=1, source_target_pairs={{0,1},{1,0},{2,3},{3,2},{4,5},{5,4},{6,7},{7,6},{8,9},{9,8},{10,11... | collective-permute-start | bytes 786440 | tf_op jit(solution)/shard_map/ppermute | solution.py:350
  1.9 4.1 %collective-permute-start.16 = (bf16[64,75]{1,0:T(8,128)(2,1)}, bf16[64,75]{1,0:T(8,128)(2,1)S(1)}, u32[]{:S(2)}, u32[]{:S(2)}) collective-permute-start(bf16[64,75]{1,0:T(8,128)(2,1)} %anch_own.1), channel_id=1, source_target_pairs={{0,1},{1,0},{2,3},{3,2},{4,5},{5,4},{6,7},{7,6},{8,9},{9,8},{10,11... | collective-permute-start | bytes 28808 | tf_op jit(solution)/shard_map/ppermute | solution.py:350
  2.5 11.0 %collective-permute-start.1 = (bf16[64,2048]{1,0:T(8,128)(2,1)S(1)}, bf16[64,2048]{1,0:T(8,128)(2,1)S(1)}, u32[]{:S(2)}, u32[]{:S(2)}) collective-permute-start(bf16[64,2048]{1,0:T(8,128)(2,1)S(1)} %bitcast.9), channel_id=1, source_target_pairs={{0,2},{1,3},{2,0},{3,1},{4,6},{5,7},{6,4},{7,5},{8,10},{9,11},{10,... | collective-permute-start | bytes 786440 | tf_op jit(solution)/shard_map/ppermute | solution.py:350
  4.5 11.5 %collective-permute-start.2 = (bf16[64,2048]{1,0:T(8,128)(2,1)S(1)}, bf16[64,2048]{1,0:T(8,128)(2,1)S(1)}, u32[]{:S(2)}, u32[]{:S(2)}) collective-permute-start(bf16[64,2048]{1,0:T(8,128)(2,1)S(1)} %bitcast.17), channel_id=1, source_target_pairs={{0,3},{1,2},{2,1},{3,0},{4,7},{5,6},{6,5},{7,4},{8,11},{9,10},{10,... | collective-permute-start | bytes 786440 | tf_op jit(solution)/shard_map/ppermute | solution.py:350
  4.5 14.7 %collective-permute-start.5 = (bf16[64,2048]{1,0:T(8,128)(2,1)S(1)}, bf16[64,2048]{1,0:T(8,128)(2,1)S(1)}, u32[]{:S(2)}, u32[]{:S(2)}) collective-permute-start(bf16[64,2048]{1,0:T(8,128)(2,1)S(1)} %bitcast.10), channel_id=1, source_target_pairs={{0,4},{1,5},{2,6},{3,7},{4,8},{5,9},{6,10},{7,11},{8,12},{9,13},{1... | collective-permute-start | bytes 786440 | tf_op jit(solution)/shard_map/ppermute | solution.py:350
  6.0 13.2 %collective-permute-start.3 = (bf16[64,2048]{1,0:T(8,128)(2,1)S(1)}, bf16[64,2048]{1,0:T(8,128)(2,1)S(1)}, u32[]{:S(2)}, u32[]{:S(2)}) collective-permute-start(bf16[64,2048]{1,0:T(8,128)(2,1)S(1)} %bitcast.11), channel_id=1, source_target_pairs={{0,12},{1,13},{2,14},{3,15},{4,0},{5,1},{6,2},{7,3},{8,4},{9,5},{1... | collective-permute-start | bytes 786440 | tf_op jit(solution)/shard_map/ppermute | solution.py:350
  8.8 1.9 %collective-permute-start.17 = (bf16[1024,64]{1,0:T(8,128)(2,1)S(1)}, bf16[1024,64]{1,0:T(8,128)(2,1)S(1)}, u32[]{:S(2)}, u32[]{:S(2)}) collective-permute-start(bf16[1024,64]{1,0:T(8,128)(2,1)S(1)} %copy.16.w_own), channel_id=1, source_target_pairs={{0,1},{1,0},{2,3},{3,2},{4,5},{5,4},{6,7},{7,6},{8,9},{9,8},{10,11... | collective-permute-start | bytes 393224 | tf_op jit(solution)/shard_map/ppermute | solution.py:350
  8.9 0.9 copy-start
  9.8 0.8 copy-start.2
  10.7 11.7 %collective-permute-start.15 = (bf16[4,32,128]{2,1,0:T(8,128)(2,1)S(1)}, bf16[4,32,128]{2,1,0:T(8,128)(2,1)S(1)}, u32[]{:S(2)}, u32[]{:S(2)}) collective-permute-start(bf16[4,32,128]{2,1,0:T(8,128)(2,1)S(1)} %shard_map.139), channel_id=1, source_target_pairs={{16,1},{18,3},{20,5},{22,7},{24,9},{26,11},{28,13},{30,15},{32,17}... | collective-permute-start | bytes 98312 | tf_op jit(solution)/shard_map/ppermute | solution.py:353
  13.5 16.5 %collective-permute-start.6 = (bf16[64,2048]{1,0:T(8,128)(2,1)S(1)}, bf16[64,2048]{1,0:T(8,128)(2,1)S(1)}, u32[]{:S(2)}, u32[]{:S(2)}) collective-permute-start(bf16[64,2048]{1,0:T(8,128)(2,1)S(1)} %bitcast.18), channel_id=1, source_target_pairs={{0,5},{1,4},{2,7},{3,6},{4,9},{5,8},{6,11},{7,10},{8,13},{9,12},{1... | collective-permute-start | bytes 786440 | tf_op jit(solution)/shard_map/ppermute | solution.py:350
  16.0 16.1 %collective-permute-start.4 = (bf16[64,2048]{1,0:T(8,128)(2,1)S(1)}, bf16[64,2048]{1,0:T(8,128)(2,1)S(1)}, u32[]{:S(2)}, u32[]{:S(2)}) collective-permute-start(bf16[64,2048]{1,0:T(8,128)(2,1)S(1)} %bitcast.19), channel_id=1, source_target_pairs={{0,13},{1,12},{2,15},{3,14},{4,1},{5,0},{6,3},{7,2},{8,5},{9,4},{1... | collective-permute-start | bytes 786440 | tf_op jit(solution)/shard_map/ppermute | solution.py:350
  19.2 13.1 %collective-permute-start.9 = (bf16[64,2048]{1,0:T(8,128)(2,1)S(1)}, bf16[64,2048]{1,0:T(8,128)(2,1)S(1)}, u32[]{:S(2)}, u32[]{:S(2)}) collective-permute-start(bf16[64,2048]{1,0:T(8,128)(2,1)S(1)} %collective-permute-done.1.refs_2_), channel_id=1, source_target_pairs={{0,4},{1,5},{2,6},{3,7},{4,8},{5,9},{6,10},{7,11},{8,12},{9,13},{1... | collective-permute-start | bytes 786440 | tf_op jit(solution)/shard_map/ppermute | solution.py:350
  19.2 16.4 %collective-permute-start.8 = (bf16[64,2048]{1,0:T(8,128)(2,1)S(1)}, bf16[64,2048]{1,0:T(8,128)(2,1)S(1)}, u32[]{:S(2)}, u32[]{:S(2)}) collective-permute-start(bf16[64,2048]{1,0:T(8,128)(2,1)S(1)} %collective-permute-done.2.refs_3_), channel_id=1, source_target_pairs={{0,12},{1,13},{2,14},{3,15},{4,0},{5,1},{6,2},{7,3},{8,4},{9,5},{1... | collective-permute-start | bytes 786440 | tf_op jit(solution)/shard_map/ppermute | solution.py:350
  22.4 13.2 %collective-permute-start.11 = (bf16[64,2048]{1,0:T(8,128)(2,1)S(1)}, bf16[64,2048]{1,0:T(8,128)(2,1)S(1)}, u32[]{:S(2)}, u32[]{:S(2)}) collective-permute-start(bf16[64,2048]{1,0:T(8,128)(2,1)S(1)} %collective-permute-done.5.refs_6_), channel_id=1, source_target_pairs={{0,4},{1,5},{2,6},{3,7},{4,8},{5,9},{6,10},{7,11},{8,12},{9,13},{1... | collective-permute-start | bytes 786440 | tf_op jit(solution)/shard_map/ppermute | solution.py:350
  22.4 0.9 copy-start.1
  23.3 0.8 copy-start.3
  24.9 0.9 copy-start.7
  25.8 0.9 copy-start.9
  26.7 0.7 copy-start.11
  29.9 13.3 %collective-permute-start.7 = (bf16[64,2048]{1,0:T(8,128)(2,1)S(1)}, bf16[64,2048]{1,0:T(8,128)(2,1)S(1)}, u32[]{:S(2)}, u32[]{:S(2)}) collective-permute-start(bf16[64,2048]{1,0:T(8,128)(2,1)S(1)} %collective-permute-done.3.refs_4_), channel_id=1, source_target_pairs={{0,2},{1,3},{2,0},{3,1},{4,6},{5,7},{6,4},{7,5},{8,10},{9,11},{10,... | collective-permute-start | bytes 786440 | tf_op jit(solution)/shard_map/ppermute | solution.py:350
  32.1 11.2 %collective-permute-start.10 = (bf16[64,2048]{1,0:T(8,128)(2,1)S(1)}, bf16[64,2048]{1,0:T(8,128)(2,1)S(1)}, u32[]{:S(2)}, u32[]{:S(2)}) collective-permute-start(bf16[64,2048]{1,0:T(8,128)(2,1)S(1)} %collective-permute-done.6.refs_7_), channel_id=1, source_target_pairs={{0,2},{1,3},{2,0},{3,1},{4,6},{5,7},{6,4},{7,5},{8,10},{9,11},{10,... | collective-permute-start | bytes 786440 | tf_op jit(solution)/shard_map/ppermute | solution.py:350
  32.2 11.1 %collective-permute-start.12 = (bf16[64,2048]{1,0:T(8,128)(2,1)S(1)}, bf16[64,2048]{1,0:T(8,128)(2,1)S(1)}, u32[]{:S(2)}, u32[]{:S(2)}) collective-permute-start(bf16[64,2048]{1,0:T(8,128)(2,1)S(1)} %collective-permute-done.4.refs_5_), channel_id=1, source_target_pairs={{0,12},{1,13},{2,14},{3,15},{4,0},{5,1},{6,2},{7,3},{8,4},{9,5},{1... | collective-permute-start | bytes 786440 | tf_op jit(solution)/shard_map/ppermute | solution.py:350
  35.6 7.7 %collective-permute-start.13 = (bf16[64,2048]{1,0:T(8,128)(2,1)S(1)}, bf16[64,2048]{1,0:T(8,128)(2,1)S(1)}, u32[]{:S(2)}, u32[]{:S(2)}) collective-permute-start(bf16[64,2048]{1,0:T(8,128)(2,1)S(1)} %collective-permute-done.9.refs_10_), channel_id=1, source_target_pairs={{0,4},{1,5},{2,6},{3,7},{4,8},{5,9},{6,10},{7,11},{8,12},{9,13},{1... | collective-permute-start | bytes 786440 | tf_op jit(solution)/shard_map/ppermute | solution.py:350
  35.6 9.6 %collective-permute-start.14 = (bf16[64,2048]{1,0:T(8,128)(2,1)S(1)}, bf16[64,2048]{1,0:T(8,128)(2,1)S(1)}, u32[]{:S(2)}, u32[]{:S(2)}) collective-permute-start(bf16[64,2048]{1,0:T(8,128)(2,1)S(1)} %collective-permute-done.8.refs_9_), channel_id=1, source_target_pairs={{0,12},{1,13},{2,14},{3,15},{4,0},{5,1},{6,2},{7,3},{8,4},{9,5},{1... | collective-permute-start | bytes 786440 | tf_op jit(solution)/shard_map/ppermute | solution.py:350
  38.9 6.4 %copy-start.6 = (bf16[128,576]{1,0:T(8,128)(2,1)S(1)}, bf16[128,576]{1,0:T(8,128)(2,1)}, u32[]{:S(2)}) copy-start(bf16[128,576]{1,0:T(8,128)(2,1)} %constant.25.clone.refs_23_) | copy-start | bytes 442372
  38.9 6.4 %copy-start.8 = (bf16[128,384]{1,0:T(8,128)(2,1)S(1)}, bf16[128,384]{1,0:T(8,128)(2,1)}, u32[]{:S(2)}) copy-start(bf16[128,384]{1,0:T(8,128)(2,1)} %constant.24.clone.refs_22_) | copy-start | bytes 294916
  52.4 43.2 %copy-start.4 = (f32[75,80]{1,0:T(8,128)S(1)}, f32[75,80]{1,0:T(8,128)}, u32[]{:S(2)}) copy-start(f32[75,80]{1,0:T(8,128)} %constant.26.clone.order) | copy-start | bytes 72004
  54.5 11.3 %all-to-all-start = ((bf16[8,176,128]{2,1,0:T(8,128)(2,1)}), bf16[8,176,128]{2,1,0:T(8,128)(2,1)S(1)}, u32[]{:S(2)}, u32[]{:S(2)}) async-start(bf16[8,176,128]{2,1,0:T(8,128)(2,1)} %shard_map.143), calls=%async_computation | async-start | bytes 720896 | tf_op jit(solution)/shard_map/all_to_all | solution.py:419
  59.0 6.1 %collective-permute-start.18 = (bf16[128,128]{1,0:T(8,128)(2,1)S(1)}, bf16[128,128]{1,0:T(8,128)(2,1)S(1)}, u32[]{:S(2)}, u32[]{:S(2)}) collective-permute-start(bf16[128,128]{1,0:T(8,128)(2,1)S(1)} %get-tuple-element.30), channel_id=1, source_target_pairs={{16,1},{18,3},{20,5},{22,7},{24,9},{26,11},{28,13},{30,15},{32,17}... | collective-permute-start | bytes 98312 | tf_op jit(solution)/shard_map/ppermute | solution.py:353
  65.8 14.1 %all-to-all-start.2 = ((bf16[16,8,384]{2,1,0:T(8,128)(2,1)}), bf16[16,8,384]{2,1,0:T(8,128)(2,1)S(1)}, u32[]{:S(2)}, u32[]{:S(2)}) async-start(bf16[16,8,384]{2,1,0:T(8,128)(2,1)} %bitcast), calls=%async_computation.2 | async-start | bytes 196608 | tf_op jit(solution)/shard_map/all_to_all | solution.py:420
  (2 other events, 1.4 us)

commit v3 on v2

v3 whole, which is shorter than its diff:
```python
import math

import jax
import jax.numpy as jnp
from jax import lax
from jax.experimental import pallas as pl
from jax.experimental.pallas import tpu as pltpu
from jax.sharding import Mesh
from jax.sharding import PartitionSpec as P

EPS = 1e-05
LANES = 384
HALF = 128
ROWS = 32
GROUP = 16
OWN = 64
STEP = 4
EARLY = 14
MIB = 1024 * 1024

CHIPS = ((0, 0), (0, 1), (1, 0), (3, 0), (1, 1), (3, 1), (2, 0), (2, 1))


STRIPS = ("z_hi", "y")
CHAN = ("x", "z_lo", "core")


def route(dx, dz, core):
    return [(i, ((i // 4 + dx) % 4) * 4 + ((i // 2) % 2 ^ dz) * 2 + (i % 2 ^ core)) for i in range(16)]


def seams():
    pairs = [(16 * s + 2 * q, 16 * s - 16 + 2 * q + 1) for s in range(1, 16) for q in range(8)]
    return pairs + [(b, a) for a, b in pairs]


f32 = jnp.float32
bf16 = jnp.bfloat16


def tap(distance):
    return math.exp(-distance * distance / 8.0) if abs(distance) <= 4 else 0.0


def taps(distance):
    far = jnp.abs(distance) > 4
    distance = distance.astype(f32)
    return jnp.where(far, 0.0, jnp.exp(distance * distance * (-1.0 / 8.0)))


def places(shape):
    return tuple(lax.broadcasted_iota(jnp.int32, shape, dim) for dim in (0, 1))


def column_pool():
    lane, target = places((LANES, HALF))
    return taps(2 * target - lane + 4).astype(bf16)


def column_spread():
    target, lane = places((HALF, LANES))
    return taps(2 * target - lane + 4).astype(bf16)


def row_pool():
    a, i = places((ROWS // 2, ROWS))
    return taps(2 * a - i)


def split_group(row):
    q = row & (GROUP - 1)
    colour = jnp.where(q < 5, 0, jnp.where(q < 10, 1, jnp.where(q < 15, 2, 3)))
    return row >> 4, colour, q - 5 * colour


def ones(hit, dtype=bf16):
    return jnp.where(hit, 1.0, 0.0).astype(dtype)


def replicate_rows():
    out, src = places((36 * GROUP, 3 * ROWS))
    r, colour, _ = split_group(out)
    return ones(((src & 31) == r - 2) & ((src >> 5) == colour))


def fold_rows():
    out, src = places((128, 36 * GROUP))
    r, colour, _ = split_group(src)
    i = 2 * (out >> 3) + (out & 1)
    return ones((r == i + 2) & (colour == ((out & 7) >> 1)) & (colour < 3))


def entry_order(dtype, rows=75):
    entry, out = places((rows, 80))
    a, colour, b = split_group(out)
    return ones((entry == 25 * colour + 5 * a + b) & (colour < 3), dtype)


def on_second():
    return lax.axis_index("core") == 1


def block_of(p):
    dx, dz = CHIPS[p // 2]
    ex = lax.rem(lax.axis_index("x") + dx, 4)
    zed = lax.rem(lax.axis_index("z_lo") + dz, 2)
    core = lax.rem(lax.axis_index("core") + p % 2, 2)
    return ex * 4 + zed * 2 + core


def dot(a, b):
    return jnp.dot(a, b, preferred_element_type=f32)


def dot_nt(a, b):
    return lax.dot_general(a, b, (((1,), (1,)), ((), ())), preferred_element_type=f32)


def rim_kernel(stacked, *refs):
    tile = refs[-1]
    second = on_second()
    for c in range(4):
        value = stacked[c].astype(f32)
        tile[c] = jnp.where(second, value[:, 384:], value[:, :128]).astype(bf16)


def patch_kernel(
    stacked, beyond, own_both, partner_both,
    patches, tissue, scale, norm, inv_square, inv_density, anch, anch_t, wturned,
):
    second = on_second()

    def half(c, shift):
        middle, rim = stacked[c].astype(f32), beyond[c].astype(f32)
        wide = jnp.concatenate([rim, middle, rim], axis=1)
        part = jnp.where(second, wide[:, 256:], wide[:, :512])
        return pltpu.roll(part, 512 - shift, 1)[:, :LANES]

    colours = [half(c, 122) for c in range(3)]
    here = half(3, 124)
    lane = lax.broadcasted_iota(jnp.int32, here.shape, 1)
    here = jnp.where(lane < 263, here, 0.0)
    tissue[...] = here
    x = dot(replicate_rows(), jnp.concatenate(colours, axis=0).astype(bf16))
    offset = (lax.broadcasted_iota(jnp.int32, x.shape, 0) % GROUP) % 5
    s = x
    for b in range(1, 5):
        s = jnp.where(offset == b, pltpu.roll(x, LANES - b, 1), s)
    patches[...] = s.astype(bf16)
    square = jnp.sum((s * s).reshape(36, GROUP, LANES), axis=1)
    total = square[0:ROWS]
    for a in range(1, 5):
        total = total + square[a : a + ROWS]
    total = total + EPS
    root = lax.rsqrt(total)
    scale[...] = 4.0 * root
    norm[...] = total * root
    inv_square[...] = 1.0 / total
    counted = dot(here.astype(bf16), column_pool())
    density = jnp.dot(row_pool(), counted, precision=lax.Precision.HIGHEST, preferred_element_type=f32)
    inv_density[...] = 1.0 / jnp.maximum(density, 1.0)
    both = jnp.concatenate([own_both[1024:1088, :], partner_both[1024:1088, :]], axis=0)
    ordered = dot(both, entry_order(bf16, 128))
    anch[...] = ordered.astype(bf16)
    anch_t[...] = ordered.T.astype(bf16)
    blocks = [pl.ds(pl.multiple_of(block_of(p) * OWN, OWN), OWN) for p in range(16)]
    for at, both in ((0, own_both), (OWN, partner_both)):
        ordered = jnp.concatenate([both[block, :] for block in blocks], axis=0)
        wturned[at : at + OWN, :] = ordered.astype(f32).T[:OWN].astype(bf16)


def forward_kernel(
    patches, tissue, scale, norm, inv_density, anch,
    masked, whitened,
    columned, pool,
):
    pool[...] = column_pool()

    @pl.loop(0, ROWS // STEP)
    def _(t):
        lifted = []
        for r in range(STEP):
            i = t * STEP + r
            patch = patches[pl.ds(pl.multiple_of(i * GROUP, GROUP), 80), :]
            raw = dot(anch[...], patch)
            value = jnp.exp(raw * scale[pl.ds(i, 1), :] - 4.0) * tissue[pl.ds(i, 1), :]
            masked[i] = value.astype(bf16)
            lifted.append((value * norm[pl.ds(i, 1), :]).astype(bf16))
        result = dot(jnp.concatenate(lifted, axis=0), pool[...])
        columned[pl.ds(t * STEP, STEP)] = result.reshape(STEP, 128, HALF)

    for a in range(ROWS // 2):
        acc = None
        for i in range(max(0, 2 * a - 4), min(ROWS, 2 * a + 5)):
            term = tap(2 * a - i) * columned[i]
            acc = term if acc is None else acc + term
        whitened[:, a * HALF : (a + 1) * HALF] = (acc * inv_density[a : a + 1, :]).astype(bf16)


def fold(block, rows):
    top, low = block[:rows], block[rows:]
    left = lax.broadcasted_iota(jnp.int32, top.shape, 1) < OWN
    own = jnp.where(left, top, pltpu.roll(low, OWN, 1))
    partner = jnp.where(left, pltpu.roll(top, OWN, 1), low)
    return own.astype(bf16), partner.astype(bf16)


def gather_products(blocks, first, wturned, whitened, partial):
    grad_w, pooled = None, []
    weights = wturned[:, first * OWN : (first + len(blocks)) * OWN]
    for n in range(8):
        cols = pl.ds(n * 256, 256)
        stack = jnp.concatenate([block[:, cols] for block in blocks], axis=0)
        term = dot(weights, stack)
        pooled.append(term if partial is None else term + partial[:, cols])
        term = dot_nt(stack, whitened[:, cols])
        grad_w = term if grad_w is None else grad_w + term
    return pooled, grad_w


def place_rows(packed, grad_w, first):
    core = lax.axis_index("core")
    for n in range(grad_w.shape[0] // OWN):
        strip = block_of(first + n)
        rows = pl.ds(pl.multiple_of((strip // 4) * 32, 32), 32)
        y = lax.rem(strip, 4)
        mine, theirs = fold(grad_w[n * OWN : (n + 1) * OWN], OWN // 2)
        packed[y * 2 + core, rows, :] = mine
        packed[y * 2 + 1 - core, rows, :] = theirs


def early_kernel(*refs):
    blocks = refs[:EARLY]
    wturned, whitened, partial, packed = refs[EARLY:]
    packed[...] = jnp.zeros_like(packed)
    pooled, grad_w = gather_products(blocks, 0, wturned, whitened, None)
    for n in range(8):
        partial[:, n * 256 : (n + 1) * 256] = pooled[n]
    place_rows(packed, grad_w, 0)


def backward_kernel(*refs):
    blocks = refs[: 16 - EARLY]
    (
        partial, early, wturned, whitened, inv_density, masked, patches, inv_square, anch_t,
        packed, image, rim,
        rowed, spread_grad, anchor_grad, pool_t,
    ) = refs[16 - EARLY :]
    pool_t[...] = column_spread()
    packed[:, 0:128, :] = early[...]
    pooled, grad_w = gather_products(blocks, EARLY, wturned, whitened, partial)
    place_rows(packed, grad_w, EARLY)
    scaled = []
    for a in range(ROWS // 2):
        part = pooled[a // 2][:, (a % 2) * HALF : (a % 2 + 1) * HALF]
        scaled.append(part.astype(bf16).astype(f32) * inv_density[a : a + 1, :])
    for i in range(ROWS):
        acc = None
        for a in range(ROWS // 2):
            if abs(2 * a - i) <= 4:
                term = (4.0 * tap(2 * a - i)) * scaled[a]
                acc = term if acc is None else acc + term
        rowed[i * 128 : (i + 1) * 128, :] = acc.astype(bf16)
    spread_grad[...] = jnp.zeros_like(spread_grad)
    anchor_grad[...] = jnp.zeros_like(anchor_grad)

    @pl.loop(0, ROWS // STEP)
    def _(t):
        start = pl.multiple_of(t * (STEP * 128), STEP * 128)
        spread = dot(rowed[pl.ds(start, STEP * 128), :], pool_t[...])
        grads, wides, units = [], [], []
        for r in range(STEP):
            i = t * STEP + r
            patch = patches[pl.ds(pl.multiple_of(i * GROUP, GROUP), 80), :]
            grad = (spread[r * 128 : (r + 1) * 128] * masked[i].astype(f32)).astype(bf16)
            unit = dot(anch_t[...], grad)
            wide = patch.astype(f32)
            along = jnp.sum(wide * unit, axis=0, keepdims=True) * inv_square[pl.ds(i, 1), :]
            units.append(unit - wide * along)
            grads.append(grad)
            wides.append(patch)
        anchor_grad[...] += dot_nt(jnp.concatenate(wides, axis=1), jnp.concatenate(grads, axis=1))
        sums = []
        for g in range(STEP + 4):
            acc = None
            for r in range(STEP):
                if 0 <= g - r < 5:
                    term = units[r][(g - r) * GROUP : (g - r + 1) * GROUP]
                    acc = term if acc is None else acc + term
            sums.append(acc)
        here = pl.ds(pl.multiple_of(t * (STEP * GROUP), STEP * GROUP), (STEP + 4) * GROUP)
        spread_grad[here, :] += jnp.concatenate(sums, axis=0)

    core = lax.axis_index("core")
    mine, theirs = fold(anchor_grad[...], 40)
    pad = jnp.zeros((8, 128), bf16)
    mine = jnp.concatenate([mine, pad], axis=0)
    theirs = jnp.concatenate([theirs, pad], axis=0)
    for y in range(4):
        packed[y * 2 + core, 128:176, :] = mine
        packed[y * 2 + 1 - core, 128:176, :] = theirs

    t = spread_grad[...]
    offset = (lax.broadcasted_iota(jnp.int32, t.shape, 0) % GROUP) % 5
    moved = t
    for b in range(1, 5):
        moved = jnp.where(offset == b, pltpu.roll(t, b, 1), moved)
    high = moved.astype(bf16)
    low = (moved - high.astype(f32)).astype(bf16)
    folder = fold_rows()
    summed = dot(folder, high) + dot(folder, low)
    image[...] = summed.astype(bf16)
    first, last = summed[:, :128], summed[:, 256:]
    lane = lax.broadcasted_iota(jnp.int32, first.shape, 1)
    first, last = jnp.where(lane < 6, first, 0.0), jnp.where(lane < 6, 0.0, last)
    rim[...] = jnp.where(on_second(), last, first).astype(bf16)


def seam_kernel(image, rim, joined):
    second = on_second()
    value = rim[...].astype(f32)
    first = image[:, :128].astype(f32) + jnp.where(second, 0.0, value)
    last = image[:, 256:].astype(f32) + jnp.where(second, value, 0.0)
    joined[:, :128] = first.astype(bf16)
    joined[:, 128:256] = image[:, 128:256]
    joined[:, 256:] = last.astype(bf16)


def pack_kernel(received, kept, next_one, next_two, next_three, sums):
    total = received[0].astype(f32)
    for source in range(1, 8):
        total = total + received[source].astype(f32)
    sums[...] = total[0:128]
    anchor = total[128:176].astype(bf16)
    for step, packed in enumerate((kept, next_one, next_two, next_three)):
        z = lax.rem(lax.axis_index("z_hi") + step, 4)
        packed[0:32, :] = sums[pl.ds(pl.multiple_of(z * 32, 32), 32), :].astype(bf16)
        packed[32:80, :] = anchor


def unpack_kernel(kept, one, two, three, grad_anchors, grad_whiten):
    total = sum(ref[...].astype(f32) for ref in (one, two, three)) + kept[...].astype(f32)
    other = pltpu.roll(total, OWN, 1)
    grad_whiten[0:32, :] = total[0:32, :OWN]
    grad_whiten[32:64, :] = other[0:32, :OWN]
    turned = jnp.concatenate([total[32:72], other[32:72]], axis=0).T[:OWN]
    grad_anchors[...] = lax.dot_general(
        turned, entry_order(f32), (((1,), (1,)), ((), ())),
        precision=lax.Precision.HIGHEST, preferred_element_type=f32,
    )


def image_kernel(parts, grad_image):
    halves = []
    for k in range(2):
        acc = parts[k].astype(f32)
        for chip in range(1, 8):
            acc = acc + parts[2 * chip + k].astype(f32)
        halves.append(acc)
    gap = jnp.zeros((8, 256), f32)
    whole = jnp.concatenate([halves[0], gap], axis=1) + jnp.concatenate([gap, halves[1]], axis=1)
    image = pltpu.roll(whole, 640 - 6, 1)[:, :512]
    for colour in range(3):
        grad_image[colour] = image[2 * colour : 2 * colour + 2]


def call(kernel, outs, scratch, flops, limit, *args, loose=0):
    size = lambda shape, dtype: math.prod(shape) * jnp.dtype(dtype).itemsize
    tight = len(args) - loose
    moved = sum(size(a.shape, a.dtype) for a in args[:tight]) + sum(size(*out) for out in outs)
    return pl.pallas_call(
        kernel,
        out_shape=[jax.ShapeDtypeStruct(shape, dtype) for shape, dtype in outs],
        in_specs=[pl.BlockSpec(memory_space=pltpu.VMEM)] * tight
        + [pl.BlockSpec(memory_space=pl.ANY)] * loose,
        out_specs=[pl.BlockSpec(memory_space=pltpu.VMEM)] * len(outs),
        scratch_shapes=[pltpu.VMEM(shape, dtype) for shape, dtype in scratch],
        compiler_params=pltpu.CompilerParams(vmem_limit_bytes=limit * MIB),
        cost_estimate=pl.CostEstimate(flops=flops, bytes_accessed=moved, transcendentals=0),
    )(*args)


def shards(image, mask, anchors, whiten, cotangent):
    second = on_second()

    def send(value, dx, dz, other):
        return lax.ppermute(value, CHAN, route(dx, dz, other))

    def cross(value):
        return lax.ppermute(value, STRIPS + CHAN, seams())

    left, right = cotangent[:, :, :HALF], cotangent[:, :, HALF:]
    own = jnp.where(second, right, left).reshape(OWN, -1)
    away = jnp.where(second, left, right).reshape(OWN, -1)
    held = {(0, 0): (own, send(away, 0, 0, 1))}
    for dx, dz in ((1, 0), (3, 0), (0, 1)):
        held[(4 - dx) % 4, dz] = (send(own, dx, dz, 0), send(away, dx, dz, 1))
    far_own = send(held[0, 1][0], 1, 0, 0)
    far_partner = send(held[0, 1][1], 3, 0, 0)
    held[3, 1] = (far_own, send(held[3, 0][1], 0, 1, 0))
    held[1, 1] = (send(held[1, 0][0], 0, 1, 0), far_partner)
    held[2, 0] = (send(held[3, 0][0], 1, 0, 0), send(held[1, 0][1], 3, 0, 0))
    held[2, 1] = (send(far_own, 1, 0, 0), send(far_partner, 3, 0, 0))
    blocks = [block for chip in CHIPS for block in held[chip]]

    stacked = jnp.concatenate([image, mask.astype(bf16)[None]], axis=0)
    (tile,) = call(
        rim_kernel,
        [((4, ROWS, 128), bf16)],
        [],
        1_000_000,
        4,
        stacked, held[0, 0][1], *(block for chip in ((0, 1), (1, 0), (3, 0)) for block in held[chip]),
        loose=7,
    )
    both = jnp.concatenate(
        [jnp.pad(whiten, ((0, 0), (0, OWN))), jnp.pad(anchors, ((0, 0), (0, 53)))], axis=0
    )
    plane = ((ROWS, LANES), f32)
    patches, tissue, scale, norm, inv_square, inv_density, anch, anch_t, wturned = call(
        patch_kernel,
        [
            ((36 * GROUP, LANES), bf16),
            plane,
            plane,
            plane,
            plane,
            ((16, HALF), f32),
            ((128, 80), bf16),
            ((80, 128), bf16),
            ((128, 1024), bf16),
        ],
        [],
        1_000_000_000,
        12,
        stacked, cross(tile), both, send(both, 0, 0, 1),
    )
    masked, whitened = call(
        forward_kernel,
        [((ROWS, 128, LANES), bf16), ((128, 16 * HALF), bf16)],
        [((ROWS, 128, HALF), f32), ((LANES, HALF), bf16)],
        3_000_000_000,
        14,
        patches, tissue, scale, norm, inv_density, anch,
    )
    partial, early = call(
        early_kernel,
        [((128, 16 * HALF), f32), ((8, 128, 128), bf16)],
        [],
        2_000_000_000,
        14,
        *blocks[:EARLY], wturned, whitened,
    )
    packed, image_part, rim = call(
        backward_kernel,
        [((8, 176, 128), bf16), ((128, LANES), bf16), ((128, 128), bf16)],
        [
            ((ROWS * 128, HALF), bf16),
            ((36 * GROUP, LANES), f32),
            ((80, 128), f32),
            ((HALF, LANES), bf16),
        ],
        5_000_000_000,
        20,
        *blocks[EARLY:],
        partial, early, wturned, whitened, inv_density, masked, patches, inv_square, anch_t,
    )
    (joined,) = call(seam_kernel, [((128, LANES), bf16)], [], 1_000_000, 4, image_part, cross(rim))

    received = lax.all_to_all(packed, ("y", "core"), 0, 0)
    parts = lax.all_to_all(joined.reshape(16, 8, LANES), CHAN, 0, 0)
    quarter = ((80, 128), bf16)
    kept, *away = call(pack_kernel, [quarter] * 4, [((128, 128), f32)], 1_000_000, 4, received)
    others = [
        lax.ppermute(value, "z_hi", [(z, (z + step) % 4) for z in range(4)])
        for step, value in enumerate(away, 1)
    ]
    (grad_image,) = call(image_kernel, [((3, 2, 512), f32)], [], 1_000_000, 4, parts)
    grad_anchors, grad_whiten = call(
        unpack_kernel, [((OWN, 75), f32), ((OWN, OWN), f32)], [], 1_000_000, 4, kept, *others
    )
    return grad_anchors, grad_whiten, grad_image


def solution(mesh):
    fine = Mesh(mesh.devices.reshape(4, 4, 4, 2, 2), STRIPS + CHAN)
    placed = (
        P(None, None, STRIPS),
        P(None, STRIPS),
        P(CHAN, None),
        P(None, CHAN),
        P(CHAN, None, STRIPS),
    )
    return jax.shard_map(
        shards,
        mesh=fine,
        in_specs=placed,
        out_specs=(P(CHAN, None), P(STRIPS, CHAN), P(None, CHAN, STRIPS)),
        check_vma=False,
    )
```

time: 97.8 us -> 86.9 us (0.89)
  blocking collectives: 15.7 us -> 0 us
  starting transfers between devices: 40.9 us -> 50.7 us
  local copies, waits for them, and re-layouts: 8.63 us -> 1.21 us
  other arithmetic: 1.1 us -> 2.74 us
    all_to_all x1 -> x0, blocking collectives: 15.7 us -> none  [shards(): received = lax.all_to_all(packed, 'z_hi', 0, 0)]
    ppermute x0 -> x3, starting transfers between devices: none -> 10.6 us  [shards(): lax.ppermute(value, 'z_hi', [(z, (z + step) % 4) for z in range(4)])]
    unnamed x29 -> x5, local copies, waits for them, and re-layouts: 8.63 us -> 1.21 us
    all_to_all x1, waiting for transfers between devices: 6.25 us -> 0.01 us  [shards(): parts = lax.all_to_all(joined.reshape(16, 8, LANES), CHAN, 0, 0)]
    ppermute x17 -> x16, waiting for transfers between devices: 2.42 us -> 5.21 us  [send(): return lax.ppermute(value, CHAN, route(dx, dz, other))]
    ppermute x2, waiting for transfers between devices: 3.64 us -> 5.92 us  [cross(): return lax.ppermute(value, STRIPS + CHAN, seams())]
    all_to_all x1, starting transfers between devices: 4.51 us -> 6.63 us  [shards(): received = lax.all_to_all(packed, ('y', 'core'), 0, 0)]
    ppermute x17 -> x16, starting transfers between devices: 23.4 us -> 21.6 us  [send(): return lax.ppermute(value, CHAN, route(dx, dz, other))]
  transfers between devices with their start and end apart: 21 -> 23, of which waited for: 4 -> 7; matrix products, arithmetic and copies ran while one was open for 1% -> 3% of each run, Pallas kernels for 7% -> 11%
where the time goes in v3:
time: 86.9 us; the launch traced here: 85.4 us
  starting transfers between devices  50.7 us (58%)
  Pallas kernels  17.4 us (20%)
  waiting for transfers between devices  12.5 us (14%)
  other arithmetic  2.74 us (3%)
  local copies, waits for them, and re-layouts  1.21 us (1%)
    ppermute x16, starting transfers between devices, send(): return lax.ppermute(value, CHAN, route(dx, dz, other))  21.6 us
    pallas_call x9, Pallas kernels, call(): pl.pallas_call(kernel, out_shape=[jax.ShapeDtypeStruct(shape, dtype) for...  17.4 us
    ppermute x3, starting transfers between devices, shards(): lax.ppermute(value, 'z_hi', [(z, (z + step) % 4) for z in range(4)])  10.6 us
    all_to_all x1, starting transfers between devices, shards(): parts = lax.all_to_all(joined.reshape(16, 8, LANES), CHAN, 0, 0)  6.97 us
    all_to_all x1, starting transfers between devices, shards(): received = lax.all_to_all(packed, ('y', 'core'), 0, 0)  6.63 us
    ppermute x2, waiting for transfers between devices, cross(): return lax.ppermute(value, STRIPS + CHAN, seams())  5.92 us
    ppermute x16, waiting for transfers between devices, send(): return lax.ppermute(value, CHAN, route(dx, dz, other))  5.21 us
    ppermute x2, starting transfers between devices, cross(): return lax.ppermute(value, STRIPS + CHAN, seams())  4.97 us
  transfers between devices with their start and end apart: 23, of which 7 were waited for; matrix products, arithmetic and copies ran while one was open for 3% of the time, Pallas kernels for 11%

profile of v3, /device:TPU:24, one launch (start us, length us, event | category | flops | bytes accessed | tf_op | source)
XLA Modules:
  0.0 85.4 jit_solution(3730500455850259854)
XLA Ops:
  0.6 1.1 %broadcast_select_fusion = (bf16[64,16,128]{2,1,0:T(8,128)(2,1)S(1)}, bf16[64,16,128]{2,1,0:T(8,128)(2,1)S(1)}) fusion(pred[]{:T(512)S(6)} %eq.3, bf16[64,16,256]{2,1,0:T(8,128)(2,1)} %param.9), kind=kLoop, calls=%fused_computation.7 | loop fusion | flops 262144 | bytes 1048577 | tf_op jit(solution)/shard_map/jit(_where)/select_n | solution.py:394
  1.8 2.0 %collective-permute-start = (bf16[64,2048]{1,0:T(8,128)(2,1)S(1)}, bf16[64,2048]{1,0:T(8,128)(2,1)S(1)}, u32[]{:S(2)}, u32[]{:S(2)}) collective-permute-start(bf16[64,2048]{1,0:T(8,128)(2,1)S(1)} %bitcast.11), channel_id=1, source_target_pairs={{0,2},{1,3},{2,0},{3,1},{4,6},{5,7},{6,4},{7,5},{8,10},{9,11},{10,... | collective-permute-start | bytes 786440 | tf_op jit(solution)/shard_map/ppermute | solution.py:387
  3.9 0.7 collective-permute-start.10
  5.3 1.7 %collective-permute-start.7 = (bf16[64,2048]{1,0:T(8,128)(2,1)S(1)}, bf16[64,2048]{1,0:T(8,128)(2,1)S(1)}, u32[]{:S(2)}, u32[]{:S(2)}) collective-permute-start(bf16[64,2048]{1,0:T(8,128)(2,1)S(1)} %bitcast.12), channel_id=1, source_target_pairs={{0,12},{1,13},{2,14},{3,15},{4,0},{5,1},{6,2},{7,3},{8,4},{9,5},{1... | collective-permute-start | bytes 786440 | tf_op jit(solution)/shard_map/ppermute | solution.py:387
  7.0 1.2 %collective-permute-start.8 = (bf16[64,2048]{1,0:T(8,128)(2,1)S(1)}, bf16[64,2048]{1,0:T(8,128)(2,1)S(1)}, u32[]{:S(2)}, u32[]{:S(2)}) collective-permute-start(bf16[64,2048]{1,0:T(8,128)(2,1)S(1)} %bitcast.19), channel_id=1, source_target_pairs={{0,13},{1,12},{2,15},{3,14},{4,1},{5,0},{6,3},{7,2},{8,5},{9,4},{1... | collective-permute-start | bytes 786440 | tf_op jit(solution)/shard_map/ppermute | solution.py:387
  8.2 2.9 %collective-permute-done.refs_1_.refs_2_ = bf16[64,2048]{1,0:T(8,128)(2,1)S(1)} collective-permute-done((bf16[64,2048]{1,0:T(8,128)(2,1)S(1)}, bf16[64,2048]{1,0:T(8,128)(2,1)S(1)}, u32[]{:S(2)}, u32[]{:S(2)}) %collective-permute-start) | collective-permute-done | bytes 262176 | tf_op jit(solution)/shard_map/ppermute | solution.py:387
  11.1 1.5 %collective-permute-start.9 = (bf16[64,2048]{1,0:T(8,128)(2,1)S(1)}, bf16[64,2048]{1,0:T(8,128)(2,1)S(1)}, u32[]{:S(2)}, u32[]{:S(2)}) collective-permute-start(bf16[64,2048]{1,0:T(8,128)(2,1)S(1)} %bitcast.13), channel_id=1, source_target_pairs={{0,4},{1,5},{2,6},{3,7},{4,8},{5,9},{6,10},{7,11},{8,12},{9,13},{1... | collective-permute-start | bytes 786440 | tf_op jit(solution)/shard_map/ppermute | solution.py:387
  12.6 1.1 %copy.8 = bf16[1024,64]{1,0:T(8,128)(2,1)S(1)} copy(bf16[1024,64]{0,1:T(8,128)(2,1)} %param.8) | data formatting | bytes 262144 | tf_op args[3]
  13.7 0.8 fusion.2.own_both
  15.0 0.9 %collective-permute-start.16 = (bf16[1088,128]{1,0:T(8,128)(2,1)S(1)}, bf16[1088,128]{1,0:T(8,128)(2,1)S(1)}, u32[]{:S(2)}, u32[]{:S(2)}) collective-permute-start(bf16[1088,128]{1,0:T(8,128)(2,1)S(1)} %fusion.2.own_both), channel_id=1, source_target_pairs={{0,1},{1,0},{2,3},{3,2},{4,5},{5,4},{6,7},{7,6},{8,9},{9,8},{10,11... | collective-permute-start | bytes 835592 | tf_op jit(solution)/shard_map/ppermute | solution.py:387
  15.9 1.5 %collective-permute-start.1 = (bf16[64,2048]{1,0:T(8,128)(2,1)S(1)}, bf16[64,2048]{1,0:T(8,128)(2,1)S(1)}, u32[]{:S(2)}, u32[]{:S(2)}) collective-permute-start(bf16[64,2048]{1,0:T(8,128)(2,1)S(1)} %collective-permute-done.refs_1_.refs_2_), channel_id=1, source_target_pairs={{0,4},{1,5},{2,6},{3,7},{4,8},{5,9},{6,10},{7,11},{8,12},{9,13},{1... | collective-permute-start | bytes 786440 | tf_op jit(solution)/shard_map/ppermute | solution.py:387
  17.4 1.4 %collective-permute-done.8.refs_4_.refs_5_ = bf16[64,2048]{1,0:T(8,128)(2,1)S(1)} collective-permute-done((bf16[64,2048]{1,0:T(8,128)(2,1)S(1)}, bf16[64,2048]{1,0:T(8,128)(2,1)S(1)}, u32[]{:S(2)}, u32[]{:S(2)}) %collective-permute-start.8) | collective-permute-done | bytes 262176 | tf_op jit(solution)/shard_map/ppermute | solution.py:387
  18.8 3.0 %collective-permute-start.4 = (bf16[64,2048]{1,0:T(8,128)(2,1)S(1)}, bf16[64,2048]{1,0:T(8,128)(2,1)S(1)}, u32[]{:S(2)}, u32[]{:S(2)}) collective-permute-start(bf16[64,2048]{1,0:T(8,128)(2,1)S(1)} %collective-permute-done.3.refs_2_.refs_3_), channel_id=1, source_target_pairs={{0,12},{1,13},{2,14},{3,15},{4,0},{5,1},{6,2},{7,3},{8,4},{9,5},{1... | collective-permute-start | bytes 786440 | tf_op jit(solution)/shard_map/ppermute | solution.py:387
  21.7 1.3 %collective-permute-start.11 = (bf16[64,2048]{1,0:T(8,128)(2,1)S(1)}, bf16[64,2048]{1,0:T(8,128)(2,1)S(1)}, u32[]{:S(2)}, u32[]{:S(2)}) collective-permute-start(bf16[64,2048]{1,0:T(8,128)(2,1)S(1)} %collective-permute-done.7.refs_3_.refs_4_), channel_id=1, source_target_pairs={{0,2},{1,3},{2,0},{3,1},{4,6},{5,7},{6,4},{7,5},{8,10},{9,11},{10,... | collective-permute-start | bytes 786440 | tf_op jit(solution)/shard_map/ppermute | solution.py:387
  23.1 0.8 convert_bitcast_fusion
  24.0 2.5 %collective-permute-start.15 = (bf16[4,32,128]{2,1,0:T(8,128)(2,1)S(1)}, bf16[4,32,128]{2,1,0:T(8,128)(2,1)S(1)}, u32[]{:S(2)}, u32[]{:S(2)}) collective-permute-start(bf16[4,32,128]{2,1,0:T(8,128)(2,1)S(1)} %shard_map.76), channel_id=1, source_target_pairs={{16,1},{18,3},{20,5},{22,7},{24,9},{26,11},{28,13},{30,15},{32,17}... | collective-permute-start | bytes 98312 | tf_op jit(solution)/shard_map/ppermute | solution.py:390
  26.9 2.3 %collective-permute-done.15.beyond = bf16[4,32,128]{2,1,0:T(8,128)(2,1)S(1)} collective-permute-done((bf16[4,32,128]{2,1,0:T(8,128)(2,1)S(1)}, bf16[4,32,128]{2,1,0:T(8,128)(2,1)S(1)}, u32[]{:S(2)}, u32[]{:S(2)}) %collective-permute-start.15) | collective-permute-done | bytes 32800 | tf_op jit(solution)/shard_map/ppermute | solution.py:390
  29.2 1.8 %shard_map.77 = (bf16[576,384]{1,0:T(8,128)(2,1)S(1)}, f32[32,384]{1,0:T(8,128)S(1)}, f32[32,384]{1,0:T(8,128)S(1)}, f32[32,384]{1,0:T(8,128)S(1)}, f32[32,384]{...) custom-call(bf16[4,32,512]{2,1,0:T(8,128)(2,1)S(1)} %pad_maximum_fus, ...), custom_call_target="tpu_custom_call" | custom-call | flops 1000000000 | bytes 1671168 | tf_op jit(solution)/shard_map/pallas_call | solution.py:371
  31.1 3.3 %collective-permute-start.14 = (bf16[64,2048]{1,0:T(8,128)(2,1)S(1)}, bf16[64,2048]{1,0:T(8,128)(2,1)S(1)}, u32[]{:S(2)}, u32[]{:S(2)}) collective-permute-start(bf16[64,2048]{1,0:T(8,128)(2,1)S(1)} %collective-permute-done.8.refs_4_.refs_5_), channel_id=1, source_target_pairs={{0,12},{1,13},{2,14},{3,15},{4,0},{5,1},{6,2},{7,3},{8,4},{9,5},{1... | collective-permute-start | bytes 786440 | tf_op jit(solution)/shard_map/ppermute | solution.py:387
  34.4 3.2 %collective-permute-start.5 = (bf16[64,2048]{1,0:T(8,128)(2,1)S(1)}, bf16[64,2048]{1,0:T(8,128)(2,1)S(1)}, u32[]{:S(2)}, u32[]{:S(2)}) collective-permute-start(bf16[64,2048]{1,0:T(8,128)(2,1)S(1)} %collective-permute-done.4.refs_9_), channel_id=1, source_target_pairs={{0,12},{1,13},{2,14},{3,15},{4,0},{5,1},{6,2},{7,3},{8,4},{9,5},{1... | collective-permute-start | bytes 786440 | tf_op jit(solution)/shard_map/ppermute | solution.py:387
  37.6 4.5 %shard_map.78 = (bf16[32,128,384]{2,1,0:T(8,128)(2,1)S(1)}, bf16[128,2048]{1,0:T(8,128)(2,1)S(1)}) custom-call(bf16[576,384]{1,0:T(8,128)(2,1)S(1)} %get-tuple-element.26.patches.refs_8_, f32[32,384]{1,0:T(8,128)S(1)} %get-tuple-element.27.tissue, f32[32,384]{1,0:T(8,128)S(1)} %get-tuple-element.28.scale, f32[32,384]{1,0:T(8,128)S(1)} %get-tuple-element.29.norm, ...), custom_call_target="tpu_custom_call" | custom-call | flops 3000000000 | bytes 4288512 | tf_op jit(solution)/shard_map/pallas_call | solution.py:371
  42.1 1.8 %shard_map.79 = (f32[128,2048]{1,0:T(8,128)S(1)}, bf16[8,128,128]{2,1,0:T(8,128)(2,1)S(1)}) custom-call(bf16[64,2048]{1,0:T(8,128)(2,1)S(1)} %bitcast.14, bf16[64,2048]{1,0:T(8,128)(2,1)S(1)} %collective-permute-done.6.refs_0_.refs_1_, bf16[64,2048]{1,0:T(8,128)(2,1)S(1)} %collective-permute-done.refs_1_.refs_2_, ...), custom_call_target="tpu_custom_call" | custom-call | flops 2000000000 | bytes 5767168 | tf_op jit(solution)/shard_map/pallas_call | solution.py:371
  44.3 7.0 %shard_map.80 = (bf16[8,176,128]{2,1,0:T(8,128)(2,1)}, bf16[128,384]{1,0:T(8,128)(2,1)S(1)}, bf16[128,128]{1,0:T(8,128)(2,1)S(1)}) custom-call(bf16[64,2048]{1,0:T(8,128)(2,1)S(1)} %collective-permute-done.2.refs_0_, bf16[64,2048]{1,0:T(8,128)(2,1)S(1)} %collective-permute-done.5.refs_1_, f32[128,2048]{1,0:T(8,128)S(1)} %get-tuple-element.33.refs_2_, ...), custom_call_target="tpu_custom_call" | custom-call | flops 5000000000 | bytes 6778880 | tf_op jit(solution)/shard_map/pallas_call | solution.py:371
  51.3 6.6 %all-to-all-start = ((bf16[8,176,128]{2,1,0:T(8,128)(2,1)}), bf16[8,176,128]{2,1,0:T(8,128)(2,1)S(1)}, u32[]{:S(2)}, u32[]{:S(2)}) async-start(bf16[8,176,128]{2,1,0:T(8,128)(2,1)} %get-tuple-element.38), calls=%async_computation | async-start | bytes 720896 | tf_op jit(solution)/shard_map/all_to_all | solution.py:470
  58.0 2.5 %collective-permute-start.20 = (bf16[128,128]{1,0:T(8,128)(2,1)S(1)}, bf16[128,128]{1,0:T(8,128)(2,1)S(1)}, u32[]{:S(2)}, u32[]{:S(2)}) collective-permute-start(bf16[128,128]{1,0:T(8,128)(2,1)S(1)} %get-tuple-element.46), channel_id=1, source_target_pairs={{16,1},{18,3},{20,5},{22,7},{24,9},{26,11},{28,13},{30,15},{32,17}... | collective-permute-start | bytes 98312 | tf_op jit(solution)/shard_map/ppermute | solution.py:390
  60.5 3.6 %collective-permute-done.20.rim = bf16[128,128]{1,0:T(8,128)(2,1)S(1)} collective-permute-done((bf16[128,128]{1,0:T(8,128)(2,1)S(1)}, bf16[128,128]{1,0:T(8,128)(2,1)S(1)}, u32[]{:S(2)}, u32[]{:S(2)}) %collective-permute-start.20) | collective-permute-done | bytes 32800 | tf_op jit(solution)/shard_map/ppermute | solution.py:390
  64.8 7.0 %all-to-all-start.1 = ((bf16[16,8,384]{2,1,0:T(8,128)(2,1)}), bf16[16,8,384]{2,1,0:T(8,128)(2,1)S(1)}, u32[]{:S(2)}, u32[]{:S(2)}) async-start(bf16[16,8,384]{2,1,0:T(8,128)(2,1)} %bitcast.1), calls=%async_computation.1 | async-start | bytes 196608 | tf_op jit(solution)/shard_map/all_to_all | solution.py:471
  71.8 5.0 %collective-permute-start.17 = (bf16[80,128]{1,0:T(8,128)(2,1)S(1)}, bf16[80,128]{1,0:T(8,128)(2,1)S(1)}, u32[]{:S(2)}, u32[]{:S(2)}) collective-permute-start(bf16[80,128]{1,0:T(8,128)(2,1)S(1)} %get-tuple-element.40), channel_id=1, source_target_pairs={{0,64},{64,128},{128,192},{192,0},{1,65},{65,129},{129,193},{193,1... | collective-permute-start | bytes 61448 | tf_op jit(solution)/shard_map/ppermute | solution.py:475
  76.8 1.6 %collective-permute-start.18 = (bf16[80,128]{1,0:T(8,128)(2,1)S(1)}, bf16[80,128]{1,0:T(8,128)(2,1)S(1)}, u32[]{:S(2)}, u32[]{:S(2)}) collective-permute-start(bf16[80,128]{1,0:T(8,128)(2,1)S(1)} %get-tuple-element.41), channel_id=1, source_target_pairs={{0,128},{64,192},{128,0},{192,64},{1,129},{65,193},{129,1},{193,65... | collective-permute-start | bytes 61448 | tf_op jit(solution)/shard_map/ppermute | solution.py:475
  78.4 4.0 %collective-permute-start.19 = (bf16[80,128]{1,0:T(8,128)(2,1)S(1)}, bf16[80,128]{1,0:T(8,128)(2,1)S(1)}, u32[]{:S(2)}, u32[]{:S(2)}) collective-permute-start(bf16[80,128]{1,0:T(8,128)(2,1)S(1)} %get-tuple-element.42), channel_id=1, source_target_pairs={{0,192},{64,0},{128,64},{192,128},{1,193},{65,1},{129,65},{193,129... | collective-permute-start | bytes 61448 | tf_op jit(solution)/shard_map/ppermute | solution.py:475
  83.1 1.4 %collective-permute-done.18.two = bf16[80,128]{1,0:T(8,128)(2,1)S(1)} collective-permute-done((bf16[80,128]{1,0:T(8,128)(2,1)S(1)}, bf16[80,128]{1,0:T(8,128)(2,1)S(1)}, u32[]{:S(2)}, u32[]{:S(2)}) %collective-permute-start.18) | collective-permute-done | bytes 20512 | tf_op jit(solution)/shard_map/ppermute | solution.py:475
  84.5 0.9 %shard_map.82 = (f32[64,75]{1,0:T(8,128)}, f32[64,64]{1,0:T(8,128)}) custom-call(bf16[80,128]{1,0:T(8,128)(2,1)S(1)} %get-tuple-element.39.kept, bf16[80,128]{1,0:T(8,128)(2,1)S(1)} %collective-permute-done.17.one, bf16[80,128]{1,0:T(8,128)(2,1)S(1)} %collective-permute-done.18.two, bf16[80,128]{1,0:T(8,128)(2,1)S(1)} %collective-permute-done.19.three), custom_call_target="tpu_custom_call" | custom-call | flops 1000000 | bytes 117504 | tf_op jit(solution)/shard_map/pallas_call | solution.py:371
  (32 shorter events, 3.8 us)
Async XLA Ops:
  0.6 23.3 %copy-start = (bf16[3,32,512]{2,1,0:T(8,128)(2,1)S(1)}, bf16[3,32,512]{2,1,0:T(8,128)(2,1)}, u32[]{:S(2)}) copy-start(bf16[3,32,512]{2,1,0:T(8,128)(2,1)} %param.5) | copy-start | bytes 294916
  1.8 9.3 %collective-permute-start = (bf16[64,2048]{1,0:T(8,128)(2,1)S(1)}, bf16[64,2048]{1,0:T(8,128)(2,1)S(1)}, u32[]{:S(2)}, u32[]{:S(2)}) collective-permute-start(bf16[64,2048]{1,0:T(8,128)(2,1)S(1)} %bitcast.11), channel_id=1, source_target_pairs={{0,2},{1,3},{2,0},{3,1},{4,6},{5,7},{6,4},{7,5},{8,10},{9,11},{10,... | collective-permute-start | bytes 786440 | tf_op jit(solution)/shard_map/ppermute | solution.py:387
  3.9 10.5 %collective-permute-start.10 = (bf16[64,2048]{1,0:T(8,128)(2,1)S(1)}, bf16[64,2048]{1,0:T(8,128)(2,1)S(1)}, u32[]{:S(2)}, u32[]{:S(2)}) collective-permute-start(bf16[64,2048]{1,0:T(8,128)(2,1)S(1)} %bitcast.17), channel_id=1, source_target_pairs={{0,5},{1,4},{2,7},{3,6},{4,9},{5,8},{6,11},{7,10},{8,13},{9,12},{1... | collective-permute-start | bytes 786440 | tf_op jit(solution)/shard_map/ppermute | solution.py:387
  4.6 10.4 %collective-permute-start.3 = (bf16[64,2048]{1,0:T(8,128)(2,1)S(1)}, bf16[64,2048]{1,0:T(8,128)(2,1)S(1)}, u32[]{:S(2)}, u32[]{:S(2)}) collective-permute-start(bf16[64,2048]{1,0:T(8,128)(2,1)S(1)} %bitcast.18), channel_id=1, source_target_pairs={{0,3},{1,2},{2,1},{3,0},{4,7},{5,6},{6,5},{7,4},{8,11},{9,10},{10,... | collective-permute-start | bytes 786440 | tf_op jit(solution)/shard_map/ppermute | solution.py:387
  5.3 10.6 %collective-permute-start.7 = (bf16[64,2048]{1,0:T(8,128)(2,1)S(1)}, bf16[64,2048]{1,0:T(8,128)(2,1)S(1)}, u32[]{:S(2)}, u32[]{:S(2)}) collective-permute-start(bf16[64,2048]{1,0:T(8,128)(2,1)S(1)} %bitcast.12), channel_id=1, source_target_pairs={{0,12},{1,13},{2,14},{3,15},{4,0},{5,1},{6,2},{7,3},{8,4},{9,5},{1... | collective-permute-start | bytes 786440 | tf_op jit(solution)/shard_map/ppermute | solution.py:387
  7.0 11.7 %collective-permute-start.8 = (bf16[64,2048]{1,0:T(8,128)(2,1)S(1)}, bf16[64,2048]{1,0:T(8,128)(2,1)S(1)}, u32[]{:S(2)}, u32[]{:S(2)}) collective-permute-start(bf16[64,2048]{1,0:T(8,128)(2,1)S(1)} %bitcast.19), channel_id=1, source_target_pairs={{0,13},{1,12},{2,15},{3,14},{4,1},{5,0},{6,3},{7,2},{8,5},{9,4},{1... | collective-permute-start | bytes 786440 | tf_op jit(solution)/shard_map/ppermute | solution.py:387
  11.1 10.7 %collective-permute-start.9 = (bf16[64,2048]{1,0:T(8,128)(2,1)S(1)}, bf16[64,2048]{1,0:T(8,128)(2,1)S(1)}, u32[]{:S(2)}, u32[]{:S(2)}) collective-permute-start(bf16[64,2048]{1,0:T(8,128)(2,1)S(1)} %bitcast.13), channel_id=1, source_target_pairs={{0,4},{1,5},{2,6},{3,7},{4,8},{5,9},{6,10},{7,11},{8,12},{9,13},{1... | collective-permute-start | bytes 786440 | tf_op jit(solution)/shard_map/ppermute | solution.py:387
  14.4 9.5 %collective-permute-start.6 = (bf16[64,2048]{1,0:T(8,128)(2,1)S(1)}, bf16[64,2048]{1,0:T(8,128)(2,1)S(1)}, u32[]{:S(2)}, u32[]{:S(2)}) collective-permute-start(bf16[64,2048]{1,0:T(8,128)(2,1)S(1)} %bitcast.20), channel_id=1, source_target_pairs={{0,1},{1,0},{2,3},{3,2},{4,5},{5,4},{6,7},{7,6},{8,9},{9,8},{10,11... | collective-permute-start | bytes 786440 | tf_op jit(solution)/shard_map/ppermute | solution.py:387
  15.0 11.5 %collective-permute-start.16 = (bf16[1088,128]{1,0:T(8,128)(2,1)S(1)}, bf16[1088,128]{1,0:T(8,128)(2,1)S(1)}, u32[]{:S(2)}, u32[]{:S(2)}) collective-permute-start(bf16[1088,128]{1,0:T(8,128)(2,1)S(1)} %fusion.2.own_both), channel_id=1, source_target_pairs={{0,1},{1,0},{2,3},{3,2},{4,5},{5,4},{6,7},{7,6},{8,9},{9,8},{10,11... | collective-permute-start | bytes 835592 | tf_op jit(solution)/shard_map/ppermute | solution.py:387
  15.9 15.2 %collective-permute-start.1 = (bf16[64,2048]{1,0:T(8,128)(2,1)S(1)}, bf16[64,2048]{1,0:T(8,128)(2,1)S(1)}, u32[]{:S(2)}, u32[]{:S(2)}) collective-permute-start(bf16[64,2048]{1,0:T(8,128)(2,1)S(1)} %collective-permute-done.refs_1_.refs_2_), channel_id=1, source_target_pairs={{0,4},{1,5},{2,6},{3,7},{4,8},{5,9},{6,10},{7,11},{8,12},{9,13},{1... | collective-permute-start | bytes 786440 | tf_op jit(solution)/shard_map/ppermute | solution.py:387
  18.8 15.6 %collective-permute-start.4 = (bf16[64,2048]{1,0:T(8,128)(2,1)S(1)}, bf16[64,2048]{1,0:T(8,128)(2,1)S(1)}, u32[]{:S(2)}, u32[]{:S(2)}) collective-permute-start(bf16[64,2048]{1,0:T(8,128)(2,1)S(1)} %collective-permute-done.3.refs_2_.refs_3_), channel_id=1, source_target_pairs={{0,12},{1,13},{2,14},{3,15},{4,0},{5,1},{6,2},{7,3},{8,4},{9,5},{1... | collective-permute-start | bytes 786440 | tf_op jit(solution)/shard_map/ppermute | solution.py:387
  21.7 12.7 %collective-permute-start.11 = (bf16[64,2048]{1,0:T(8,128)(2,1)S(1)}, bf16[64,2048]{1,0:T(8,128)(2,1)S(1)}, u32[]{:S(2)}, u32[]{:S(2)}) collective-permute-start(bf16[64,2048]{1,0:T(8,128)(2,1)S(1)} %collective-permute-done.7.refs_3_.refs_4_), channel_id=1, source_target_pairs={{0,2},{1,3},{2,0},{3,1},{4,6},{5,7},{6,4},{7,5},{8,10},{9,11},{10,... | collective-permute-start | bytes 786440 | tf_op jit(solution)/shard_map/ppermute | solution.py:387
  24.0 5.2 %collective-permute-start.15 = (bf16[4,32,128]{2,1,0:T(8,128)(2,1)S(1)}, bf16[4,32,128]{2,1,0:T(8,128)(2,1)S(1)}, u32[]{:S(2)}, u32[]{:S(2)}) collective-permute-start(bf16[4,32,128]{2,1,0:T(8,128)(2,1)S(1)} %shard_map.76), channel_id=1, source_target_pairs={{16,1},{18,3},{20,5},{22,7},{24,9},{26,11},{28,13},{30,15},{32,17}... | collective-permute-start | bytes 98312 | tf_op jit(solution)/shard_map/ppermute | solution.py:390
  26.5 15.6 %collective-permute-start.12 = (bf16[64,2048]{1,0:T(8,128)(2,1)S(1)}, bf16[64,2048]{1,0:T(8,128)(2,1)S(1)}, u32[]{:S(2)}, u32[]{:S(2)}) collective-permute-start(bf16[64,2048]{1,0:T(8,128)(2,1)S(1)} %collective-permute-done.10.refs_6_.refs_7_), channel_id=1, source_target_pairs={{0,2},{1,3},{2,0},{3,1},{4,6},{5,7},{6,4},{7,5},{8,10},{9,11},{10,... | collective-permute-start | bytes 786440 | tf_op jit(solution)/shard_map/ppermute | solution.py:387
  29.2 12.9 %collective-permute-start.13 = (bf16[64,2048]{1,0:T(8,128)(2,1)S(1)}, bf16[64,2048]{1,0:T(8,128)(2,1)S(1)}, u32[]{:S(2)}, u32[]{:S(2)}) collective-permute-start(bf16[64,2048]{1,0:T(8,128)(2,1)S(1)} %collective-permute-done.9.refs_5_.refs_6_), channel_id=1, source_target_pairs={{0,4},{1,5},{2,6},{3,7},{4,8},{5,9},{6,10},{7,11},{8,12},{9,13},{1... | collective-permute-start | bytes 786440 | tf_op jit(solution)/shard_map/ppermute | solution.py:387
  31.1 11.1 %collective-permute-start.14 = (bf16[64,2048]{1,0:T(8,128)(2,1)S(1)}, bf16[64,2048]{1,0:T(8,128)(2,1)S(1)}, u32[]{:S(2)}, u32[]{:S(2)}) collective-permute-start(bf16[64,2048]{1,0:T(8,128)(2,1)S(1)} %collective-permute-done.8.refs_4_.refs_5_), channel_id=1, source_target_pairs={{0,12},{1,13},{2,14},{3,15},{4,0},{5,1},{6,2},{7,3},{8,4},{9,5},{1... | collective-permute-start | bytes 786440 | tf_op jit(solution)/shard_map/ppermute | solution.py:387
  34.4 9.5 %collective-permute-start.2 = (bf16[64,2048]{1,0:T(8,128)(2,1)S(1)}, bf16[64,2048]{1,0:T(8,128)(2,1)S(1)}, u32[]{:S(2)}, u32[]{:S(2)}) collective-permute-start(bf16[64,2048]{1,0:T(8,128)(2,1)S(1)} %collective-permute-done.1.refs_10_), channel_id=1, source_target_pairs={{0,4},{1,5},{2,6},{3,7},{4,8},{5,9},{6,10},{7,11},{8,12},{9,13},{1... | collective-permute-start | bytes 786440 | tf_op jit(solution)/shard_map/ppermute | solution.py:387
  34.4 9.9 %collective-permute-start.5 = (bf16[64,2048]{1,0:T(8,128)(2,1)S(1)}, bf16[64,2048]{1,0:T(8,128)(2,1)S(1)}, u32[]{:S(2)}, u32[]{:S(2)}) collective-permute-start(bf16[64,2048]{1,0:T(8,128)(2,1)S(1)} %collective-permute-done.4.refs_9_), channel_id=1, source_target_pairs={{0,12},{1,13},{2,14},{3,15},{4,0},{5,1},{6,2},{7,3},{8,4},{9,5},{1... | collective-permute-start | bytes 786440 | tf_op jit(solution)/shard_map/ppermute | solution.py:387
  51.3 13.5 %all-to-all-start = ((bf16[8,176,128]{2,1,0:T(8,128)(2,1)}), bf16[8,176,128]{2,1,0:T(8,128)(2,1)S(1)}, u32[]{:S(2)}, u32[]{:S(2)}) async-start(bf16[8,176,128]{2,1,0:T(8,128)(2,1)} %get-tuple-element.38), calls=%async_computation | async-start | bytes 720896 | tf_op jit(solution)/shard_map/all_to_all | solution.py:470
  58.0 6.1 %collective-permute-start.20 = (bf16[128,128]{1,0:T(8,128)(2,1)S(1)}, bf16[128,128]{1,0:T(8,128)(2,1)S(1)}, u32[]{:S(2)}, u32[]{:S(2)}) collective-permute-start(bf16[128,128]{1,0:T(8,128)(2,1)S(1)} %get-tuple-element.46), channel_id=1, source_target_pairs={{16,1},{18,3},{20,5},{22,7},{24,9},{26,11},{28,13},{30,15},{32,17}... | collective-permute-start | bytes 98312 | tf_op jit(solution)/shard_map/ppermute | solution.py:390
  64.8 17.6 %all-to-all-start.1 = ((bf16[16,8,384]{2,1,0:T(8,128)(2,1)}), bf16[16,8,384]{2,1,0:T(8,128)(2,1)S(1)}, u32[]{:S(2)}, u32[]{:S(2)}) async-start(bf16[16,8,384]{2,1,0:T(8,128)(2,1)} %bitcast.1), calls=%async_computation.1 | async-start | bytes 196608 | tf_op jit(solution)/shard_map/all_to_all | solution.py:471
  71.8 11.3 %collective-permute-start.17 = (bf16[80,128]{1,0:T(8,128)(2,1)S(1)}, bf16[80,128]{1,0:T(8,128)(2,1)S(1)}, u32[]{:S(2)}, u32[]{:S(2)}) collective-permute-start(bf16[80,128]{1,0:T(8,128)(2,1)S(1)} %get-tuple-element.40), channel_id=1, source_target_pairs={{0,64},{64,128},{128,192},{192,0},{1,65},{65,129},{129,193},{193,1... | collective-permute-start | bytes 61448 | tf_op jit(solution)/shard_map/ppermute | solution.py:475
  76.8 7.7 %collective-permute-start.18 = (bf16[80,128]{1,0:T(8,128)(2,1)S(1)}, bf16[80,128]{1,0:T(8,128)(2,1)S(1)}, u32[]{:S(2)}, u32[]{:S(2)}) collective-permute-start(bf16[80,128]{1,0:T(8,128)(2,1)S(1)} %get-tuple-element.41), channel_id=1, source_target_pairs={{0,128},{64,192},{128,0},{192,64},{1,129},{65,193},{129,1},{193,65... | collective-permute-start | bytes 61448 | tf_op jit(solution)/shard_map/ppermute | solution.py:475
  78.4 6.1 %collective-permute-start.19 = (bf16[80,128]{1,0:T(8,128)(2,1)S(1)}, bf16[80,128]{1,0:T(8,128)(2,1)S(1)}, u32[]{:S(2)}, u32[]{:S(2)}) collective-permute-start(bf16[80,128]{1,0:T(8,128)(2,1)S(1)} %get-tuple-element.42), channel_id=1, source_target_pairs={{0,192},{64,0},{128,64},{192,128},{1,193},{65,1},{129,65},{193,129... | collective-permute-start | bytes 61448 | tf_op jit(solution)/shard_map/ppermute | solution.py:475

commit v4 on v3

--- a/solution.py
+++ b/solution.py
@@ -15,10 +15,10 @@
 GROUP = 16
 OWN = 64
 STEP = 4
-EARLY = 14
+EARLY = 10
 MIB = 1024 * 1024
 
-CHIPS = ((0, 0), (0, 1), (1, 0), (3, 0), (1, 1), (3, 1), (2, 0), (2, 1))
+CHIPS = ((0, 0), (0, 1), (1, 0), (3, 0), (2, 0), (1, 1), (3, 1), (2, 1))
 
 
 STRIPS = ("z_hi", "y")
@@ -207,7 +207,7 @@
 
 def gather_products(blocks, first, wturned, whitened, partial):
     grad_w, pooled = None, []
-    weights = wturned[:, first * OWN : (first + len(blocks)) * OWN]
+    weights = wturned[:, first * OWN : first * OWN + sum(block.shape[0] for block in blocks)]
     for n in range(8):
         cols = pl.ds(n * 256, 256)
         stack = jnp.concatenate([block[:, cols] for block in blocks], axis=0)
@@ -230,8 +230,7 @@
 
 
 def early_kernel(*refs):
-    blocks = refs[:EARLY]
-    wturned, whitened, partial, packed = refs[EARLY:]
+    blocks, (wturned, whitened, partial, packed) = refs[:6], refs[6:]
     packed[...] = jnp.zeros_like(packed)
     pooled, grad_w = gather_products(blocks, 0, wturned, whitened, None)
     for n in range(8):
@@ -240,12 +239,12 @@
 
 
 def backward_kernel(*refs):
-    blocks = refs[: 16 - EARLY]
+    blocks = refs[:4]
     (
         partial, early, wturned, whitened, inv_density, masked, patches, inv_square, anch_t,
-        packed, image, rim,
+        packed, image,
         rowed, spread_grad, anchor_grad, pool_t,
-    ) = refs[16 - EARLY :]
+    ) = refs[4:]
     pool_t[...] = column_spread()
     packed[:, 0:128, :] = early[...]
     pooled, grad_w = gather_products(blocks, EARLY, wturned, whitened, partial)
@@ -308,22 +307,7 @@
     high = moved.astype(bf16)
     low = (moved - high.astype(f32)).astype(bf16)
     folder = fold_rows()
-    summed = dot(folder, high) + dot(folder, low)
-    image[...] = summed.astype(bf16)
-    first, last = summed[:, :128], summed[:, 256:]
-    lane = lax.broadcasted_iota(jnp.int32, first.shape, 1)
-    first, last = jnp.where(lane < 6, first, 0.0), jnp.where(lane < 6, 0.0, last)
-    rim[...] = jnp.where(on_second(), last, first).astype(bf16)
-
-
-def seam_kernel(image, rim, joined):
-    second = on_second()
-    value = rim[...].astype(f32)
-    first = image[:, :128].astype(f32) + jnp.where(second, 0.0, value)
-    last = image[:, 256:].astype(f32) + jnp.where(second, value, 0.0)
-    joined[:, :128] = first.astype(bf16)
-    joined[:, 128:256] = image[:, 128:256]
-    joined[:, 256:] = last.astype(bf16)
+    image[...] = (dot(folder, high) + dot(folder, low)).astype(bf16)
 
 
 def pack_kernel(received, kept, next_one, next_two, next_three, sums):
@@ -338,7 +322,24 @@
         packed[32:80, :] = anchor
 
 
-def unpack_kernel(kept, one, two, three, grad_anchors, grad_whiten):
+def image_kernel(parts, middle, rims):
+    halves = []
+    for k in range(2):
+        acc = parts[k].astype(f32)
+        for chip in range(1, 8):
+            acc = acc + parts[2 * chip + k].astype(f32)
+        halves.append(acc)
+    gap = jnp.zeros((8, 256), f32)
+    whole = jnp.concatenate([halves[0], gap], axis=1) + jnp.concatenate([gap, halves[1]], axis=1)
+    turned = pltpu.roll(whole, 640 - 6, 1)
+    middle[...] = turned[:, :512]
+    rims[...] = turned[:, 512:]
+
+
+def unpack_kernel(
+    kept, one, two, three, middle, before, after,
+    grad_anchors, grad_whiten, grad_image,
+):
     total = sum(ref[...].astype(f32) for ref in (one, two, three)) + kept[...].astype(f32)
     other = pltpu.roll(total, OWN, 1)
     grad_whiten[0:32, :] = total[0:32, :OWN]
@@ -348,20 +349,28 @@
         turned, entry_order(f32), (((1,), (1,)), ((), ())),
         precision=lax.Precision.HIGHEST, preferred_element_type=f32,
     )
-
-
-def image_kernel(parts, grad_image):
-    halves = []
-    for k in range(2):
-        acc = parts[k].astype(f32)
-        for chip in range(1, 8):
-            acc = acc + parts[2 * chip + k].astype(f32)
-        halves.append(acc)
+    lane = lax.broadcasted_iota(jnp.int32, before.shape, 1)
+    first = jnp.where(lane < 6, before[...], 0.0)
+    last = jnp.where(lane >= 122, after[...], 0.0)
     gap = jnp.zeros((8, 256), f32)
-    whole = jnp.concatenate([halves[0], gap], axis=1) + jnp.concatenate([gap, halves[1]], axis=1)
-    image = pltpu.roll(whole, 640 - 6, 1)[:, :512]
+    image = middle[...] + jnp.concatenate([first, gap, last], axis=1)
     for colour in range(3):
         grad_image[colour] = image[2 * colour : 2 * colour + 2]
+
+
+def hold(value, *after):
+    def kernel(*refs):
+        del refs
+
+    return pl.pallas_call(
+        kernel,
+        out_shape=jax.ShapeDtypeStruct(value.shape, value.dtype),
+        in_specs=[pl.BlockSpec(memory_space=pl.ANY)] * (1 + len(after)),
+        out_specs=pl.BlockSpec(memory_space=pl.ANY),
+        input_output_aliases={0: 0},
+        compiler_params=pltpu.CompilerParams(vmem_limit_bytes=MIB),
+        cost_estimate=pl.CostEstimate(flops=1000, bytes_accessed=1000, transcendentals=0),
+    )(value, *after)
 
 
 def call(kernel, outs, scratch, flops, limit, *args, loose=0):
@@ -392,16 +401,18 @@
     left, right = cotangent[:, :, :HALF], cotangent[:, :, HALF:]
     own = jnp.where(second, right, left).reshape(OWN, -1)
     away = jnp.where(second, left, right).reshape(OWN, -1)
-    held = {(0, 0): (own, send(away, 0, 0, 1))}
+    block = jnp.concatenate([own, send(away, 0, 0, 1)], axis=0)
+    held = {(0, 0): [block]}
     for dx, dz in ((1, 0), (3, 0), (0, 1)):
-        held[(4 - dx) % 4, dz] = (send(own, dx, dz, 0), send(away, dx, dz, 1))
-    far_own = send(held[0, 1][0], 1, 0, 0)
-    far_partner = send(held[0, 1][1], 3, 0, 0)
-    held[3, 1] = (far_own, send(held[3, 0][1], 0, 1, 0))
-    held[1, 1] = (send(held[1, 0][0], 0, 1, 0), far_partner)
-    held[2, 0] = (send(held[3, 0][0], 1, 0, 0), send(held[1, 0][1], 3, 0, 0))
-    held[2, 1] = (send(far_own, 1, 0, 0), send(far_partner, 3, 0, 0))
-    blocks = [block for chip in CHIPS for block in held[chip]]
+        held[(4 - dx) % 4, dz] = [send(block, dx, dz, 0)]
+    far = [send(held[3, 0][0][:OWN], 1, 0, 0), send(held[1, 0][0][OWN:], 3, 0, 0)]
+    beside = hold(held[0, 1][0], *far)
+    held[2, 0] = far
+    held[3, 1] = [send(beside, 1, 0, 0)]
+    held[1, 1] = [send(beside, 3, 0, 0)]
+    held[2, 1] = [send(half, 0, 1, 0) for half in far]
+    held[0, 1] = [beside]
+    blocks = [part for chip in CHIPS for part in held[chip]]
 
     stacked = jnp.concatenate([image, mask.astype(bf16)[None]], axis=0)
     (tile,) = call(
@@ -410,8 +421,8 @@
         [],
         1_000_000,
         4,
-        stacked, held[0, 0][1], *(block for chip in ((0, 1), (1, 0), (3, 0)) for block in held[chip]),
-        loose=7,
+        stacked, held[3, 0][0],
+        loose=1,
     )
     both = jnp.concatenate(
         [jnp.pad(whiten, ((0, 0), (0, OWN))), jnp.pad(anchors, ((0, 0), (0, 53)))], axis=0
@@ -449,11 +460,11 @@
         [],
         2_000_000_000,
         14,
-        *blocks[:EARLY], wturned, whitened,
-    )
-    packed, image_part, rim = call(
+        *blocks[:6], wturned, whitened,
+    )
+    packed, image_part = call(
         backward_kernel,
-        [((8, 176, 128), bf16), ((128, LANES), bf16), ((128, 128), bf16)],
+        [((8, 176, 128), bf16), ((128, LANES), bf16)],
         [
             ((ROWS * 128, HALF), bf16),
             ((36 * GROUP, LANES), f32),
@@ -462,24 +473,31 @@
         ],
         5_000_000_000,
         20,
-        *blocks[EARLY:],
+        *blocks[6:],
         partial, early, wturned, whitened, inv_density, masked, patches, inv_square, anch_t,
     )
-    (joined,) = call(seam_kernel, [((128, LANES), bf16)], [], 1_000_000, 4, image_part, cross(rim))
 
     received = lax.all_to_all(packed, ("y", "core"), 0, 0)
-    parts = lax.all_to_all(joined.reshape(16, 8, LANES), CHAN, 0, 0)
+    parts = lax.all_to_all(image_part.reshape(16, 8, LANES), CHAN, 0, 0)
     quarter = ((80, 128), bf16)
     kept, *away = call(pack_kernel, [quarter] * 4, [((128, 128), f32)], 1_000_000, 4, received)
     others = [
         lax.ppermute(value, "z_hi", [(z, (z + step) % 4) for z in range(4)])
         for step, value in enumerate(away, 1)
     ]
-    (grad_image,) = call(image_kernel, [((3, 2, 512), f32)], [], 1_000_000, 4, parts)
-    grad_anchors, grad_whiten = call(
-        unpack_kernel, [((OWN, 75), f32), ((OWN, OWN), f32)], [], 1_000_000, 4, kept, *others
-    )
-    return grad_anchors, grad_whiten, grad_image
+    middle, rims = call(image_kernel, [((8, 512), f32), ((8, 128), f32)], [], 1_000_000, 4, parts)
+    before = lax.ppermute(rims, STRIPS, [(i, i + 1) for i in range(15)])
+    after = lax.ppermute(rims, STRIPS, [(i + 1, i) for i in range(15)])
+    return tuple(
+        call(
+            unpack_kernel,
+            [((OWN, 75), f32), ((OWN, OWN), f32), ((3, 2, 512), f32)],
+            [],
+            1_000_000,
+            4,
+            kept, *others, middle, before, after,
+        )
+    )
 
 
 def solution(mesh):

time: 86.9 us -> 93.4 us (1.075)
  starting transfers between devices: 50.7 us -> 37.4 us
  waiting for transfers between devices: 12.5 us -> 23.8 us
  blocking collectives: 0 us -> 10.8 us
    ppermute x16 -> x11, waiting for transfers between devices: 5.21 us -> 17.4 us  [send(): return lax.ppermute(value, CHAN, route(dx, dz, other))]
    all_to_all x0 -> x1, blocking collectives: none -> 10.8 us  [shards(): received = lax.all_to_all(packed, ('y', 'core'), 0, 0)]
    all_to_all x2 -> x1, starting transfers between devices: 13.6 us -> 4.93 us  [shards(): parts = lax.all_to_all(image_part.reshape(16, 8, LANES), CHAN, 0, 0)]
    ppermute x16 -> x11, starting transfers between devices: 21.6 us -> 14.2 us  [send(): return lax.ppermute(value, CHAN, route(dx, dz, other))]
    ppermute x0 -> x2, waiting for transfers between devices: none -> 6.33 us  [the longest x1 6.32 us: shards(): after = lax.ppermute(rims, STRIPS, [(i + 1, i) for i in range(15)])]
    ppermute x2 -> x1, waiting for transfers between devices: 5.92 us -> 0.01 us  [cross(): return lax.ppermute(value, STRIPS + CHAN, seams())]
    ppermute x0 -> x2, starting transfers between devices: none -> 5.84 us  [the longest x1 3.67 us: shards(): before = lax.ppermute(rims, STRIPS, [(i, i + 1) for i in range(15)])]
    ppermute x2 -> x1, starting transfers between devices: 4.97 us -> 1.92 us  [cross(): return lax.ppermute(value, STRIPS + CHAN, seams())]
  transfers between devices with their start and end apart: 23 -> 18, of which waited for: 7 -> 6; matrix products, arithmetic and copies ran while one was open for 3% -> 2% of each run, Pallas kernels for 11% -> 8%
where the time goes in v4:
time: 93.4 us; the launch traced here: 92.6 us
  starting transfers between devices  37.4 us (40%)
  waiting for transfers between devices  23.8 us (25%)
  Pallas kernels  16.6 us (18%)
  blocking collectives  10.8 us (12%)
  other arithmetic  1.9 us (2%)
  local copies, waits for them, and re-layouts  1.26 us (1%)
    ppermute x11, waiting for transfers between devices, send(): return lax.ppermute(value, CHAN, route(dx, dz, other))  17.4 us
    pallas_call x8, Pallas kernels, call(): pl.pallas_call(kernel, out_shape=[jax.ShapeDtypeStruct(shape, dtype) for...  16.6 us
    ppermute x11, starting transfers between devices, send(): return lax.ppermute(value, CHAN, route(dx, dz, other))  14.2 us
    all_to_all x1, blocking collectives, shards(): received = lax.all_to_all(packed, ('y', 'core'), 0, 0)  10.8 us
    ppermute x3, starting transfers between devices, shards(): lax.ppermute(value, 'z_hi', [(z, (z + step) % 4) for z in range(4)])  10.5 us
    ppermute x1, waiting for transfers between devices, shards(): after = lax.ppermute(rims, STRIPS, [(i + 1, i) for i in range(15)])  6.32 us
    all_to_all x1, starting transfers between devices, shards(): parts = lax.all_to_all(image_part.reshape(16, 8, LANES), CHAN, 0, 0)  4.93 us
    ppermute x1, starting transfers between devices, shards(): before = lax.ppermute(rims, STRIPS, [(i, i + 1) for i in range(15)])  3.67 us
  transfers between devices with their start and end apart: 18, of which 6 were waited for; matrix products, arithmetic and copies ran while one was open for 2% of the time, Pallas kernels for 8%

profile of v4, /device:TPU:24, one launch (start us, length us, event | category | flops | bytes accessed | tf_op | source)
XLA Modules:
  0.0 92.6 jit_solution(2146275072709245665)
XLA Ops:
  0.7 1.1 %broadcast_select_fusion = (bf16[64,16,128]{2,1,0:T(8,128)(2,1)S(1)}, bf16[64,16,128]{2,1,0:T(8,128)(2,1)S(1)}) fusion(pred[]{:T(512)S(6)} %eq.3, bf16[64,16,256]{2,1,0:T(8,128)(2,1)} %param.9), kind=kLoop, calls=%fused_computation.7 | loop fusion | flops 262144 | bytes 1048577 | tf_op jit(solution)/shard_map/jit(_where)/select_n | solution.py:403
  1.8 0.1 collective-permute-start
  2.0 1.5 %collective-permute-done = bf16[64,2048]{1,0:T(8,128)(2,1)S(1)} collective-permute-done((bf16[64,2048]{1,0:T(8,128)(2,1)S(1)}, bf16[64,2048]{1,0:T(8,128)(2,1)S(1)}, u32[]{:S(2)}, u32[]{:S(2)}) %collective-permute-start) | collective-permute-done | bytes 262176 | tf_op jit(solution)/shard_map/ppermute | solution.py:396
  3.5 1.6 %collective-permute-start.2 = (bf16[128,2048]{1,0:T(8,128)(2,1)S(1)}, bf16[128,2048]{1,0:T(8,128)(2,1)S(1)}, u32[]{:S(2)}, u32[]{:S(2)}) collective-permute-start(bf16[128,2048]{1,0:T(8,128)(2,1)S(1)} %constant_dynamic-update-slice_fusion.refs_0_), channel_id=1, source_target_pairs={{0,4},{1,5},{2,6},{3,7},{4,8},{5,9},{6,10},{7,11},{8,12},{9,13},{1... | collective-permute-start | bytes 1572872 | tf_op jit(solution)/shard_map/ppermute | solution.py:396
  5.1 1.7 %collective-permute-start.4 = (bf16[128,2048]{1,0:T(8,128)(2,1)S(1)}, bf16[128,2048]{1,0:T(8,128)(2,1)S(1)}, u32[]{:S(2)}, u32[]{:S(2)}) collective-permute-start(bf16[128,2048]{1,0:T(8,128)(2,1)S(1)} %constant_dynamic-update-slice_fusion.refs_0_), channel_id=1, source_target_pairs={{0,12},{1,13},{2,14},{3,15},{4,0},{5,1},{6,2},{7,3},{8,4},{9,5},{1... | collective-permute-start | bytes 1572872 | tf_op jit(solution)/shard_map/ppermute | solution.py:396
  6.8 1.1 %copy.9 = bf16[1024,64]{1,0:T(8,128)(2,1)S(1)} copy(bf16[1024,64]{0,1:T(8,128)(2,1)} %param.8) | data formatting | bytes 262144 | tf_op args[3]
  7.9 2.0 %collective-permute-start.1 = (bf16[128,2048]{1,0:T(8,128)(2,1)S(1)}, bf16[128,2048]{1,0:T(8,128)(2,1)S(1)}, u32[]{:S(2)}, u32[]{:S(2)}) collective-permute-start(bf16[128,2048]{1,0:T(8,128)(2,1)S(1)} %constant_dynamic-update-slice_fusion.refs_0_), channel_id=1, source_target_pairs={{0,2},{1,3},{2,0},{3,1},{4,6},{5,7},{6,4},{7,5},{8,10},{9,11},{10,... | collective-permute-start | bytes 1572872 | tf_op jit(solution)/shard_map/ppermute | solution.py:396
  9.9 0.8 fusion.2.own_both
  10.7 0.1 collective-permute-start.11
  10.8 8.0 %collective-permute-done.2.refs_0_.refs_3_ = bf16[128,2048]{1,0:T(8,128)(2,1)S(1)} collective-permute-done((bf16[128,2048]{1,0:T(8,128)(2,1)S(1)}, bf16[128,2048]{1,0:T(8,128)(2,1)S(1)}, u32[]{:S(2)}, u32[]{:S(2)}) %collective-permute-start.2) | collective-permute-done | bytes 524320 | tf_op jit(solution)/shard_map/ppermute | solution.py:396
  18.8 0.4 collective-permute-start.3
  19.1 3.0 %collective-permute-start.5 = (bf16[64,2048]{1,0:T(8,128)(2,1)S(1)}, bf16[64,2048]{1,0:T(8,128)(2,1)S(1)}, u32[]{:S(2)}, u32[]{:S(2)}) collective-permute-start(bf16[64,2048]{1,0:T(8,128)(2,1)S(1)} %slice.17), channel_id=1, source_target_pairs={{0,12},{1,13},{2,14},{3,15},{4,0},{5,1},{6,2},{7,3},{8,4},{9,5},{1... | collective-permute-start | bytes 786440 | tf_op jit(solution)/shard_map/ppermute | solution.py:396
  22.2 1.9 %collective-permute-start.10 = (bf16[4,32,128]{2,1,0:T(8,128)(2,1)S(1)}, bf16[4,32,128]{2,1,0:T(8,128)(2,1)S(1)}, u32[]{:S(2)}, u32[]{:S(2)}) collective-permute-start(bf16[4,32,128]{2,1,0:T(8,128)(2,1)S(1)} %shard_map.77), channel_id=1, source_target_pairs={{16,1},{18,3},{20,5},{22,7},{24,9},{26,11},{28,13},{30,15},{32,17}... | collective-permute-start | bytes 98312 | tf_op jit(solution)/shard_map/ppermute | solution.py:399
  24.2 3.4 %collective-permute-done.3.refs_1_.refs_4_ = bf16[64,2048]{1,0:T(8,128)(2,1)S(1)} collective-permute-done((bf16[64,2048]{1,0:T(8,128)(2,1)S(1)}, bf16[64,2048]{1,0:T(8,128)(2,1)S(1)}, u32[]{:S(2)}, u32[]{:S(2)}) %collective-permute-start.3) | collective-permute-done | bytes 262176 | tf_op jit(solution)/shard_map/ppermute | solution.py:396
  27.6 3.1 %collective-permute-start.6 = (bf16[128,2048]{1,0:T(8,128)(2,1)S(1)}, bf16[128,2048]{1,0:T(8,128)(2,1)S(1)}, u32[]{:S(2)}, u32[]{:S(2)}) collective-permute-start(bf16[128,2048]{1,0:T(8,128)(2,1)S(1)} %shard_map.76.refs_1_), channel_id=1, source_target_pairs={{0,12},{1,13},{2,14},{3,15},{4,0},{5,1},{6,2},{7,3},{8,4},{9,5},{1... | collective-permute-start | bytes 1572872 | tf_op jit(solution)/shard_map/ppermute | solution.py:396
  30.6 1.8 %shard_map.78 = (bf16[576,384]{1,0:T(8,128)(2,1)S(1)}, f32[32,384]{1,0:T(8,128)S(1)}, f32[32,384]{1,0:T(8,128)S(1)}, f32[32,384]{1,0:T(8,128)S(1)}, f32[32,384]{...) custom-call(bf16[4,32,512]{2,1,0:T(8,128)(2,1)S(1)} %pad_maximum_fus, ...), custom_call_target="tpu_custom_call" | custom-call | flops 1000000000 | bytes 1671168 | tf_op jit(solution)/shard_map/pallas_call | solution.py:380
  32.5 2.0 %collective-permute-start.8 = (bf16[64,2048]{1,0:T(8,128)(2,1)S(1)}, bf16[64,2048]{1,0:T(8,128)(2,1)S(1)}, u32[]{:S(2)}, u32[]{:S(2)}) collective-permute-start(bf16[64,2048]{1,0:T(8,128)(2,1)S(1)} %collective-permute-done.3.refs_1_.refs_4_), channel_id=1, source_target_pairs={{0,2},{1,3},{2,0},{3,1},{4,6},{5,7},{6,4},{7,5},{8,10},{9,11},{10,... | collective-permute-start | bytes 786440 | tf_op jit(solution)/shard_map/ppermute | solution.py:396
  34.5 0.3 collective-permute-start.9
  34.8 4.5 %shard_map.79 = (bf16[32,128,384]{2,1,0:T(8,128)(2,1)S(1)}, bf16[128,2048]{1,0:T(8,128)(2,1)S(1)}) custom-call(bf16[576,384]{1,0:T(8,128)(2,1)S(1)} %get-tuple-element.25.patches.refs_10_, f32[32,384]{1,0:T(8,128)S(1)} %get-tuple-element.26.tissue, f32[32,384]{1,0:T(8,128)S(1)} %get-tuple-element.27.scale, f32[32,384]{1,0:T(8,128)S(1)} %get-tuple-element.28.norm, ...), custom_call_target="tpu_custom_call" | custom-call | flops 3000000000 | bytes 4288512 | tf_op jit(solution)/shard_map/pallas_call | solution.py:380
  39.2 1.3 %shard_map.80 = (f32[128,2048]{1,0:T(8,128)S(1)}, bf16[8,128,128]{2,1,0:T(8,128)(2,1)S(1)}) custom-call(bf16[128,2048]{1,0:T(8,128)(2,1)S(1)} %constant_dynamic-update-slice_fusion.refs_0_, bf16[128,2048]{1,0:T(8,128)(2,1)S(1)} %shard_map.76.refs_1_, bf16[128,2048]{1,0:T(8,128)(2,1)S(1)} %collective-permute-done.4.refs_2_, ...), custom_call_target="tpu_custom_call" | custom-call | flops 2000000000 | bytes 4718592 | tf_op jit(solution)/shard_map/pallas_call | solution.py:380
  40.6 1.2 %collective-permute-done.8.refs_2_ = bf16[64,2048]{1,0:T(8,128)(2,1)S(1)} collective-permute-done((bf16[64,2048]{1,0:T(8,128)(2,1)S(1)}, bf16[64,2048]{1,0:T(8,128)(2,1)S(1)}, u32[]{:S(2)}, u32[]{:S(2)}) %collective-permute-start.8) | collective-permute-done | bytes 262176 | tf_op jit(solution)/shard_map/ppermute | solution.py:396
  41.8 3.4 %collective-permute-done.9.refs_3_ = bf16[64,2048]{1,0:T(8,128)(2,1)S(1)} collective-permute-done((bf16[64,2048]{1,0:T(8,128)(2,1)S(1)}, bf16[64,2048]{1,0:T(8,128)(2,1)S(1)}, u32[]{:S(2)}, u32[]{:S(2)}) %collective-permute-start.9) | collective-permute-done | bytes 262176 | tf_op jit(solution)/shard_map/ppermute | solution.py:396
  45.2 7.9 %shard_map.81 = (bf16[8,176,128]{2,1,0:T(8,128)(2,1)S(1)}, bf16[128,384]{1,0:T(8,128)(2,1)}) custom-call(bf16[128,2048]{1,0:T(8,128)(2,1)S(1)} %collective-permute-done.6.refs_0_, bf16[128,2048]{1,0:T(8,128)(2,1)S(1)} %collective-permute-done.7.refs_1_, bf16[64,2048]{1,0:T(8,128)(2,1)S(1)} %collective-permute-done.8.refs_2_, ...), custom_call_target="tpu_custom_call" | custom-call | flops 5000000000 | bytes 7794688 | tf_op jit(solution)/shard_map/pallas_call | solution.py:380
  53.1 10.8 %all_to_all.10.received = bf16[8,176,128]{2,1,0:T(8,128)(2,1)S(1)} all-to-all(bf16[8,176,128]{2,1,0:T(8,128)(2,1)S(1)} %get-tuple-element.37), channel_id=1, replica_groups=mesh['z_hi'=4,'y'=4,'x'=4,'z_lo'=2,'core'=2] {'y','core'}, dimensions={0} | all-to-all | bytes 720896 | tf_op jit(solution)/shard_map/all_to_all | solution.py:480
  63.9 4.9 %all-to-all-start.1 = ((bf16[16,8,384]{2,1,0:T(8,128)(2,1)}), bf16[16,8,384]{2,1,0:T(8,128)(2,1)S(1)}, u32[]{:S(2)}, u32[]{:S(2)}) async-start(bf16[16,8,384]{2,1,0:T(8,128)(2,1)} %bitcast.1), calls=%async_computation.1 | async-start | bytes 196608 | tf_op jit(solution)/shard_map/all_to_all | solution.py:481
  68.9 3.3 %collective-permute-start.12 = (bf16[80,128]{1,0:T(8,128)(2,1)S(1)}, bf16[80,128]{1,0:T(8,128)(2,1)S(1)}, u32[]{:S(2)}, u32[]{:S(2)}) collective-permute-start(bf16[80,128]{1,0:T(8,128)(2,1)S(1)} %get-tuple-element.39), channel_id=1, source_target_pairs={{0,64},{64,128},{128,192},{192,0},{1,65},{65,129},{129,193},{193,1... | collective-permute-start | bytes 61448 | tf_op jit(solution)/shard_map/ppermute | solution.py:485
  72.3 4.5 %collective-permute-start.13 = (bf16[80,128]{1,0:T(8,128)(2,1)S(1)}, bf16[80,128]{1,0:T(8,128)(2,1)S(1)}, u32[]{:S(2)}, u32[]{:S(2)}) collective-permute-start(bf16[80,128]{1,0:T(8,128)(2,1)S(1)} %get-tuple-element.40), channel_id=1, source_target_pairs={{0,128},{64,192},{128,0},{192,64},{1,129},{65,193},{129,1},{193,65... | collective-permute-start | bytes 61448 | tf_op jit(solution)/shard_map/ppermute | solution.py:485
  76.7 2.7 %collective-permute-start.14 = (bf16[80,128]{1,0:T(8,128)(2,1)S(1)}, bf16[80,128]{1,0:T(8,128)(2,1)S(1)}, u32[]{:S(2)}, u32[]{:S(2)}) collective-permute-start(bf16[80,128]{1,0:T(8,128)(2,1)S(1)} %get-tuple-element.41), channel_id=1, source_target_pairs={{0,192},{64,0},{128,64},{192,128},{1,193},{65,1},{129,65},{193,129... | collective-permute-start | bytes 61448 | tf_op jit(solution)/shard_map/ppermute | solution.py:485
  79.5 3.7 %collective-permute-start.15 = (f32[8,128]{1,0:T(8,128)S(1)}, f32[8,128]{1,0:T(8,128)S(1)}, u32[]{:S(2)}, u32[]{:S(2)}) collective-permute-start(f32[8,128]{1,0:T(8,128)S(1)} %get-tuple-element.44), channel_id=1, source_target_pairs={{0,16},{16,32},{32,48},{48,64},{64,80},{80,96},{96,112},{112,128},... | collective-permute-start | bytes 12296 | tf_op jit(solution)/shard_map/ppermute | solution.py:489
  83.2 2.2 %collective-permute-start.16 = (f32[8,128]{1,0:T(8,128)S(1)}, f32[8,128]{1,0:T(8,128)S(1)}, u32[]{:S(2)}, u32[]{:S(2)}) collective-permute-start(f32[8,128]{1,0:T(8,128)S(1)} %get-tuple-element.44), channel_id=1, source_target_pairs={{16,0},{32,16},{48,32},{64,48},{80,64},{96,80},{112,96},{128,112},... | collective-permute-start | bytes 12296 | tf_op jit(solution)/shard_map/ppermute | solution.py:490
  85.4 6.3 %collective-permute-done.16.after = f32[8,128]{1,0:T(8,128)S(1)} collective-permute-done((f32[8,128]{1,0:T(8,128)S(1)}, f32[8,128]{1,0:T(8,128)S(1)}, u32[]{:S(2)}, u32[]{:S(2)}) %collective-permute-start.16) | collective-permute-done | bytes 4128 | tf_op jit(solution)/shard_map/ppermute | solution.py:490
  91.7 0.9 shard_map.84
  (28 shorter events, 0.4 us)
Async XLA Ops:
  0.6 21.6 %copy-start.1 = (s32[32,512]{1,0:T(8,128)S(1)}, s32[32,512]{1,0:T(8,128)}, u32[]{:S(2)}) copy-start(s32[32,512]{1,0:T(8,128)} %param.6) | copy-start | bytes 196612
  0.6 21.6 %copy-start = (bf16[3,32,512]{2,1,0:T(8,128)(2,1)S(1)}, bf16[3,32,512]{2,1,0:T(8,128)(2,1)}, u32[]{:S(2)}) copy-start(bf16[3,32,512]{2,1,0:T(8,128)(2,1)} %param.5) | copy-start | bytes 294916
  1.8 1.6 %collective-permute-start = (bf16[64,2048]{1,0:T(8,128)(2,1)S(1)}, bf16[64,2048]{1,0:T(8,128)(2,1)S(1)}, u32[]{:S(2)}, u32[]{:S(2)}) collective-permute-start(bf16[64,2048]{1,0:T(8,128)(2,1)S(1)} %bitcast.12), channel_id=1, source_target_pairs={{0,1},{1,0},{2,3},{3,2},{4,5},{5,4},{6,7},{7,6},{8,9},{9,8},{10,11... | collective-permute-start | bytes 786440 | tf_op jit(solution)/shard_map/ppermute | solution.py:396
  3.5 15.3 %collective-permute-start.2 = (bf16[128,2048]{1,0:T(8,128)(2,1)S(1)}, bf16[128,2048]{1,0:T(8,128)(2,1)S(1)}, u32[]{:S(2)}, u32[]{:S(2)}) collective-permute-start(bf16[128,2048]{1,0:T(8,128)(2,1)S(1)} %constant_dynamic-update-slice_fusion.refs_0_), channel_id=1, source_target_pairs={{0,4},{1,5},{2,6},{3,7},{4,8},{5,9},{6,10},{7,11},{8,12},{9,13},{1... | collective-permute-start | bytes 1572872 | tf_op jit(solution)/shard_map/ppermute | solution.py:396
  5.1 14.1 %collective-permute-start.4 = (bf16[128,2048]{1,0:T(8,128)(2,1)S(1)}, bf16[128,2048]{1,0:T(8,128)(2,1)S(1)}, u32[]{:S(2)}, u32[]{:S(2)}) collective-permute-start(bf16[128,2048]{1,0:T(8,128)(2,1)S(1)} %constant_dynamic-update-slice_fusion.refs_0_), channel_id=1, source_target_pairs={{0,12},{1,13},{2,14},{3,15},{4,0},{5,1},{6,2},{7,3},{8,4},{9,5},{1... | collective-permute-start | bytes 1572872 | tf_op jit(solution)/shard_map/ppermute | solution.py:396
  7.9 16.3 %collective-permute-start.1 = (bf16[128,2048]{1,0:T(8,128)(2,1)S(1)}, bf16[128,2048]{1,0:T(8,128)(2,1)S(1)}, u32[]{:S(2)}, u32[]{:S(2)}) collective-permute-start(bf16[128,2048]{1,0:T(8,128)(2,1)S(1)} %constant_dynamic-update-slice_fusion.refs_0_), channel_id=1, source_target_pairs={{0,2},{1,3},{2,0},{3,1},{4,6},{5,7},{6,4},{7,5},{8,10},{9,11},{10,... | collective-permute-start | bytes 1572872 | tf_op jit(solution)/shard_map/ppermute | solution.py:396
  10.7 20.0 %collective-permute-start.11 = (bf16[1088,128]{1,0:T(8,128)(2,1)S(1)}, bf16[1088,128]{1,0:T(8,128)(2,1)S(1)}, u32[]{:S(2)}, u32[]{:S(2)}) collective-permute-start(bf16[1088,128]{1,0:T(8,128)(2,1)S(1)} %fusion.2.own_both), channel_id=1, source_target_pairs={{0,1},{1,0},{2,3},{3,2},{4,5},{5,4},{6,7},{7,6},{8,9},{9,8},{10,11... | collective-permute-start | bytes 835592 | tf_op jit(solution)/shard_map/ppermute | solution.py:396
  18.8 8.8 %collective-permute-start.3 = (bf16[64,2048]{1,0:T(8,128)(2,1)S(1)}, bf16[64,2048]{1,0:T(8,128)(2,1)S(1)}, u32[]{:S(2)}, u32[]{:S(2)}) collective-permute-start(bf16[64,2048]{1,0:T(8,128)(2,1)S(1)} %slice.16), channel_id=1, source_target_pairs={{0,4},{1,5},{2,6},{3,7},{4,8},{5,9},{6,10},{7,11},{8,12},{9,13},{1... | collective-permute-start | bytes 786440 | tf_op jit(solution)/shard_map/ppermute | solution.py:396
  19.1 8.4 %collective-permute-start.5 = (bf16[64,2048]{1,0:T(8,128)(2,1)S(1)}, bf16[64,2048]{1,0:T(8,128)(2,1)S(1)}, u32[]{:S(2)}, u32[]{:S(2)}) collective-permute-start(bf16[64,2048]{1,0:T(8,128)(2,1)S(1)} %slice.17), channel_id=1, source_target_pairs={{0,12},{1,13},{2,14},{3,15},{4,0},{5,1},{6,2},{7,3},{8,4},{9,5},{1... | collective-permute-start | bytes 786440 | tf_op jit(solution)/shard_map/ppermute | solution.py:396
  22.2 8.4 %collective-permute-start.10 = (bf16[4,32,128]{2,1,0:T(8,128)(2,1)S(1)}, bf16[4,32,128]{2,1,0:T(8,128)(2,1)S(1)}, u32[]{:S(2)}, u32[]{:S(2)}) collective-permute-start(bf16[4,32,128]{2,1,0:T(8,128)(2,1)S(1)} %shard_map.77), channel_id=1, source_target_pairs={{16,1},{18,3},{20,5},{22,7},{24,9},{26,11},{28,13},{30,15},{32,17}... | collective-permute-start | bytes 98312 | tf_op jit(solution)/shard_map/ppermute | solution.py:399
  27.6 17.6 %collective-permute-start.6 = (bf16[128,2048]{1,0:T(8,128)(2,1)S(1)}, bf16[128,2048]{1,0:T(8,128)(2,1)S(1)}, u32[]{:S(2)}, u32[]{:S(2)}) collective-permute-start(bf16[128,2048]{1,0:T(8,128)(2,1)S(1)} %shard_map.76.refs_1_), channel_id=1, source_target_pairs={{0,12},{1,13},{2,14},{3,15},{4,0},{5,1},{6,2},{7,3},{8,4},{9,5},{1... | collective-permute-start | bytes 1572872 | tf_op jit(solution)/shard_map/ppermute | solution.py:396
  30.6 14.5 %collective-permute-start.7 = (bf16[128,2048]{1,0:T(8,128)(2,1)S(1)}, bf16[128,2048]{1,0:T(8,128)(2,1)S(1)}, u32[]{:S(2)}, u32[]{:S(2)}) collective-permute-start(bf16[128,2048]{1,0:T(8,128)(2,1)S(1)} %shard_map.76.refs_1_), channel_id=1, source_target_pairs={{0,4},{1,5},{2,6},{3,7},{4,8},{5,9},{6,10},{7,11},{8,12},{9,13},{1... | collective-permute-start | bytes 1572872 | tf_op jit(solution)/shard_map/ppermute | solution.py:396
  32.5 9.3 %collective-permute-start.8 = (bf16[64,2048]{1,0:T(8,128)(2,1)S(1)}, bf16[64,2048]{1,0:T(8,128)(2,1)S(1)}, u32[]{:S(2)}, u32[]{:S(2)}) collective-permute-start(bf16[64,2048]{1,0:T(8,128)(2,1)S(1)} %collective-permute-done.3.refs_1_.refs_4_), channel_id=1, source_target_pairs={{0,2},{1,3},{2,0},{3,1},{4,6},{5,7},{6,4},{7,5},{8,10},{9,11},{10,... | collective-permute-start | bytes 786440 | tf_op jit(solution)/shard_map/ppermute | solution.py:396
  34.5 10.7 %collective-permute-start.9 = (bf16[64,2048]{1,0:T(8,128)(2,1)S(1)}, bf16[64,2048]{1,0:T(8,128)(2,1)S(1)}, u32[]{:S(2)}, u32[]{:S(2)}) collective-permute-start(bf16[64,2048]{1,0:T(8,128)(2,1)S(1)} %collective-permute-done.5.refs_2_.refs_5_), channel_id=1, source_target_pairs={{0,2},{1,3},{2,0},{3,1},{4,6},{5,7},{6,4},{7,5},{8,10},{9,11},{10,... | collective-permute-start | bytes 786440 | tf_op jit(solution)/shard_map/ppermute | solution.py:396
  63.9 15.5 %all-to-all-start.1 = ((bf16[16,8,384]{2,1,0:T(8,128)(2,1)}), bf16[16,8,384]{2,1,0:T(8,128)(2,1)S(1)}, u32[]{:S(2)}, u32[]{:S(2)}) async-start(bf16[16,8,384]{2,1,0:T(8,128)(2,1)} %bitcast.1), calls=%async_computation.1 | async-start | bytes 196608 | tf_op jit(solution)/shard_map/all_to_all | solution.py:481
  68.9 22.8 %collective-permute-start.12 = (bf16[80,128]{1,0:T(8,128)(2,1)S(1)}, bf16[80,128]{1,0:T(8,128)(2,1)S(1)}, u32[]{:S(2)}, u32[]{:S(2)}) collective-permute-start(bf16[80,128]{1,0:T(8,128)(2,1)S(1)} %get-tuple-element.39), channel_id=1, source_target_pairs={{0,64},{64,128},{128,192},{192,0},{1,65},{65,129},{129,193},{193,1... | collective-permute-start | bytes 61448 | tf_op jit(solution)/shard_map/ppermute | solution.py:485
  72.3 19.4 %collective-permute-start.13 = (bf16[80,128]{1,0:T(8,128)(2,1)S(1)}, bf16[80,128]{1,0:T(8,128)(2,1)S(1)}, u32[]{:S(2)}, u32[]{:S(2)}) collective-permute-start(bf16[80,128]{1,0:T(8,128)(2,1)S(1)} %get-tuple-element.40), channel_id=1, source_target_pairs={{0,128},{64,192},{128,0},{192,64},{1,129},{65,193},{129,1},{193,65... | collective-permute-start | bytes 61448 | tf_op jit(solution)/shard_map/ppermute | solution.py:485
  76.7 14.9 %collective-permute-start.14 = (bf16[80,128]{1,0:T(8,128)(2,1)S(1)}, bf16[80,128]{1,0:T(8,128)(2,1)S(1)}, u32[]{:S(2)}, u32[]{:S(2)}) collective-permute-start(bf16[80,128]{1,0:T(8,128)(2,1)S(1)} %get-tuple-element.41), channel_id=1, source_target_pairs={{0,192},{64,0},{128,64},{192,128},{1,193},{65,1},{129,65},{193,129... | collective-permute-start | bytes 61448 | tf_op jit(solution)/shard_map/ppermute | solution.py:485
  79.5 5.9 %collective-permute-start.15 = (f32[8,128]{1,0:T(8,128)S(1)}, f32[8,128]{1,0:T(8,128)S(1)}, u32[]{:S(2)}, u32[]{:S(2)}) collective-permute-start(f32[8,128]{1,0:T(8,128)S(1)} %get-tuple-element.44), channel_id=1, source_target_pairs={{0,16},{16,32},{32,48},{48,64},{64,80},{80,96},{96,112},{112,128},... | collective-permute-start | bytes 12296 | tf_op jit(solution)/shard_map/ppermute | solution.py:489
  83.2 8.5 %collective-permute-start.16 = (f32[8,128]{1,0:T(8,128)S(1)}, f32[8,128]{1,0:T(8,128)S(1)}, u32[]{:S(2)}, u32[]{:S(2)}) collective-permute-start(f32[8,128]{1,0:T(8,128)S(1)} %get-tuple-element.44), channel_id=1, source_target_pairs={{16,0},{32,16},{48,32},{64,48},{80,64},{96,80},{112,96},{128,112},... | collective-permute-start | bytes 12296 | tf_op jit(solution)/shard_map/ppermute | solution.py:490

commit v5 on v3

--- a/solution.py
+++ b/solution.py
@@ -15,10 +15,10 @@
 GROUP = 16
 OWN = 64
 STEP = 4
-EARLY = 14
+EARLY = 10
 MIB = 1024 * 1024
 
-CHIPS = ((0, 0), (0, 1), (1, 0), (3, 0), (1, 1), (3, 1), (2, 0), (2, 1))
+CHIPS = ((0, 0), (0, 1), (1, 0), (3, 0), (2, 0), (1, 1), (3, 1), (2, 1))
 
 
 STRIPS = ("z_hi", "y")
@@ -207,7 +207,7 @@
 
 def gather_products(blocks, first, wturned, whitened, partial):
     grad_w, pooled = None, []
-    weights = wturned[:, first * OWN : (first + len(blocks)) * OWN]
+    weights = wturned[:, first * OWN : first * OWN + sum(block.shape[0] for block in blocks)]
     for n in range(8):
         cols = pl.ds(n * 256, 256)
         stack = jnp.concatenate([block[:, cols] for block in blocks], axis=0)
@@ -230,8 +230,7 @@
 
 
 def early_kernel(*refs):
-    blocks = refs[:EARLY]
-    wturned, whitened, partial, packed = refs[EARLY:]
+    blocks, (wturned, whitened, partial, packed) = refs[:6], refs[6:]
     packed[...] = jnp.zeros_like(packed)
     pooled, grad_w = gather_products(blocks, 0, wturned, whitened, None)
     for n in range(8):
@@ -240,12 +239,12 @@
 
 
 def backward_kernel(*refs):
-    blocks = refs[: 16 - EARLY]
+    blocks = refs[:4]
     (
         partial, early, wturned, whitened, inv_density, masked, patches, inv_square, anch_t,
         packed, image, rim,
         rowed, spread_grad, anchor_grad, pool_t,
-    ) = refs[16 - EARLY :]
+    ) = refs[4:]
     pool_t[...] = column_spread()
     packed[:, 0:128, :] = early[...]
     pooled, grad_w = gather_products(blocks, EARLY, wturned, whitened, partial)
@@ -364,6 +363,27 @@
         grad_image[colour] = image[2 * colour : 2 * colour + 2]
 
 
+def halve_kernel(first, second, after, upper, lower):
+    del after
+    upper[...] = first[:OWN]
+    lower[...] = second[OWN:]
+
+
+def hold(value, *after):
+    def kernel(*refs):
+        del refs
+
+    return pl.pallas_call(
+        kernel,
+        out_shape=jax.ShapeDtypeStruct(value.shape, value.dtype),
+        in_specs=[pl.BlockSpec(memory_space=pl.ANY)] * (1 + len(after)),
+        out_specs=pl.BlockSpec(memory_space=pl.ANY),
+        input_output_aliases={0: 0},
+        compiler_params=pltpu.CompilerParams(vmem_limit_bytes=MIB),
+        cost_estimate=pl.CostEstimate(flops=1000, bytes_accessed=1000, transcendentals=0),
+    )(value, *after)
+
+
 def call(kernel, outs, scratch, flops, limit, *args, loose=0):
     size = lambda shape, dtype: math.prod(shape) * jnp.dtype(dtype).itemsize
     tight = len(args) - loose
@@ -392,16 +412,14 @@
     left, right = cotangent[:, :, :HALF], cotangent[:, :, HALF:]
     own = jnp.where(second, right, left).reshape(OWN, -1)
     away = jnp.where(second, left, right).reshape(OWN, -1)
-    held = {(0, 0): (own, send(away, 0, 0, 1))}
+    block = jnp.concatenate([own, send(away, 0, 0, 1)], axis=0)
+    held = {(0, 0): [block]}
     for dx, dz in ((1, 0), (3, 0), (0, 1)):
-        held[(4 - dx) % 4, dz] = (send(own, dx, dz, 0), send(away, dx, dz, 1))
-    far_own = send(held[0, 1][0], 1, 0, 0)
-    far_partner = send(held[0, 1][1], 3, 0, 0)
-    held[3, 1] = (far_own, send(held[3, 0][1], 0, 1, 0))
-    held[1, 1] = (send(held[1, 0][0], 0, 1, 0), far_partner)
-    held[2, 0] = (send(held[3, 0][0], 1, 0, 0), send(held[1, 0][1], 3, 0, 0))
-    held[2, 1] = (send(far_own, 1, 0, 0), send(far_partner, 3, 0, 0))
-    blocks = [block for chip in CHIPS for block in held[chip]]
+        held[(4 - dx) % 4, dz] = [send(block, dx, dz, 0)]
+    both = jnp.concatenate(
+        [jnp.pad(whiten, ((0, 0), (0, OWN))), jnp.pad(anchors, ((0, 0), (0, 53)))], axis=0
+    )
+    partner_both = send(both, 0, 0, 1)
 
     stacked = jnp.concatenate([image, mask.astype(bf16)[None]], axis=0)
     (tile,) = call(
@@ -410,11 +428,8 @@
         [],
         1_000_000,
         4,
-        stacked, held[0, 0][1], *(block for chip in ((0, 1), (1, 0), (3, 0)) for block in held[chip]),
-        loose=7,
-    )
-    both = jnp.concatenate(
-        [jnp.pad(whiten, ((0, 0), (0, OWN))), jnp.pad(anchors, ((0, 0), (0, 53)))], axis=0
+        stacked, partner_both,
+        loose=1,
     )
     plane = ((ROWS, LANES), f32)
     patches, tissue, scale, norm, inv_square, inv_density, anch, anch_t, wturned = call(
@@ -433,8 +448,21 @@
         [],
         1_000_000_000,
         12,
-        stacked, cross(tile), both, send(both, 0, 0, 1),
-    )
+        stacked, cross(tile), both, partner_both,
+    )
+    half = ((OWN, 16 * HALF), bf16)
+    upper, lower = call(
+        halve_kernel, [half, half], [], 1_000_000, 4, held[3, 0][0], held[1, 0][0], inv_density, loose=1
+    )
+    far = [send(upper, 1, 0, 0), send(lower, 3, 0, 0)]
+    beside = hold(held[0, 1][0], *far)
+    held[2, 0] = far
+    held[3, 1] = [send(beside, 1, 0, 0)]
+    held[1, 1] = [send(beside, 3, 0, 0)]
+    held[2, 1] = [send(half, 0, 1, 0) for half in far]
+    held[0, 1] = [beside]
+    blocks = [part for chip in CHIPS for part in held[chip]]
+
     masked, whitened = call(
         forward_kernel,
         [((ROWS, 128, LANES), bf16), ((128, 16 * HALF), bf16)],
@@ -449,7 +477,7 @@
         [],
         2_000_000_000,
         14,
-        *blocks[:EARLY], wturned, whitened,
+        *blocks[:6], wturned, whitened,
     )
     packed, image_part, rim = call(
         backward_kernel,
@@ -462,9 +490,10 @@
         ],
         5_000_000_000,
         20,
-        *blocks[EARLY:],
+        *blocks[6:],
         partial, early, wturned, whitened, inv_density, masked, patches, inv_square, anch_t,
     )
+
     (joined,) = call(seam_kernel, [((128, LANES), bf16)], [], 1_000_000, 4, image_part, cross(rim))
 
     received = lax.all_to_all(packed, ("y", "core"), 0, 0)

time: 86.9 us -> 89.1 us (1.025)
  the two profiles are of different devices: /device:TPU:24 before, /device:TPU:2 now
where the time goes in v5:
time: 89.1 us; the launch traced here: 88.7 us
  starting transfers between devices  39.4 us (44%)
  waiting for transfers between devices  28.1 us (32%)
  Pallas kernels  17.3 us (19%)
  other arithmetic  1.9 us (2%)
  local copies, waits for them, and re-layouts  1.22 us (1%)
    ppermute x11, waiting for transfers between devices, send(): return lax.ppermute(value, CHAN, route(dx, dz, other))  19.7 us
    pallas_call x10, Pallas kernels, call(): pl.pallas_call(kernel, out_shape=[jax.ShapeDtypeStruct(shape, dtype) for...  17.3 us
    ppermute x3, starting transfers between devices, shards(): lax.ppermute(value, 'z_hi', [(z, (z + step) % 4) for z in range(4)])  15.5 us
    ppermute x11, starting transfers between devices, send(): return lax.ppermute(value, CHAN, route(dx, dz, other))  10.8 us
    all_to_all x1, waiting for transfers between devices, shards(): received = lax.all_to_all(packed, ('y', 'core'), 0, 0)  7.61 us
    all_to_all x1, starting transfers between devices, shards(): parts = lax.all_to_all(joined.reshape(16, 8, LANES), CHAN, 0, 0)  7.5 us
    all_to_all x1, starting transfers between devices, shards(): received = lax.all_to_all(packed, ('y', 'core'), 0, 0)  4.39 us
  transfers between devices with their start and end apart: 18, of which 11 were waited for; matrix products, arithmetic and copies ran while one was open for 2% of the time, Pallas kernels for 10%

profile of v5, /device:TPU:2, one launch (start us, length us, event | category | flops | bytes accessed | tf_op | source)
XLA Modules:
  0.0 88.7 jit_solution(12751502874814361121)
XLA Ops:
  0.7 1.1 %broadcast_select_fusion = (bf16[64,16,128]{2,1,0:T(8,128)(2,1)S(1)}, bf16[64,16,128]{2,1,0:T(8,128)(2,1)S(1)}) fusion(pred[]{:T(512)S(6)} %eq.3, bf16[64,16,256]{2,1,0:T(8,128)(2,1)} %param.9), kind=kLoop, calls=%fused_computation.7 | loop fusion | flops 262144 | bytes 1048577 | tf_op jit(solution)/shard_map/jit(_where)/select_n | solution.py:414
  1.9 1.1 %copy.9 = bf16[1024,64]{1,0:T(8,128)(2,1)S(1)} copy(bf16[1024,64]{0,1:T(8,128)(2,1)} %param.8) | data formatting | bytes 262144 | tf_op args[3]
  3.5 1.6 %collective-permute-start.2 = (bf16[128,2048]{1,0:T(8,128)(2,1)S(1)}, bf16[128,2048]{1,0:T(8,128)(2,1)S(1)}, u32[]{:S(2)}, u32[]{:S(2)}) collective-permute-start(bf16[128,2048]{1,0:T(8,128)(2,1)S(1)} %constant_dynamic-update-slice_fusion.refs_0_), channel_id=1, source_target_pairs={{0,4},{1,5},{2,6},{3,7},{4,8},{5,9},{6,10},{7,11},{8,12},{9,13},{1... | collective-permute-start | bytes 1572872 | tf_op jit(solution)/shard_map/ppermute | solution.py:407
  5.1 0.9 collective-permute-start.3
  5.9 0.8 fusion.2.own_both
  6.8 1.7 %collective-permute-start.1 = (bf16[128,2048]{1,0:T(8,128)(2,1)S(1)}, bf16[128,2048]{1,0:T(8,128)(2,1)S(1)}, u32[]{:S(2)}, u32[]{:S(2)}) collective-permute-start(bf16[128,2048]{1,0:T(8,128)(2,1)S(1)} %constant_dynamic-update-slice_fusion.refs_0_), channel_id=1, source_target_pairs={{0,2},{1,3},{2,0},{3,1},{4,6},{5,7},{6,4},{7,5},{8,10},{9,11},{10,... | collective-permute-start | bytes 1572872 | tf_op jit(solution)/shard_map/ppermute | solution.py:407
  8.6 0.7 collective-permute-start.5
  9.2 1.8 %shard_map.77 = (bf16[576,384]{1,0:T(8,128)(2,1)S(1)}, f32[32,384]{1,0:T(8,128)S(1)}, f32[32,384]{1,0:T(8,128)S(1)}, f32[32,384]{1,0:T(8,128)S(1)}, f32[32,384]{...) custom-call(bf16[4,32,512]{2,1,0:T(8,128)(2,1)S(1)} %pad_maximum_fus, ...), custom_call_target="tpu_custom_call" | custom-call | flops 1000000000 | bytes 1671168 | tf_op jit(solution)/shard_map/pallas_call | solution.py:391
  11.1 7.0 %collective-permute-done.2.first.refs_3_ = bf16[128,2048]{1,0:T(8,128)(2,1)S(1)} collective-permute-done((bf16[128,2048]{1,0:T(8,128)(2,1)S(1)}, bf16[128,2048]{1,0:T(8,128)(2,1)S(1)}, u32[]{:S(2)}, u32[]{:S(2)}) %collective-permute-start.2) | collective-permute-done | bytes 524320 | tf_op jit(solution)/shard_map/ppermute | solution.py:407
  18.1 0.7 collective-permute-done.3.second.refs_2_
  18.8 1.7 %collective-permute-start.6 = (bf16[64,2048]{1,0:T(8,128)(2,1)S(1)}, bf16[64,2048]{1,0:T(8,128)(2,1)S(1)}, u32[]{:S(2)}, u32[]{:S(2)}) collective-permute-start(bf16[64,2048]{1,0:T(8,128)(2,1)S(1)} %get-tuple-element.28), channel_id=1, source_target_pairs={{0,4},{1,5},{2,6},{3,7},{4,8},{5,9},{6,10},{7,11},{8,12},{9,13},{1... | collective-permute-start | bytes 786440 | tf_op jit(solution)/shard_map/ppermute | solution.py:407
  20.5 0.7 collective-permute-start.7
  21.5 5.4 %collective-permute-done.6.refs_1_.refs_4_ = bf16[64,2048]{1,0:T(8,128)(2,1)S(1)} collective-permute-done((bf16[64,2048]{1,0:T(8,128)(2,1)S(1)}, bf16[64,2048]{1,0:T(8,128)(2,1)S(1)}, u32[]{:S(2)}, u32[]{:S(2)}) %collective-permute-start.6) | collective-permute-done | bytes 262176 | tf_op jit(solution)/shard_map/ppermute | solution.py:407
  26.9 1.7 %collective-permute-done.7.refs_2_.refs_5_ = bf16[64,2048]{1,0:T(8,128)(2,1)S(1)} collective-permute-done((bf16[64,2048]{1,0:T(8,128)(2,1)S(1)}, bf16[64,2048]{1,0:T(8,128)(2,1)S(1)}, u32[]{:S(2)}, u32[]{:S(2)}) %collective-permute-start.7) | collective-permute-done | bytes 262176 | tf_op jit(solution)/shard_map/ppermute | solution.py:407
  28.7 1.2 %collective-permute-start.8 = (bf16[128,2048]{1,0:T(8,128)(2,1)S(1)}, bf16[128,2048]{1,0:T(8,128)(2,1)S(1)}, u32[]{:S(2)}, u32[]{:S(2)}) collective-permute-start(bf16[128,2048]{1,0:T(8,128)(2,1)S(1)} %shard_map.79.refs_1_), channel_id=1, source_target_pairs={{0,12},{1,13},{2,14},{3,15},{4,0},{5,1},{6,2},{7,3},{8,4},{9,5},{1... | collective-permute-start | bytes 1572872 | tf_op jit(solution)/shard_map/ppermute | solution.py:407
  29.9 0.8 collective-permute-start.9
  30.9 1.8 %collective-permute-start.11 = (bf16[64,2048]{1,0:T(8,128)(2,1)S(1)}, bf16[64,2048]{1,0:T(8,128)(2,1)S(1)}, u32[]{:S(2)}, u32[]{:S(2)}) collective-permute-start(bf16[64,2048]{1,0:T(8,128)(2,1)S(1)} %collective-permute-done.7.refs_2_.refs_5_), channel_id=1, source_target_pairs={{0,2},{1,3},{2,0},{3,1},{4,6},{5,7},{6,4},{7,5},{8,10},{9,11},{10,... | collective-permute-start | bytes 786440 | tf_op jit(solution)/shard_map/ppermute | solution.py:407
  32.7 4.5 %shard_map.80 = (bf16[32,128,384]{2,1,0:T(8,128)(2,1)S(1)}, bf16[128,2048]{1,0:T(8,128)(2,1)S(1)}) custom-call(bf16[576,384]{1,0:T(8,128)(2,1)S(1)} %get-tuple-element.31.patches.refs_10_, f32[32,384]{1,0:T(8,128)S(1)} %get-tuple-element.32.tissue, f32[32,384]{1,0:T(8,128)S(1)} %get-tuple-element.33.scale, f32[32,384]{1,0:T(8,128)S(1)} %get-tuple-element.34.norm, ...), custom_call_target="tpu_custom_call" | custom-call | flops 3000000000 | bytes 4288512 | tf_op jit(solution)/shard_map/pallas_call | solution.py:391
  37.2 1.4 %shard_map.81 = (f32[128,2048]{1,0:T(8,128)S(1)}, bf16[8,128,128]{2,1,0:T(8,128)(2,1)S(1)}) custom-call(bf16[128,2048]{1,0:T(8,128)(2,1)S(1)} %constant_dynamic-update-slice_fusion.refs_0_, bf16[128,2048]{1,0:T(8,128)(2,1)S(1)} %shard_map.79.refs_1_, bf16[128,2048]{1,0:T(8,128)(2,1)S(1)} %collective-permute-done.3.second.refs_2_, ...), custom_call_target="tpu_custom_call" | custom-call | flops 2000000000 | bytes 4718592 | tf_op jit(solution)/shard_map/pallas_call | solution.py:391
  38.5 0.7 collective-permute-done.10.refs_2_
  39.2 2.8 %collective-permute-done.11.refs_3_ = bf16[64,2048]{1,0:T(8,128)(2,1)S(1)} collective-permute-done((bf16[64,2048]{1,0:T(8,128)(2,1)S(1)}, bf16[64,2048]{1,0:T(8,128)(2,1)S(1)}, u32[]{:S(2)}, u32[]{:S(2)}) %collective-permute-start.11) | collective-permute-done | bytes 262176 | tf_op jit(solution)/shard_map/ppermute | solution.py:407
  42.0 0.7 collective-permute-done.9.refs_1_
  42.7 7.3 %shard_map.82 = (bf16[8,176,128]{2,1,0:T(8,128)(2,1)}, bf16[128,384]{1,0:T(8,128)(2,1)S(1)}, bf16[128,128]{1,0:T(8,128)(2,1)S(1)}) custom-call(bf16[128,2048]{1,0:T(8,128)(2,1)S(1)} %collective-permute-done.8.refs_0_, bf16[128,2048]{1,0:T(8,128)(2,1)S(1)} %collective-permute-done.9.refs_1_, bf16[64,2048]{1,0:T(8,128)(2,1)S(1)} %collective-permute-done.10.refs_2_, ...), custom_call_target="tpu_custom_call" | custom-call | flops 5000000000 | bytes 7827456 | tf_op jit(solution)/shard_map/pallas_call | solution.py:391
  50.0 4.4 %all-to-all-start = ((bf16[8,176,128]{2,1,0:T(8,128)(2,1)}), bf16[8,176,128]{2,1,0:T(8,128)(2,1)S(1)}, u32[]{:S(2)}, u32[]{:S(2)}) async-start(bf16[8,176,128]{2,1,0:T(8,128)(2,1)} %get-tuple-element.42), calls=%async_computation | async-start | bytes 720896 | tf_op jit(solution)/shard_map/all_to_all | solution.py:499
  55.7 7.6 %all-to-all-done.received = bf16[8,176,128]{2,1,0:T(8,128)(2,1)S(1)} async-done(((bf16[8,176,128]{2,1,0:T(8,128)(2,1)}), bf16[8,176,128]{2,1,0:T(8,128)(2,1)S(1)}, u32[]{:S(2)}, u32[]{:S(2)}) %all-to-all-start) | async-done | bytes 360480 | tf_op jit(solution)/shard_map/all_to_all | solution.py:499
  63.3 7.5 %all-to-all-start.1 = ((bf16[16,8,384]{2,1,0:T(8,128)(2,1)}), bf16[16,8,384]{2,1,0:T(8,128)(2,1)S(1)}, u32[]{:S(2)}, u32[]{:S(2)}) async-start(bf16[16,8,384]{2,1,0:T(8,128)(2,1)} %bitcast.1), calls=%async_computation.1 | async-start | bytes 196608 | tf_op jit(solution)/shard_map/all_to_all | solution.py:500
  70.9 6.4 %collective-permute-start.12 = (bf16[80,128]{1,0:T(8,128)(2,1)S(1)}, bf16[80,128]{1,0:T(8,128)(2,1)S(1)}, u32[]{:S(2)}, u32[]{:S(2)}) collective-permute-start(bf16[80,128]{1,0:T(8,128)(2,1)S(1)} %get-tuple-element.44), channel_id=1, source_target_pairs={{0,64},{64,128},{128,192},{192,0},{1,65},{65,129},{129,193},{193,1... | collective-permute-start | bytes 61448 | tf_op jit(solution)/shard_map/ppermute | solution.py:504
  77.3 5.4 %collective-permute-start.13 = (bf16[80,128]{1,0:T(8,128)(2,1)S(1)}, bf16[80,128]{1,0:T(8,128)(2,1)S(1)}, u32[]{:S(2)}, u32[]{:S(2)}) collective-permute-start(bf16[80,128]{1,0:T(8,128)(2,1)S(1)} %get-tuple-element.45), channel_id=1, source_target_pairs={{0,128},{64,192},{128,0},{192,64},{1,129},{65,193},{129,1},{193,65... | collective-permute-start | bytes 61448 | tf_op jit(solution)/shard_map/ppermute | solution.py:504
  82.7 3.6 %collective-permute-start.14 = (bf16[80,128]{1,0:T(8,128)(2,1)S(1)}, bf16[80,128]{1,0:T(8,128)(2,1)S(1)}, u32[]{:S(2)}, u32[]{:S(2)}) collective-permute-start(bf16[80,128]{1,0:T(8,128)(2,1)S(1)} %get-tuple-element.46), channel_id=1, source_target_pairs={{0,192},{64,0},{128,64},{192,128},{1,193},{65,1},{129,65},{193,129... | collective-permute-start | bytes 61448 | tf_op jit(solution)/shard_map/ppermute | solution.py:504
  86.3 0.7 shard_map.86
  87.0 0.8 collective-permute-done.14.three
  87.8 0.9 %shard_map.84 = (f32[64,75]{1,0:T(8,128)}, f32[64,64]{1,0:T(8,128)}) custom-call(bf16[80,128]{1,0:T(8,128)(2,1)S(1)} %get-tuple-element.43.kept, bf16[80,128]{1,0:T(8,128)(2,1)S(1)} %collective-permute-done.12.one, bf16[80,128]{1,0:T(8,128)(2,1)S(1)} %collective-permute-done.13.two, bf16[80,128]{1,0:T(8,128)(2,1)S(1)} %collective-permute-done.14.three), custom_call_target="tpu_custom_call" | custom-call | flops 1000000 | bytes 117504 | tf_op jit(solution)/shard_map/pallas_call | solution.py:391
  (27 shorter events, 2.7 us)
Async XLA Ops:
  0.6 7.8 %copy-start.1 = (s32[32,512]{1,0:T(8,128)S(1)}, s32[32,512]{1,0:T(8,128)}, u32[]{:S(2)}) copy-start(s32[32,512]{1,0:T(8,128)} %param.6) | copy-start | bytes 196612
  0.6 7.8 %copy-start = (bf16[3,32,512]{2,1,0:T(8,128)(2,1)S(1)}, bf16[3,32,512]{2,1,0:T(8,128)(2,1)}, u32[]{:S(2)}) copy-start(bf16[3,32,512]{2,1,0:T(8,128)(2,1)} %param.5) | copy-start | bytes 294916
  1.8 1.6 %collective-permute-start = (bf16[64,2048]{1,0:T(8,128)(2,1)S(1)}, bf16[64,2048]{1,0:T(8,128)(2,1)S(1)}, u32[]{:S(2)}, u32[]{:S(2)}) collective-permute-start(bf16[64,2048]{1,0:T(8,128)(2,1)S(1)} %bitcast.12), channel_id=1, source_target_pairs={{0,1},{1,0},{2,3},{3,2},{4,5},{5,4},{6,7},{7,6},{8,9},{9,8},{10,11... | collective-permute-start | bytes 786440 | tf_op jit(solution)/shard_map/ppermute | solution.py:407
  3.5 14.6 %collective-permute-start.2 = (bf16[128,2048]{1,0:T(8,128)(2,1)S(1)}, bf16[128,2048]{1,0:T(8,128)(2,1)S(1)}, u32[]{:S(2)}, u32[]{:S(2)}) collective-permute-start(bf16[128,2048]{1,0:T(8,128)(2,1)S(1)} %constant_dynamic-update-slice_fusion.refs_0_), channel_id=1, source_target_pairs={{0,4},{1,5},{2,6},{3,7},{4,8},{5,9},{6,10},{7,11},{8,12},{9,13},{1... | collective-permute-start | bytes 1572872 | tf_op jit(solution)/shard_map/ppermute | solution.py:407
  5.1 13.7 %collective-permute-start.3 = (bf16[128,2048]{1,0:T(8,128)(2,1)S(1)}, bf16[128,2048]{1,0:T(8,128)(2,1)S(1)}, u32[]{:S(2)}, u32[]{:S(2)}) collective-permute-start(bf16[128,2048]{1,0:T(8,128)(2,1)S(1)} %constant_dynamic-update-slice_fusion.refs_0_), channel_id=1, source_target_pairs={{0,12},{1,13},{2,14},{3,15},{4,0},{5,1},{6,2},{7,3},{8,4},{9,5},{1... | collective-permute-start | bytes 1572872 | tf_op jit(solution)/shard_map/ppermute | solution.py:407
  6.7 1.8 %collective-permute-start.4 = (bf16[1088,128]{1,0:T(8,128)(2,1)S(1)}, bf16[1088,128]{1,0:T(8,128)(2,1)S(1)}, u32[]{:S(2)}, u32[]{:S(2)}) collective-permute-start(bf16[1088,128]{1,0:T(8,128)(2,1)S(1)} %fusion.2.own_both), channel_id=1, source_target_pairs={{0,1},{1,0},{2,3},{3,2},{4,5},{5,4},{6,7},{7,6},{8,9},{9,8},{10,11... | collective-permute-start | bytes 835592 | tf_op jit(solution)/shard_map/ppermute | solution.py:407
  6.8 14.7 %collective-permute-start.1 = (bf16[128,2048]{1,0:T(8,128)(2,1)S(1)}, bf16[128,2048]{1,0:T(8,128)(2,1)S(1)}, u32[]{:S(2)}, u32[]{:S(2)}) collective-permute-start(bf16[128,2048]{1,0:T(8,128)(2,1)S(1)} %constant_dynamic-update-slice_fusion.refs_0_), channel_id=1, source_target_pairs={{0,2},{1,3},{2,0},{3,1},{4,6},{5,7},{6,4},{7,5},{8,10},{9,11},{10,... | collective-permute-start | bytes 1572872 | tf_op jit(solution)/shard_map/ppermute | solution.py:407
  8.6 0.7 collective-permute-start.5
  18.8 8.1 %collective-permute-start.6 = (bf16[64,2048]{1,0:T(8,128)(2,1)S(1)}, bf16[64,2048]{1,0:T(8,128)(2,1)S(1)}, u32[]{:S(2)}, u32[]{:S(2)}) collective-permute-start(bf16[64,2048]{1,0:T(8,128)(2,1)S(1)} %get-tuple-element.28), channel_id=1, source_target_pairs={{0,4},{1,5},{2,6},{3,7},{4,8},{5,9},{6,10},{7,11},{8,12},{9,13},{1... | collective-permute-start | bytes 786440 | tf_op jit(solution)/shard_map/ppermute | solution.py:407
  20.5 8.1 %collective-permute-start.7 = (bf16[64,2048]{1,0:T(8,128)(2,1)S(1)}, bf16[64,2048]{1,0:T(8,128)(2,1)S(1)}, u32[]{:S(2)}, u32[]{:S(2)}) collective-permute-start(bf16[64,2048]{1,0:T(8,128)(2,1)S(1)} %get-tuple-element.29), channel_id=1, source_target_pairs={{0,12},{1,13},{2,14},{3,15},{4,0},{5,1},{6,2},{7,3},{8,4},{9,5},{1... | collective-permute-start | bytes 786440 | tf_op jit(solution)/shard_map/ppermute | solution.py:407
  28.7 13.4 %collective-permute-start.8 = (bf16[128,2048]{1,0:T(8,128)(2,1)S(1)}, bf16[128,2048]{1,0:T(8,128)(2,1)S(1)}, u32[]{:S(2)}, u32[]{:S(2)}) collective-permute-start(bf16[128,2048]{1,0:T(8,128)(2,1)S(1)} %shard_map.79.refs_1_), channel_id=1, source_target_pairs={{0,12},{1,13},{2,14},{3,15},{4,0},{5,1},{6,2},{7,3},{8,4},{9,5},{1... | collective-permute-start | bytes 1572872 | tf_op jit(solution)/shard_map/ppermute | solution.py:407
  29.9 12.9 %collective-permute-start.9 = (bf16[128,2048]{1,0:T(8,128)(2,1)S(1)}, bf16[128,2048]{1,0:T(8,128)(2,1)S(1)}, u32[]{:S(2)}, u32[]{:S(2)}) collective-permute-start(bf16[128,2048]{1,0:T(8,128)(2,1)S(1)} %shard_map.79.refs_1_), channel_id=1, source_target_pairs={{0,4},{1,5},{2,6},{3,7},{4,8},{5,9},{6,10},{7,11},{8,12},{9,13},{1... | collective-permute-start | bytes 1572872 | tf_op jit(solution)/shard_map/ppermute | solution.py:407
  30.7 8.5 %collective-permute-start.10 = (bf16[64,2048]{1,0:T(8,128)(2,1)S(1)}, bf16[64,2048]{1,0:T(8,128)(2,1)S(1)}, u32[]{:S(2)}, u32[]{:S(2)}) collective-permute-start(bf16[64,2048]{1,0:T(8,128)(2,1)S(1)} %collective-permute-done.6.refs_1_.refs_4_), channel_id=1, source_target_pairs={{0,2},{1,3},{2,0},{3,1},{4,6},{5,7},{6,4},{7,5},{8,10},{9,11},{10,... | collective-permute-start | bytes 786440 | tf_op jit(solution)/shard_map/ppermute | solution.py:407
  30.9 11.1 %collective-permute-start.11 = (bf16[64,2048]{1,0:T(8,128)(2,1)S(1)}, bf16[64,2048]{1,0:T(8,128)(2,1)S(1)}, u32[]{:S(2)}, u32[]{:S(2)}) collective-permute-start(bf16[64,2048]{1,0:T(8,128)(2,1)S(1)} %collective-permute-done.7.refs_2_.refs_5_), channel_id=1, source_target_pairs={{0,2},{1,3},{2,0},{3,1},{4,6},{5,7},{6,4},{7,5},{8,10},{9,11},{10,... | collective-permute-start | bytes 786440 | tf_op jit(solution)/shard_map/ppermute | solution.py:407
  50.0 13.3 %all-to-all-start = ((bf16[8,176,128]{2,1,0:T(8,128)(2,1)}), bf16[8,176,128]{2,1,0:T(8,128)(2,1)S(1)}, u32[]{:S(2)}, u32[]{:S(2)}) async-start(bf16[8,176,128]{2,1,0:T(8,128)(2,1)} %get-tuple-element.42), calls=%async_computation | async-start | bytes 720896 | tf_op jit(solution)/shard_map/all_to_all | solution.py:499
  54.4 0.7 collective-permute-start.15
  63.3 23.0 %all-to-all-start.1 = ((bf16[16,8,384]{2,1,0:T(8,128)(2,1)}), bf16[16,8,384]{2,1,0:T(8,128)(2,1)S(1)}, u32[]{:S(2)}, u32[]{:S(2)}) async-start(bf16[16,8,384]{2,1,0:T(8,128)(2,1)} %bitcast.1), calls=%async_computation.1 | async-start | bytes 196608 | tf_op jit(solution)/shard_map/all_to_all | solution.py:500
  70.9 16.1 %collective-permute-start.12 = (bf16[80,128]{1,0:T(8,128)(2,1)S(1)}, bf16[80,128]{1,0:T(8,128)(2,1)S(1)}, u32[]{:S(2)}, u32[]{:S(2)}) collective-permute-start(bf16[80,128]{1,0:T(8,128)(2,1)S(1)} %get-tuple-element.44), channel_id=1, source_target_pairs={{0,64},{64,128},{128,192},{192,0},{1,65},{65,129},{129,193},{193,1... | collective-permute-start | bytes 61448 | tf_op jit(solution)/shard_map/ppermute | solution.py:504
  77.3 9.7 %collective-permute-start.13 = (bf16[80,128]{1,0:T(8,128)(2,1)S(1)}, bf16[80,128]{1,0:T(8,128)(2,1)S(1)}, u32[]{:S(2)}, u32[]{:S(2)}) collective-permute-start(bf16[80,128]{1,0:T(8,128)(2,1)S(1)} %get-tuple-element.45), channel_id=1, source_target_pairs={{0,128},{64,192},{128,0},{192,64},{1,129},{65,193},{129,1},{193,65... | collective-permute-start | bytes 61448 | tf_op jit(solution)/shard_map/ppermute | solution.py:504
  82.7 5.1 %collective-permute-start.14 = (bf16[80,128]{1,0:T(8,128)(2,1)S(1)}, bf16[80,128]{1,0:T(8,128)(2,1)S(1)}, u32[]{:S(2)}, u32[]{:S(2)}) collective-permute-start(bf16[80,128]{1,0:T(8,128)(2,1)S(1)} %get-tuple-element.46), channel_id=1, source_target_pairs={{0,192},{64,0},{128,64},{192,128},{1,193},{65,1},{129,65},{193,129... | collective-permute-start | bytes 61448 | tf_op jit(solution)/shard_map/ppermute | solution.py:504

commit v6 on v4

--- a/solution.py
+++ b/solution.py
@@ -125,9 +125,10 @@
 
 
 def patch_kernel(
-    stacked, beyond, own_both, partner_both,
+    stacked, beyond, own_both, partner_both, after,
     patches, tissue, scale, norm, inv_square, inv_density, anch, anch_t, wturned,
 ):
+    del after
     second = on_second()
 
     def half(c, shift):
@@ -205,17 +206,14 @@
     return own.astype(bf16), partner.astype(bf16)
 
 
-def gather_products(blocks, first, wturned, whitened, partial):
-    grad_w, pooled = None, []
-    weights = wturned[:, first * OWN : first * OWN + sum(block.shape[0] for block in blocks)]
+def stacks(blocks):
     for n in range(8):
-        cols = pl.ds(n * 256, 256)
-        stack = jnp.concatenate([block[:, cols] for block in blocks], axis=0)
-        term = dot(weights, stack)
-        pooled.append(term if partial is None else term + partial[:, cols])
-        term = dot_nt(stack, whitened[:, cols])
-        grad_w = term if grad_w is None else grad_w + term
-    return pooled, grad_w
+        cols = slice(n * 256, (n + 1) * 256)
+        yield cols, jnp.concatenate([block[:, cols] for block in blocks], axis=0)
+
+
+def whiten_rows(blocks, whitened):
+    return sum(dot_nt(stack, whitened[:, cols]) for cols, stack in stacks(blocks))
 
 
 def place_rows(packed, grad_w, first):
@@ -230,25 +228,24 @@
 
 
 def early_kernel(*refs):
-    blocks, (wturned, whitened, partial, packed) = refs[:6], refs[6:]
+    blocks, (wturned, whitened, partial, packed) = refs[:5], refs[5:]
     packed[...] = jnp.zeros_like(packed)
-    pooled, grad_w = gather_products(blocks, 0, wturned, whitened, None)
-    for n in range(8):
-        partial[:, n * 256 : (n + 1) * 256] = pooled[n]
-    place_rows(packed, grad_w, 0)
+    for cols, stack in stacks(blocks):
+        partial[:, cols] = dot(wturned[:, : EARLY * OWN], stack)
+    place_rows(packed, whiten_rows(blocks, whitened), 0)
 
 
 def backward_kernel(*refs):
-    blocks = refs[:4]
+    blocks = refs[:3]
     (
-        partial, early, wturned, whitened, inv_density, masked, patches, inv_square, anch_t,
-        packed, image,
-        rowed, spread_grad, anchor_grad, pool_t,
-    ) = refs[4:]
+        partial, wturned, inv_density, masked, patches, inv_square, anch_t,
+        anchor_grad, image,
+        rowed, spread_grad, pool_t,
+    ) = refs[3:]
     pool_t[...] = column_spread()
-    packed[:, 0:128, :] = early[...]
-    pooled, grad_w = gather_products(blocks, EARLY, wturned, whitened, partial)
-    place_rows(packed, grad_w, EARLY)
+    pooled = [
+        partial[:, cols] + dot(wturned[:, EARLY * OWN :], stack) for cols, stack in stacks(blocks)
+    ]
     scaled = []
     for a in range(ROWS // 2):
         part = pooled[a // 2][:, (a % 2) * HALF : (a % 2 + 1) * HALF]
@@ -290,15 +287,6 @@
         here = pl.ds(pl.multiple_of(t * (STEP * GROUP), STEP * GROUP), (STEP + 4) * GROUP)
         spread_grad[here, :] += jnp.concatenate(sums, axis=0)
 
-    core = lax.axis_index("core")
-    mine, theirs = fold(anchor_grad[...], 40)
-    pad = jnp.zeros((8, 128), bf16)
-    mine = jnp.concatenate([mine, pad], axis=0)
-    theirs = jnp.concatenate([theirs, pad], axis=0)
-    for y in range(4):
-        packed[y * 2 + core, 128:176, :] = mine
-        packed[y * 2 + 1 - core, 128:176, :] = theirs
-
     t = spread_grad[...]
     offset = (lax.broadcasted_iota(jnp.int32, t.shape, 0) % GROUP) % 5
     moved = t
@@ -310,19 +298,23 @@
     image[...] = (dot(folder, high) + dot(folder, low)).astype(bf16)
 
 
-def pack_kernel(received, kept, next_one, next_two, next_three, sums):
-    total = received[0].astype(f32)
-    for source in range(1, 8):
-        total = total + received[source].astype(f32)
-    sums[...] = total[0:128]
-    anchor = total[128:176].astype(bf16)
-    for step, packed in enumerate((kept, next_one, next_two, next_three)):
-        z = lax.rem(lax.axis_index("z_hi") + step, 4)
-        packed[0:32, :] = sums[pl.ds(pl.multiple_of(z * 32, 32), 32), :].astype(bf16)
-        packed[32:80, :] = anchor
-
-
-def image_kernel(parts, middle, rims):
+def finish_kernel(first, second, third, whitened, early, anchor_grad, packed):
+    packed[:, 0:128, :] = early[...]
+    place_rows(packed, whiten_rows((first, second, third), whitened), EARLY)
+    core = lax.axis_index("core")
+    pad = jnp.zeros((8, 128), bf16)
+    mine, theirs = (jnp.concatenate([part, pad], axis=0) for part in fold(anchor_grad[...], 40))
+    for y in range(4):
+        packed[y * 2 + core, 128:176, :] = mine
+        packed[y * 2 + 1 - core, 128:176, :] = theirs
+
+
+def rim_lanes(rims):
+    lane = lax.broadcasted_iota(jnp.int32, rims.shape, 1)
+    return jnp.where(lane < 6, rims, 0.0), jnp.where(lane >= 122, rims, 0.0)
+
+
+def image_kernel(parts, packed, middle, carried):
     halves = []
     for k in range(2):
         acc = parts[k].astype(f32)
@@ -333,13 +325,37 @@
     whole = jnp.concatenate([halves[0], gap], axis=1) + jnp.concatenate([gap, halves[1]], axis=1)
     turned = pltpu.roll(whole, 640 - 6, 1)
     middle[...] = turned[:, :512]
-    rims[...] = turned[:, 512:]
-
-
-def unpack_kernel(
-    kept, one, two, three, middle, before, after,
-    grad_anchors, grad_whiten, grad_image,
-):
+    later, earlier = rim_lanes(turned[:, 512:])
+    y, z, core = (lax.axis_index(name) for name in ("y", "z_hi", "core"))
+    later = jnp.where((y == 3) & (z == 3), 0.0, later)
+    earlier = jnp.where((y == 0) & (z == 0), 0.0, earlier)
+    carried[...] = packed[...]
+    for target in range(4):
+        rims = jnp.where(y + 1 == target, later, 0.0) + jnp.where(y - 1 == target, earlier, 0.0)
+        if target == 0:
+            rims = rims + jnp.where(y == 3, pltpu.roll(later, 64, 1), 0.0)
+        if target == 3:
+            rims = rims + jnp.where(y == 0, pltpu.roll(earlier, 64, 1), 0.0)
+        slot = target * 2 + core
+        anchor = packed[slot, 128:176, :].astype(f32)[:40]
+        carried[slot, 128:176, :] = jnp.concatenate([anchor, rims], axis=0).astype(bf16)
+
+
+def pack_kernel(received, kept, next_one, next_two, next_three, sums):
+    total = received[0].astype(f32)
+    for source in range(1, 8):
+        total = total + received[source].astype(f32)
+    sums[...] = total[0:128]
+    straight = rim_lanes(total[168:176])
+    onward = rim_lanes(pltpu.roll(total[168:176], 64, 1))
+    rims = (straight[0] + straight[1], onward[0], jnp.zeros((8, 128), f32), onward[1])
+    for step, packed in enumerate((kept, next_one, next_two, next_three)):
+        z = lax.rem(lax.axis_index("z_hi") + step, 4)
+        packed[0:32, :] = sums[pl.ds(pl.multiple_of(z * 32, 32), 32), :].astype(bf16)
+        packed[32:80, :] = jnp.concatenate([total[128:168], rims[step]], axis=0).astype(bf16)
+
+
+def unpack_kernel(kept, one, two, three, middle, grad_anchors, grad_whiten, grad_image):
     total = sum(ref[...].astype(f32) for ref in (one, two, three)) + kept[...].astype(f32)
     other = pltpu.roll(total, OWN, 1)
     grad_whiten[0:32, :] = total[0:32, :OWN]
@@ -349,13 +365,21 @@
         turned, entry_order(f32), (((1,), (1,)), ((), ())),
         precision=lax.Precision.HIGHEST, preferred_element_type=f32,
     )
-    lane = lax.broadcasted_iota(jnp.int32, before.shape, 1)
-    first = jnp.where(lane < 6, before[...], 0.0)
-    last = jnp.where(lane >= 122, after[...], 0.0)
-    gap = jnp.zeros((8, 256), f32)
-    image = middle[...] + jnp.concatenate([first, gap, last], axis=1)
+    first, last = rim_lanes(total[72:80])
+    image = middle[...] + jnp.concatenate([first, jnp.zeros((8, 256), f32), last], axis=1)
     for colour in range(3):
         grad_image[colour] = image[2 * colour : 2 * colour + 2]
+
+
+def halve_kernel(first, second, after, upper, lower):
+    del after
+    upper[...] = first[:OWN]
+    lower[...] = second[OWN:]
+
+
+def join_kernel(upper, lower, joined):
+    joined[:OWN] = upper[...]
+    joined[OWN:] = lower[...]
 
 
 def hold(value, *after):
@@ -405,14 +429,10 @@
     held = {(0, 0): [block]}
     for dx, dz in ((1, 0), (3, 0), (0, 1)):
         held[(4 - dx) % 4, dz] = [send(block, dx, dz, 0)]
-    far = [send(held[3, 0][0][:OWN], 1, 0, 0), send(held[1, 0][0][OWN:], 3, 0, 0)]
-    beside = hold(held[0, 1][0], *far)
-    held[2, 0] = far
-    held[3, 1] = [send(beside, 1, 0, 0)]
-    held[1, 1] = [send(beside, 3, 0, 0)]
-    held[2, 1] = [send(half, 0, 1, 0) for half in far]
-    held[0, 1] = [beside]
-    blocks = [part for chip in CHIPS for part in held[chip]]
+    both = jnp.concatenate(
+        [jnp.pad(whiten, ((0, 0), (0, OWN))), jnp.pad(anchors, ((0, 0), (0, 53)))], axis=0
+    )
+    partner_both = send(both, 0, 0, 1)
 
     stacked = jnp.concatenate([image, mask.astype(bf16)[None]], axis=0)
     (tile,) = call(
@@ -421,12 +441,23 @@
         [],
         1_000_000,
         4,
-        stacked, held[3, 0][0],
+        stacked, partner_both,
         loose=1,
     )
-    both = jnp.concatenate(
-        [jnp.pad(whiten, ((0, 0), (0, OWN))), jnp.pad(anchors, ((0, 0), (0, 53)))], axis=0
-    )
+    half = ((OWN, 16 * HALF), bf16)
+    upper, lower = call(
+        halve_kernel, [half, half], [], 1_000_000, 4, held[3, 0][0], held[1, 0][0], tile, loose=1
+    )
+    far = [send(upper, 1, 0, 0), send(lower, 3, 0, 0)]
+    (opposite,) = call(join_kernel, [((2 * OWN, 16 * HALF), bf16)], [], 1_000_000, 4, *far)
+    beside = hold(held[0, 1][0], opposite)
+    held[2, 0] = [opposite]
+    held[3, 1] = [send(beside, 1, 0, 0)]
+    held[1, 1] = [send(beside, 3, 0, 0)]
+    held[2, 1] = [send(opposite, 0, 1, 0)]
+    held[0, 1] = [beside]
+    blocks = [part for chip in CHIPS for part in held[chip]]
+
     plane = ((ROWS, LANES), f32)
     patches, tissue, scale, norm, inv_square, inv_density, anch, anch_t, wturned = call(
         patch_kernel,
@@ -444,7 +475,8 @@
         [],
         1_000_000_000,
         12,
-        stacked, cross(tile), both, send(both, 0, 0, 1),
+        stacked, cross(tile), both, partner_both, beside,
+        loose=1,
     )
     masked, whitened = call(
         forward_kernel,
@@ -460,34 +492,33 @@
         [],
         2_000_000_000,
         14,
-        *blocks[:6], wturned, whitened,
-    )
-    packed, image_part = call(
+        *blocks[:5], wturned, whitened,
+    )
+    anchor_grad, image_part = call(
         backward_kernel,
-        [((8, 176, 128), bf16), ((128, LANES), bf16)],
-        [
-            ((ROWS * 128, HALF), bf16),
-            ((36 * GROUP, LANES), f32),
-            ((80, 128), f32),
-            ((HALF, LANES), bf16),
-        ],
+        [((80, 128), f32), ((128, LANES), bf16)],
+        [((ROWS * 128, HALF), bf16), ((36 * GROUP, LANES), f32), ((HALF, LANES), bf16)],
         5_000_000_000,
         20,
-        *blocks[6:],
-        partial, early, wturned, whitened, inv_density, masked, patches, inv_square, anch_t,
-    )
-
+        *blocks[5:],
+        partial, wturned, inv_density, masked, patches, inv_square, anch_t,
+    )
+
+    parts = lax.all_to_all(image_part.reshape(16, 8, LANES), CHAN, 0, 0)
+    packed_shape = ((8, 176, 128), bf16)
+    (packed,) = call(
+        finish_kernel, [packed_shape], [], 1_000_000_000, 12, *blocks[5:], whitened, early, anchor_grad
+    )
+    middle, packed = call(
+        image_kernel, [((8, 512), f32), packed_shape], [], 1_000_000, 6, parts, packed
+    )
     received = lax.all_to_all(packed, ("y", "core"), 0, 0)
-    parts = lax.all_to_all(image_part.reshape(16, 8, LANES), CHAN, 0, 0)
     quarter = ((80, 128), bf16)
     kept, *away = call(pack_kernel, [quarter] * 4, [((128, 128), f32)], 1_000_000, 4, received)
     others = [
         lax.ppermute(value, "z_hi", [(z, (z + step) % 4) for z in range(4)])
         for step, value in enumerate(away, 1)
     ]
-    middle, rims = call(image_kernel, [((8, 512), f32), ((8, 128), f32)], [], 1_000_000, 4, parts)
-    before = lax.ppermute(rims, STRIPS, [(i, i + 1) for i in range(15)])
-    after = lax.ppermute(rims, STRIPS, [(i + 1, i) for i in range(15)])
     return tuple(
         call(
             unpack_kernel,
@@ -495,7 +526,7 @@
             [],
             1_000_000,
             4,
-            kept, *others, middle, before, after,
+            kept, *others, middle,
         )
     )
 

time: 93.4 us -> 88.3 us (0.945)
  starting transfers between devices: 37.4 us -> 30.6 us
    ppermute x2 -> x0, waiting for transfers between devices: 6.33 us -> none  [the longest x1 6.32 us: shards(): after = lax.ppermute(rims, STRIPS, [(i + 1, i) for i in range(15)])]
    ppermute x2 -> x0, starting transfers between devices: 5.84 us -> none  [the longest x1 3.67 us: shards(): before = lax.ppermute(rims, STRIPS, [(i, i + 1) for i in range(15)])]
    all_to_all x1, waiting for transfers between devices: 0.01 us -> 5.66 us  [shards(): parts = lax.all_to_all(image_part.reshape(16, 8, LANES), CHAN, 0, 0)]
    ppermute x3, waiting for transfers between devices: 0.01 us -> 2.34 us  [shards(): lax.ppermute(value, 'z_hi', [(z, (z + step) % 4) for z in range(4)])]
    ppermute x11 -> x10, waiting for transfers between devices: 17.4 us -> 16.4 us  [send(): return lax.ppermute(value, CHAN, route(dx, dz, other))]
    pallas_call x8 -> x11, Pallas kernels: 16.6 us -> 17.1 us  [call(): pl.pallas_call(kernel, out_shape=[jax.ShapeDtypeStruct(shape, dtype) for...]
    ppermute x11 -> x10, starting transfers between devices: 14.2 us -> 13.8 us  [send(): return lax.ppermute(value, CHAN, route(dx, dz, other))]
  transfers between devices with their start and end apart: 18 -> 15, of which waited for: 6 -> 8; matrix products, arithmetic and copies ran while one was open for 2% -> 2% of each run, Pallas kernels for 8% -> 10%
where the time goes in v6:
time: 88.3 us; the launch traced here: 86.9 us
  starting transfers between devices  30.6 us (35%)
  waiting for transfers between devices  24.4 us (28%)
  Pallas kernels  17.1 us (19%)
  blocking collectives  10.9 us (12%)
  other arithmetic  1.9 us (2%)
  local copies, waits for them, and re-layouts  1.22 us (1%)
    pallas_call x11, Pallas kernels, call(): pl.pallas_call(kernel, out_shape=[jax.ShapeDtypeStruct(shape, dtype) for...  17.1 us
    ppermute x10, waiting for transfers between devices, send(): return lax.ppermute(value, CHAN, route(dx, dz, other))  16.4 us
    ppermute x10, starting transfers between devices, send(): return lax.ppermute(value, CHAN, route(dx, dz, other))  13.8 us
    all_to_all x1, blocking collectives, shards(): received = lax.all_to_all(packed, ('y', 'core'), 0, 0)  10.9 us
    ppermute x3, starting transfers between devices, shards(): lax.ppermute(value, 'z_hi', [(z, (z + step) % 4) for z in range(4)])  10.4 us
    all_to_all x1, waiting for transfers between devices, shards(): parts = lax.all_to_all(image_part.reshape(16, 8, LANES), CHAN, 0, 0)  5.66 us
    all_to_all x1, starting transfers between devices, shards(): parts = lax.all_to_all(image_part.reshape(16, 8, LANES), CHAN, 0, 0)  4.47 us
    ppermute x3, waiting for transfers between devices, shards(): lax.ppermute(value, 'z_hi', [(z, (z + step) % 4) for z in range(4)])  2.34 us
  transfers between devices with their start and end apart: 15, of which 8 were waited for; matrix products, arithmetic and copies ran while one was open for 2% of the time, Pallas kernels for 10%

profile of v6, /device:TPU:24, one launch (start us, length us, event | category | flops | bytes accessed | tf_op | source)
XLA Modules:
  0.0 86.9 jit_solution(12011564696358917818)
XLA Ops:
  0.7 1.1 %broadcast_select_fusion = (bf16[64,16,128]{2,1,0:T(8,128)(2,1)S(1)}, bf16[64,16,128]{2,1,0:T(8,128)(2,1)S(1)}) fusion(pred[]{:T(512)S(6)} %eq.3, bf16[64,16,256]{2,1,0:T(8,128)(2,1)} %param.9), kind=kLoop, calls=%fused_computation.7 | loop fusion | flops 262144 | bytes 1048577 | tf_op jit(solution)/shard_map/jit(_where)/select_n | solution.py:427
  1.9 1.1 %copy.9 = bf16[1024,64]{1,0:T(8,128)(2,1)S(1)} copy(bf16[1024,64]{0,1:T(8,128)(2,1)} %param.8) | data formatting | bytes 262144 | tf_op args[3]
  3.1 0.4 collective-permute-done
  3.5 1.6 %collective-permute-start.2 = (bf16[128,2048]{1,0:T(8,128)(2,1)S(1)}, bf16[128,2048]{1,0:T(8,128)(2,1)S(1)}, u32[]{:S(2)}, u32[]{:S(2)}) collective-permute-start(bf16[128,2048]{1,0:T(8,128)(2,1)S(1)} %constant_dynamic-update-slice_fusion.refs_0_), channel_id=1, source_target_pairs={{0,4},{1,5},{2,6},{3,7},{4,8},{5,9},{6,10},{7,11},{8,12},{9,13},{1... | collective-permute-start | bytes 1572872 | tf_op jit(solution)/shard_map/ppermute | solution.py:420
  5.1 1.7 %collective-permute-start.3 = (bf16[128,2048]{1,0:T(8,128)(2,1)S(1)}, bf16[128,2048]{1,0:T(8,128)(2,1)S(1)}, u32[]{:S(2)}, u32[]{:S(2)}) collective-permute-start(bf16[128,2048]{1,0:T(8,128)(2,1)S(1)} %constant_dynamic-update-slice_fusion.refs_0_), channel_id=1, source_target_pairs={{0,12},{1,13},{2,14},{3,15},{4,0},{5,1},{6,2},{7,3},{8,4},{9,5},{1... | collective-permute-start | bytes 1572872 | tf_op jit(solution)/shard_map/ppermute | solution.py:420
  6.8 0.8 fusion.2.own_both
  7.7 2.0 %collective-permute-start.1 = (bf16[128,2048]{1,0:T(8,128)(2,1)S(1)}, bf16[128,2048]{1,0:T(8,128)(2,1)S(1)}, u32[]{:S(2)}, u32[]{:S(2)}) collective-permute-start(bf16[128,2048]{1,0:T(8,128)(2,1)S(1)} %constant_dynamic-update-slice_fusion.refs_0_), channel_id=1, source_target_pairs={{0,2},{1,3},{2,0},{3,1},{4,6},{5,7},{6,4},{7,5},{8,10},{9,11},{10,... | collective-permute-start | bytes 1572872 | tf_op jit(solution)/shard_map/ppermute | solution.py:420
  9.8 9.0 %collective-permute-done.2.first.refs_3_ = bf16[128,2048]{1,0:T(8,128)(2,1)S(1)} collective-permute-done((bf16[128,2048]{1,0:T(8,128)(2,1)S(1)}, bf16[128,2048]{1,0:T(8,128)(2,1)S(1)}, u32[]{:S(2)}, u32[]{:S(2)}) %collective-permute-start.2) | collective-permute-done | bytes 524320 | tf_op jit(solution)/shard_map/ppermute | solution.py:420
  18.8 1.6 %collective-permute-start.5 = (bf16[64,2048]{1,0:T(8,128)(2,1)S(1)}, bf16[64,2048]{1,0:T(8,128)(2,1)S(1)}, u32[]{:S(2)}, u32[]{:S(2)}) collective-permute-start(bf16[64,2048]{1,0:T(8,128)(2,1)S(1)} %get-tuple-element.26), channel_id=1, source_target_pairs={{0,4},{1,5},{2,6},{3,7},{4,8},{5,9},{6,10},{7,11},{8,12},{9,13},{1... | collective-permute-start | bytes 786440 | tf_op jit(solution)/shard_map/ppermute | solution.py:420
  20.3 1.7 %collective-permute-start.6 = (bf16[64,2048]{1,0:T(8,128)(2,1)S(1)}, bf16[64,2048]{1,0:T(8,128)(2,1)S(1)}, u32[]{:S(2)}, u32[]{:S(2)}) collective-permute-start(bf16[64,2048]{1,0:T(8,128)(2,1)S(1)} %get-tuple-element.27), channel_id=1, source_target_pairs={{0,12},{1,13},{2,14},{3,15},{4,0},{5,1},{6,2},{7,3},{8,4},{9,5},{1... | collective-permute-start | bytes 786440 | tf_op jit(solution)/shard_map/ppermute | solution.py:420
  22.1 1.9 %collective-permute-start.10 = (bf16[4,32,128]{2,1,0:T(8,128)(2,1)S(1)}, bf16[4,32,128]{2,1,0:T(8,128)(2,1)S(1)}, u32[]{:S(2)}, u32[]{:S(2)}) collective-permute-start(bf16[4,32,128]{2,1,0:T(8,128)(2,1)S(1)} %shard_map.76.after), channel_id=1, source_target_pairs={{16,1},{18,3},{20,5},{22,7},{24,9},{26,11},{28,13},{30,15},{32,17}... | collective-permute-start | bytes 98312 | tf_op jit(solution)/shard_map/ppermute | solution.py:423
  24.0 3.6 %collective-permute-done.5.upper = bf16[64,2048]{1,0:T(8,128)(2,1)S(1)} collective-permute-done((bf16[64,2048]{1,0:T(8,128)(2,1)S(1)}, bf16[64,2048]{1,0:T(8,128)(2,1)S(1)}, u32[]{:S(2)}, u32[]{:S(2)}) %collective-permute-start.5) | collective-permute-done | bytes 262176 | tf_op jit(solution)/shard_map/ppermute | solution.py:420
  27.7 3.0 %collective-permute-start.7 = (bf16[128,2048]{1,0:T(8,128)(2,1)S(1)}, bf16[128,2048]{1,0:T(8,128)(2,1)S(1)}, u32[]{:S(2)}, u32[]{:S(2)}) collective-permute-start(bf16[128,2048]{1,0:T(8,128)(2,1)S(1)} %shard_map.79.after.refs_1_), channel_id=1, source_target_pairs={{0,12},{1,13},{2,14},{3,15},{4,0},{5,1},{6,2},{7,3},{8,4},{9,5},{1... | collective-permute-start | bytes 1572872 | tf_op jit(solution)/shard_map/ppermute | solution.py:420
  30.7 1.9 %collective-permute-start.9 = (bf16[128,2048]{1,0:T(8,128)(2,1)S(1)}, bf16[128,2048]{1,0:T(8,128)(2,1)S(1)}, u32[]{:S(2)}, u32[]{:S(2)}) collective-permute-start(bf16[128,2048]{1,0:T(8,128)(2,1)S(1)} %shard_map.78.refs_1_.refs_4_), channel_id=1, source_target_pairs={{0,2},{1,3},{2,0},{3,1},{4,6},{5,7},{6,4},{7,5},{8,10},{9,11},{10,... | collective-permute-start | bytes 1572872 | tf_op jit(solution)/shard_map/ppermute | solution.py:420
  32.6 1.8 %shard_map.80 = (bf16[576,384]{1,0:T(8,128)(2,1)S(1)}, f32[32,384]{1,0:T(8,128)S(1)}, f32[32,384]{1,0:T(8,128)S(1)}, f32[32,384]{1,0:T(8,128)S(1)}, f32[32,384]{...) custom-call(bf16[4,32,512]{2,1,0:T(8,128)(2,1)S(1)} %pad_maximum_fus, ...), custom_call_target="tpu_custom_call" | custom-call | flops 1000000000 | bytes 1671168 | tf_op jit(solution)/shard_map/pallas_call | solution.py:404
  34.4 4.5 %shard_map.81 = (bf16[32,128,384]{2,1,0:T(8,128)(2,1)S(1)}, bf16[128,2048]{1,0:T(8,128)(2,1)S(1)}) custom-call(bf16[576,384]{1,0:T(8,128)(2,1)S(1)} %get-tuple-element.29.patches.refs_7_, f32[32,384]{1,0:T(8,128)S(1)} %get-tuple-element.30.tissue, f32[32,384]{1,0:T(8,128)S(1)} %get-tuple-element.31.scale, f32[32,384]{1,0:T(8,128)S(1)} %get-tuple-element.32.norm, ...), custom_call_target="tpu_custom_call" | custom-call | flops 3000000000 | bytes 4288512 | tf_op jit(solution)/shard_map/pallas_call | solution.py:404
  38.9 1.3 %shard_map.82 = (f32[128,2048]{1,0:T(8,128)S(1)}, bf16[8,128,128]{2,1,0:T(8,128)(2,1)S(1)}) custom-call(bf16[128,2048]{1,0:T(8,128)(2,1)S(1)} %constant_dynamic-update-slice_fusion.refs_0_, bf16[128,2048]{1,0:T(8,128)(2,1)S(1)} %shard_map.79.after.refs_1_, bf16[128,2048]{1,0:T(8,128)(2,1)S(1)} %collective-permute-done.3.second.refs_2_, ...), custom_call_target="tpu_custom_call" | custom-call | flops 2000000000 | bytes 4718592 | tf_op jit(solution)/shard_map/pallas_call | solution.py:404
  40.2 0.8 collective-permute-done.7.refs_0_.first
  41.0 2.7 %collective-permute-done.8.refs_1_.second = bf16[128,2048]{1,0:T(8,128)(2,1)S(1)} collective-permute-done((bf16[128,2048]{1,0:T(8,128)(2,1)S(1)}, bf16[128,2048]{1,0:T(8,128)(2,1)S(1)}, u32[]{:S(2)}, u32[]{:S(2)}) %collective-permute-start.8) | collective-permute-done | bytes 524320 | tf_op jit(solution)/shard_map/ppermute | solution.py:420
  43.7 7.6 %shard_map.83 = (f32[80,128]{1,0:T(8,128)S(1)}, bf16[128,384]{1,0:T(8,128)(2,1)}) custom-call(bf16[128,2048]{1,0:T(8,128)(2,1)S(1)} %collective-permute-done.7.refs_0_.first, bf16[128,2048]{1,0:T(8,128)(2,1)S(1)} %collective-permute-done.8.refs_1_.second, bf16[128,2048]{1,0:T(8,128)(2,1)S(1)} %collective-permute-done.9.refs_2_.third, ...), custom_call_target="tpu_custom_call" | custom-call | flops 5000000000 | bytes 6688768 | tf_op jit(solution)/shard_map/pallas_call | solution.py:404
  51.3 4.5 %all-to-all-start = ((bf16[16,8,384]{2,1,0:T(8,128)(2,1)}), bf16[16,8,384]{2,1,0:T(8,128)(2,1)S(1)}, u32[]{:S(2)}, u32[]{:S(2)}) async-start(bf16[16,8,384]{2,1,0:T(8,128)(2,1)} %bitcast.1), calls=%async_computation | async-start | bytes 196608 | tf_op jit(solution)/shard_map/all_to_all | solution.py:507
  55.8 0.6 shard_map.84.packed
  56.5 5.7 %all-to-all-done.parts = bf16[16,8,384]{2,1,0:T(8,128)(2,1)S(1)} async-done(((bf16[16,8,384]{2,1,0:T(8,128)(2,1)}), bf16[16,8,384]{2,1,0:T(8,128)(2,1)S(1)}, u32[]{:S(2)}, u32[]{:S(2)}) %all-to-all-start) | async-done | bytes 98336 | tf_op jit(solution)/shard_map/all_to_all | solution.py:507
  62.1 0.2 shard_map.85
  62.3 10.9 %all_to_all.10.received = bf16[8,176,128]{2,1,0:T(8,128)(2,1)S(1)} all-to-all(bf16[8,176,128]{2,1,0:T(8,128)(2,1)S(1)} %get-tuple-element.43), channel_id=1, replica_groups=mesh['z_hi'=4,'y'=4,'x'=4,'z_lo'=2,'core'=2] {'y','core'}, dimensions={0} | all-to-all | bytes 720896 | tf_op jit(solution)/shard_map/all_to_all | solution.py:515
  73.1 0.1 shard_map.86
  73.2 3.6 %collective-permute-start.11 = (bf16[80,128]{1,0:T(8,128)(2,1)S(1)}, bf16[80,128]{1,0:T(8,128)(2,1)S(1)}, u32[]{:S(2)}, u32[]{:S(2)}) collective-permute-start(bf16[80,128]{1,0:T(8,128)(2,1)S(1)} %get-tuple-element.45), channel_id=1, source_target_pairs={{0,64},{64,128},{128,192},{192,0},{1,65},{65,129},{129,193},{193,1... | collective-permute-start | bytes 61448 | tf_op jit(solution)/shard_map/ppermute | solution.py:519
  76.8 4.2 %collective-permute-start.12 = (bf16[80,128]{1,0:T(8,128)(2,1)S(1)}, bf16[80,128]{1,0:T(8,128)(2,1)S(1)}, u32[]{:S(2)}, u32[]{:S(2)}) collective-permute-start(bf16[80,128]{1,0:T(8,128)(2,1)S(1)} %get-tuple-element.46), channel_id=1, source_target_pairs={{0,128},{64,192},{128,0},{192,64},{1,129},{65,193},{129,1},{193,65... | collective-permute-start | bytes 61448 | tf_op jit(solution)/shard_map/ppermute | solution.py:519
  81.0 2.7 %collective-permute-start.13 = (bf16[80,128]{1,0:T(8,128)(2,1)S(1)}, bf16[80,128]{1,0:T(8,128)(2,1)S(1)}, u32[]{:S(2)}, u32[]{:S(2)}) collective-permute-start(bf16[80,128]{1,0:T(8,128)(2,1)S(1)} %get-tuple-element.47), channel_id=1, source_target_pairs={{0,192},{64,0},{128,64},{192,128},{1,193},{65,1},{129,65},{193,129... | collective-permute-start | bytes 61448 | tf_op jit(solution)/shard_map/ppermute | solution.py:519
  83.7 1.1 %collective-permute-done.12.two = bf16[80,128]{1,0:T(8,128)(2,1)S(1)} collective-permute-done((bf16[80,128]{1,0:T(8,128)(2,1)S(1)}, bf16[80,128]{1,0:T(8,128)(2,1)S(1)}, u32[]{:S(2)}, u32[]{:S(2)}) %collective-permute-start.12) | collective-permute-done | bytes 20512 | tf_op jit(solution)/shard_map/ppermute | solution.py:519
  84.7 1.3 %collective-permute-done.13.three = bf16[80,128]{1,0:T(8,128)(2,1)S(1)} collective-permute-done((bf16[80,128]{1,0:T(8,128)(2,1)S(1)}, bf16[80,128]{1,0:T(8,128)(2,1)S(1)}, u32[]{:S(2)}, u32[]{:S(2)}) %collective-permute-start.13) | collective-permute-done | bytes 20512 | tf_op jit(solution)/shard_map/ppermute | solution.py:519
  86.0 0.9 %shard_map.87 = (f32[64,75]{1,0:T(8,128)}, f32[64,64]{1,0:T(8,128)}, f32[3,2,512]{2,1,0:T(2,128)}) custom-call(bf16[80,128]{1,0:T(8,128)(2,1)S(1)} %get-tuple-element.44.kept, bf16[80,128]{1,0:T(8,128)(2,1)S(1)} %collective-permute-done.11.one, bf16[80,128]{1,0:T(8,128)(2,1)S(1)} %collective-permute-done.12.two, ...), custom_call_target="tpu_custom_call" | custom-call | flops 1000000 | bytes 146176 | tf_op jit(solution)/shard_map/pallas_call | solution.py:404
  (23 shorter events, 0.5 us)
Async XLA Ops:
  0.6 9.1 %copy-start.1 = (s32[32,512]{1,0:T(8,128)S(1)}, s32[32,512]{1,0:T(8,128)}, u32[]{:S(2)}) copy-start(s32[32,512]{1,0:T(8,128)} %param.6) | copy-start | bytes 196612
  0.6 9.1 %copy-start = (bf16[3,32,512]{2,1,0:T(8,128)(2,1)S(1)}, bf16[3,32,512]{2,1,0:T(8,128)(2,1)}, u32[]{:S(2)}) copy-start(bf16[3,32,512]{2,1,0:T(8,128)(2,1)} %param.5) | copy-start | bytes 294916
  1.8 1.6 %collective-permute-start = (bf16[64,2048]{1,0:T(8,128)(2,1)S(1)}, bf16[64,2048]{1,0:T(8,128)(2,1)S(1)}, u32[]{:S(2)}, u32[]{:S(2)}) collective-permute-start(bf16[64,2048]{1,0:T(8,128)(2,1)S(1)} %bitcast.12), channel_id=1, source_target_pairs={{0,1},{1,0},{2,3},{3,2},{4,5},{5,4},{6,7},{7,6},{8,9},{9,8},{10,11... | collective-permute-start | bytes 786440 | tf_op jit(solution)/shard_map/ppermute | solution.py:420
  3.5 15.3 %collective-permute-start.2 = (bf16[128,2048]{1,0:T(8,128)(2,1)S(1)}, bf16[128,2048]{1,0:T(8,128)(2,1)S(1)}, u32[]{:S(2)}, u32[]{:S(2)}) collective-permute-start(bf16[128,2048]{1,0:T(8,128)(2,1)S(1)} %constant_dynamic-update-slice_fusion.refs_0_), channel_id=1, source_target_pairs={{0,4},{1,5},{2,6},{3,7},{4,8},{5,9},{6,10},{7,11},{8,12},{9,13},{1... | collective-permute-start | bytes 1572872 | tf_op jit(solution)/shard_map/ppermute | solution.py:420
  5.1 13.7 %collective-permute-start.3 = (bf16[128,2048]{1,0:T(8,128)(2,1)S(1)}, bf16[128,2048]{1,0:T(8,128)(2,1)S(1)}, u32[]{:S(2)}, u32[]{:S(2)}) collective-permute-start(bf16[128,2048]{1,0:T(8,128)(2,1)S(1)} %constant_dynamic-update-slice_fusion.refs_0_), channel_id=1, source_target_pairs={{0,12},{1,13},{2,14},{3,15},{4,0},{5,1},{6,2},{7,3},{8,4},{9,5},{1... | collective-permute-start | bytes 1572872 | tf_op jit(solution)/shard_map/ppermute | solution.py:420
  7.6 2.2 %collective-permute-start.4 = (bf16[1088,128]{1,0:T(8,128)(2,1)S(1)}, bf16[1088,128]{1,0:T(8,128)(2,1)S(1)}, u32[]{:S(2)}, u32[]{:S(2)}) collective-permute-start(bf16[1088,128]{1,0:T(8,128)(2,1)S(1)} %fusion.2.own_both), channel_id=1, source_target_pairs={{0,1},{1,0},{2,3},{3,2},{4,5},{5,4},{6,7},{7,6},{8,9},{9,8},{10,11... | collective-permute-start | bytes 835592 | tf_op jit(solution)/shard_map/ppermute | solution.py:420
  7.7 20.0 %collective-permute-start.1 = (bf16[128,2048]{1,0:T(8,128)(2,1)S(1)}, bf16[128,2048]{1,0:T(8,128)(2,1)S(1)}, u32[]{:S(2)}, u32[]{:S(2)}) collective-permute-start(bf16[128,2048]{1,0:T(8,128)(2,1)S(1)} %constant_dynamic-update-slice_fusion.refs_0_), channel_id=1, source_target_pairs={{0,2},{1,3},{2,0},{3,1},{4,6},{5,7},{6,4},{7,5},{8,10},{9,11},{10,... | collective-permute-start | bytes 1572872 | tf_op jit(solution)/shard_map/ppermute | solution.py:420
  18.8 8.8 %collective-permute-start.5 = (bf16[64,2048]{1,0:T(8,128)(2,1)S(1)}, bf16[64,2048]{1,0:T(8,128)(2,1)S(1)}, u32[]{:S(2)}, u32[]{:S(2)}) collective-permute-start(bf16[64,2048]{1,0:T(8,128)(2,1)S(1)} %get-tuple-element.26), channel_id=1, source_target_pairs={{0,4},{1,5},{2,6},{3,7},{4,8},{5,9},{6,10},{7,11},{8,12},{9,13},{1... | collective-permute-start | bytes 786440 | tf_op jit(solution)/shard_map/ppermute | solution.py:420
  20.3 7.2 %collective-permute-start.6 = (bf16[64,2048]{1,0:T(8,128)(2,1)S(1)}, bf16[64,2048]{1,0:T(8,128)(2,1)S(1)}, u32[]{:S(2)}, u32[]{:S(2)}) collective-permute-start(bf16[64,2048]{1,0:T(8,128)(2,1)S(1)} %get-tuple-element.27), channel_id=1, source_target_pairs={{0,12},{1,13},{2,14},{3,15},{4,0},{5,1},{6,2},{7,3},{8,4},{9,5},{1... | collective-permute-start | bytes 786440 | tf_op jit(solution)/shard_map/ppermute | solution.py:420
  22.1 10.5 %collective-permute-start.10 = (bf16[4,32,128]{2,1,0:T(8,128)(2,1)S(1)}, bf16[4,32,128]{2,1,0:T(8,128)(2,1)S(1)}, u32[]{:S(2)}, u32[]{:S(2)}) collective-permute-start(bf16[4,32,128]{2,1,0:T(8,128)(2,1)S(1)} %shard_map.76.after), channel_id=1, source_target_pairs={{16,1},{18,3},{20,5},{22,7},{24,9},{26,11},{28,13},{30,15},{32,17}... | collective-permute-start | bytes 98312 | tf_op jit(solution)/shard_map/ppermute | solution.py:423
  27.7 13.4 %collective-permute-start.7 = (bf16[128,2048]{1,0:T(8,128)(2,1)S(1)}, bf16[128,2048]{1,0:T(8,128)(2,1)S(1)}, u32[]{:S(2)}, u32[]{:S(2)}) collective-permute-start(bf16[128,2048]{1,0:T(8,128)(2,1)S(1)} %shard_map.79.after.refs_1_), channel_id=1, source_target_pairs={{0,12},{1,13},{2,14},{3,15},{4,0},{5,1},{6,2},{7,3},{8,4},{9,5},{1... | collective-permute-start | bytes 1572872 | tf_op jit(solution)/shard_map/ppermute | solution.py:420
  30.7 13.0 %collective-permute-start.8 = (bf16[128,2048]{1,0:T(8,128)(2,1)S(1)}, bf16[128,2048]{1,0:T(8,128)(2,1)S(1)}, u32[]{:S(2)}, u32[]{:S(2)}) collective-permute-start(bf16[128,2048]{1,0:T(8,128)(2,1)S(1)} %shard_map.79.after.refs_1_), channel_id=1, source_target_pairs={{0,4},{1,5},{2,6},{3,7},{4,8},{5,9},{6,10},{7,11},{8,12},{9,13},{1... | collective-permute-start | bytes 1572872 | tf_op jit(solution)/shard_map/ppermute | solution.py:420
  30.7 13.0 %collective-permute-start.9 = (bf16[128,2048]{1,0:T(8,128)(2,1)S(1)}, bf16[128,2048]{1,0:T(8,128)(2,1)S(1)}, u32[]{:S(2)}, u32[]{:S(2)}) collective-permute-start(bf16[128,2048]{1,0:T(8,128)(2,1)S(1)} %shard_map.78.refs_1_.refs_4_), channel_id=1, source_target_pairs={{0,2},{1,3},{2,0},{3,1},{4,6},{5,7},{6,4},{7,5},{8,10},{9,11},{10,... | collective-permute-start | bytes 1572872 | tf_op jit(solution)/shard_map/ppermute | solution.py:420
  51.3 10.8 %all-to-all-start = ((bf16[16,8,384]{2,1,0:T(8,128)(2,1)}), bf16[16,8,384]{2,1,0:T(8,128)(2,1)S(1)}, u32[]{:S(2)}, u32[]{:S(2)}) async-start(bf16[16,8,384]{2,1,0:T(8,128)(2,1)} %bitcast.1), calls=%async_computation | async-start | bytes 196608 | tf_op jit(solution)/shard_map/all_to_all | solution.py:507
  73.2 10.4 %collective-permute-start.11 = (bf16[80,128]{1,0:T(8,128)(2,1)S(1)}, bf16[80,128]{1,0:T(8,128)(2,1)S(1)}, u32[]{:S(2)}, u32[]{:S(2)}) collective-permute-start(bf16[80,128]{1,0:T(8,128)(2,1)S(1)} %get-tuple-element.45), channel_id=1, source_target_pairs={{0,64},{64,128},{128,192},{192,0},{1,65},{65,129},{129,193},{193,1... | collective-permute-start | bytes 61448 | tf_op jit(solution)/shard_map/ppermute | solution.py:519
  76.8 7.9 %collective-permute-start.12 = (bf16[80,128]{1,0:T(8,128)(2,1)S(1)}, bf16[80,128]{1,0:T(8,128)(2,1)S(1)}, u32[]{:S(2)}, u32[]{:S(2)}) collective-permute-start(bf16[80,128]{1,0:T(8,128)(2,1)S(1)} %get-tuple-element.46), channel_id=1, source_target_pairs={{0,128},{64,192},{128,0},{192,64},{1,129},{65,193},{129,1},{193,65... | collective-permute-start | bytes 61448 | tf_op jit(solution)/shard_map/ppermute | solution.py:519
  81.0 5.0 %collective-permute-start.13 = (bf16[80,128]{1,0:T(8,128)(2,1)S(1)}, bf16[80,128]{1,0:T(8,128)(2,1)S(1)}, u32[]{:S(2)}, u32[]{:S(2)}) collective-permute-start(bf16[80,128]{1,0:T(8,128)(2,1)S(1)} %get-tuple-element.47), channel_id=1, source_target_pairs={{0,192},{64,0},{128,64},{192,128},{1,193},{65,1},{129,65},{193,129... | collective-permute-start | bytes 61448 | tf_op jit(solution)/shard_map/ppermute | solution.py:519

commit v7 on v4

--- a/solution.py
+++ b/solution.py
@@ -15,12 +15,14 @@
 GROUP = 16
 OWN = 64
 STEP = 4
-EARLY = 10
+EARLY = 14
 MIB = 1024 * 1024
 
-CHIPS = ((0, 0), (0, 1), (1, 0), (3, 0), (2, 0), (1, 1), (3, 1), (2, 1))
-
-
+ORDER = (
+    (0, 0, 0), (0, 0, 1), (0, 1, 0), (0, 1, 1), (1, 0, 0), (1, 0, 1), (3, 0, 0), (3, 0, 1),
+    (2, 0, 0), (3, 1, 0), (2, 0, 1), (1, 1, 1), (3, 1, 1), (1, 1, 0),
+    (2, 1, 0), (2, 1, 1),
+)
 STRIPS = ("z_hi", "y")
 CHAN = ("x", "z_lo", "core")
 
@@ -101,10 +103,10 @@
 
 
 def block_of(p):
-    dx, dz = CHIPS[p // 2]
+    dx, dz, other = ORDER[p]
     ex = lax.rem(lax.axis_index("x") + dx, 4)
     zed = lax.rem(lax.axis_index("z_lo") + dz, 2)
-    core = lax.rem(lax.axis_index("core") + p % 2, 2)
+    core = lax.rem(lax.axis_index("core") + other, 2)
     return ex * 4 + zed * 2 + core
 
 
@@ -205,50 +207,44 @@
     return own.astype(bf16), partner.astype(bf16)
 
 
-def gather_products(blocks, first, wturned, whitened, partial):
-    grad_w, pooled = None, []
-    weights = wturned[:, first * OWN : first * OWN + sum(block.shape[0] for block in blocks)]
+def stacks(blocks):
     for n in range(8):
-        cols = pl.ds(n * 256, 256)
-        stack = jnp.concatenate([block[:, cols] for block in blocks], axis=0)
-        term = dot(weights, stack)
-        pooled.append(term if partial is None else term + partial[:, cols])
-        term = dot_nt(stack, whitened[:, cols])
-        grad_w = term if grad_w is None else grad_w + term
-    return pooled, grad_w
-
-
-def place_rows(packed, grad_w, first):
-    core = lax.axis_index("core")
+        cols = slice(n * 256, (n + 1) * 256)
+        yield cols, jnp.concatenate([block[:, cols] for block in blocks], axis=0)
+
+
+def whiten_rows(blocks, whitened):
+    return sum(dot_nt(stack, whitened[:, cols]) for cols, stack in stacks(blocks))
+
+
+def place_rows(own, partner, grad_w, first):
     for n in range(grad_w.shape[0] // OWN):
         strip = block_of(first + n)
-        rows = pl.ds(pl.multiple_of((strip // 4) * 32, 32), 32)
-        y = lax.rem(strip, 4)
-        mine, theirs = fold(grad_w[n * OWN : (n + 1) * OWN], OWN // 2)
-        packed[y * 2 + core, rows, :] = mine
-        packed[y * 2 + 1 - core, rows, :] = theirs
+        place = lax.rem(strip, 4) * 4 + strip // 4
+        rows = pl.ds(pl.multiple_of(place * 32, 32), 32)
+        own[rows, :], partner[rows, :] = fold(grad_w[n * OWN : (n + 1) * OWN], OWN // 2)
 
 
 def early_kernel(*refs):
-    blocks, (wturned, whitened, partial, packed) = refs[:6], refs[6:]
-    packed[...] = jnp.zeros_like(packed)
-    pooled, grad_w = gather_products(blocks, 0, wturned, whitened, None)
-    for n in range(8):
-        partial[:, n * 256 : (n + 1) * 256] = pooled[n]
-    place_rows(packed, grad_w, 0)
+    blocks, (wturned, whitened, partial, own, partner) = refs[:7], refs[7:]
+    own[...] = jnp.zeros_like(own)
+    partner[...] = jnp.zeros_like(partner)
+    for cols, stack in stacks(blocks):
+        partial[:, cols] = dot(wturned[:, : EARLY * OWN], stack)
+    place_rows(own, partner, whiten_rows(blocks, whitened), 0)
 
 
 def backward_kernel(*refs):
-    blocks = refs[:4]
+    blocks = refs[:2]
     (
-        partial, early, wturned, whitened, inv_density, masked, patches, inv_square, anch_t,
-        packed, image,
-        rowed, spread_grad, anchor_grad, pool_t,
-    ) = refs[4:]
+        partial, wturned, inv_density, masked, patches, inv_square, anch_t,
+        anchor_grad, image,
+        rowed, spread_grad, pool_t,
+    ) = refs[2:]
     pool_t[...] = column_spread()
-    packed[:, 0:128, :] = early[...]
-    pooled, grad_w = gather_products(blocks, EARLY, wturned, whitened, partial)
-    place_rows(packed, grad_w, EARLY)
+    pooled = [
+        partial[:, cols] + dot(wturned[:, EARLY * OWN :], stack) for cols, stack in stacks(blocks)
+    ]
     scaled = []
     for a in range(ROWS // 2):
         part = pooled[a // 2][:, (a % 2) * HALF : (a % 2 + 1) * HALF]
@@ -290,15 +286,6 @@
         here = pl.ds(pl.multiple_of(t * (STEP * GROUP), STEP * GROUP), (STEP + 4) * GROUP)
         spread_grad[here, :] += jnp.concatenate(sums, axis=0)
 
-    core = lax.axis_index("core")
-    mine, theirs = fold(anchor_grad[...], 40)
-    pad = jnp.zeros((8, 128), bf16)
-    mine = jnp.concatenate([mine, pad], axis=0)
-    theirs = jnp.concatenate([theirs, pad], axis=0)
-    for y in range(4):
-        packed[y * 2 + core, 128:176, :] = mine
-        packed[y * 2 + 1 - core, 128:176, :] = theirs
-
     t = spread_grad[...]
     offset = (lax.broadcasted_iota(jnp.int32, t.shape, 0) % GROUP) % 5
     moved = t
@@ -310,16 +297,37 @@
     image[...] = (dot(folder, high) + dot(folder, low)).astype(bf16)
 
 
-def pack_kernel(received, kept, next_one, next_two, next_three, sums):
-    total = received[0].astype(f32)
-    for source in range(1, 8):
-        total = total + received[source].astype(f32)
-    sums[...] = total[0:128]
-    anchor = total[128:176].astype(bf16)
-    for step, packed in enumerate((kept, next_one, next_two, next_three)):
-        z = lax.rem(lax.axis_index("z_hi") + step, 4)
-        packed[0:32, :] = sums[pl.ds(pl.multiple_of(z * 32, 32), 32), :].astype(bf16)
-        packed[32:80, :] = anchor
+def finish_kernel(first, second, whitened, early_own, early_partner, anchor_grad, own, partner):
+    own[0:512, :] = early_own[...]
+    partner[0:512, :] = early_partner[...]
+    place_rows(own, partner, whiten_rows((first, second), whitened), EARLY)
+    pad = jnp.zeros((8, 128), bf16)
+    mine, theirs = fold(anchor_grad[...], 40)
+    own[512:560, :] = jnp.concatenate([mine, pad], axis=0)
+    partner[512:560, :] = jnp.concatenate([theirs, pad], axis=0)
+
+
+def chip_kernel(own, partner, kept, next_one, next_two, next_three, sums):
+    sums[...] = own[...].astype(f32) + partner[...].astype(f32)
+    for step, part in enumerate((kept, next_one, next_two, next_three)):
+        y = lax.rem(lax.axis_index("y") + step, 4)
+        part[0:128, :] = sums[pl.ds(pl.multiple_of(y * 128, 128), 128), :].astype(bf16)
+        part[128:176, :] = sums[512:560, :].astype(bf16)
+
+
+def add_four(refs):
+    first, *others = refs
+    total = first[...].astype(f32)
+    for ref in others:
+        total = total + ref[...].astype(f32)
+    return total
+
+
+def pack_kernel(kept, one, two, three, packed):
+    total = add_four((kept, one, two, three)).astype(bf16)
+    for z in range(4):
+        packed[z, 0:32, :] = total[z * 32 : (z + 1) * 32]
+        packed[z, 32:80, :] = total[128:176]
 
 
 def image_kernel(parts, middle, rims):
@@ -337,10 +345,10 @@
 
 
 def unpack_kernel(
-    kept, one, two, three, middle, before, after,
+    received, middle, before, after,
     grad_anchors, grad_whiten, grad_image,
 ):
-    total = sum(ref[...].astype(f32) for ref in (one, two, three)) + kept[...].astype(f32)
+    total = add_four([received.at[z] for z in range(4)])
     other = pltpu.roll(total, OWN, 1)
     grad_whiten[0:32, :] = total[0:32, :OWN]
     grad_whiten[32:64, :] = other[0:32, :OWN]
@@ -358,19 +366,16 @@
         grad_image[colour] = image[2 * colour : 2 * colour + 2]
 
 
-def hold(value, *after):
-    def kernel(*refs):
-        del refs
-
-    return pl.pallas_call(
-        kernel,
-        out_shape=jax.ShapeDtypeStruct(value.shape, value.dtype),
-        in_specs=[pl.BlockSpec(memory_space=pl.ANY)] * (1 + len(after)),
-        out_specs=pl.BlockSpec(memory_space=pl.ANY),
-        input_output_aliases={0: 0},
-        compiler_params=pltpu.CompilerParams(vmem_limit_bytes=MIB),
-        cost_estimate=pl.CostEstimate(flops=1000, bytes_accessed=1000, transcendentals=0),
-    )(value, *after)
+def mix_kernel(last, following, beside, right, left, across):
+    right[:OWN], right[OWN:] = last[:OWN], beside[:OWN]
+    left[:OWN], left[OWN:] = following[OWN:], beside[OWN:]
+    across[:OWN], across[OWN:] = last[OWN:], following[:OWN]
+
+
+def cut_kernel(right, left, across, after, onward, over):
+    del across, after
+    onward[...] = right[OWN:]
+    over[...] = left[:OWN]
 
 
 def call(kernel, outs, scratch, flops, limit, *args, loose=0):
@@ -402,17 +407,14 @@
     own = jnp.where(second, right, left).reshape(OWN, -1)
     away = jnp.where(second, left, right).reshape(OWN, -1)
     block = jnp.concatenate([own, send(away, 0, 0, 1)], axis=0)
-    held = {(0, 0): [block]}
-    for dx, dz in ((1, 0), (3, 0), (0, 1)):
-        held[(4 - dx) % 4, dz] = [send(block, dx, dz, 0)]
-    far = [send(held[3, 0][0][:OWN], 1, 0, 0), send(held[1, 0][0][OWN:], 3, 0, 0)]
-    beside = hold(held[0, 1][0], *far)
-    held[2, 0] = far
-    held[3, 1] = [send(beside, 1, 0, 0)]
-    held[1, 1] = [send(beside, 3, 0, 0)]
-    held[2, 1] = [send(half, 0, 1, 0) for half in far]
-    held[0, 1] = [beside]
-    blocks = [part for chip in CHIPS for part in held[chip]]
+    last, following, beside = send(block, 1, 0, 0), send(block, 3, 0, 0), send(block, 0, 1, 0)
+    pair = ((2 * OWN, 16 * HALF), bf16)
+    right, left, across = call(mix_kernel, [pair] * 3, [], 1_000_000, 6, last, following, beside)
+    right, left, across = send(right, 1, 0, 0), send(left, 3, 0, 0), send(across, 0, 1, 0)
+    both = jnp.concatenate(
+        [jnp.pad(whiten, ((0, 0), (0, OWN))), jnp.pad(anchors, ((0, 0), (0, 53)))], axis=0
+    )
+    partner_both = send(both, 0, 0, 1)
 
     stacked = jnp.concatenate([image, mask.astype(bf16)[None]], axis=0)
     (tile,) = call(
@@ -421,11 +423,8 @@
         [],
         1_000_000,
         4,
-        stacked, held[3, 0][0],
+        stacked, partner_both,
         loose=1,
-    )
-    both = jnp.concatenate(
-        [jnp.pad(whiten, ((0, 0), (0, OWN))), jnp.pad(anchors, ((0, 0), (0, 53)))], axis=0
     )
     plane = ((ROWS, LANES), f32)
     patches, tissue, scale, norm, inv_square, inv_density, anch, anch_t, wturned = call(
@@ -442,49 +441,70 @@
             ((128, 1024), bf16),
         ],
         [],
-        1_000_000_000,
+        10_000_000_000,
         12,
-        stacked, cross(tile), both, send(both, 0, 0, 1),
+        stacked, cross(tile), both, partner_both,
     )
     masked, whitened = call(
         forward_kernel,
         [((ROWS, 128, LANES), bf16), ((128, 16 * HALF), bf16)],
         [((ROWS, 128, HALF), f32), ((LANES, HALF), bf16)],
-        3_000_000_000,
+        30_000_000_000,
         14,
         patches, tissue, scale, norm, inv_density, anch,
     )
-    partial, early = call(
+    onward, over = call(
+        cut_kernel, [((OWN, 16 * HALF), bf16)] * 2, [], 1_000_000, 6, right, left, across, whitened, loose=2
+    )
+    first_blocks = (block, beside, following, last, right, left, across)
+    last_blocks = (send(onward, 1, 0, 0), send(over, 0, 1, 0))
+    rows = ((512, 128), bf16)
+    partial, early_own, early_partner = call(
         early_kernel,
-        [((128, 16 * HALF), f32), ((8, 128, 128), bf16)],
+        [((128, 16 * HALF), f32), rows, rows],
         [],
         2_000_000_000,
         14,
-        *blocks[:6], wturned, whitened,
-    )
-    packed, image_part = call(
+        *first_blocks, wturned, whitened,
+    )
+    anchor_grad, image_part = call(
         backward_kernel,
-        [((8, 176, 128), bf16), ((128, LANES), bf16)],
-        [
-            ((ROWS * 128, HALF), bf16),
-            ((36 * GROUP, LANES), f32),
-            ((80, 128), f32),
-            ((HALF, LANES), bf16),
-        ],
+        [((80, 128), f32), ((128, LANES), bf16)],
+        [((ROWS * 128, HALF), bf16), ((36 * GROUP, LANES), f32), ((HALF, LANES), bf16)],
         5_000_000_000,
         20,
-        *blocks[6:],
-        partial, early, wturned, whitened, inv_density, masked, patches, inv_square, anch_t,
-    )
-
-    received = lax.all_to_all(packed, ("y", "core"), 0, 0)
+        *last_blocks, partial, wturned, inv_density, masked, patches, inv_square, anch_t,
+    )
+
     parts = lax.all_to_all(image_part.reshape(16, 8, LANES), CHAN, 0, 0)
-    quarter = ((80, 128), bf16)
-    kept, *away = call(pack_kernel, [quarter] * 4, [((128, 128), f32)], 1_000_000, 4, received)
-    others = [
-        lax.ppermute(value, "z_hi", [(z, (z + step) % 4) for z in range(4)])
-        for step, value in enumerate(away, 1)
-    ]
+    rows = ((560, 128), bf16)
+    mine, theirs = call(
+        finish_kernel,
+        [rows, rows],
+        [],
+        1_000_000_000,
+        12,
+        *last_blocks, whitened, early_own, early_partner, anchor_grad,
+    )
+
+    def exchange(values, axis):
+        return [
+            lax.ppermute(value, axis, [(i, (i + step) % 4) for i in range(4)])
+            for step, value in enumerate(values, 1)
+        ]
+
+    kept, *away = call(
+        chip_kernel,
+        [((176, 128), bf16)] * 4,
+        [((560, 128), f32)],
+        1_000_000,
+        6,
+        mine, send(theirs, 0, 0, 1),
+    )
+    (packed,) = call(
+        pack_kernel, [((4, 80, 128), bf16)], [], 1_000_000, 4, kept, *exchange(away, "y")
+    )
+    received = lax.all_to_all(packed, "z_hi", 0, 0)
     middle, rims = call(image_kernel, [((8, 512), f32), ((8, 128), f32)], [], 1_000_000, 4, parts)
     before = lax.ppermute(rims, STRIPS, [(i, i + 1) for i in range(15)])
     after = lax.ppermute(rims, STRIPS, [(i + 1, i) for i in range(15)])
@@ -495,7 +515,7 @@
             [],
             1_000_000,
             4,
-            kept, *others, middle, before, after,
+            received, middle, before, after,
         )
     )
 

time: 93.4 us -> 96.4 us (1.032)
  the two profiles are of different devices: /device:TPU:24 before, /device:TPU:162 now
where the time goes in v7:
time: 96.4 us; the launch traced here: 95.9 us
  starting transfers between devices  41.4 us (43%)
  waiting for transfers between devices  32 us (33%)
  Pallas kernels  17.8 us (18%)
  other arithmetic  2.71 us (3%)
  local copies, waits for them, and re-layouts  1.25 us (1%)
    ppermute x11, waiting for transfers between devices, send(): return lax.ppermute(value, CHAN, route(dx, dz, other))  19.2 us
    pallas_call x12, Pallas kernels, call(): pl.pallas_call(kernel, out_shape=[jax.ShapeDtypeStruct(shape, dtype) for...  17.8 us
    ppermute x11, starting transfers between devices, send(): return lax.ppermute(value, CHAN, route(dx, dz, other))  8.12 us
    ppermute x1, waiting for transfers between devices, shards(): before = lax.ppermute(rims, STRIPS, [(i, i + 1) for i in range(15)])  7.82 us
    all_to_all x1, starting transfers between devices, shards(): parts = lax.all_to_all(image_part.reshape(16, 8, LANES), CHAN, 0, 0)  7.55 us
    all_to_all x1, starting transfers between devices, shards(): received = lax.all_to_all(packed, 'z_hi', 0, 0)  7.2 us
    ppermute x3, starting transfers between devices, exchange(): lax.ppermute(value, axis, [(i, (i + step) % 4) for i in range(4)])  7.04 us
    ppermute x1, starting transfers between devices, shards(): after = lax.ppermute(rims, STRIPS, [(i + 1, i) for i in range(15)])  5.01 us
  transfers between devices with their start and end apart: 19, of which 10 were waited for; matrix products, arithmetic and copies ran while one was open for 2% of the time, Pallas kernels for 9%

profile of v7, /device:TPU:162, one launch (start us, length us, event | category | flops | bytes accessed | tf_op | source)
XLA Modules:
  0.0 95.9 jit_solution(212919705582080728)
XLA Ops:
  0.6 1.1 %copy.8 = bf16[1024,64]{1,0:T(8,128)(2,1)S(1)} copy(bf16[1024,64]{0,1:T(8,128)(2,1)} %param.8) | data formatting | bytes 262144 | tf_op args[3]
  1.8 0.8 fusion.2.own_both
  2.6 1.1 %broadcast_select_fusion = (bf16[64,16,128]{2,1,0:T(8,128)(2,1)S(1)}, bf16[64,16,128]{2,1,0:T(8,128)(2,1)S(1)}) fusion(pred[]{:T(512)S(6)} %eq.3, bf16[64,16,256]{2,1,0:T(8,128)(2,1)} %param.9), kind=kLoop, calls=%fused_computation.7 | loop fusion | flops 262144 | bytes 1048577 | tf_op jit(solution)/shard_map/jit(_where)/select_n | solution.py:408
  3.8 0.6 collective-permute-start
  4.4 0.8 convert_bitcast_fusion
  5.3 4.5 %collective-permute-start.8 = (bf16[4,32,128]{2,1,0:T(8,128)(2,1)S(1)}, bf16[4,32,128]{2,1,0:T(8,128)(2,1)S(1)}, u32[]{:S(2)}, u32[]{:S(2)}) collective-permute-start(bf16[4,32,128]{2,1,0:T(8,128)(2,1)S(1)} %shard_map.77), channel_id=1, source_target_pairs={{16,1},{18,3},{20,5},{22,7},{24,9},{26,11},{28,13},{30,15},{32,17}... | collective-permute-start | bytes 98312 | tf_op jit(solution)/shard_map/ppermute | solution.py:404
  10.6 1.5 %collective-permute-start.1 = (bf16[128,2048]{1,0:T(8,128)(2,1)S(1)}, bf16[128,2048]{1,0:T(8,128)(2,1)S(1)}, u32[]{:S(2)}, u32[]{:S(2)}) collective-permute-start(bf16[128,2048]{1,0:T(8,128)(2,1)S(1)} %constant_dynamic-update-slice_fusion.refs_0_), channel_id=1, source_target_pairs={{0,4},{1,5},{2,6},{3,7},{4,8},{5,9},{6,10},{7,11},{8,12},{9,13},{1... | collective-permute-start | bytes 1572872 | tf_op jit(solution)/shard_map/ppermute | solution.py:401
  12.1 2.8 %collective-permute-done.8.beyond = bf16[4,32,128]{2,1,0:T(8,128)(2,1)S(1)} collective-permute-done((bf16[4,32,128]{2,1,0:T(8,128)(2,1)S(1)}, bf16[4,32,128]{2,1,0:T(8,128)(2,1)S(1)}, u32[]{:S(2)}, u32[]{:S(2)}) %collective-permute-start.8) | collective-permute-done | bytes 32800 | tf_op jit(solution)/shard_map/ppermute | solution.py:404
  14.9 1.8 %shard_map.78 = (bf16[576,384]{1,0:T(8,128)(2,1)S(1)}, f32[32,384]{1,0:T(8,128)S(1)}, f32[32,384]{1,0:T(8,128)S(1)}, f32[32,384]{1,0:T(8,128)S(1)}, f32[32,384]{...) custom-call(bf16[4,32,512]{2,1,0:T(8,128)(2,1)S(1)} %pad_maximum_fus, ...), custom_call_target="tpu_custom_call" | custom-call | flops 10000000000 | bytes 1671168 | tf_op jit(solution)/shard_map/pallas_call | solution.py:385
  16.7 6.2 %collective-permute-done.3.beside.refs_1_ = bf16[128,2048]{1,0:T(8,128)(2,1)S(1)} collective-permute-done((bf16[128,2048]{1,0:T(8,128)(2,1)S(1)}, bf16[128,2048]{1,0:T(8,128)(2,1)S(1)}, u32[]{:S(2)}, u32[]{:S(2)}) %collective-permute-start.3) | collective-permute-done | bytes 524320 | tf_op jit(solution)/shard_map/ppermute | solution.py:401
  22.9 0.7 collective-permute-done.2.following.refs_2_
  23.6 1.3 %collective-permute-done.1.last.refs_3_ = bf16[128,2048]{1,0:T(8,128)(2,1)S(1)} collective-permute-done((bf16[128,2048]{1,0:T(8,128)(2,1)S(1)}, bf16[128,2048]{1,0:T(8,128)(2,1)S(1)}, u32[]{:S(2)}, u32[]{:S(2)}) %collective-permute-start.1) | collective-permute-done | bytes 524320 | tf_op jit(solution)/shard_map/ppermute | solution.py:401
  25.6 2.6 %collective-permute-start.5 = (bf16[128,2048]{1,0:T(8,128)(2,1)S(1)}, bf16[128,2048]{1,0:T(8,128)(2,1)S(1)}, u32[]{:S(2)}, u32[]{:S(2)}) collective-permute-start(bf16[128,2048]{1,0:T(8,128)(2,1)S(1)} %get-tuple-element.33), channel_id=1, source_target_pairs={{0,12},{1,13},{2,14},{3,15},{4,0},{5,1},{6,2},{7,3},{8,4},{9,5},{1... | collective-permute-start | bytes 1572872 | tf_op jit(solution)/shard_map/ppermute | solution.py:401
  28.1 1.0 %collective-permute-start.6 = (bf16[128,2048]{1,0:T(8,128)(2,1)S(1)}, bf16[128,2048]{1,0:T(8,128)(2,1)S(1)}, u32[]{:S(2)}, u32[]{:S(2)}) collective-permute-start(bf16[128,2048]{1,0:T(8,128)(2,1)S(1)} %get-tuple-element.34), channel_id=1, source_target_pairs={{0,2},{1,3},{2,0},{3,1},{4,6},{5,7},{6,4},{7,5},{8,10},{9,11},{10,... | collective-permute-start | bytes 1572872 | tf_op jit(solution)/shard_map/ppermute | solution.py:401
  29.1 4.5 %shard_map.79 = (bf16[32,128,384]{2,1,0:T(8,128)(2,1)S(1)}, bf16[128,2048]{1,0:T(8,128)(2,1)S(1)}) custom-call(bf16[576,384]{1,0:T(8,128)(2,1)S(1)} %get-tuple-element.35.patches.refs_6_, f32[32,384]{1,0:T(8,128)S(1)} %get-tuple-element.36.tissue, f32[32,384]{1,0:T(8,128)S(1)} %get-tuple-element.37.scale, f32[32,384]{1,0:T(8,128)S(1)} %get-tuple-element.38.norm, ...), custom_call_target="tpu_custom_call" | custom-call | flops 30000001024 | bytes 4288512 | tf_op jit(solution)/shard_map/pallas_call | solution.py:385
  33.6 5.0 %collective-permute-done.4.right.refs_4_ = bf16[128,2048]{1,0:T(8,128)(2,1)S(1)} collective-permute-done((bf16[128,2048]{1,0:T(8,128)(2,1)S(1)}, bf16[128,2048]{1,0:T(8,128)(2,1)S(1)}, u32[]{:S(2)}, u32[]{:S(2)}) %collective-permute-start.4) | collective-permute-done | bytes 524320 | tf_op jit(solution)/shard_map/ppermute | solution.py:401
  38.6 1.5 %collective-permute-done.6.across.refs_6_ = bf16[128,2048]{1,0:T(8,128)(2,1)S(1)} collective-permute-done((bf16[128,2048]{1,0:T(8,128)(2,1)S(1)}, bf16[128,2048]{1,0:T(8,128)(2,1)S(1)}, u32[]{:S(2)}, u32[]{:S(2)}) %collective-permute-start.6) | collective-permute-done | bytes 524320 | tf_op jit(solution)/shard_map/ppermute | solution.py:401
  40.2 0.9 collective-permute-start.9
  41.2 1.8 %shard_map.81 = (f32[128,2048]{1,0:T(8,128)S(1)}, bf16[512,128]{1,0:T(8,128)(2,1)S(1)}, bf16[512,128]{1,0:T(8,128)(2,1)S(1)}) custom-call(bf16[128,2048]{1,0:T(8,128)(2,1)S(1)} %constant_dynamic-update-slice_fusion.refs_0_, bf16[128,2048]{1,0:T(8,128)(2,1)S(1)} %collective-permute-done.3.beside.refs_1_, ...), custom_call_target="tpu_custom_call" | custom-call | flops 2000000000 | bytes 5767168 | tf_op jit(solution)/shard_map/pallas_call | solution.py:385
  43.0 4.5 %collective-permute-done.9.refs_0_.first = bf16[64,2048]{1,0:T(8,128)(2,1)S(1)} collective-permute-done((bf16[64,2048]{1,0:T(8,128)(2,1)S(1)}, bf16[64,2048]{1,0:T(8,128)(2,1)S(1)}, u32[]{:S(2)}, u32[]{:S(2)}) %collective-permute-start.9) | collective-permute-done | bytes 262176 | tf_op jit(solution)/shard_map/ppermute | solution.py:401
  47.5 7.5 %shard_map.82 = (f32[80,128]{1,0:T(8,128)S(1)}, bf16[128,384]{1,0:T(8,128)(2,1)}) custom-call(bf16[64,2048]{1,0:T(8,128)(2,1)S(1)} %collective-permute-done.9.refs_0_.first, bf16[64,2048]{1,0:T(8,128)(2,1)S(1)} %collective-permute-done.10.refs_1_.second, f32[128,2048]{1,0:T(8,128)S(1)} %get-tuple-element.47.refs_2_, ...), custom_call_target="tpu_custom_call" | custom-call | flops 5000000000 | bytes 5640192 | tf_op jit(solution)/shard_map/pallas_call | solution.py:385
  55.4 7.5 %all-to-all-start.1 = ((bf16[16,8,384]{2,1,0:T(8,128)(2,1)}), bf16[16,8,384]{2,1,0:T(8,128)(2,1)S(1)}, u32[]{:S(2)}, u32[]{:S(2)}) async-start(bf16[16,8,384]{2,1,0:T(8,128)(2,1)} %bitcast.1), calls=%async_computation.1 | async-start | bytes 196608 | tf_op jit(solution)/shard_map/all_to_all | solution.py:479
  63.1 3.4 %collective-permute-start.12 = (bf16[176,128]{1,0:T(8,128)(2,1)S(1)}, bf16[176,128]{1,0:T(8,128)(2,1)S(1)}, u32[]{:S(2)}, u32[]{:S(2)}) collective-permute-start(bf16[176,128]{1,0:T(8,128)(2,1)S(1)} %get-tuple-element.55), channel_id=1, source_target_pairs={{0,16},{16,32},{32,48},{48,0},{1,17},{17,33},{33,49},{49,1},{2,18}... | collective-permute-start | bytes 135176 | tf_op jit(solution)/shard_map/ppermute | solution.py:492
  66.4 1.8 %collective-permute-start.13 = (bf16[176,128]{1,0:T(8,128)(2,1)S(1)}, bf16[176,128]{1,0:T(8,128)(2,1)S(1)}, u32[]{:S(2)}, u32[]{:S(2)}) collective-permute-start(bf16[176,128]{1,0:T(8,128)(2,1)S(1)} %get-tuple-element.56), channel_id=1, source_target_pairs={{0,32},{16,48},{32,0},{48,16},{1,33},{17,49},{33,1},{49,17},{2,34}... | collective-permute-start | bytes 135176 | tf_op jit(solution)/shard_map/ppermute | solution.py:492
  68.2 1.9 %collective-permute-start.14 = (bf16[176,128]{1,0:T(8,128)(2,1)S(1)}, bf16[176,128]{1,0:T(8,128)(2,1)S(1)}, u32[]{:S(2)}, u32[]{:S(2)}) collective-permute-start(bf16[176,128]{1,0:T(8,128)(2,1)S(1)} %get-tuple-element.57), channel_id=1, source_target_pairs={{0,48},{16,0},{32,16},{48,32},{1,49},{17,1},{33,17},{49,33},{2,50}... | collective-permute-start | bytes 135176 | tf_op jit(solution)/shard_map/ppermute | solution.py:492
  70.1 1.9 %collective-permute-done.13.two = bf16[176,128]{1,0:T(8,128)(2,1)S(1)} collective-permute-done((bf16[176,128]{1,0:T(8,128)(2,1)S(1)}, bf16[176,128]{1,0:T(8,128)(2,1)S(1)}, u32[]{:S(2)}, u32[]{:S(2)}) %collective-permute-start.13) | collective-permute-done | bytes 45088 | tf_op jit(solution)/shard_map/ppermute | solution.py:492
  72.3 0.7 shard_map.85
  72.9 7.2 %all-to-all-start = ((bf16[4,80,128]{2,1,0:T(8,128)(2,1)}), bf16[4,80,128]{2,1,0:T(8,128)(2,1)S(1)}, u32[]{:S(2)}, u32[]{:S(2)}) async-start(bf16[4,80,128]{2,1,0:T(8,128)(2,1)} %shard_map.85), calls=%async_computation | async-start | bytes 163840 | tf_op jit(solution)/shard_map/all_to_all | solution.py:507
  80.2 5.0 %collective-permute-start.16 = (f32[8,128]{1,0:T(8,128)S(1)}, f32[8,128]{1,0:T(8,128)S(1)}, u32[]{:S(2)}, u32[]{:S(2)}) collective-permute-start(f32[8,128]{1,0:T(8,128)S(1)} %get-tuple-element.60), channel_id=1, source_target_pairs={{16,0},{32,16},{48,32},{64,48},{80,64},{96,80},{112,96},{128,112},... | collective-permute-start | bytes 12296 | tf_op jit(solution)/shard_map/ppermute | solution.py:510
  85.2 1.9 %collective-permute-start.15 = (f32[8,128]{1,0:T(8,128)S(1)}, f32[8,128]{1,0:T(8,128)S(1)}, u32[]{:S(2)}, u32[]{:S(2)}) collective-permute-start(f32[8,128]{1,0:T(8,128)S(1)} %get-tuple-element.60), channel_id=1, source_target_pairs={{0,16},{16,32},{32,48},{48,64},{64,80},{80,96},{96,112},{112,128},... | collective-permute-start | bytes 12296 | tf_op jit(solution)/shard_map/ppermute | solution.py:509
  87.2 7.8 %collective-permute-done.15.before = f32[8,128]{1,0:T(8,128)S(1)} collective-permute-done((f32[8,128]{1,0:T(8,128)S(1)}, f32[8,128]{1,0:T(8,128)S(1)}, u32[]{:S(2)}, u32[]{:S(2)}) %collective-permute-start.15) | collective-permute-done | bytes 4128 | tf_op jit(solution)/shard_map/ppermute | solution.py:509
  95.0 0.9 shard_map.87
  (28 shorter events, 2.7 us)
Async XLA Ops:
  0.6 4.6 %copy-start = (bf16[3,32,512]{2,1,0:T(8,128)(2,1)S(1)}, bf16[3,32,512]{2,1,0:T(8,128)(2,1)}, u32[]{:S(2)}) copy-start(bf16[3,32,512]{2,1,0:T(8,128)(2,1)} %param.5) | copy-start | bytes 294916
  2.5 2.8 %collective-permute-start.7 = (bf16[1088,128]{1,0:T(8,128)(2,1)S(1)}, bf16[1088,128]{1,0:T(8,128)(2,1)S(1)}, u32[]{:S(2)}, u32[]{:S(2)}) collective-permute-start(bf16[1088,128]{1,0:T(8,128)(2,1)S(1)} %fusion.2.own_both), channel_id=1, source_target_pairs={{0,1},{1,0},{2,3},{3,2},{4,5},{5,4},{6,7},{7,6},{8,9},{9,8},{10,11... | collective-permute-start | bytes 835592 | tf_op jit(solution)/shard_map/ppermute | solution.py:401
  3.8 6.1 %collective-permute-start = (bf16[64,2048]{1,0:T(8,128)(2,1)S(1)}, bf16[64,2048]{1,0:T(8,128)(2,1)S(1)}, u32[]{:S(2)}, u32[]{:S(2)}) collective-permute-start(bf16[64,2048]{1,0:T(8,128)(2,1)S(1)} %bitcast.12), channel_id=1, source_target_pairs={{0,1},{1,0},{2,3},{3,2},{4,5},{5,4},{6,7},{7,6},{8,9},{9,8},{10,11... | collective-permute-start | bytes 786440 | tf_op jit(solution)/shard_map/ppermute | solution.py:401
  5.3 9.6 %collective-permute-start.8 = (bf16[4,32,128]{2,1,0:T(8,128)(2,1)S(1)}, bf16[4,32,128]{2,1,0:T(8,128)(2,1)S(1)}, u32[]{:S(2)}, u32[]{:S(2)}) collective-permute-start(bf16[4,32,128]{2,1,0:T(8,128)(2,1)S(1)} %shard_map.77), channel_id=1, source_target_pairs={{16,1},{18,3},{20,5},{22,7},{24,9},{26,11},{28,13},{30,15},{32,17}... | collective-permute-start | bytes 98312 | tf_op jit(solution)/shard_map/ppermute | solution.py:404
  9.9 13.0 %collective-permute-start.3 = (bf16[128,2048]{1,0:T(8,128)(2,1)S(1)}, bf16[128,2048]{1,0:T(8,128)(2,1)S(1)}, u32[]{:S(2)}, u32[]{:S(2)}) collective-permute-start(bf16[128,2048]{1,0:T(8,128)(2,1)S(1)} %constant_dynamic-update-slice_fusion.refs_0_), channel_id=1, source_target_pairs={{0,2},{1,3},{2,0},{3,1},{4,6},{5,7},{6,4},{7,5},{8,10},{9,11},{10,... | collective-permute-start | bytes 1572872 | tf_op jit(solution)/shard_map/ppermute | solution.py:401
  10.1 13.5 %collective-permute-start.2 = (bf16[128,2048]{1,0:T(8,128)(2,1)S(1)}, bf16[128,2048]{1,0:T(8,128)(2,1)S(1)}, u32[]{:S(2)}, u32[]{:S(2)}) collective-permute-start(bf16[128,2048]{1,0:T(8,128)(2,1)S(1)} %constant_dynamic-update-slice_fusion.refs_0_), channel_id=1, source_target_pairs={{0,12},{1,13},{2,14},{3,15},{4,0},{5,1},{6,2},{7,3},{8,4},{9,5},{1... | collective-permute-start | bytes 1572872 | tf_op jit(solution)/shard_map/ppermute | solution.py:401
  10.6 14.2 %collective-permute-start.1 = (bf16[128,2048]{1,0:T(8,128)(2,1)S(1)}, bf16[128,2048]{1,0:T(8,128)(2,1)S(1)}, u32[]{:S(2)}, u32[]{:S(2)}) collective-permute-start(bf16[128,2048]{1,0:T(8,128)(2,1)S(1)} %constant_dynamic-update-slice_fusion.refs_0_), channel_id=1, source_target_pairs={{0,4},{1,5},{2,6},{3,7},{4,8},{5,9},{6,10},{7,11},{8,12},{9,13},{1... | collective-permute-start | bytes 1572872 | tf_op jit(solution)/shard_map/ppermute | solution.py:401
  25.0 13.6 %collective-permute-start.4 = (bf16[128,2048]{1,0:T(8,128)(2,1)S(1)}, bf16[128,2048]{1,0:T(8,128)(2,1)S(1)}, u32[]{:S(2)}, u32[]{:S(2)}) collective-permute-start(bf16[128,2048]{1,0:T(8,128)(2,1)S(1)} %get-tuple-element.32), channel_id=1, source_target_pairs={{0,4},{1,5},{2,6},{3,7},{4,8},{5,9},{6,10},{7,11},{8,12},{9,13},{1... | collective-permute-start | bytes 1572872 | tf_op jit(solution)/shard_map/ppermute | solution.py:401
  25.6 13.1 %collective-permute-start.5 = (bf16[128,2048]{1,0:T(8,128)(2,1)S(1)}, bf16[128,2048]{1,0:T(8,128)(2,1)S(1)}, u32[]{:S(2)}, u32[]{:S(2)}) collective-permute-start(bf16[128,2048]{1,0:T(8,128)(2,1)S(1)} %get-tuple-element.33), channel_id=1, source_target_pairs={{0,12},{1,13},{2,14},{3,15},{4,0},{5,1},{6,2},{7,3},{8,4},{9,5},{1... | collective-permute-start | bytes 1572872 | tf_op jit(solution)/shard_map/ppermute | solution.py:401
  28.1 12.0 %collective-permute-start.6 = (bf16[128,2048]{1,0:T(8,128)(2,1)S(1)}, bf16[128,2048]{1,0:T(8,128)(2,1)S(1)}, u32[]{:S(2)}, u32[]{:S(2)}) collective-permute-start(bf16[128,2048]{1,0:T(8,128)(2,1)S(1)} %get-tuple-element.34), channel_id=1, source_target_pairs={{0,2},{1,3},{2,0},{3,1},{4,6},{5,7},{6,4},{7,5},{8,10},{9,11},{10,... | collective-permute-start | bytes 1572872 | tf_op jit(solution)/shard_map/ppermute | solution.py:401
  40.2 7.3 %collective-permute-start.9 = (bf16[64,2048]{1,0:T(8,128)(2,1)S(1)}, bf16[64,2048]{1,0:T(8,128)(2,1)S(1)}, u32[]{:S(2)}, u32[]{:S(2)}) collective-permute-start(bf16[64,2048]{1,0:T(8,128)(2,1)S(1)} %get-tuple-element.42), channel_id=1, source_target_pairs={{0,4},{1,5},{2,6},{3,7},{4,8},{5,9},{6,10},{7,11},{8,12},{9,13},{1... | collective-permute-start | bytes 786440 | tf_op jit(solution)/shard_map/ppermute | solution.py:401
  41.1 6.4 %collective-permute-start.10 = (bf16[64,2048]{1,0:T(8,128)(2,1)S(1)}, bf16[64,2048]{1,0:T(8,128)(2,1)S(1)}, u32[]{:S(2)}, u32[]{:S(2)}) collective-permute-start(bf16[64,2048]{1,0:T(8,128)(2,1)S(1)} %get-tuple-element.43), channel_id=1, source_target_pairs={{0,2},{1,3},{2,0},{3,1},{4,6},{5,7},{6,4},{7,5},{8,10},{9,11},{10,... | collective-permute-start | bytes 786440 | tf_op jit(solution)/shard_map/ppermute | solution.py:401
  55.3 7.7 %collective-permute-start.11 = (bf16[560,128]{1,0:T(8,128)(2,1)S(1)}, bf16[560,128]{1,0:T(8,128)(2,1)S(1)}, u32[]{:S(2)}, u32[]{:S(2)}) collective-permute-start(bf16[560,128]{1,0:T(8,128)(2,1)S(1)} %get-tuple-element.53), channel_id=1, source_target_pairs={{0,1},{1,0},{2,3},{3,2},{4,5},{5,4},{6,7},{7,6},{8,9},{9,8},{10,11... | collective-permute-start | bytes 430088 | tf_op jit(solution)/shard_map/ppermute | solution.py:401
  55.4 17.5 %all-to-all-start.1 = ((bf16[16,8,384]{2,1,0:T(8,128)(2,1)}), bf16[16,8,384]{2,1,0:T(8,128)(2,1)S(1)}, u32[]{:S(2)}, u32[]{:S(2)}) async-start(bf16[16,8,384]{2,1,0:T(8,128)(2,1)} %bitcast.1), calls=%async_computation.1 | async-start | bytes 196608 | tf_op jit(solution)/shard_map/all_to_all | solution.py:479
  63.1 7.0 %collective-permute-start.12 = (bf16[176,128]{1,0:T(8,128)(2,1)S(1)}, bf16[176,128]{1,0:T(8,128)(2,1)S(1)}, u32[]{:S(2)}, u32[]{:S(2)}) collective-permute-start(bf16[176,128]{1,0:T(8,128)(2,1)S(1)} %get-tuple-element.55), channel_id=1, source_target_pairs={{0,16},{16,32},{32,48},{48,0},{1,17},{17,33},{33,49},{49,1},{2,18}... | collective-permute-start | bytes 135176 | tf_op jit(solution)/shard_map/ppermute | solution.py:492
  66.4 5.6 %collective-permute-start.13 = (bf16[176,128]{1,0:T(8,128)(2,1)S(1)}, bf16[176,128]{1,0:T(8,128)(2,1)S(1)}, u32[]{:S(2)}, u32[]{:S(2)}) collective-permute-start(bf16[176,128]{1,0:T(8,128)(2,1)S(1)} %get-tuple-element.56), channel_id=1, source_target_pairs={{0,32},{16,48},{32,0},{48,16},{1,33},{17,49},{33,1},{49,17},{2,34}... | collective-permute-start | bytes 135176 | tf_op jit(solution)/shard_map/ppermute | solution.py:492
  68.2 4.0 %collective-permute-start.14 = (bf16[176,128]{1,0:T(8,128)(2,1)S(1)}, bf16[176,128]{1,0:T(8,128)(2,1)S(1)}, u32[]{:S(2)}, u32[]{:S(2)}) collective-permute-start(bf16[176,128]{1,0:T(8,128)(2,1)S(1)} %get-tuple-element.57), channel_id=1, source_target_pairs={{0,48},{16,0},{32,16},{48,32},{1,49},{17,1},{33,17},{49,33},{2,50}... | collective-permute-start | bytes 135176 | tf_op jit(solution)/shard_map/ppermute | solution.py:492
  72.9 22.1 %all-to-all-start = ((bf16[4,80,128]{2,1,0:T(8,128)(2,1)}), bf16[4,80,128]{2,1,0:T(8,128)(2,1)S(1)}, u32[]{:S(2)}, u32[]{:S(2)}) async-start(bf16[4,80,128]{2,1,0:T(8,128)(2,1)} %shard_map.85), calls=%async_computation | async-start | bytes 163840 | tf_op jit(solution)/shard_map/all_to_all | solution.py:507
  80.2 7.0 %collective-permute-start.16 = (f32[8,128]{1,0:T(8,128)S(1)}, f32[8,128]{1,0:T(8,128)S(1)}, u32[]{:S(2)}, u32[]{:S(2)}) collective-permute-start(f32[8,128]{1,0:T(8,128)S(1)} %get-tuple-element.60), channel_id=1, source_target_pairs={{16,0},{32,16},{48,32},{64,48},{80,64},{96,80},{112,96},{128,112},... | collective-permute-start | bytes 12296 | tf_op jit(solution)/shard_map/ppermute | solution.py:510
  85.2 9.8 %collective-permute-start.15 = (f32[8,128]{1,0:T(8,128)S(1)}, f32[8,128]{1,0:T(8,128)S(1)}, u32[]{:S(2)}, u32[]{:S(2)}) collective-permute-start(f32[8,128]{1,0:T(8,128)S(1)} %get-tuple-element.60), channel_id=1, source_target_pairs={{0,16},{16,32},{32,48},{48,64},{64,80},{80,96},{96,112},{112,128},... | collective-permute-start | bytes 12296 | tf_op jit(solution)/shard_map/ppermute | solution.py:509

commit v8 on v7

v8 whole, which is shorter than its diff:
```python
import math

import jax
import jax.numpy as jnp
from jax import lax
from jax.experimental import pallas as pl
from jax.experimental.pallas import tpu as pltpu
from jax.sharding import Mesh
from jax.sharding import PartitionSpec as P

EPS = 1e-05
LANES = 256
REACH = 135
QUARTER = 64
FLAT = 16 * QUARTER
ROWS = 32
GROUP = 16
OWN = 64
KEPT = 4 * OWN
STEP = 4
EARLY = 12
MIB = 1024 * 1024

STRIPS = ("z_hi", "y")
CHAN = ("x", "z_lo", "core")


def route(dx, other):
    return [(i, (i // 4 + dx) % 4 * 4 + (i % 4 ^ other)) for i in range(16)]


def seams():
    pairs = [(16 * s + 4 * x, 16 * s - 16 + 4 * x + 3) for s in range(1, 16) for x in range(4)]
    return pairs + [(b, a) for a, b in pairs]


f32 = jnp.float32
bf16 = jnp.bfloat16


def tap(distance):
    return math.exp(-distance * distance / 8.0) if abs(distance) <= 4 else 0.0


def taps(distance):
    far = jnp.abs(distance) > 4
    distance = distance.astype(f32)
    return jnp.where(far, 0.0, jnp.exp(distance * distance * (-1.0 / 8.0)))


def places(shape):
    return tuple(lax.broadcasted_iota(jnp.int32, shape, dim) for dim in (0, 1))


def column_pool():
    lane, target = places((LANES, 128))
    return taps(2 * (target & 63) - lane + 4).astype(bf16)


def column_spread():
    target, lane = places((128, LANES))
    return taps(2 * (target & 63) - lane + 4).astype(bf16)


def row_weights(t, i):
    low, high = tap(4 * t - i), tap(4 * t + 2 - i)
    if low == 0.0 and high == 0.0:
        return None
    return jnp.where(lax.broadcasted_iota(jnp.int32, (1, 128), 1) < QUARTER, low, high)


def row_pool(odd):
    t, i = places((8, ROWS))
    return taps(4 * t + 2 * odd - i)


def split_group(row):
    q = row & (GROUP - 1)
    colour = jnp.where(q < 5, 0, jnp.where(q < 10, 1, jnp.where(q < 15, 2, 3)))
    return row >> 4, colour, q - 5 * colour


def ones(hit, dtype=bf16):
    return jnp.where(hit, 1.0, 0.0).astype(dtype)


def replicate_rows():
    out, src = places((36 * GROUP, 3 * ROWS))
    r, colour, _ = split_group(out)
    return ones(((src & 31) == r - 2) & ((src >> 5) == colour))


def fold_rows():
    out, src = places((128, 36 * GROUP))
    r, colour, _ = split_group(src)
    i = 2 * (out >> 3) + (out & 1)
    return ones((r == i + 2) & (colour == ((out & 7) >> 1)) & (colour < 3))


def entry_order(dtype, rows=75):
    entry, out = places((rows, 80))
    a, colour, b = split_group(out)
    return ones((entry == 25 * colour + 5 * a + b) & (colour < 3), dtype)


def quarter():
    return lax.axis_index("z_lo") * 2 + lax.axis_index("core")


def flipped(axis, bit):
    return lax.rem(lax.axis_index(axis) + bit, 2)


def block_of(p):
    dx, other = (0, 1, 3, 2)[p // 4], p % 4
    ex = lax.rem(lax.axis_index("x") + dx, 4)
    return ex * 4 + flipped("z_lo", other // 2) * 2 + flipped("core", other % 2)


def dot(a, b):
    return jnp.dot(a, b, preferred_element_type=f32)


def dot_nt(a, b):
    return lax.dot_general(a, b, (((1,), (1,)), ((), ())), preferred_element_type=f32)


def quarter_kernel(cotangent, own, core, zed, both, parts):
    lane = lax.broadcasted_iota(jnp.int32, (OWN, 128), 1)
    for t in range(8):
        low, high = (cotangent[:, 2 * t + n, :].astype(f32) for n in (0, 1))
        for side in range(2):
            cols = slice(side * 128, side * 128 + 128)
            even = jnp.where(lane < QUARTER, low[:, cols], pltpu.roll(high[:, cols], QUARTER, 1))
            odd = jnp.where(lane < QUARTER, pltpu.roll(low[:, cols], QUARTER, 1), high[:, cols])
            parts[2 * side, :, t * 128 : (t + 1) * 128] = even.astype(bf16)
            parts[2 * side + 1, :, t * 128 : (t + 1) * 128] = odd.astype(bf16)
    for other, part in enumerate((own, core, zed, both)):
        part[...] = parts[flipped("z_lo", other // 2) * 2 + flipped("core", other % 2)]


def join_kernel(*refs):
    joined = refs[-1]
    start = 0
    for ref in refs[:-1]:
        joined[start : start + ref.shape[0]] = ref[...]
        start += ref.shape[0]


def halve_kernel(first, second, after, upper, lower):
    del after
    upper[...] = first[: KEPT // 2]
    lower[...] = second[KEPT // 2 :]


def rim_kernel(stacked, *refs):
    tile = refs[-1]
    first = quarter() == 0
    for c in range(4):
        value = stacked[c].astype(f32)
        tile[c] = jnp.where(first, value[:, :128], value[:, 384:]).astype(bf16)


def patch_kernel(
    stacked, beyond, *refs,
):
    shared = refs[:4]
    patches, tissue, scale, norm, inv_square, inv_density, anch, anch_t, wturned, wide = refs[4:]
    start = pl.multiple_of(quarter() * 128, 128)

    def part(c, shift):
        rim = beyond[c].astype(f32)
        wide[:, 0:128] = rim
        wide[:, 128:640] = stacked[c].astype(f32)
        wide[:, 640:768] = rim
        return pltpu.roll(wide[:, pl.ds(start, 384)], 384 - shift, 1)[:, :LANES]

    colours = [part(c, 122) for c in range(3)]
    here = part(3, 124)
    lane = lax.broadcasted_iota(jnp.int32, here.shape, 1)
    here = jnp.where(lane < REACH, here, 0.0)
    tissue[...] = here
    x = dot(replicate_rows(), jnp.concatenate(colours, axis=0).astype(bf16))
    offset = (lax.broadcasted_iota(jnp.int32, x.shape, 0) % GROUP) % 5
    s = x
    for b in range(1, 5):
        s = jnp.where(offset == b, pltpu.roll(x, LANES - b, 1), s)
    patches[...] = s.astype(bf16)
    square = jnp.sum((s * s).reshape(36, GROUP, LANES), axis=1)
    total = square[0:ROWS]
    for a in range(1, 5):
        total = total + square[a : a + ROWS]
    total = total + EPS
    root = lax.rsqrt(total)
    scale[...] = 4.0 * root
    norm[...] = total * root
    inv_square[...] = 1.0 / total
    counted = dot(here.astype(bf16), column_pool())
    even, odd = (
        jnp.dot(row_pool(n), counted, precision=lax.Precision.HIGHEST, preferred_element_type=f32)
        for n in (0, 1)
    )
    lane = lax.broadcasted_iota(jnp.int32, even.shape, 1)
    inv_density[...] = 1.0 / jnp.maximum(jnp.where(lane < QUARTER, even, odd), 1.0)
    anchors = jnp.concatenate([both[1024:1088, :] for both in shared], axis=0)
    ordered = dot(anchors, entry_order(bf16, 128))
    anch[...] = ordered.astype(bf16)
    anch_t[...] = ordered.T.astype(bf16)
    blocks = [pl.ds(pl.multiple_of(block_of(p) * OWN, OWN), OWN) for p in range(16)]
    for n, both in enumerate(shared):
        ordered = jnp.concatenate([both[block, :] for block in blocks], axis=0)
        wturned[n * OWN : (n + 1) * OWN, :] = ordered.astype(f32).T[:OWN].astype(bf16)


def forward_kernel(
    patches, tissue, scale, norm, inv_density, anch,
    masked, whitened,
    columned, pool,
):
    pool[...] = column_pool()

    @pl.loop(0, ROWS // STEP)
    def _(t):
        lifted = []
        for r in range(STEP):
            i = t * STEP + r
            patch = patches[pl.ds(pl.multiple_of(i * GROUP, GROUP), 80), :]
            raw = dot(anch[...], patch)
            value = jnp.exp(raw * scale[pl.ds(i, 1), :] - 4.0) * tissue[pl.ds(i, 1), :]
            masked[i] = value.astype(bf16)
            lifted.append((value * norm[pl.ds(i, 1), :]).astype(bf16))
        result = dot(jnp.concatenate(lifted, axis=0), pool[...])
        columned[pl.ds(t * STEP, STEP)] = result.reshape(STEP, KEPT, 128)

    for t in range(8):
        acc = None
        for i in range(ROWS):
            weights = row_weights(t, i)
            if weights is not None:
                term = weights * columned[i]
                acc = term if acc is None else acc + term
        whitened[:, t * 128 : (t + 1) * 128] = (acc * inv_density[t : t + 1, :]).astype(bf16)


def fold(block, rows):
    top, low = block[:rows], block[rows:]
    left = lax.broadcasted_iota(jnp.int32, top.shape, 1) < OWN
    own = jnp.where(left, top, pltpu.roll(low, OWN, 1))
    partner = jnp.where(left, pltpu.roll(top, OWN, 1), low)
    return own.astype(bf16), partner.astype(bf16)


def stacks(blocks):
    for n in range(FLAT // 256):
        cols = slice(n * 256, (n + 1) * 256)
        yield cols, jnp.concatenate([block[:, cols] for block in blocks], axis=0)


def whiten_rows(blocks, whitened):
    return sum(dot_nt(stack, whitened[:, cols]) for cols, stack in stacks(blocks))


def four_folds(block, rows):
    return fold(block[:, :128], rows) + fold(block[:, 128:], rows)


def place_rows(sums, grad_w, first):
    for n in range(grad_w.shape[0] // OWN):
        strip = block_of(first + n)
        place = lax.rem(strip, 4) * 4 + strip // 4
        rows = pl.ds(pl.multiple_of(place * 32, 32), 32)
        for ref, value in zip(sums, four_folds(grad_w[n * OWN : (n + 1) * OWN], OWN // 2)):
            ref[rows, :] = value


def early_kernel(*refs):
    blocks, (wturned, whitened, partial, *sums) = refs[:3], refs[3:]
    for ref in sums:
        ref[...] = jnp.zeros_like(ref)
    for cols, stack in stacks(blocks):
        partial[:, cols] = dot(wturned[:, : EARLY * OWN], stack)
    place_rows(sums, whiten_rows(blocks, whitened), 0)


def backward_kernel(
    first, second, partial, wturned, inv_density, masked, patches, inv_square, anch_t,
    anchor_grad, image,
    rowed, spread_grad, pool_t,
):
    pool_t[...] = column_spread()
    scaled = []
    for cols, stack in stacks((first, second)):
        pooled = partial[:, cols] + dot(wturned[:, EARLY * OWN :], stack)
        for side in range(2):
            t = len(scaled)
            part = pooled[:, side * 128 : (side + 1) * 128]
            scaled.append(part.astype(bf16).astype(f32) * (4.0 * inv_density[t : t + 1, :]))
    for i in range(ROWS):
        acc = None
        for t in range(8):
            weights = row_weights(t, i)
            if weights is not None:
                term = weights * scaled[t]
                acc = term if acc is None else acc + term
        rowed[i * KEPT : (i + 1) * KEPT, :] = acc.astype(bf16)
    spread_grad[...] = jnp.zeros_like(spread_grad)
    anchor_grad[...] = jnp.zeros_like(anchor_grad)

    @pl.loop(0, ROWS // STEP)
    def _(t):
        start = pl.multiple_of(t * (STEP * KEPT), STEP * KEPT)
        spread = dot(rowed[pl.ds(start, STEP * KEPT), :], pool_t[...])
        grads, wides, units = [], [], []
        for r in range(STEP):
            i = t * STEP + r
            patch = patches[pl.ds(pl.multiple_of(i * GROUP, GROUP), 80), :]
            grad = (spread[r * KEPT : (r + 1) * KEPT] * masked[i].astype(f32)).astype(bf16)
            unit = dot(anch_t[...], grad)
            wide = patch.astype(f32)
            along = jnp.sum(wide * unit, axis=0, keepdims=True) * inv_square[pl.ds(i, 1), :]
            units.append(unit - wide * along)
            grads.append(grad)
            wides.append(patch)
        anchor_grad[...] += dot_nt(jnp.concatenate(wides, axis=1), jnp.concatenate(grads, axis=1))
        sums = []
        for g in range(STEP + 4):
            acc = None
            for r in range(STEP):
                if 0 <= g - r < 5:
                    term = units[r][(g - r) * GROUP : (g - r + 1) * GROUP]
                    acc = term if acc is None else acc + term
            sums.append(acc)
        here = pl.ds(pl.multiple_of(t * (STEP * GROUP), STEP * GROUP), (STEP + 4) * GROUP)
        spread_grad[here, :] += jnp.concatenate(sums, axis=0)

    t = spread_grad[...]
    offset = (lax.broadcasted_iota(jnp.int32, t.shape, 0) % GROUP) % 5
    moved = t
    for b in range(1, 5):
        moved = jnp.where(offset == b, pltpu.roll(t, b, 1), moved)
    high = moved.astype(bf16)
    low = (moved - high.astype(f32)).astype(bf16)
    folder = fold_rows()
    image[...] = (dot(folder, high) + dot(folder, low)).astype(bf16)


def finish_kernel(*refs):
    first, second, whitened, *early = refs[:7]
    anchor_grad, *sums = refs[7:]
    pad = jnp.zeros((8, 128), bf16)
    for ref, start, part in zip(sums, early, four_folds(anchor_grad[...], 40)):
        ref[0:512, :] = start[...]
        ref[512:560, :] = jnp.concatenate([part, pad], axis=0)
    place_rows(sums, whiten_rows((first, second), whitened), EARLY)


def add_up(refs):
    total = refs[0][...].astype(f32)
    for ref in refs[1:]:
        total = total + ref[...].astype(f32)
    return total


def rim_lanes(rims):
    lane = lax.broadcasted_iota(jnp.int32, rims.shape, 1)
    return jnp.where(lane < 6, rims, 0.0), jnp.where(lane >= 122, rims, 0.0)


def chip_kernel(parts, own, one, two, three, middle, kept, next_one, next_two, next_three, sums):
    gap = jnp.zeros((8, 128), f32)
    whole = None
    for q in range(4):
        part = add_up([parts.at[4 * x + q] for x in range(4)])
        pieces = [gap] * q + [part] + [gap] * (3 - q)
        placed = jnp.concatenate(pieces, axis=1)
        whole = placed if whole is None else whole + placed
    turned = pltpu.roll(whole, 640 - 6, 1)
    middle[...] = turned[:, :512]
    later, earlier = rim_lanes(turned[:, 512:])
    y, z = lax.axis_index("y"), lax.axis_index("z_hi")
    later = jnp.where((y == 3) & (z == 3), 0.0, later)
    earlier = jnp.where((y == 0) & (z == 0), 0.0, earlier)
    later = jnp.where(y == 3, pltpu.roll(later, 64, 1), later)
    earlier = jnp.where(y == 0, pltpu.roll(earlier, 64, 1), earlier)
    sums[...] = add_up((own, one, two, three))
    for step, part in enumerate((kept, next_one, next_two, next_three)):
        target = lax.rem(y + step, 4)
        part[0:128, :] = sums[pl.ds(pl.multiple_of(target * 128, 128), 128), :].astype(bf16)
        rims = {1: later, 3: earlier}.get(step, gap)
        part[128:176, :] = jnp.concatenate([sums[512:552, :], rims], axis=0).astype(bf16)


def pack_kernel(kept, one, two, three, packed, sums):
    total = add_up((kept, one, two, three))
    sums[...] = total[0:128]
    straight = rim_lanes(total[168:176])
    onward = rim_lanes(pltpu.roll(total[168:176], 64, 1))
    rims = (straight[0] + straight[1], onward[0], jnp.zeros((8, 128), f32), onward[1])
    for step in range(4):
        z = lax.rem(lax.axis_index("z_hi") + step, 4)
        packed[z, 0:32, :] = sums[pl.ds(pl.multiple_of(z * 32, 32), 32), :].astype(bf16)
        packed[z, 32:80, :] = jnp.concatenate([total[128:168], rims[step]], axis=0).astype(bf16)


def unpack_kernel(received, middle, grad_anchors, grad_whiten, grad_image):
    total = add_up([received.at[z] for z in range(4)])
    other = pltpu.roll(total, OWN, 1)
    grad_whiten[0:32, :] = total[0:32, :OWN]
    grad_whiten[32:64, :] = other[0:32, :OWN]
    turned = jnp.concatenate([total[32:72], other[32:72]], axis=0).T[:OWN]
    grad_anchors[...] = lax.dot_general(
        turned, entry_order(f32), (((1,), (1,)), ((), ())),
        precision=lax.Precision.HIGHEST, preferred_element_type=f32,
    )
    first, last = rim_lanes(total[72:80])
    image = middle[...] + jnp.concatenate([first, jnp.zeros((8, 256), f32), last], axis=1)
    for colour in range(3):
        grad_image[colour] = image[2 * colour : 2 * colour + 2]


def call(kernel, outs, scratch, flops, limit, *args, loose=0):
    size = lambda shape, dtype: math.prod(shape) * jnp.dtype(dtype).itemsize
    tight = len(args) - loose
    moved = sum(size(a.shape, a.dtype) for a in args[:tight]) + sum(size(*out) for out in outs)
    return pl.pallas_call(
        kernel,
        out_shape=[jax.ShapeDtypeStruct(shape, dtype) for shape, dtype in outs],
        in_specs=[pl.BlockSpec(memory_space=pltpu.VMEM)] * tight
        + [pl.BlockSpec(memory_space=pl.ANY)] * loose,
        out_specs=[pl.BlockSpec(memory_space=pltpu.VMEM)] * len(outs),
        scratch_shapes=[pltpu.VMEM(shape, dtype) for shape, dtype in scratch],
        compiler_params=pltpu.CompilerParams(vmem_limit_bytes=limit * MIB),
        cost_estimate=pl.CostEstimate(flops=flops, bytes_accessed=moved, transcendentals=0),
    )(*args)


def shards(image, mask, anchors, whiten, cotangent):
    def send(value, dx, other):
        return lax.ppermute(value, CHAN, route(dx, other))

    part = ((OWN, FLAT), bf16)
    own, *away = call(
        quarter_kernel, [part] * 4, [((4, OWN, FLAT), bf16)], 1_000_000, 6, cotangent
    )
    (block,) = call(
        join_kernel,
        [((KEPT, FLAT), bf16)],
        [],
        1_000_000,
        4,
        own, *(send(value, 0, other) for other, value in enumerate(away, 1)),
    )
    last, following = send(block, 1, 0), send(block, 3, 0)

    both = jnp.concatenate(
        [jnp.pad(whiten, ((0, 0), (0, OWN))), jnp.pad(anchors, ((0, 0), (0, 53)))], axis=0
    )
    shared = [both] + [send(both, 0, other) for other in (1, 2, 3)]

    stacked = jnp.concatenate([image, mask.astype(bf16)[None]], axis=0)
    (tile,) = call(
        rim_kernel, [((4, ROWS, 128), bf16)], [], 1_000_000, 4, stacked, block, loose=1
    )
    half = ((KEPT // 2, FLAT), bf16)
    upper, lower = call(
        halve_kernel, [half, half], [], 1_000_000, 4, last, following, tile, loose=1
    )
    first_blocks = (block, following, last)
    last_blocks = (send(upper, 1, 0), send(lower, 3, 0))

    plane = ((ROWS, LANES), f32)
    patches, tissue, scale, norm, inv_square, inv_density, anch, anch_t, wturned = call(
        patch_kernel,
        [
            ((36 * GROUP, LANES), bf16),
            plane,
            plane,
            plane,
            plane,
            ((8, 128), f32),
            ((KEPT, 80), bf16),
            ((80, KEPT), bf16),
            ((KEPT, 1024), bf16),
        ],
        [((ROWS, 768), f32)],
        1_000_000_000,
        12,
        stacked, lax.ppermute(tile, STRIPS + CHAN, seams()), *shared,
    )
    masked, whitened = call(
        forward_kernel,
        [((ROWS, KEPT, LANES), bf16), ((KEPT, FLAT), bf16)],
        [((ROWS, KEPT, 128), f32), ((LANES, 128), bf16)],
        3_000_000_000,
        18,
        patches, tissue, scale, norm, inv_density, anch,
    )
    rows = ((512, 128), bf16)
    partial, *early = call(
        early_kernel,
        [((KEPT, FLAT), f32)] + [rows] * 4,
        [],
        2_000_000_000,
        14,
        *first_blocks, wturned, whitened,
    )
    anchor_grad, image_part = call(
        backward_kernel,
        [((80, KEPT), f32), ((128, LANES), bf16)],
        [((ROWS * KEPT, 128), bf16), ((36 * GROUP, LANES), f32), ((128, LANES), bf16)],
        5_000_000_000,
        24,
        *last_blocks, partial, wturned, inv_density, masked, patches, inv_square, anch_t,
    )

    parts = lax.all_to_all(image_part.reshape(16, 8, LANES), CHAN, 0, 0)
    rows = ((560, 128), bf16)
    own, *away = call(
        finish_kernel,
        [rows] * 4,
        [],
        1_000_000_000,
        12,
        *last_blocks, whitened, *early, anchor_grad,
    )
    middle, kept, *others = call(
        chip_kernel,
        [((8, 512), f32)] + [((176, 128), bf16)] * 4,
        [((560, 128), f32)],
        1_000_000,
        8,
        parts, own, *(send(value, 0, other) for other, value in enumerate(away, 1)),
    )
    others = [
        lax.ppermute(value, "y", [(y, (y + step) % 4) for y in range(4)])
        for step, value in enumerate(others, 1)
    ]
    (packed,) = call(
        pack_kernel, [((4, 80, 128), bf16)], [((128, 128), f32)], 1_000_000, 4, kept, *others
    )
    return tuple(
        call(
            unpack_kernel,
            [((OWN, 75), f32), ((OWN, OWN), f32), ((3, 2, 512), f32)],
            [],
            1_000_000,
            4,
            lax.all_to_all(packed, "z_hi", 0, 0), middle,
        )
    )


def solution(mesh):
    fine = Mesh(mesh.devices.reshape(4, 4, 4, 2, 2), STRIPS + CHAN)
    placed = (
        P(None, None, STRIPS),
        P(None, STRIPS),
        P(CHAN, None),
        P(None, CHAN),
        P(CHAN, None, STRIPS),
    )
    return jax.shard_map(
        shards,
        mesh=fine,
        in_specs=placed,
        out_specs=(P(CHAN, None), P(STRIPS, CHAN), P(None, CHAN, STRIPS)),
        check_vma=False,
    )
```

time: 96.4 us -> 89.2 us (0.925)
  the two profiles are of different devices: /device:TPU:162 before, /device:TPU:24 now
where the time goes in v8:
time: 89.2 us; the launch traced here: 88.9 us
  blocking collectives  26.5 us (30%)
  waiting for transfers between devices  19.4 us (22%)
  starting transfers between devices  19.3 us (22%)
  Pallas kernels  18.3 us (21%)
  other arithmetic  2.53 us (3%)
  local copies, waits for them, and re-layouts  2.1 us (2%)
    pallas_call x12, Pallas kernels, call(): pl.pallas_call(kernel, out_shape=[jax.ShapeDtypeStruct(shape, dtype) for...  18.3 us
    all_to_all x1, blocking collectives, shards(): lax.all_to_all(packed, 'z_hi', 0, 0)  16 us
    ppermute x13, waiting for transfers between devices, send(): return lax.ppermute(value, CHAN, route(dx, other))  13.7 us
    ppermute x13, starting transfers between devices, send(): return lax.ppermute(value, CHAN, route(dx, other))  13.3 us
    all_to_all x1, blocking collectives, shards(): parts = lax.all_to_all(image_part.reshape(16, 8, LANES), CHAN, 0, 0)  10.4 us
    ppermute x3, waiting for transfers between devices, shards(): lax.ppermute(value, 'y', [(y, (y + step) % 4) for y in range(4)])  5.25 us
    ppermute x1, starting transfers between devices, shards(): lax.ppermute(tile, STRIPS + CHAN, seams())  3.01 us
    ppermute x3, starting transfers between devices, shards(): lax.ppermute(value, 'y', [(y, (y + step) % 4) for y in range(4)])  3 us
  transfers between devices with their start and end apart: 17, of which 9 were waited for; matrix products, arithmetic and copies ran while one was open for 4% of the time, Pallas kernels for 8%

profile of v8, /device:TPU:24, one launch (start us, length us, event | category | flops | bytes accessed | tf_op | source)
XLA Modules:
  0.0 88.9 jit_solution(6187064879053239267)
XLA Ops:
  0.6 1.0 %copy-done = bf16[64,16,256]{2,1,0:T(8,128)(2,1)S(1)} copy-done((bf16[64,16,256]{2,1,0:T(8,128)(2,1)S(1)}, bf16[64,16,256]{2,1,0:T(8,128)(2,1)}, u32[]{:S(2)}) %copy-start) | copy-done | bytes 524312
  1.7 0.9 %shard_map.76 = (bf16[64,1024]{1,0:T(8,128)(2,1)S(1)}, bf16[64,1024]{1,0:T(8,128)(2,1)S(1)}, bf16[64,1024]{1,0:T(8,128)(2,1)S(1)}, bf16[64,1024]{1,0:T(8,128)(2,1)S(1)}) custom-call(bf16[64,16,256]{2,1,0:T(8,128)(2,1)S(1)} %copy-done), custom_call_target="tpu_custom_call" | custom-call | flops 1000000 | bytes 1048576 | tf_op jit(solution)/shard_map/pallas_call | solution.py:425
  2.7 2.0 %collective-permute-start.1 = (bf16[64,1024]{1,0:T(8,128)(2,1)S(1)}, bf16[64,1024]{1,0:T(8,128)(2,1)S(1)}, u32[]{:S(2)}, u32[]{:S(2)}) collective-permute-start(bf16[64,1024]{1,0:T(8,128)(2,1)S(1)} %get-tuple-element.38), channel_id=1, source_target_pairs={{0,2},{1,3},{2,0},{3,1},{4,6},{5,7},{6,4},{7,5},{8,10},{9,11},{10,... | collective-permute-start | bytes 393224 | tf_op jit(solution)/shard_map/ppermute | solution.py:439
  4.8 0.8 convert_bitcast_fusion
  5.6 1.1 %copy.8 = bf16[1024,64]{1,0:T(8,128)(2,1)S(1)} copy(bf16[1024,64]{0,1:T(8,128)(2,1)} %param.8) | data formatting | bytes 262144 | tf_op args[3]
  6.7 0.9 %pad_maximum_fusion.stacked = bf16[4,32,512]{2,1,0:T(8,128)(2,1)S(1)} fusion(bf16[1,32,512]{2,1,0:T(8,128)(2,1)S(1)} %convert_bitcast_fusion, bf16[3,32,512]{2,1,0:T(8,128)(2,1)} %param.5), kind=kLoop, calls=%fused_computation.5 | loop fusion | flops 65536 | bytes 262144 | tf_op jit(solution)/shard_map/concatenate | solution.py:460
  7.6 1.5 %collective-permute-done.1.refs_2_ = bf16[64,1024]{1,0:T(8,128)(2,1)S(1)} collective-permute-done((bf16[64,1024]{1,0:T(8,128)(2,1)S(1)}, bf16[64,1024]{1,0:T(8,128)(2,1)S(1)}, u32[]{:S(2)}, u32[]{:S(2)}) %collective-permute-start.1) | collective-permute-done | bytes 131104 | tf_op jit(solution)/shard_map/ppermute | solution.py:439
  9.1 2.2 %collective-permute-done.2.refs_3_ = bf16[64,1024]{1,0:T(8,128)(2,1)S(1)} collective-permute-done((bf16[64,1024]{1,0:T(8,128)(2,1)S(1)}, bf16[64,1024]{1,0:T(8,128)(2,1)S(1)}, u32[]{:S(2)}, u32[]{:S(2)}) %collective-permute-start.2) | collective-permute-done | bytes 131104 | tf_op jit(solution)/shard_map/ppermute | solution.py:439
  11.4 1.6 %collective-permute-start.3 = (bf16[256,1024]{1,0:T(8,128)(2,1)S(1)}, bf16[256,1024]{1,0:T(8,128)(2,1)S(1)}, u32[]{:S(2)}, u32[]{:S(2)}) collective-permute-start(bf16[256,1024]{1,0:T(8,128)(2,1)S(1)} %shard_map.77.refs_0_), channel_id=1, source_target_pairs={{0,4},{1,5},{2,6},{3,7},{4,8},{5,9},{6,10},{7,11},{8,12},{9,13},{1... | collective-permute-start | bytes 1572872 | tf_op jit(solution)/shard_map/ppermute | solution.py:439
  12.9 1.7 %collective-permute-start.4 = (bf16[256,1024]{1,0:T(8,128)(2,1)S(1)}, bf16[256,1024]{1,0:T(8,128)(2,1)S(1)}, u32[]{:S(2)}, u32[]{:S(2)}) collective-permute-start(bf16[256,1024]{1,0:T(8,128)(2,1)S(1)} %shard_map.77.refs_0_), channel_id=1, source_target_pairs={{0,12},{1,13},{2,14},{3,15},{4,0},{5,1},{6,2},{7,3},{8,4},{9,5},{1... | collective-permute-start | bytes 1572872 | tf_op jit(solution)/shard_map/ppermute | solution.py:439
  14.7 3.0 %collective-permute-start.7 = (bf16[4,32,128]{2,1,0:T(8,128)(2,1)S(1)}, bf16[4,32,128]{2,1,0:T(8,128)(2,1)S(1)}, u32[]{:S(2)}, u32[]{:S(2)}) collective-permute-start(bf16[4,32,128]{2,1,0:T(8,128)(2,1)S(1)} %shard_map.78.after), channel_id=1, source_target_pairs={{16,3},{20,7},{24,11},{28,15},{32,19},{36,23},{40,27},{44,31},{48,... | collective-permute-start | bytes 98312 | tf_op jit(solution)/shard_map/ppermute | solution.py:488
  17.7 0.8 fusion.2.refs_0_
  18.5 2.2 %collective-permute-start.10 = (bf16[1088,128]{1,0:T(8,128)(2,1)S(1)}, bf16[1088,128]{1,0:T(8,128)(2,1)S(1)}, u32[]{:S(2)}, u32[]{:S(2)}) collective-permute-start(bf16[1088,128]{1,0:T(8,128)(2,1)S(1)} %fusion.2.refs_0_), channel_id=1, source_target_pairs={{0,3},{1,2},{2,1},{3,0},{4,7},{5,6},{6,5},{7,4},{8,11},{9,10},{10,... | collective-permute-start | bytes 835592 | tf_op jit(solution)/shard_map/ppermute | solution.py:439
  20.7 0.5 collective-permute-done.7.beyond
  21.2 4.8 %collective-permute-done.10.refs_3_ = bf16[1088,128]{1,0:T(8,128)(2,1)S(1)} collective-permute-done((bf16[1088,128]{1,0:T(8,128)(2,1)S(1)}, bf16[1088,128]{1,0:T(8,128)(2,1)S(1)}, u32[]{:S(2)}, u32[]{:S(2)}) %collective-permute-start.10) | collective-permute-done | bytes 278560 | tf_op jit(solution)/shard_map/ppermute | solution.py:439
  26.0 4.8 %collective-permute-done.9.refs_2_ = bf16[1088,128]{1,0:T(8,128)(2,1)S(1)} collective-permute-done((bf16[1088,128]{1,0:T(8,128)(2,1)S(1)}, bf16[1088,128]{1,0:T(8,128)(2,1)S(1)}, u32[]{:S(2)}, u32[]{:S(2)}) %collective-permute-start.9) | collective-permute-done | bytes 278560 | tf_op jit(solution)/shard_map/ppermute | solution.py:439
  30.8 1.5 %shard_map.80 = (bf16[576,256]{1,0:T(8,128)(2,1)S(1)}, f32[32,256]{1,0:T(8,128)S(1)}, f32[32,256]{1,0:T(8,128)S(1)}, f32[32,256]{1,0:T(8,128)S(1)}, f32[32,256]{...) custom-call(bf16[4,32,512]{2,1,0:T(8,128)(2,1)S(1)} %pad_maximum_fus, ...), custom_call_target="tpu_custom_call" | custom-call | flops 1000000000 | bytes 2314240 | tf_op jit(solution)/shard_map/pallas_call | solution.py:425
  32.7 3.0 %collective-permute-start.6 = (bf16[128,1024]{1,0:T(8,128)(2,1)S(1)}, bf16[128,1024]{1,0:T(8,128)(2,1)S(1)}, u32[]{:S(2)}, u32[]{:S(2)}) collective-permute-start(bf16[128,1024]{1,0:T(8,128)(2,1)S(1)} %get-tuple-element.41), channel_id=1, source_target_pairs={{0,12},{1,13},{2,14},{3,15},{4,0},{5,1},{6,2},{7,3},{8,4},{9,5},{1... | collective-permute-start | bytes 786440 | tf_op jit(solution)/shard_map/ppermute | solution.py:439
  35.6 5.0 %shard_map.81 = (bf16[32,256,256]{2,1,0:T(8,128)(2,1)S(1)}, bf16[256,1024]{1,0:T(8,128)(2,1)S(1)}) custom-call(bf16[576,256]{1,0:T(8,128)(2,1)S(1)} %get-tuple-element.43.patches, f32[32,256]{1,0:T(8,128)S(1)} %get-tuple-element.44.tissue, f32[32,256]{1,0:T(8,128)S(1)} %get-tuple-element.45.scale, f32[32,256]{1,0:T(8,128)S(1)} %get-tuple-element.46.norm, ...), custom_call_target="tpu_custom_call" | custom-call | flops 3000000000 | bytes 5156864 | tf_op jit(solution)/shard_map/pallas_call | solution.py:425
  40.6 1.1 %shard_map.82 = (f32[256,1024]{1,0:T(8,128)S(1)}, bf16[512,128]{1,0:T(8,128)(2,1)S(1)}, bf16[512,128]{1,0:T(8,128)(2,1)S(1)}, bf16[512,128]{1,0:T(8,128)(2,1)S(1)}, bf16[512,128]{1,0:T(8,128)(2,1)S(1)}) custom-call(bf16[256,1024]{1,0:T(8,128)(2,1)S(1)} %shard_map.77.refs_0_, bf16[256,1024]{1,0:T(8,128)(2,1)S(1)} %collective-permute-done.4.second.refs_1_, ...), custom_call_target="tpu_custom_call" | custom-call | flops 2000000000 | bytes 4194304 | tf_op jit(solution)/shard_map/pallas_call | solution.py:425
  41.7 0.5 collective-permute-done.5.first.refs_0_
  42.1 8.1 %shard_map.83 = (f32[80,256]{1,0:T(8,128)S(1)}, bf16[128,256]{1,0:T(8,128)(2,1)S(1)}) custom-call(bf16[128,1024]{1,0:T(8,128)(2,1)S(1)} %collective-permute-done.5.first.refs_0_, bf16[128,1024]{1,0:T(8,128)(2,1)S(1)} %collective-permute-done.6.second.refs_1_, f32[256,1024]{1,0:T(8,128)S(1)} %get-tuple-element.50.partial, ...), custom_call_target="tpu_custom_call" | custom-call | flops 5000000000 | bytes 6811648 | tf_op jit(solution)/shard_map/pallas_call | solution.py:425
  50.3 0.4 shard_map.84
  50.8 2.1 %collective-permute-start.12 = (bf16[560,128]{1,0:T(8,128)(2,1)S(1)}, bf16[560,128]{1,0:T(8,128)(2,1)S(1)}, u32[]{:S(2)}, u32[]{:S(2)}) collective-permute-start(bf16[560,128]{1,0:T(8,128)(2,1)S(1)} %get-tuple-element.62), channel_id=1, source_target_pairs={{0,2},{1,3},{2,0},{3,1},{4,6},{5,7},{6,4},{7,5},{8,10},{9,11},{10,... | collective-permute-start | bytes 430088 | tf_op jit(solution)/shard_map/ppermute | solution.py:439
  52.9 10.4 %all_to_all.10.parts = bf16[16,8,256]{2,1,0:T(8,128)(2,1)S(1)} all-to-all(bf16[16,8,256]{2,1,0:T(8,128)(2,1)S(1)} %bitcast.3), channel_id=1, replica_groups=mesh['z_hi'=4,'y'=4,'x'=4,'z_lo'=2,'core'=2] {'x','z_lo','core'}, dimensions={0} | all-to-all | bytes 131072 | tf_op jit(solution)/shard_map/all_to_all | solution.py:516
  63.6 1.6 %collective-permute-start.14 = (bf16[176,128]{1,0:T(8,128)(2,1)S(1)}, bf16[176,128]{1,0:T(8,128)(2,1)S(1)}, u32[]{:S(2)}, u32[]{:S(2)}) collective-permute-start(bf16[176,128]{1,0:T(8,128)(2,1)S(1)} %get-tuple-element.65), channel_id=1, source_target_pairs={{0,16},{16,32},{32,48},{48,0},{1,17},{17,33},{33,49},{49,1},{2,18}... | collective-permute-start | bytes 135176 | tf_op jit(solution)/shard_map/ppermute | solution.py:535
  65.2 1.4 %collective-permute-start.15 = (bf16[176,128]{1,0:T(8,128)(2,1)S(1)}, bf16[176,128]{1,0:T(8,128)(2,1)S(1)}, u32[]{:S(2)}, u32[]{:S(2)}) collective-permute-start(bf16[176,128]{1,0:T(8,128)(2,1)S(1)} %get-tuple-element.66), channel_id=1, source_target_pairs={{0,32},{16,48},{32,0},{48,16},{1,33},{17,49},{33,1},{49,17},{2,34}... | collective-permute-start | bytes 135176 | tf_op jit(solution)/shard_map/ppermute | solution.py:535
  66.6 1.2 %collective-permute-done.14.one = bf16[176,128]{1,0:T(8,128)(2,1)S(1)} collective-permute-done((bf16[176,128]{1,0:T(8,128)(2,1)S(1)}, bf16[176,128]{1,0:T(8,128)(2,1)S(1)}, u32[]{:S(2)}, u32[]{:S(2)}) %collective-permute-start.14) | collective-permute-done | bytes 45088 | tf_op jit(solution)/shard_map/ppermute | solution.py:535
  67.8 3.1 %collective-permute-done.15.two = bf16[176,128]{1,0:T(8,128)(2,1)S(1)} collective-permute-done((bf16[176,128]{1,0:T(8,128)(2,1)S(1)}, bf16[176,128]{1,0:T(8,128)(2,1)S(1)}, u32[]{:S(2)}, u32[]{:S(2)}) %collective-permute-start.15) | collective-permute-done | bytes 45088 | tf_op jit(solution)/shard_map/ppermute | solution.py:535
  70.8 1.0 %collective-permute-done.16.three = bf16[176,128]{1,0:T(8,128)(2,1)S(1)} collective-permute-done((bf16[176,128]{1,0:T(8,128)(2,1)S(1)}, bf16[176,128]{1,0:T(8,128)(2,1)S(1)}, u32[]{:S(2)}, u32[]{:S(2)}) %collective-permute-start.16) | collective-permute-done | bytes 45088 | tf_op jit(solution)/shard_map/ppermute | solution.py:535
  71.9 16.0 %all_to_all.11.received = bf16[4,80,128]{2,1,0:T(8,128)(2,1)S(1)} all-to-all(bf16[4,80,128]{2,1,0:T(8,128)(2,1)S(1)} %shard_map.86), channel_id=1, replica_groups=mesh['z_hi'=4,'y'=4,'x'=4,'z_lo'=2,'core'=2] {'z_hi'}, dimensions={0} | all-to-all | bytes 163840 | tf_op jit(solution)/shard_map/all_to_all | solution.py:548
  87.9 0.9 %shard_map.87 = (f32[64,75]{1,0:T(8,128)}, f32[64,64]{1,0:T(8,128)}, f32[3,2,512]{2,1,0:T(2,128)}) custom-call(bf16[4,80,128]{2,1,0:T(8,128)(2,1)S(1)} %all_to_all.11.received, f32[8,512]{1,0:T(8,128)S(1)} %get-tuple-element.68.middle), custom_call_target="tpu_custom_call" | custom-call | flops 1000000 | bytes 146176 | tf_op jit(solution)/shard_map/pallas_call | solution.py:425
  (22 shorter events, 1.1 us)
Async XLA Ops:
  0.6 1.0 %copy-start = (bf16[64,16,256]{2,1,0:T(8,128)(2,1)S(1)}, bf16[64,16,256]{2,1,0:T(8,128)(2,1)}, u32[]{:S(2)}) copy-start(bf16[64,16,256]{2,1,0:T(8,128)(2,1)} %cotangent.1) | copy-start | bytes 1572868
  2.6 5.0 %collective-permute-start = (bf16[64,1024]{1,0:T(8,128)(2,1)S(1)}, bf16[64,1024]{1,0:T(8,128)(2,1)S(1)}, u32[]{:S(2)}, u32[]{:S(2)}) collective-permute-start(bf16[64,1024]{1,0:T(8,128)(2,1)S(1)} %get-tuple-element.37), channel_id=1, source_target_pairs={{0,1},{1,0},{2,3},{3,2},{4,5},{5,4},{6,7},{7,6},{8,9},{9,8},{10,11... | collective-permute-start | bytes 393224 | tf_op jit(solution)/shard_map/ppermute | solution.py:439
  2.7 6.4 %collective-permute-start.1 = (bf16[64,1024]{1,0:T(8,128)(2,1)S(1)}, bf16[64,1024]{1,0:T(8,128)(2,1)S(1)}, u32[]{:S(2)}, u32[]{:S(2)}) collective-permute-start(bf16[64,1024]{1,0:T(8,128)(2,1)S(1)} %get-tuple-element.38), channel_id=1, source_target_pairs={{0,2},{1,3},{2,0},{3,1},{4,6},{5,7},{6,4},{7,5},{8,10},{9,11},{10,... | collective-permute-start | bytes 393224 | tf_op jit(solution)/shard_map/ppermute | solution.py:439
  4.7 6.6 %collective-permute-start.2 = (bf16[64,1024]{1,0:T(8,128)(2,1)S(1)}, bf16[64,1024]{1,0:T(8,128)(2,1)S(1)}, u32[]{:S(2)}, u32[]{:S(2)}) collective-permute-start(bf16[64,1024]{1,0:T(8,128)(2,1)S(1)} %get-tuple-element.39), channel_id=1, source_target_pairs={{0,3},{1,2},{2,1},{3,0},{4,7},{5,6},{6,5},{7,4},{8,11},{9,10},{10,... | collective-permute-start | bytes 393224 | tf_op jit(solution)/shard_map/ppermute | solution.py:439
  11.4 20.9 %collective-permute-start.3 = (bf16[256,1024]{1,0:T(8,128)(2,1)S(1)}, bf16[256,1024]{1,0:T(8,128)(2,1)S(1)}, u32[]{:S(2)}, u32[]{:S(2)}) collective-permute-start(bf16[256,1024]{1,0:T(8,128)(2,1)S(1)} %shard_map.77.refs_0_), channel_id=1, source_target_pairs={{0,4},{1,5},{2,6},{3,7},{4,8},{5,9},{6,10},{7,11},{8,12},{9,13},{1... | collective-permute-start | bytes 1572872 | tf_op jit(solution)/shard_map/ppermute | solution.py:439
  12.9 19.3 %collective-permute-start.4 = (bf16[256,1024]{1,0:T(8,128)(2,1)S(1)}, bf16[256,1024]{1,0:T(8,128)(2,1)S(1)}, u32[]{:S(2)}, u32[]{:S(2)}) collective-permute-start(bf16[256,1024]{1,0:T(8,128)(2,1)S(1)} %shard_map.77.refs_0_), channel_id=1, source_target_pairs={{0,12},{1,13},{2,14},{3,15},{4,0},{5,1},{6,2},{7,3},{8,4},{9,5},{1... | collective-permute-start | bytes 1572872 | tf_op jit(solution)/shard_map/ppermute | solution.py:439
  14.7 6.5 %collective-permute-start.7 = (bf16[4,32,128]{2,1,0:T(8,128)(2,1)S(1)}, bf16[4,32,128]{2,1,0:T(8,128)(2,1)S(1)}, u32[]{:S(2)}, u32[]{:S(2)}) collective-permute-start(bf16[4,32,128]{2,1,0:T(8,128)(2,1)S(1)} %shard_map.78.after), channel_id=1, source_target_pairs={{16,3},{20,7},{24,11},{28,15},{32,19},{36,23},{40,27},{44,31},{48,... | collective-permute-start | bytes 98312 | tf_op jit(solution)/shard_map/ppermute | solution.py:488
  18.5 7.5 %collective-permute-start.10 = (bf16[1088,128]{1,0:T(8,128)(2,1)S(1)}, bf16[1088,128]{1,0:T(8,128)(2,1)S(1)}, u32[]{:S(2)}, u32[]{:S(2)}) collective-permute-start(bf16[1088,128]{1,0:T(8,128)(2,1)S(1)} %fusion.2.refs_0_), channel_id=1, source_target_pairs={{0,3},{1,2},{2,1},{3,0},{4,7},{5,6},{6,5},{7,4},{8,11},{9,10},{10,... | collective-permute-start | bytes 835592 | tf_op jit(solution)/shard_map/ppermute | solution.py:439
  20.7 5.3 %collective-permute-start.8 = (bf16[1088,128]{1,0:T(8,128)(2,1)S(1)}, bf16[1088,128]{1,0:T(8,128)(2,1)S(1)}, u32[]{:S(2)}, u32[]{:S(2)}) collective-permute-start(bf16[1088,128]{1,0:T(8,128)(2,1)S(1)} %fusion.2.refs_0_), channel_id=1, source_target_pairs={{0,1},{1,0},{2,3},{3,2},{4,5},{5,4},{6,7},{7,6},{8,9},{9,8},{10,11... | collective-permute-start | bytes 835592 | tf_op jit(solution)/shard_map/ppermute | solution.py:439
  21.2 9.6 %collective-permute-start.9 = (bf16[1088,128]{1,0:T(8,128)(2,1)S(1)}, bf16[1088,128]{1,0:T(8,128)(2,1)S(1)}, u32[]{:S(2)}, u32[]{:S(2)}) collective-permute-start(bf16[1088,128]{1,0:T(8,128)(2,1)S(1)} %fusion.2.refs_0_), channel_id=1, source_target_pairs={{0,2},{1,3},{2,0},{3,1},{4,6},{5,7},{6,4},{7,5},{8,10},{9,11},{10,... | collective-permute-start | bytes 835592 | tf_op jit(solution)/shard_map/ppermute | solution.py:439
  32.3 9.9 %collective-permute-start.5 = (bf16[128,1024]{1,0:T(8,128)(2,1)S(1)}, bf16[128,1024]{1,0:T(8,128)(2,1)S(1)}, u32[]{:S(2)}, u32[]{:S(2)}) collective-permute-start(bf16[128,1024]{1,0:T(8,128)(2,1)S(1)} %get-tuple-element.40), channel_id=1, source_target_pairs={{0,4},{1,5},{2,6},{3,7},{4,8},{5,9},{6,10},{7,11},{8,12},{9,13},{1... | collective-permute-start | bytes 786440 | tf_op jit(solution)/shard_map/ppermute | solution.py:439
  32.7 9.5 %collective-permute-start.6 = (bf16[128,1024]{1,0:T(8,128)(2,1)S(1)}, bf16[128,1024]{1,0:T(8,128)(2,1)S(1)}, u32[]{:S(2)}, u32[]{:S(2)}) collective-permute-start(bf16[128,1024]{1,0:T(8,128)(2,1)S(1)} %get-tuple-element.41), channel_id=1, source_target_pairs={{0,12},{1,13},{2,14},{3,15},{4,0},{5,1},{6,2},{7,3},{8,4},{9,5},{1... | collective-permute-start | bytes 786440 | tf_op jit(solution)/shard_map/ppermute | solution.py:439
  50.7 12.7 %collective-permute-start.11 = (bf16[560,128]{1,0:T(8,128)(2,1)S(1)}, bf16[560,128]{1,0:T(8,128)(2,1)S(1)}, u32[]{:S(2)}, u32[]{:S(2)}) collective-permute-start(bf16[560,128]{1,0:T(8,128)(2,1)S(1)} %get-tuple-element.61), channel_id=1, source_target_pairs={{0,1},{1,0},{2,3},{3,2},{4,5},{5,4},{6,7},{7,6},{8,9},{9,8},{10,11... | collective-permute-start | bytes 430088 | tf_op jit(solution)/shard_map/ppermute | solution.py:439
  50.8 12.6 %collective-permute-start.12 = (bf16[560,128]{1,0:T(8,128)(2,1)S(1)}, bf16[560,128]{1,0:T(8,128)(2,1)S(1)}, u32[]{:S(2)}, u32[]{:S(2)}) collective-permute-start(bf16[560,128]{1,0:T(8,128)(2,1)S(1)} %get-tuple-element.62), channel_id=1, source_target_pairs={{0,2},{1,3},{2,0},{3,1},{4,6},{5,7},{6,4},{7,5},{8,10},{9,11},{10,... | collective-permute-start | bytes 430088 | tf_op jit(solution)/shard_map/ppermute | solution.py:439
  52.9 10.5 %collective-permute-start.13 = (bf16[560,128]{1,0:T(8,128)(2,1)S(1)}, bf16[560,128]{1,0:T(8,128)(2,1)S(1)}, u32[]{:S(2)}, u32[]{:S(2)}) collective-permute-start(bf16[560,128]{1,0:T(8,128)(2,1)S(1)} %get-tuple-element.63), channel_id=1, source_target_pairs={{0,3},{1,2},{2,1},{3,0},{4,7},{5,6},{6,5},{7,4},{8,11},{9,10},{10,... | collective-permute-start | bytes 430088 | tf_op jit(solution)/shard_map/ppermute | solution.py:439
  63.6 4.2 %collective-permute-start.14 = (bf16[176,128]{1,0:T(8,128)(2,1)S(1)}, bf16[176,128]{1,0:T(8,128)(2,1)S(1)}, u32[]{:S(2)}, u32[]{:S(2)}) collective-permute-start(bf16[176,128]{1,0:T(8,128)(2,1)S(1)} %get-tuple-element.65), channel_id=1, source_target_pairs={{0,16},{16,32},{32,48},{48,0},{1,17},{17,33},{33,49},{49,1},{2,18}... | collective-permute-start | bytes 135176 | tf_op jit(solution)/shard_map/ppermute | solution.py:535
  65.2 5.7 %collective-permute-start.15 = (bf16[176,128]{1,0:T(8,128)(2,1)S(1)}, bf16[176,128]{1,0:T(8,128)(2,1)S(1)}, u32[]{:S(2)}, u32[]{:S(2)}) collective-permute-start(bf16[176,128]{1,0:T(8,128)(2,1)S(1)} %get-tuple-element.66), channel_id=1, source_target_pairs={{0,32},{16,48},{32,0},{48,16},{1,33},{17,49},{33,1},{49,17},{2,34}... | collective-permute-start | bytes 135176 | tf_op jit(solution)/shard_map/ppermute | solution.py:535
  66.6 5.3 %collective-permute-start.16 = (bf16[176,128]{1,0:T(8,128)(2,1)S(1)}, bf16[176,128]{1,0:T(8,128)(2,1)S(1)}, u32[]{:S(2)}, u32[]{:S(2)}) collective-permute-start(bf16[176,128]{1,0:T(8,128)(2,1)S(1)} %get-tuple-element.67), channel_id=1, source_target_pairs={{0,48},{16,0},{32,16},{48,32},{1,49},{17,1},{33,17},{49,33},{2,50}... | collective-permute-start | bytes 135176 | tf_op jit(solution)/shard_map/ppermute | solution.py:535

commit v9 on v8

--- a/solution.py
+++ b/solution.py
@@ -140,11 +140,19 @@
 
 
 def join_kernel(*refs):
-    joined = refs[-1]
+    *parts, _, _, joined = refs
     start = 0
-    for ref in refs[:-1]:
+    for ref in parts:
         joined[start : start + ref.shape[0]] = ref[...]
         start += ref.shape[0]
+
+
+def bundle_kernel(whiten, anchors, after, bundle):
+    del after
+    bundle[0:512, :OWN] = whiten[0:512, :]
+    bundle[0:512, OWN:] = whiten[512:1024, :]
+    bundle[512:576, :] = jnp.zeros((OWN, 128), bf16)
+    bundle[512:576, :75] = anchors[...]
 
 
 def halve_kernel(first, second, after, upper, lower):
@@ -202,21 +210,27 @@
     )
     lane = lax.broadcasted_iota(jnp.int32, even.shape, 1)
     inv_density[...] = 1.0 / jnp.maximum(jnp.where(lane < QUARTER, even, odd), 1.0)
-    anchors = jnp.concatenate([both[1024:1088, :] for both in shared], axis=0)
+    anchors = jnp.concatenate([bundle[512:576, :] for bundle in shared], axis=0)
     ordered = dot(anchors, entry_order(bf16, 128))
     anch[...] = ordered.astype(bf16)
     anch_t[...] = ordered.T.astype(bf16)
-    blocks = [pl.ds(pl.multiple_of(block_of(p) * OWN, OWN), OWN) for p in range(16)]
-    for n, both in enumerate(shared):
-        ordered = jnp.concatenate([both[block, :] for block in blocks], axis=0)
-        wturned[n * OWN : (n + 1) * OWN, :] = ordered.astype(f32).T[:OWN].astype(bf16)
+    blocks = [block_of(p) for p in range(16)]
+    for n, bundle in enumerate(shared):
+        ordered = []
+        for block in blocks:
+            rows = pl.ds(pl.multiple_of(lax.rem(block, 8) * OWN, OWN), OWN)
+            value = bundle[rows, :].astype(f32)
+            ordered.append(jnp.where(block >= 8, pltpu.roll(value, OWN, 1), value))
+        turned = jnp.concatenate(ordered, axis=0).T
+        wturned[n * OWN : (n + 1) * OWN, :] = turned[:OWN].astype(bf16)
 
 
 def forward_kernel(
-    patches, tissue, scale, norm, inv_density, anch,
+    patches, tissue, scale, norm, inv_density, anch, after,
     masked, whitened,
     columned, pool,
 ):
+    del after
     pool[...] = column_pool()
 
     @pl.loop(0, ROWS // STEP)
@@ -418,6 +432,21 @@
         grad_image[colour] = image[2 * colour : 2 * colour + 2]
 
 
+def hold(value, *after):
+    def kernel(*refs):
+        del refs
+
+    return pl.pallas_call(
+        kernel,
+        out_shape=jax.ShapeDtypeStruct(value.shape, value.dtype),
+        in_specs=[pl.BlockSpec(memory_space=pl.ANY)] * (1 + len(after)),
+        out_specs=pl.BlockSpec(memory_space=pl.ANY),
+        input_output_aliases={0: 0},
+        compiler_params=pltpu.CompilerParams(vmem_limit_bytes=MIB),
+        cost_estimate=pl.CostEstimate(flops=1000, bytes_accessed=1000, transcendentals=0),
+    )(value, *after)
+
+
 def call(kernel, outs, scratch, flops, limit, *args, loose=0):
     size = lambda shape, dtype: math.prod(shape) * jnp.dtype(dtype).itemsize
     tight = len(args) - loose
@@ -442,25 +471,26 @@
     own, *away = call(
         quarter_kernel, [part] * 4, [((4, OWN, FLAT), bf16)], 1_000_000, 6, cotangent
     )
+    (bundle,) = call(
+        bundle_kernel, [((576, 128), bf16)], [], 1_000_000, 4, whiten, anchors, away[2], loose=1
+    )
+
+    stacked = jnp.concatenate([image, mask.astype(bf16)[None]], axis=0)
+    (tile,) = call(
+        rim_kernel, [((4, ROWS, 128), bf16)], [], 1_000_000, 4, stacked, away[2], loose=1
+    )
     (block,) = call(
         join_kernel,
         [((KEPT, FLAT), bf16)],
         [],
         1_000_000,
         4,
-        own, *(send(value, 0, other) for other, value in enumerate(away, 1)),
+        own, *(send(value, 0, other) for other, value in enumerate(away, 1)), tile, bundle,
+        loose=2,
     )
     last, following = send(block, 1, 0), send(block, 3, 0)
-
-    both = jnp.concatenate(
-        [jnp.pad(whiten, ((0, 0), (0, OWN))), jnp.pad(anchors, ((0, 0), (0, 53)))], axis=0
-    )
-    shared = [both] + [send(both, 0, other) for other in (1, 2, 3)]
-
-    stacked = jnp.concatenate([image, mask.astype(bf16)[None]], axis=0)
-    (tile,) = call(
-        rim_kernel, [((4, ROWS, 128), bf16)], [], 1_000_000, 4, stacked, block, loose=1
-    )
+    bundle = hold(bundle, block)
+    shared = [bundle] + [send(bundle, 0, other) for other in (1, 2, 3)]
     half = ((KEPT // 2, FLAT), bf16)
     upper, lower = call(
         halve_kernel, [half, half], [], 1_000_000, 4, last, following, tile, loose=1
@@ -493,7 +523,8 @@
         [((ROWS, KEPT, 128), f32), ((LANES, 128), bf16)],
         3_000_000_000,
         18,
-        patches, tissue, scale, norm, inv_density, anch,
+        patches, tissue, scale, norm, inv_density, anch, upper,
+        loose=1,
     )
     rows = ((512, 128), bf16)
     partial, *early = call(

time: 89.2 us -> 84.3 us (0.945)
  starting transfers between devices: 19.3 us -> 16.5 us
  waiting for transfers between devices: 19.4 us -> 17.5 us
    ppermute x13, starting transfers between devices: 13.3 us -> 11 us  [send(): return lax.ppermute(value, CHAN, route(dx, other))]
    ppermute x13, waiting for transfers between devices: 13.7 us -> 11.5 us  [send(): return lax.ppermute(value, CHAN, route(dx, other))]
    all_to_all x1, blocking collectives: 10.4 us -> 9.5 us  [shards(): parts = lax.all_to_all(image_part.reshape(16, 8, LANES), CHAN, 0, 0)]
    unnamed x3 -> x5, local copies, waits for them, and re-layouts: 2.1 us -> 2.82 us
    pallas_call x12 -> x13, Pallas kernels: 18.3 us -> 18.7 us  [call(): pl.pallas_call(kernel, out_shape=[jax.ShapeDtypeStruct(shape, dtype) for...]
  transfers between devices with their start and end apart: 17 -> 17, of which waited for: 9 -> 10; matrix products, arithmetic and copies ran while one was open for 4% -> 3% of each run, Pallas kernels for 8% -> 10%
where the time goes in v9:
time: 84.3 us; the launch traced here: 83.9 us
  blocking collectives  25.7 us (30%)
  Pallas kernels  18.7 us (22%)
  waiting for transfers between devices  17.5 us (21%)
  starting transfers between devices  16.5 us (20%)
  local copies, waits for them, and re-layouts  2.82 us (3%)
  other arithmetic  1.76 us (2%)
    pallas_call x13, Pallas kernels, call(): pl.pallas_call(kernel, out_shape=[jax.ShapeDtypeStruct(shape, dtype) for...  18.7 us
    all_to_all x1, blocking collectives, shards(): lax.all_to_all(packed, 'z_hi', 0, 0)  16.2 us
    ppermute x13, waiting for transfers between devices, send(): return lax.ppermute(value, CHAN, route(dx, other))  11.5 us
    ppermute x13, starting transfers between devices, send(): return lax.ppermute(value, CHAN, route(dx, other))  11 us
    all_to_all x1, blocking collectives, shards(): parts = lax.all_to_all(image_part.reshape(16, 8, LANES), CHAN, 0, 0)  9.5 us
    ppermute x3, waiting for transfers between devices, shards(): lax.ppermute(value, 'y', [(y, (y + step) % 4) for y in range(4)])  5.12 us
    ppermute x1, starting transfers between devices, shards(): lax.ppermute(tile, STRIPS + CHAN, seams())  3.28 us
    unnamed x5, local copies, waits for them, and re-layouts  2.82 us
  transfers between devices with their start and end apart: 17, of which 10 were waited for; matrix products, arithmetic and copies ran while one was open for 3% of the time, Pallas kernels for 10%

profile of v9, /device:TPU:24, one launch (start us, length us, event | category | flops | bytes accessed | tf_op | source)
XLA Modules:
  0.0 83.9 jit_solution(2895947716498702064)
XLA Ops:
  0.6 1.0 %copy-done = bf16[64,16,256]{2,1,0:T(8,128)(2,1)S(1)} copy-done((bf16[64,16,256]{2,1,0:T(8,128)(2,1)S(1)}, bf16[64,16,256]{2,1,0:T(8,128)(2,1)}, u32[]{:S(2)}) %copy-start) | copy-done | bytes 524312
  1.7 0.9 %shard_map.76 = (bf16[64,1024]{1,0:T(8,128)(2,1)S(1)}, bf16[64,1024]{1,0:T(8,128)(2,1)S(1)}, bf16[64,1024]{1,0:T(8,128)(2,1)S(1)}, bf16[64,1024]{1,0:T(8,128)(2,1)S(1)}) custom-call(bf16[64,16,256]{2,1,0:T(8,128)(2,1)S(1)} %copy-done), custom_call_target="tpu_custom_call" | custom-call | flops 1000000 | bytes 1048576 | tf_op jit(solution)/shard_map/pallas_call | solution.py:454
  2.7 2.0 %collective-permute-start.1 = (bf16[64,1024]{1,0:T(8,128)(2,1)S(1)}, bf16[64,1024]{1,0:T(8,128)(2,1)S(1)}, u32[]{:S(2)}, u32[]{:S(2)}) collective-permute-start(bf16[64,1024]{1,0:T(8,128)(2,1)S(1)} %get-tuple-element.38), channel_id=1, source_target_pairs={{0,2},{1,3},{2,0},{3,1},{4,6},{5,7},{6,4},{7,5},{8,10},{9,11},{10,... | collective-permute-start | bytes 393224 | tf_op jit(solution)/shard_map/ppermute | solution.py:468
  4.8 0.8 %convert_bitcast_fusion = bf16[1,32,512]{2,1,0:T(8,128)(2,1)S(1)} fusion(s32[32,512]{1,0:T(8,128)} %param.6), kind=kLoop, calls=%fused_computation.1 | loop fusion | flops 16384 | bytes 98304 | tf_op jit(solution)/shard_map/broadcast_in_dim | solution.py:478
  5.6 1.1 %copy.9.whiten = bf16[1024,64]{1,0:T(8,128)(2,1)S(1)} copy(bf16[1024,64]{0,1:T(8,128)(2,1)} %param.8) | data formatting | bytes 262144 | tf_op args[3]
  6.7 0.9 %pad_maximum_fusion.stacked = bf16[4,32,512]{2,1,0:T(8,128)(2,1)S(1)} fusion(bf16[1,32,512]{2,1,0:T(8,128)(2,1)S(1)} %convert_bitcast_fusion, bf16[3,32,512]{2,1,0:T(8,128)(2,1)} %param.5), kind=kLoop, calls=%fused_computation | loop fusion | flops 65536 | bytes 262144 | tf_op jit(solution)/shard_map/concatenate | solution.py:478
  7.7 0.7 copy-done.1
  8.5 0.6 collective-permute-done.1.refs_2_
  9.1 2.2 %collective-permute-done.2.refs_3_ = bf16[64,1024]{1,0:T(8,128)(2,1)S(1)} collective-permute-done((bf16[64,1024]{1,0:T(8,128)(2,1)S(1)}, bf16[64,1024]{1,0:T(8,128)(2,1)S(1)}, u32[]{:S(2)}, u32[]{:S(2)}) %collective-permute-start.2) | collective-permute-done | bytes 131104 | tf_op jit(solution)/shard_map/ppermute | solution.py:468
  11.4 2.8 %collective-permute-start.4 = (bf16[256,1024]{1,0:T(8,128)(2,1)S(1)}, bf16[256,1024]{1,0:T(8,128)(2,1)S(1)}, u32[]{:S(2)}, u32[]{:S(2)}) collective-permute-start(bf16[256,1024]{1,0:T(8,128)(2,1)S(1)} %shard_map.79.refs_1_.refs_0_), channel_id=1, source_target_pairs={{0,12},{1,13},{2,14},{3,15},{4,0},{5,1},{6,2},{7,3},{8,4},{9,5},{1... | collective-permute-start | bytes 1572872 | tf_op jit(solution)/shard_map/ppermute | solution.py:468
  14.2 3.3 %collective-permute-start.7 = (bf16[4,32,128]{2,1,0:T(8,128)(2,1)S(1)}, bf16[4,32,128]{2,1,0:T(8,128)(2,1)S(1)}, u32[]{:S(2)}, u32[]{:S(2)}) collective-permute-start(bf16[4,32,128]{2,1,0:T(8,128)(2,1)S(1)} %shard_map.77.refs_4_.after), channel_id=1, source_target_pairs={{16,3},{20,7},{24,11},{28,15},{32,19},{36,23},{40,27},{44,31},{48,... | collective-permute-start | bytes 98312 | tf_op jit(solution)/shard_map/ppermute | solution.py:518
  17.5 1.9 %collective-permute-start.10 = (bf16[576,128]{1,0:T(8,128)(2,1)S(1)}, bf16[576,128]{1,0:T(8,128)(2,1)S(1)}, u32[]{:S(2)}, u32[]{:S(2)}) collective-permute-start(bf16[576,128]{1,0:T(8,128)(2,1)S(1)} %shard_map.81.refs_0_), channel_id=1, source_target_pairs={{0,3},{1,2},{2,1},{3,0},{4,7},{5,6},{6,5},{7,4},{8,11},{9,10},{10,... | collective-permute-start | bytes 442376 | tf_op jit(solution)/shard_map/ppermute | solution.py:468
  19.4 0.9 %collective-permute-done.7.beyond = bf16[4,32,128]{2,1,0:T(8,128)(2,1)S(1)} collective-permute-done((bf16[4,32,128]{2,1,0:T(8,128)(2,1)S(1)}, bf16[4,32,128]{2,1,0:T(8,128)(2,1)S(1)}, u32[]{:S(2)}, u32[]{:S(2)}) %collective-permute-start.7) | collective-permute-done | bytes 32800 | tf_op jit(solution)/shard_map/ppermute | solution.py:518
  20.3 2.9 %collective-permute-done.10.refs_3_ = bf16[576,128]{1,0:T(8,128)(2,1)S(1)} collective-permute-done((bf16[576,128]{1,0:T(8,128)(2,1)S(1)}, bf16[576,128]{1,0:T(8,128)(2,1)S(1)}, u32[]{:S(2)}, u32[]{:S(2)}) %collective-permute-start.10) | collective-permute-done | bytes 147488 | tf_op jit(solution)/shard_map/ppermute | solution.py:468
  23.2 2.2 %collective-permute-done.9.refs_2_ = bf16[576,128]{1,0:T(8,128)(2,1)S(1)} collective-permute-done((bf16[576,128]{1,0:T(8,128)(2,1)S(1)}, bf16[576,128]{1,0:T(8,128)(2,1)S(1)}, u32[]{:S(2)}, u32[]{:S(2)}) %collective-permute-start.9) | collective-permute-done | bytes 147488 | tf_op jit(solution)/shard_map/ppermute | solution.py:468
  25.4 1.8 %shard_map.82 = (bf16[576,256]{1,0:T(8,128)(2,1)S(1)}, f32[32,256]{1,0:T(8,128)S(1)}, f32[32,256]{1,0:T(8,128)S(1)}, f32[32,256]{1,0:T(8,128)S(1)}, f32[32,256]{...) custom-call(bf16[4,32,512]{2,1,0:T(8,128)(2,1)S(1)} %pad_maximum_fus, ...), custom_call_target="tpu_custom_call" | custom-call | flops 1000000000 | bytes 1789952 | tf_op jit(solution)/shard_map/pallas_call | solution.py:454
  27.2 1.9 %collective-permute-done.3.first.refs_2_ = bf16[256,1024]{1,0:T(8,128)(2,1)S(1)} collective-permute-done((bf16[256,1024]{1,0:T(8,128)(2,1)S(1)}, bf16[256,1024]{1,0:T(8,128)(2,1)S(1)}, u32[]{:S(2)}, u32[]{:S(2)}) %collective-permute-start.3) | collective-permute-done | bytes 524320 | tf_op jit(solution)/shard_map/ppermute | solution.py:468
  29.1 1.5 %collective-permute-start.6 = (bf16[128,1024]{1,0:T(8,128)(2,1)S(1)}, bf16[128,1024]{1,0:T(8,128)(2,1)S(1)}, u32[]{:S(2)}, u32[]{:S(2)}) collective-permute-start(bf16[128,1024]{1,0:T(8,128)(2,1)S(1)} %get-tuple-element.41), channel_id=1, source_target_pairs={{0,12},{1,13},{2,14},{3,15},{4,0},{5,1},{6,2},{7,3},{8,4},{9,5},{1... | collective-permute-start | bytes 786440 | tf_op jit(solution)/shard_map/ppermute | solution.py:468
  30.6 0.6 collective-permute-start.5
  31.2 5.0 %shard_map.83 = (bf16[32,256,256]{2,1,0:T(8,128)(2,1)S(1)}, bf16[256,1024]{1,0:T(8,128)(2,1)S(1)}) custom-call(bf16[576,256]{1,0:T(8,128)(2,1)S(1)} %get-tuple-element.43.patches, f32[32,256]{1,0:T(8,128)S(1)} %get-tuple-element.44.tissue, f32[32,256]{1,0:T(8,128)S(1)} %get-tuple-element.45.scale, f32[32,256]{1,0:T(8,128)S(1)} %get-tuple-element.46.norm, ...), custom_call_target="tpu_custom_call" | custom-call | flops 3000000000 | bytes 5156864 | tf_op jit(solution)/shard_map/pallas_call | solution.py:454
  36.2 1.1 %shard_map.84 = (f32[256,1024]{1,0:T(8,128)S(1)}, bf16[512,128]{1,0:T(8,128)(2,1)S(1)}, bf16[512,128]{1,0:T(8,128)(2,1)S(1)}, bf16[512,128]{1,0:T(8,128)(2,1)S(1)}, bf16[512,128]{1,0:T(8,128)(2,1)S(1)}) custom-call(bf16[256,1024]{1,0:T(8,128)(2,1)S(1)} %shard_map.79.refs_1_.refs_0_, bf16[256,1024]{1,0:T(8,128)(2,1)S(1)} %collective-permute-done.4.second.refs_1_, ...), custom_call_target="tpu_custom_call" | custom-call | flops 2000000000 | bytes 4194304 | tf_op jit(solution)/shard_map/pallas_call | solution.py:454
  37.3 1.7 %collective-permute-done.5.first.refs_0_ = bf16[128,1024]{1,0:T(8,128)(2,1)S(1)} collective-permute-done((bf16[128,1024]{1,0:T(8,128)(2,1)S(1)}, bf16[128,1024]{1,0:T(8,128)(2,1)S(1)}, u32[]{:S(2)}, u32[]{:S(2)}) %collective-permute-start.5) | collective-permute-done | bytes 262176 | tf_op jit(solution)/shard_map/ppermute | solution.py:468
  39.0 8.1 %shard_map.85 = (f32[80,256]{1,0:T(8,128)S(1)}, bf16[128,256]{1,0:T(8,128)(2,1)S(1)}) custom-call(bf16[128,1024]{1,0:T(8,128)(2,1)S(1)} %collective-permute-done.5.first.refs_0_, bf16[128,1024]{1,0:T(8,128)(2,1)S(1)} %collective-permute-done.6.second.refs_1_, f32[256,1024]{1,0:T(8,128)S(1)} %get-tuple-element.50.partial, ...), custom_call_target="tpu_custom_call" | custom-call | flops 5000000000 | bytes 6811648 | tf_op jit(solution)/shard_map/pallas_call | solution.py:454
  47.7 1.2 %collective-permute-start.12 = (bf16[560,128]{1,0:T(8,128)(2,1)S(1)}, bf16[560,128]{1,0:T(8,128)(2,1)S(1)}, u32[]{:S(2)}, u32[]{:S(2)}) collective-permute-start(bf16[560,128]{1,0:T(8,128)(2,1)S(1)} %get-tuple-element.62), channel_id=1, source_target_pairs={{0,2},{1,3},{2,0},{3,1},{4,6},{5,7},{6,4},{7,5},{8,10},{9,11},{10,... | collective-permute-start | bytes 430088 | tf_op jit(solution)/shard_map/ppermute | solution.py:468
  48.8 0.7 collective-permute-start.13
  49.5 9.5 %all_to_all.10.parts = bf16[16,8,256]{2,1,0:T(8,128)(2,1)S(1)} all-to-all(bf16[16,8,256]{2,1,0:T(8,128)(2,1)S(1)} %bitcast.3), channel_id=1, replica_groups=mesh['z_hi'=4,'y'=4,'x'=4,'z_lo'=2,'core'=2] {'x','z_lo','core'}, dimensions={0} | all-to-all | bytes 131072 | tf_op jit(solution)/shard_map/all_to_all | solution.py:547
  59.3 2.1 %collective-permute-start.15 = (bf16[176,128]{1,0:T(8,128)(2,1)S(1)}, bf16[176,128]{1,0:T(8,128)(2,1)S(1)}, u32[]{:S(2)}, u32[]{:S(2)}) collective-permute-start(bf16[176,128]{1,0:T(8,128)(2,1)S(1)} %get-tuple-element.66), channel_id=1, source_target_pairs={{0,32},{16,48},{32,0},{48,16},{1,33},{17,49},{33,1},{49,17},{2,34}... | collective-permute-start | bytes 135176 | tf_op jit(solution)/shard_map/ppermute | solution.py:566
  61.5 1.9 %collective-permute-done.14.one = bf16[176,128]{1,0:T(8,128)(2,1)S(1)} collective-permute-done((bf16[176,128]{1,0:T(8,128)(2,1)S(1)}, bf16[176,128]{1,0:T(8,128)(2,1)S(1)}, u32[]{:S(2)}, u32[]{:S(2)}) %collective-permute-start.14) | collective-permute-done | bytes 45088 | tf_op jit(solution)/shard_map/ppermute | solution.py:566
  63.4 1.6 %collective-permute-done.15.two = bf16[176,128]{1,0:T(8,128)(2,1)S(1)} collective-permute-done((bf16[176,128]{1,0:T(8,128)(2,1)S(1)}, bf16[176,128]{1,0:T(8,128)(2,1)S(1)}, u32[]{:S(2)}, u32[]{:S(2)}) %collective-permute-start.15) | collective-permute-done | bytes 45088 | tf_op jit(solution)/shard_map/ppermute | solution.py:566
  65.0 1.6 %collective-permute-done.16.three = bf16[176,128]{1,0:T(8,128)(2,1)S(1)} collective-permute-done((bf16[176,128]{1,0:T(8,128)(2,1)S(1)}, bf16[176,128]{1,0:T(8,128)(2,1)S(1)}, u32[]{:S(2)}, u32[]{:S(2)}) %collective-permute-start.16) | collective-permute-done | bytes 45088 | tf_op jit(solution)/shard_map/ppermute | solution.py:566
  66.7 16.2 %all_to_all.11.received = bf16[4,80,128]{2,1,0:T(8,128)(2,1)S(1)} all-to-all(bf16[4,80,128]{2,1,0:T(8,128)(2,1)S(1)} %shard_map.88), channel_id=1, replica_groups=mesh['z_hi'=4,'y'=4,'x'=4,'z_lo'=2,'core'=2] {'z_hi'}, dimensions={0} | all-to-all | bytes 163840 | tf_op jit(solution)/shard_map/all_to_all | solution.py:579
  83.0 0.9 %shard_map.89 = (f32[64,75]{1,0:T(8,128)}, f32[64,64]{1,0:T(8,128)}, f32[3,2,512]{2,1,0:T(2,128)}) custom-call(bf16[4,80,128]{2,1,0:T(8,128)(2,1)S(1)} %all_to_all.11.received, f32[8,512]{1,0:T(8,128)S(1)} %get-tuple-element.68.middle), custom_call_target="tpu_custom_call" | custom-call | flops 1000000 | bytes 146176 | tf_op jit(solution)/shard_map/pallas_call | solution.py:454
  (25 shorter events, 1.4 us)
Async XLA Ops:
  0.6 1.0 %copy-start = (bf16[64,16,256]{2,1,0:T(8,128)(2,1)S(1)}, bf16[64,16,256]{2,1,0:T(8,128)(2,1)}, u32[]{:S(2)}) copy-start(bf16[64,16,256]{2,1,0:T(8,128)(2,1)} %cotangent.1) | copy-start | bytes 1572868
  2.6 5.9 %collective-permute-start = (bf16[64,1024]{1,0:T(8,128)(2,1)S(1)}, bf16[64,1024]{1,0:T(8,128)(2,1)S(1)}, u32[]{:S(2)}, u32[]{:S(2)}) collective-permute-start(bf16[64,1024]{1,0:T(8,128)(2,1)S(1)} %get-tuple-element.37), channel_id=1, source_target_pairs={{0,1},{1,0},{2,3},{3,2},{4,5},{5,4},{6,7},{7,6},{8,9},{9,8},{10,11... | collective-permute-start | bytes 393224 | tf_op jit(solution)/shard_map/ppermute | solution.py:468
  2.7 6.4 %collective-permute-start.1 = (bf16[64,1024]{1,0:T(8,128)(2,1)S(1)}, bf16[64,1024]{1,0:T(8,128)(2,1)S(1)}, u32[]{:S(2)}, u32[]{:S(2)}) collective-permute-start(bf16[64,1024]{1,0:T(8,128)(2,1)S(1)} %get-tuple-element.38), channel_id=1, source_target_pairs={{0,2},{1,3},{2,0},{3,1},{4,6},{5,7},{6,4},{7,5},{8,10},{9,11},{10,... | collective-permute-start | bytes 393224 | tf_op jit(solution)/shard_map/ppermute | solution.py:468
  4.7 6.6 %collective-permute-start.2 = (bf16[64,1024]{1,0:T(8,128)(2,1)S(1)}, bf16[64,1024]{1,0:T(8,128)(2,1)S(1)}, u32[]{:S(2)}, u32[]{:S(2)}) collective-permute-start(bf16[64,1024]{1,0:T(8,128)(2,1)S(1)} %get-tuple-element.39.refs_0_.after), channel_id=1, source_target_pairs={{0,3},{1,2},{2,1},{3,0},{4,7},{5,6},{6,5},{7,4},{8,11},{9,10},{10,... | collective-permute-start | bytes 393224 | tf_op jit(solution)/shard_map/ppermute | solution.py:468
  7.7 0.7 copy-start.1
  11.4 15.8 %collective-permute-start.4 = (bf16[256,1024]{1,0:T(8,128)(2,1)S(1)}, bf16[256,1024]{1,0:T(8,128)(2,1)S(1)}, u32[]{:S(2)}, u32[]{:S(2)}) collective-permute-start(bf16[256,1024]{1,0:T(8,128)(2,1)S(1)} %shard_map.79.refs_1_.refs_0_), channel_id=1, source_target_pairs={{0,12},{1,13},{2,14},{3,15},{4,0},{5,1},{6,2},{7,3},{8,4},{9,5},{1... | collective-permute-start | bytes 1572872 | tf_op jit(solution)/shard_map/ppermute | solution.py:468
  14.2 14.9 %collective-permute-start.3 = (bf16[256,1024]{1,0:T(8,128)(2,1)S(1)}, bf16[256,1024]{1,0:T(8,128)(2,1)S(1)}, u32[]{:S(2)}, u32[]{:S(2)}) collective-permute-start(bf16[256,1024]{1,0:T(8,128)(2,1)S(1)} %shard_map.79.refs_1_.refs_0_), channel_id=1, source_target_pairs={{0,4},{1,5},{2,6},{3,7},{4,8},{5,9},{6,10},{7,11},{8,12},{9,13},{1... | collective-permute-start | bytes 1572872 | tf_op jit(solution)/shard_map/ppermute | solution.py:468
  14.2 6.1 %collective-permute-start.7 = (bf16[4,32,128]{2,1,0:T(8,128)(2,1)S(1)}, bf16[4,32,128]{2,1,0:T(8,128)(2,1)S(1)}, u32[]{:S(2)}, u32[]{:S(2)}) collective-permute-start(bf16[4,32,128]{2,1,0:T(8,128)(2,1)S(1)} %shard_map.77.refs_4_.after), channel_id=1, source_target_pairs={{16,3},{20,7},{24,11},{28,15},{32,19},{36,23},{40,27},{44,31},{48,... | collective-permute-start | bytes 98312 | tf_op jit(solution)/shard_map/ppermute | solution.py:518
  17.5 5.7 %collective-permute-start.10 = (bf16[576,128]{1,0:T(8,128)(2,1)S(1)}, bf16[576,128]{1,0:T(8,128)(2,1)S(1)}, u32[]{:S(2)}, u32[]{:S(2)}) collective-permute-start(bf16[576,128]{1,0:T(8,128)(2,1)S(1)} %shard_map.81.refs_0_), channel_id=1, source_target_pairs={{0,3},{1,2},{2,1},{3,0},{4,7},{5,6},{6,5},{7,4},{8,11},{9,10},{10,... | collective-permute-start | bytes 442376 | tf_op jit(solution)/shard_map/ppermute | solution.py:468
  19.4 6.0 %collective-permute-start.9 = (bf16[576,128]{1,0:T(8,128)(2,1)S(1)}, bf16[576,128]{1,0:T(8,128)(2,1)S(1)}, u32[]{:S(2)}, u32[]{:S(2)}) collective-permute-start(bf16[576,128]{1,0:T(8,128)(2,1)S(1)} %shard_map.81.refs_0_), channel_id=1, source_target_pairs={{0,2},{1,3},{2,0},{3,1},{4,6},{5,7},{6,4},{7,5},{8,10},{9,11},{10,... | collective-permute-start | bytes 442376 | tf_op jit(solution)/shard_map/ppermute | solution.py:468
  20.3 5.1 %collective-permute-start.8 = (bf16[576,128]{1,0:T(8,128)(2,1)S(1)}, bf16[576,128]{1,0:T(8,128)(2,1)S(1)}, u32[]{:S(2)}, u32[]{:S(2)}) collective-permute-start(bf16[576,128]{1,0:T(8,128)(2,1)S(1)} %shard_map.81.refs_0_), channel_id=1, source_target_pairs={{0,1},{1,0},{2,3},{3,2},{4,5},{5,4},{6,7},{7,6},{8,9},{9,8},{10,11... | collective-permute-start | bytes 442376 | tf_op jit(solution)/shard_map/ppermute | solution.py:468
  29.1 8.2 %collective-permute-start.6 = (bf16[128,1024]{1,0:T(8,128)(2,1)S(1)}, bf16[128,1024]{1,0:T(8,128)(2,1)S(1)}, u32[]{:S(2)}, u32[]{:S(2)}) collective-permute-start(bf16[128,1024]{1,0:T(8,128)(2,1)S(1)} %get-tuple-element.41), channel_id=1, source_target_pairs={{0,12},{1,13},{2,14},{3,15},{4,0},{5,1},{6,2},{7,3},{8,4},{9,5},{1... | collective-permute-start | bytes 786440 | tf_op jit(solution)/shard_map/ppermute | solution.py:468
  30.6 8.5 %collective-permute-start.5 = (bf16[128,1024]{1,0:T(8,128)(2,1)S(1)}, bf16[128,1024]{1,0:T(8,128)(2,1)S(1)}, u32[]{:S(2)}, u32[]{:S(2)}) collective-permute-start(bf16[128,1024]{1,0:T(8,128)(2,1)S(1)} %get-tuple-element.40.after), channel_id=1, source_target_pairs={{0,4},{1,5},{2,6},{3,7},{4,8},{5,9},{6,10},{7,11},{8,12},{9,13},{1... | collective-permute-start | bytes 786440 | tf_op jit(solution)/shard_map/ppermute | solution.py:468
  47.6 11.5 %collective-permute-start.11 = (bf16[560,128]{1,0:T(8,128)(2,1)S(1)}, bf16[560,128]{1,0:T(8,128)(2,1)S(1)}, u32[]{:S(2)}, u32[]{:S(2)}) collective-permute-start(bf16[560,128]{1,0:T(8,128)(2,1)S(1)} %get-tuple-element.61), channel_id=1, source_target_pairs={{0,1},{1,0},{2,3},{3,2},{4,5},{5,4},{6,7},{7,6},{8,9},{9,8},{10,11... | collective-permute-start | bytes 430088 | tf_op jit(solution)/shard_map/ppermute | solution.py:468
  47.7 11.4 %collective-permute-start.12 = (bf16[560,128]{1,0:T(8,128)(2,1)S(1)}, bf16[560,128]{1,0:T(8,128)(2,1)S(1)}, u32[]{:S(2)}, u32[]{:S(2)}) collective-permute-start(bf16[560,128]{1,0:T(8,128)(2,1)S(1)} %get-tuple-element.62), channel_id=1, source_target_pairs={{0,2},{1,3},{2,0},{3,1},{4,6},{5,7},{6,4},{7,5},{8,10},{9,11},{10,... | collective-permute-start | bytes 430088 | tf_op jit(solution)/shard_map/ppermute | solution.py:468
  48.8 10.2 %collective-permute-start.13 = (bf16[560,128]{1,0:T(8,128)(2,1)S(1)}, bf16[560,128]{1,0:T(8,128)(2,1)S(1)}, u32[]{:S(2)}, u32[]{:S(2)}) collective-permute-start(bf16[560,128]{1,0:T(8,128)(2,1)S(1)} %get-tuple-element.63), channel_id=1, source_target_pairs={{0,3},{1,2},{2,1},{3,0},{4,7},{5,6},{6,5},{7,4},{8,11},{9,10},{10,... | collective-permute-start | bytes 430088 | tf_op jit(solution)/shard_map/ppermute | solution.py:468
  59.2 4.2 %collective-permute-start.14 = (bf16[176,128]{1,0:T(8,128)(2,1)S(1)}, bf16[176,128]{1,0:T(8,128)(2,1)S(1)}, u32[]{:S(2)}, u32[]{:S(2)}) collective-permute-start(bf16[176,128]{1,0:T(8,128)(2,1)S(1)} %get-tuple-element.65), channel_id=1, source_target_pairs={{0,16},{16,32},{32,48},{48,0},{1,17},{17,33},{33,49},{49,1},{2,18}... | collective-permute-start | bytes 135176 | tf_op jit(solution)/shard_map/ppermute | solution.py:566
  59.3 5.7 %collective-permute-start.15 = (bf16[176,128]{1,0:T(8,128)(2,1)S(1)}, bf16[176,128]{1,0:T(8,128)(2,1)S(1)}, u32[]{:S(2)}, u32[]{:S(2)}) collective-permute-start(bf16[176,128]{1,0:T(8,128)(2,1)S(1)} %get-tuple-element.66), channel_id=1, source_target_pairs={{0,32},{16,48},{32,0},{48,16},{1,33},{17,49},{33,1},{49,17},{2,34}... | collective-permute-start | bytes 135176 | tf_op jit(solution)/shard_map/ppermute | solution.py:566
  61.4 5.3 %collective-permute-start.16 = (bf16[176,128]{1,0:T(8,128)(2,1)S(1)}, bf16[176,128]{1,0:T(8,128)(2,1)S(1)}, u32[]{:S(2)}, u32[]{:S(2)}) collective-permute-start(bf16[176,128]{1,0:T(8,128)(2,1)S(1)} %get-tuple-element.67), channel_id=1, source_target_pairs={{0,48},{16,0},{32,16},{48,32},{1,49},{17,1},{33,17},{49,33},{2,50}... | collective-permute-start | bytes 135176 | tf_op jit(solution)/shard_map/ppermute | solution.py:566

commit v10 on v9

--- a/solution.py
+++ b/solution.py
@@ -125,7 +125,7 @@
     return lax.dot_general(a, b, (((1,), (1,)), ((), ())), preferred_element_type=f32)
 
 
-def quarter_kernel(cotangent, own, core, zed, both, parts):
+def quarter_kernel(cotangent, anchors, own, core, zed, both, parts):
     lane = lax.broadcasted_iota(jnp.int32, (OWN, 128), 1)
     for t in range(8):
         low, high = (cotangent[:, 2 * t + n, :].astype(f32) for n in (0, 1))
@@ -136,23 +136,23 @@
             parts[2 * side, :, t * 128 : (t + 1) * 128] = even.astype(bf16)
             parts[2 * side + 1, :, t * 128 : (t + 1) * 128] = odd.astype(bf16)
     for other, part in enumerate((own, core, zed, both)):
-        part[...] = parts[flipped("z_lo", other // 2) * 2 + flipped("core", other % 2)]
+        part[:, :FLAT] = parts[flipped("z_lo", other // 2) * 2 + flipped("core", other % 2)]
+        part[:, FLAT:] = jnp.zeros((OWN, 128), bf16)
+        part[:, FLAT : FLAT + 75] = anchors[...]
 
 
 def join_kernel(*refs):
     *parts, _, _, joined = refs
     start = 0
     for ref in parts:
-        joined[start : start + ref.shape[0]] = ref[...]
+        joined[start : start + ref.shape[0]] = ref[:, :FLAT]
         start += ref.shape[0]
 
 
-def bundle_kernel(whiten, anchors, after, bundle):
+def bundle_kernel(whiten, after, bundle):
     del after
-    bundle[0:512, :OWN] = whiten[0:512, :]
-    bundle[0:512, OWN:] = whiten[512:1024, :]
-    bundle[512:576, :] = jnp.zeros((OWN, 128), bf16)
-    bundle[512:576, :75] = anchors[...]
+    bundle[:, :OWN] = whiten[0:512, :]
+    bundle[:, OWN:] = whiten[512:1024, :]
 
 
 def halve_kernel(first, second, after, upper, lower):
@@ -172,8 +172,8 @@
 def patch_kernel(
     stacked, beyond, *refs,
 ):
-    shared = refs[:4]
-    patches, tissue, scale, norm, inv_square, inv_density, anch, anch_t, wturned, wide = refs[4:]
+    quarters = refs[:4]
+    patches, tissue, scale, norm, inv_square, inv_density, anch, anch_t, wide = refs[4:]
     start = pl.multiple_of(quarter() * 128, 128)
 
     def part(c, shift):
@@ -210,10 +210,13 @@
     )
     lane = lax.broadcasted_iota(jnp.int32, even.shape, 1)
     inv_density[...] = 1.0 / jnp.maximum(jnp.where(lane < QUARTER, even, odd), 1.0)
-    anchors = jnp.concatenate([bundle[512:576, :] for bundle in shared], axis=0)
+    anchors = jnp.concatenate([part[:, FLAT:] for part in quarters], axis=0)
     ordered = dot(anchors, entry_order(bf16, 128))
     anch[...] = ordered.astype(bf16)
     anch_t[...] = ordered.T.astype(bf16)
+
+def turn_kernel(*refs):
+    *shared, wturned = refs
     blocks = [block_of(p) for p in range(16)]
     for n, bundle in enumerate(shared):
         ordered = []
@@ -226,11 +229,10 @@
 
 
 def forward_kernel(
-    patches, tissue, scale, norm, inv_density, anch, after,
+    patches, tissue, scale, norm, inv_density, anch,
     masked, whitened,
     columned, pool,
 ):
-    del after
     pool[...] = column_pool()
 
     @pl.loop(0, ROWS // STEP)
@@ -467,12 +469,13 @@
     def send(value, dx, other):
         return lax.ppermute(value, CHAN, route(dx, other))
 
-    part = ((OWN, FLAT), bf16)
+    part = ((OWN, FLAT + 128), bf16)
     own, *away = call(
-        quarter_kernel, [part] * 4, [((4, OWN, FLAT), bf16)], 1_000_000, 6, cotangent
-    )
+        quarter_kernel, [part] * 4, [((4, OWN, FLAT), bf16)], 1_000_000, 6, cotangent, anchors
+    )
+    quarters = [own] + [send(value, 0, other) for other, value in enumerate(away, 1)]
     (bundle,) = call(
-        bundle_kernel, [((576, 128), bf16)], [], 1_000_000, 4, whiten, anchors, away[2], loose=1
+        bundle_kernel, [((512, 128), bf16)], [], 1_000_000, 4, whiten, away[2], loose=1
     )
 
     stacked = jnp.concatenate([image, mask.astype(bf16)[None]], axis=0)
@@ -485,7 +488,7 @@
         [],
         1_000_000,
         4,
-        own, *(send(value, 0, other) for other, value in enumerate(away, 1)), tile, bundle,
+        *quarters, tile, bundle,
         loose=2,
     )
     last, following = send(block, 1, 0), send(block, 3, 0)
@@ -499,7 +502,7 @@
     last_blocks = (send(upper, 1, 0), send(lower, 3, 0))
 
     plane = ((ROWS, LANES), f32)
-    patches, tissue, scale, norm, inv_square, inv_density, anch, anch_t, wturned = call(
+    patches, tissue, scale, norm, inv_square, inv_density, anch, anch_t = call(
         patch_kernel,
         [
             ((36 * GROUP, LANES), bf16),
@@ -510,21 +513,20 @@
             ((8, 128), f32),
             ((KEPT, 80), bf16),
             ((80, KEPT), bf16),
-            ((KEPT, 1024), bf16),
         ],
         [((ROWS, 768), f32)],
         1_000_000_000,
         12,
-        stacked, lax.ppermute(tile, STRIPS + CHAN, seams()), *shared,
-    )
+        stacked, lax.ppermute(tile, STRIPS + CHAN, seams()), *quarters,
+    )
+    (wturned,) = call(turn_kernel, [((KEPT, 1024), bf16)], [], 500_000_000, 8, *shared)
     masked, whitened = call(
         forward_kernel,
         [((ROWS, KEPT, LANES), bf16), ((KEPT, FLAT), bf16)],
         [((ROWS, KEPT, 128), f32), ((LANES, 128), bf16)],
         3_000_000_000,
         18,
-        patches, tissue, scale, norm, inv_density, anch, upper,
-        loose=1,
+        patches, tissue, scale, norm, inv_density, anch,
     )
     rows = ((512, 128), bf16)
     partial, *early = call(
@@ -550,7 +552,7 @@
         finish_kernel,
         [rows] * 4,
         [],
-        1_000_000_000,
+        20_000_000_000,
         12,
         *last_blocks, whitened, *early, anchor_grad,
     )

time: 84.3 us -> 84.5 us (level)
  starting transfers between devices: 16.5 us -> 22.2 us
  waiting for transfers between devices: 17.5 us -> 11.9 us
    ppermute x13, waiting for transfers between devices: 11.5 us -> 6.11 us  [send(): return lax.ppermute(value, CHAN, route(dx, other))]
    ppermute x13, starting transfers between devices: 11 us -> 16.1 us  [send(): return lax.ppermute(value, CHAN, route(dx, other))]
    pallas_call x13 -> x14, Pallas kernels: 18.7 us -> 18.8 us  [call(): pl.pallas_call(kernel, out_shape=[jax.ShapeDtypeStruct(shape, dtype) for...]
  transfers between devices with their start and end apart: 17 -> 17, of which waited for: 10 -> 7; matrix products, arithmetic and copies ran while one was open for 3% -> 3% of each run, Pallas kernels for 10% -> 10%
where the time goes in v10:
time: 84.5 us; the launch traced here: 84.1 us
  blocking collectives  25.9 us (31%)
  starting transfers between devices  22.2 us (26%)
  Pallas kernels  18.8 us (22%)
  waiting for transfers between devices  11.9 us (14%)
  local copies, waits for them, and re-layouts  2.82 us (3%)
  other arithmetic  1.76 us (2%)
    pallas_call x14, Pallas kernels, call(): pl.pallas_call(kernel, out_shape=[jax.ShapeDtypeStruct(shape, dtype) for...  18.8 us
    ppermute x13, starting transfers between devices, send(): return lax.ppermute(value, CHAN, route(dx, other))  16.1 us
    all_to_all x1, blocking collectives, shards(): lax.all_to_all(packed, 'z_hi', 0, 0)  15.7 us
    all_to_all x1, blocking collectives, shards(): parts = lax.all_to_all(image_part.reshape(16, 8, LANES), CHAN, 0, 0)  10.2 us
    ppermute x13, waiting for transfers between devices, send(): return lax.ppermute(value, CHAN, route(dx, other))  6.11 us
    ppermute x3, waiting for transfers between devices, shards(): lax.ppermute(value, 'y', [(y, (y + step) % 4) for y in range(4)])  5.25 us
    ppermute x1, starting transfers between devices, shards(): lax.ppermute(tile, STRIPS + CHAN, seams())  3.13 us
    ppermute x3, starting transfers between devices, shards(): lax.ppermute(value, 'y', [(y, (y + step) % 4) for y in range(4)])  2.89 us
  transfers between devices with their start and end apart: 17, of which 7 were waited for; matrix products, arithmetic and copies ran while one was open for 3% of the time, Pallas kernels for 10%

profile of v10, /device:TPU:24, one launch (start us, length us, event | category | flops | bytes accessed | tf_op | source)
XLA Modules:
  0.0 84.1 jit_solution(17109451408251457088)
XLA Ops:
  0.6 1.0 %copy-done = bf16[64,16,256]{2,1,0:T(8,128)(2,1)S(1)} copy-done((bf16[64,16,256]{2,1,0:T(8,128)(2,1)S(1)}, bf16[64,16,256]{2,1,0:T(8,128)(2,1)}, u32[]{:S(2)}) %copy-start) | copy-done | bytes 524312
  1.7 0.7 copy-done.1
  2.4 1.0 %shard_map.76 = (bf16[64,1152]{1,0:T(8,128)(2,1)S(1)}, bf16[64,1152]{1,0:T(8,128)(2,1)S(1)}, bf16[64,1152]{1,0:T(8,128)(2,1)S(1)}, bf16[64,1152]{1,0:T(8,128)(2,1)S(1)}) custom-call(bf16[64,16,256]{2,1,0:T(8,128)(2,1)S(1)} %copy-done, bf16[64,75]{1,0:T(8,128)(2,1)S(1)} %copy-done.1), custom_call_target="tpu_custom_call" | custom-call | flops 1000000 | bytes 1123712 | tf_op jit(solution)/shard_map/pallas_call | solution.py:456
  3.4 1.5 %collective-permute-start.2 = (bf16[64,1152]{1,0:T(8,128)(2,1)S(1)}, bf16[64,1152]{1,0:T(8,128)(2,1)S(1)}, u32[]{:S(2)}, u32[]{:S(2)}) collective-permute-start(bf16[64,1152]{1,0:T(8,128)(2,1)S(1)} %get-tuple-element.38.refs_0_.after), channel_id=1, source_target_pairs={{0,3},{1,2},{2,1},{3,0},{4,7},{5,6},{6,5},{7,4},{8,11},{9,10},{10,... | collective-permute-start | bytes 442376 | tf_op jit(solution)/shard_map/ppermute | solution.py:470
  4.8 0.7 collective-permute-start
  5.6 0.8 %convert_bitcast_fusion = bf16[1,32,512]{2,1,0:T(8,128)(2,1)S(1)} fusion(s32[32,512]{1,0:T(8,128)} %param.6), kind=kLoop, calls=%fused_computation.1 | loop fusion | flops 16384 | bytes 98304 | tf_op jit(solution)/shard_map/broadcast_in_dim | solution.py:481
  6.5 1.1 %copy.9.whiten = bf16[1024,64]{1,0:T(8,128)(2,1)S(1)} copy(bf16[1024,64]{0,1:T(8,128)(2,1)} %param.8) | data formatting | bytes 262144 | tf_op args[3]
  7.5 0.9 %pad_maximum_fusion.stacked = bf16[4,32,512]{2,1,0:T(8,128)(2,1)S(1)} fusion(bf16[1,32,512]{2,1,0:T(8,128)(2,1)S(1)} %convert_bitcast_fusion, bf16[3,32,512]{2,1,0:T(8,128)(2,1)} %param.5), kind=kLoop, calls=%fused_computation | loop fusion | flops 65536 | bytes 262144 | tf_op jit(solution)/shard_map/concatenate | solution.py:481
  8.6 0.6 collective-permute-done.2.refs_3_
  9.2 3.6 %collective-permute-done.1.refs_2_ = bf16[64,1152]{1,0:T(8,128)(2,1)S(1)} collective-permute-done((bf16[64,1152]{1,0:T(8,128)(2,1)S(1)}, bf16[64,1152]{1,0:T(8,128)(2,1)S(1)}, u32[]{:S(2)}, u32[]{:S(2)}) %collective-permute-start.1) | collective-permute-done | bytes 147488 | tf_op jit(solution)/shard_map/ppermute | solution.py:470
  12.8 1.6 %collective-permute-start.3 = (bf16[256,1024]{1,0:T(8,128)(2,1)S(1)}, bf16[256,1024]{1,0:T(8,128)(2,1)S(1)}, u32[]{:S(2)}, u32[]{:S(2)}) collective-permute-start(bf16[256,1024]{1,0:T(8,128)(2,1)S(1)} %shard_map.79.refs_1_.refs_0_), channel_id=1, source_target_pairs={{0,4},{1,5},{2,6},{3,7},{4,8},{5,9},{6,10},{7,11},{8,12},{9,13},{1... | collective-permute-start | bytes 1572872 | tf_op jit(solution)/shard_map/ppermute | solution.py:470
  14.4 1.7 %collective-permute-start.4 = (bf16[256,1024]{1,0:T(8,128)(2,1)S(1)}, bf16[256,1024]{1,0:T(8,128)(2,1)S(1)}, u32[]{:S(2)}, u32[]{:S(2)}) collective-permute-start(bf16[256,1024]{1,0:T(8,128)(2,1)S(1)} %shard_map.79.refs_1_.refs_0_), channel_id=1, source_target_pairs={{0,12},{1,13},{2,14},{3,15},{4,0},{5,1},{6,2},{7,3},{8,4},{9,5},{1... | collective-permute-start | bytes 1572872 | tf_op jit(solution)/shard_map/ppermute | solution.py:470
  16.1 3.1 %collective-permute-start.10 = (bf16[4,32,128]{2,1,0:T(8,128)(2,1)S(1)}, bf16[4,32,128]{2,1,0:T(8,128)(2,1)S(1)}, u32[]{:S(2)}, u32[]{:S(2)}) collective-permute-start(bf16[4,32,128]{2,1,0:T(8,128)(2,1)S(1)} %shard_map.77.refs_4_.after), channel_id=1, source_target_pairs={{16,3},{20,7},{24,11},{28,15},{32,19},{36,23},{40,27},{44,31},{48,... | collective-permute-start | bytes 98312 | tf_op jit(solution)/shard_map/ppermute | solution.py:520
  19.4 2.4 %collective-permute-start.8 = (bf16[512,128]{1,0:T(8,128)(2,1)S(1)}, bf16[512,128]{1,0:T(8,128)(2,1)S(1)}, u32[]{:S(2)}, u32[]{:S(2)}) collective-permute-start(bf16[512,128]{1,0:T(8,128)(2,1)S(1)} %shard_map.81.refs_0_), channel_id=1, source_target_pairs={{0,2},{1,3},{2,0},{3,1},{4,6},{5,7},{6,4},{7,5},{8,10},{9,11},{10,... | collective-permute-start | bytes 393224 | tf_op jit(solution)/shard_map/ppermute | solution.py:470
  21.7 0.5 collective-permute-done.10.beyond
  22.2 2.3 %collective-permute-start.9 = (bf16[512,128]{1,0:T(8,128)(2,1)S(1)}, bf16[512,128]{1,0:T(8,128)(2,1)S(1)}, u32[]{:S(2)}, u32[]{:S(2)}) collective-permute-start(bf16[512,128]{1,0:T(8,128)(2,1)S(1)} %shard_map.81.refs_0_), channel_id=1, source_target_pairs={{0,3},{1,2},{2,1},{3,0},{4,7},{5,6},{6,5},{7,4},{8,11},{9,10},{10,... | collective-permute-start | bytes 393224 | tf_op jit(solution)/shard_map/ppermute | solution.py:470
  24.5 1.2 %shard_map.83 = (bf16[576,256]{1,0:T(8,128)(2,1)S(1)}, f32[32,256]{1,0:T(8,128)S(1)}, f32[32,256]{1,0:T(8,128)S(1)}, f32[32,256]{1,0:T(8,128)S(1)}, f32[32,256]{...) custom-call(bf16[4,32,512]{2,1,0:T(8,128)(2,1)S(1)} %pad_maximum_fusion.stacked, ...), custom_call_target="tpu_custom_call" | custom-call | flops 1000000000 | bytes 1265664 | tf_op jit(solution)/shard_map/pallas_call | solution.py:456
  25.7 1.9 %collective-permute-done.3.first.refs_2_ = bf16[256,1024]{1,0:T(8,128)(2,1)S(1)} collective-permute-done((bf16[256,1024]{1,0:T(8,128)(2,1)S(1)}, bf16[256,1024]{1,0:T(8,128)(2,1)S(1)}, u32[]{:S(2)}, u32[]{:S(2)}) %collective-permute-start.3) | collective-permute-done | bytes 524320 | tf_op jit(solution)/shard_map/ppermute | solution.py:470
  27.7 1.6 %collective-permute-start.5 = (bf16[128,1024]{1,0:T(8,128)(2,1)S(1)}, bf16[128,1024]{1,0:T(8,128)(2,1)S(1)}, u32[]{:S(2)}, u32[]{:S(2)}) collective-permute-start(bf16[128,1024]{1,0:T(8,128)(2,1)S(1)} %get-tuple-element.39), channel_id=1, source_target_pairs={{0,4},{1,5},{2,6},{3,7},{4,8},{5,9},{6,10},{7,11},{8,12},{9,13},{1... | collective-permute-start | bytes 786440 | tf_op jit(solution)/shard_map/ppermute | solution.py:470
  29.2 1.7 %collective-permute-start.6 = (bf16[128,1024]{1,0:T(8,128)(2,1)S(1)}, bf16[128,1024]{1,0:T(8,128)(2,1)S(1)}, u32[]{:S(2)}, u32[]{:S(2)}) collective-permute-start(bf16[128,1024]{1,0:T(8,128)(2,1)S(1)} %get-tuple-element.40), channel_id=1, source_target_pairs={{0,12},{1,13},{2,14},{3,15},{4,0},{5,1},{6,2},{7,3},{8,4},{9,5},{1... | collective-permute-start | bytes 786440 | tf_op jit(solution)/shard_map/ppermute | solution.py:470
  31.0 5.0 %shard_map.84 = (bf16[32,256,256]{2,1,0:T(8,128)(2,1)S(1)}, bf16[256,1024]{1,0:T(8,128)(2,1)S(1)}) custom-call(bf16[576,256]{1,0:T(8,128)(2,1)S(1)} %get-tuple-element.41.patches, f32[32,256]{1,0:T(8,128)S(1)} %get-tuple-element.42.tissue, f32[32,256]{1,0:T(8,128)S(1)} %get-tuple-element.43.scale, f32[32,256]{1,0:T(8,128)S(1)} %get-tuple-element.44.norm, ...), custom_call_target="tpu_custom_call" | custom-call | flops 3000000000 | bytes 5156864 | tf_op jit(solution)/shard_map/pallas_call | solution.py:456
  36.0 0.7 shard_map.82.refs_3_.wturned
  36.7 1.1 %shard_map.85 = (f32[256,1024]{1,0:T(8,128)S(1)}, bf16[512,128]{1,0:T(8,128)(2,1)S(1)}, bf16[512,128]{1,0:T(8,128)(2,1)S(1)}, bf16[512,128]{1,0:T(8,128)(2,1)S(1)}, bf16[512,128]{1,0:T(8,128)(2,1)S(1)}) custom-call(bf16[256,1024]{1,0:T(8,128)(2,1)S(1)} %shard_map.79.refs_1_.refs_0_, bf16[256,1024]{1,0:T(8,128)(2,1)S(1)} %collective-permute-done.4.second.refs_1_, ...), custom_call_target="tpu_custom_call" | custom-call | flops 2000000000 | bytes 4194304 | tf_op jit(solution)/shard_map/pallas_call | solution.py:456
  37.8 8.1 %shard_map.86 = (f32[80,256]{1,0:T(8,128)S(1)}, bf16[128,256]{1,0:T(8,128)(2,1)S(1)}) custom-call(bf16[128,1024]{1,0:T(8,128)(2,1)S(1)} %collective-permute-done.5.first.refs_0_, bf16[128,1024]{1,0:T(8,128)(2,1)S(1)} %collective-permute-done.6.second.refs_1_, f32[256,1024]{1,0:T(8,128)S(1)} %get-tuple-element.48.partial, ...), custom_call_target="tpu_custom_call" | custom-call | flops 5000000000 | bytes 6811648 | tf_op jit(solution)/shard_map/pallas_call | solution.py:456
  46.4 2.4 %collective-permute-start.12 = (bf16[560,128]{1,0:T(8,128)(2,1)S(1)}, bf16[560,128]{1,0:T(8,128)(2,1)S(1)}, u32[]{:S(2)}, u32[]{:S(2)}) collective-permute-start(bf16[560,128]{1,0:T(8,128)(2,1)S(1)} %get-tuple-element.60), channel_id=1, source_target_pairs={{0,2},{1,3},{2,0},{3,1},{4,6},{5,7},{6,4},{7,5},{8,10},{9,11},{10,... | collective-permute-start | bytes 430088 | tf_op jit(solution)/shard_map/ppermute | solution.py:470
  48.8 10.2 %all_to_all.10.parts = bf16[16,8,256]{2,1,0:T(8,128)(2,1)S(1)} all-to-all(bf16[16,8,256]{2,1,0:T(8,128)(2,1)S(1)} %bitcast.3), channel_id=1, replica_groups=mesh['z_hi'=4,'y'=4,'x'=4,'z_lo'=2,'core'=2] {'x','z_lo','core'}, dimensions={0} | all-to-all | bytes 131072 | tf_op jit(solution)/shard_map/all_to_all | solution.py:549
  59.5 2.7 %collective-permute-start.15 = (bf16[176,128]{1,0:T(8,128)(2,1)S(1)}, bf16[176,128]{1,0:T(8,128)(2,1)S(1)}, u32[]{:S(2)}, u32[]{:S(2)}) collective-permute-start(bf16[176,128]{1,0:T(8,128)(2,1)S(1)} %get-tuple-element.64), channel_id=1, source_target_pairs={{0,32},{16,48},{32,0},{48,16},{1,33},{17,49},{33,1},{49,17},{2,34}... | collective-permute-start | bytes 135176 | tf_op jit(solution)/shard_map/ppermute | solution.py:568
  62.2 1.3 %collective-permute-done.14.one = bf16[176,128]{1,0:T(8,128)(2,1)S(1)} collective-permute-done((bf16[176,128]{1,0:T(8,128)(2,1)S(1)}, bf16[176,128]{1,0:T(8,128)(2,1)S(1)}, u32[]{:S(2)}, u32[]{:S(2)}) %collective-permute-start.14) | collective-permute-done | bytes 45088 | tf_op jit(solution)/shard_map/ppermute | solution.py:568
  63.5 1.5 %collective-permute-done.15.two = bf16[176,128]{1,0:T(8,128)(2,1)S(1)} collective-permute-done((bf16[176,128]{1,0:T(8,128)(2,1)S(1)}, bf16[176,128]{1,0:T(8,128)(2,1)S(1)}, u32[]{:S(2)}, u32[]{:S(2)}) %collective-permute-start.15) | collective-permute-done | bytes 45088 | tf_op jit(solution)/shard_map/ppermute | solution.py:568
  65.0 2.4 %collective-permute-done.16.three = bf16[176,128]{1,0:T(8,128)(2,1)S(1)} collective-permute-done((bf16[176,128]{1,0:T(8,128)(2,1)S(1)}, bf16[176,128]{1,0:T(8,128)(2,1)S(1)}, u32[]{:S(2)}, u32[]{:S(2)}) %collective-permute-start.16) | collective-permute-done | bytes 45088 | tf_op jit(solution)/shard_map/ppermute | solution.py:568
  67.5 15.7 %all_to_all.11.received = bf16[4,80,128]{2,1,0:T(8,128)(2,1)S(1)} all-to-all(bf16[4,80,128]{2,1,0:T(8,128)(2,1)S(1)} %shard_map.89), channel_id=1, replica_groups=mesh['z_hi'=4,'y'=4,'x'=4,'z_lo'=2,'core'=2] {'z_hi'}, dimensions={0} | all-to-all | bytes 163840 | tf_op jit(solution)/shard_map/all_to_all | solution.py:581
  83.2 0.9 %shard_map.90 = (f32[64,75]{1,0:T(8,128)}, f32[64,64]{1,0:T(8,128)}, f32[3,2,512]{2,1,0:T(2,128)}) custom-call(bf16[4,80,128]{2,1,0:T(8,128)(2,1)S(1)} %all_to_all.11.received, f32[8,512]{1,0:T(8,128)S(1)} %get-tuple-element.66.middle), custom_call_target="tpu_custom_call" | custom-call | flops 1000000 | bytes 146176 | tf_op jit(solution)/shard_map/pallas_call | solution.py:456
  (26 shorter events, 1.5 us)
Async XLA Ops:
  0.6 1.0 %copy-start = (bf16[64,16,256]{2,1,0:T(8,128)(2,1)S(1)}, bf16[64,16,256]{2,1,0:T(8,128)(2,1)}, u32[]{:S(2)}) copy-start(bf16[64,16,256]{2,1,0:T(8,128)(2,1)} %cotangent.1) | copy-start | bytes 1572868
  1.7 0.7 copy-start.1
  3.4 5.8 %collective-permute-start.2 = (bf16[64,1152]{1,0:T(8,128)(2,1)S(1)}, bf16[64,1152]{1,0:T(8,128)(2,1)S(1)}, u32[]{:S(2)}, u32[]{:S(2)}) collective-permute-start(bf16[64,1152]{1,0:T(8,128)(2,1)S(1)} %get-tuple-element.38.refs_0_.after), channel_id=1, source_target_pairs={{0,3},{1,2},{2,1},{3,0},{4,7},{5,6},{6,5},{7,4},{8,11},{9,10},{10,... | collective-permute-start | bytes 442376 | tf_op jit(solution)/shard_map/ppermute | solution.py:470
  4.8 4.4 %collective-permute-start = (bf16[64,1152]{1,0:T(8,128)(2,1)S(1)}, bf16[64,1152]{1,0:T(8,128)(2,1)S(1)}, u32[]{:S(2)}, u32[]{:S(2)}) collective-permute-start(bf16[64,1152]{1,0:T(8,128)(2,1)S(1)} %get-tuple-element.36), channel_id=1, source_target_pairs={{0,1},{1,0},{2,3},{3,2},{4,5},{5,4},{6,7},{7,6},{8,9},{9,8},{10,11... | collective-permute-start | bytes 442376 | tf_op jit(solution)/shard_map/ppermute | solution.py:470
  5.5 7.3 %collective-permute-start.1 = (bf16[64,1152]{1,0:T(8,128)(2,1)S(1)}, bf16[64,1152]{1,0:T(8,128)(2,1)S(1)}, u32[]{:S(2)}, u32[]{:S(2)}) collective-permute-start(bf16[64,1152]{1,0:T(8,128)(2,1)S(1)} %get-tuple-element.37), channel_id=1, source_target_pairs={{0,2},{1,3},{2,0},{3,1},{4,6},{5,7},{6,4},{7,5},{8,10},{9,11},{10,... | collective-permute-start | bytes 442376 | tf_op jit(solution)/shard_map/ppermute | solution.py:470
  12.8 14.8 %collective-permute-start.3 = (bf16[256,1024]{1,0:T(8,128)(2,1)S(1)}, bf16[256,1024]{1,0:T(8,128)(2,1)S(1)}, u32[]{:S(2)}, u32[]{:S(2)}) collective-permute-start(bf16[256,1024]{1,0:T(8,128)(2,1)S(1)} %shard_map.79.refs_1_.refs_0_), channel_id=1, source_target_pairs={{0,4},{1,5},{2,6},{3,7},{4,8},{5,9},{6,10},{7,11},{8,12},{9,13},{1... | collective-permute-start | bytes 1572872 | tf_op jit(solution)/shard_map/ppermute | solution.py:470
  14.4 13.3 %collective-permute-start.4 = (bf16[256,1024]{1,0:T(8,128)(2,1)S(1)}, bf16[256,1024]{1,0:T(8,128)(2,1)S(1)}, u32[]{:S(2)}, u32[]{:S(2)}) collective-permute-start(bf16[256,1024]{1,0:T(8,128)(2,1)S(1)} %shard_map.79.refs_1_.refs_0_), channel_id=1, source_target_pairs={{0,12},{1,13},{2,14},{3,15},{4,0},{5,1},{6,2},{7,3},{8,4},{9,5},{1... | collective-permute-start | bytes 1572872 | tf_op jit(solution)/shard_map/ppermute | solution.py:470
  16.1 6.1 %collective-permute-start.10 = (bf16[4,32,128]{2,1,0:T(8,128)(2,1)S(1)}, bf16[4,32,128]{2,1,0:T(8,128)(2,1)S(1)}, u32[]{:S(2)}, u32[]{:S(2)}) collective-permute-start(bf16[4,32,128]{2,1,0:T(8,128)(2,1)S(1)} %shard_map.77.refs_4_.after), channel_id=1, source_target_pairs={{16,3},{20,7},{24,11},{28,15},{32,19},{36,23},{40,27},{44,31},{48,... | collective-permute-start | bytes 98312 | tf_op jit(solution)/shard_map/ppermute | solution.py:520
  19.3 16.7 %collective-permute-start.7 = (bf16[512,128]{1,0:T(8,128)(2,1)S(1)}, bf16[512,128]{1,0:T(8,128)(2,1)S(1)}, u32[]{:S(2)}, u32[]{:S(2)}) collective-permute-start(bf16[512,128]{1,0:T(8,128)(2,1)S(1)} %shard_map.81.refs_0_), channel_id=1, source_target_pairs={{0,1},{1,0},{2,3},{3,2},{4,5},{5,4},{6,7},{7,6},{8,9},{9,8},{10,11... | collective-permute-start | bytes 393224 | tf_op jit(solution)/shard_map/ppermute | solution.py:470
  19.4 16.6 %collective-permute-start.8 = (bf16[512,128]{1,0:T(8,128)(2,1)S(1)}, bf16[512,128]{1,0:T(8,128)(2,1)S(1)}, u32[]{:S(2)}, u32[]{:S(2)}) collective-permute-start(bf16[512,128]{1,0:T(8,128)(2,1)S(1)} %shard_map.81.refs_0_), channel_id=1, source_target_pairs={{0,2},{1,3},{2,0},{3,1},{4,6},{5,7},{6,4},{7,5},{8,10},{9,11},{10,... | collective-permute-start | bytes 393224 | tf_op jit(solution)/shard_map/ppermute | solution.py:470
  22.2 13.8 %collective-permute-start.9 = (bf16[512,128]{1,0:T(8,128)(2,1)S(1)}, bf16[512,128]{1,0:T(8,128)(2,1)S(1)}, u32[]{:S(2)}, u32[]{:S(2)}) collective-permute-start(bf16[512,128]{1,0:T(8,128)(2,1)S(1)} %shard_map.81.refs_0_), channel_id=1, source_target_pairs={{0,3},{1,2},{2,1},{3,0},{4,7},{5,6},{6,5},{7,4},{8,11},{9,10},{10,... | collective-permute-start | bytes 393224 | tf_op jit(solution)/shard_map/ppermute | solution.py:470
  27.7 10.1 %collective-permute-start.5 = (bf16[128,1024]{1,0:T(8,128)(2,1)S(1)}, bf16[128,1024]{1,0:T(8,128)(2,1)S(1)}, u32[]{:S(2)}, u32[]{:S(2)}) collective-permute-start(bf16[128,1024]{1,0:T(8,128)(2,1)S(1)} %get-tuple-element.39), channel_id=1, source_target_pairs={{0,4},{1,5},{2,6},{3,7},{4,8},{5,9},{6,10},{7,11},{8,12},{9,13},{1... | collective-permute-start | bytes 786440 | tf_op jit(solution)/shard_map/ppermute | solution.py:470
  29.2 8.5 %collective-permute-start.6 = (bf16[128,1024]{1,0:T(8,128)(2,1)S(1)}, bf16[128,1024]{1,0:T(8,128)(2,1)S(1)}, u32[]{:S(2)}, u32[]{:S(2)}) collective-permute-start(bf16[128,1024]{1,0:T(8,128)(2,1)S(1)} %get-tuple-element.40), channel_id=1, source_target_pairs={{0,12},{1,13},{2,14},{3,15},{4,0},{5,1},{6,2},{7,3},{8,4},{9,5},{1... | collective-permute-start | bytes 786440 | tf_op jit(solution)/shard_map/ppermute | solution.py:470
  46.3 12.8 %collective-permute-start.11 = (bf16[560,128]{1,0:T(8,128)(2,1)S(1)}, bf16[560,128]{1,0:T(8,128)(2,1)S(1)}, u32[]{:S(2)}, u32[]{:S(2)}) collective-permute-start(bf16[560,128]{1,0:T(8,128)(2,1)S(1)} %get-tuple-element.59), channel_id=1, source_target_pairs={{0,1},{1,0},{2,3},{3,2},{4,5},{5,4},{6,7},{7,6},{8,9},{9,8},{10,11... | collective-permute-start | bytes 430088 | tf_op jit(solution)/shard_map/ppermute | solution.py:470
  46.4 12.7 %collective-permute-start.12 = (bf16[560,128]{1,0:T(8,128)(2,1)S(1)}, bf16[560,128]{1,0:T(8,128)(2,1)S(1)}, u32[]{:S(2)}, u32[]{:S(2)}) collective-permute-start(bf16[560,128]{1,0:T(8,128)(2,1)S(1)} %get-tuple-element.60), channel_id=1, source_target_pairs={{0,2},{1,3},{2,0},{3,1},{4,6},{5,7},{6,4},{7,5},{8,10},{9,11},{10,... | collective-permute-start | bytes 430088 | tf_op jit(solution)/shard_map/ppermute | solution.py:470
  48.8 10.3 %collective-permute-start.13 = (bf16[560,128]{1,0:T(8,128)(2,1)S(1)}, bf16[560,128]{1,0:T(8,128)(2,1)S(1)}, u32[]{:S(2)}, u32[]{:S(2)}) collective-permute-start(bf16[560,128]{1,0:T(8,128)(2,1)S(1)} %get-tuple-element.61), channel_id=1, source_target_pairs={{0,3},{1,2},{2,1},{3,0},{4,7},{5,6},{6,5},{7,4},{8,11},{9,10},{10,... | collective-permute-start | bytes 430088 | tf_op jit(solution)/shard_map/ppermute | solution.py:470
  59.3 4.2 %collective-permute-start.14 = (bf16[176,128]{1,0:T(8,128)(2,1)S(1)}, bf16[176,128]{1,0:T(8,128)(2,1)S(1)}, u32[]{:S(2)}, u32[]{:S(2)}) collective-permute-start(bf16[176,128]{1,0:T(8,128)(2,1)S(1)} %get-tuple-element.63), channel_id=1, source_target_pairs={{0,16},{16,32},{32,48},{48,0},{1,17},{17,33},{33,49},{49,1},{2,18}... | collective-permute-start | bytes 135176 | tf_op jit(solution)/shard_map/ppermute | solution.py:568
  59.5 5.6 %collective-permute-start.15 = (bf16[176,128]{1,0:T(8,128)(2,1)S(1)}, bf16[176,128]{1,0:T(8,128)(2,1)S(1)}, u32[]{:S(2)}, u32[]{:S(2)}) collective-permute-start(bf16[176,128]{1,0:T(8,128)(2,1)S(1)} %get-tuple-element.64), channel_id=1, source_target_pairs={{0,32},{16,48},{32,0},{48,16},{1,33},{17,49},{33,1},{49,17},{2,34}... | collective-permute-start | bytes 135176 | tf_op jit(solution)/shard_map/ppermute | solution.py:568
  62.2 5.3 %collective-permute-start.16 = (bf16[176,128]{1,0:T(8,128)(2,1)S(1)}, bf16[176,128]{1,0:T(8,128)(2,1)S(1)}, u32[]{:S(2)}, u32[]{:S(2)}) collective-permute-start(bf16[176,128]{1,0:T(8,128)(2,1)S(1)} %get-tuple-element.65), channel_id=1, source_target_pairs={{0,48},{16,0},{32,16},{48,32},{1,49},{17,1},{33,17},{49,33},{2,50}... | collective-permute-start | bytes 135176 | tf_op jit(solution)/shard_map/ppermute | solution.py:568

commit v11 on v10

--- a/solution.py
+++ b/solution.py
@@ -17,7 +17,7 @@
 GROUP = 16
 OWN = 64
 KEPT = 4 * OWN
-STEP = 4
+STEP = 16
 EARLY = 12
 MIB = 1024 * 1024
 
@@ -494,13 +494,6 @@
     last, following = send(block, 1, 0), send(block, 3, 0)
     bundle = hold(bundle, block)
     shared = [bundle] + [send(bundle, 0, other) for other in (1, 2, 3)]
-    half = ((KEPT // 2, FLAT), bf16)
-    upper, lower = call(
-        halve_kernel, [half, half], [], 1_000_000, 4, last, following, tile, loose=1
-    )
-    first_blocks = (block, following, last)
-    last_blocks = (send(upper, 1, 0), send(lower, 3, 0))
-
     plane = ((ROWS, LANES), f32)
     patches, tissue, scale, norm, inv_square, inv_density, anch, anch_t = call(
         patch_kernel,
@@ -528,6 +521,12 @@
         18,
         patches, tissue, scale, norm, inv_density, anch,
     )
+    half = ((KEPT // 2, FLAT), bf16)
+    upper, lower = call(
+        halve_kernel, [half, half], [], 1_000_000, 4, last, following, whitened, loose=1
+    )
+    first_blocks = (block, following, last)
+    last_blocks = (send(upper, 1, 0), send(lower, 3, 0))
     rows = ((512, 128), bf16)
     partial, *early = call(
         early_kernel,

time: 84.5 us -> 83.3 us (0.986)
  waiting for transfers between devices: 11.9 us -> 16.2 us
  starting transfers between devices: 22.2 us -> 18.8 us
  Pallas kernels: 18.8 us -> 15.8 us
    ppermute x13, waiting for transfers between devices: 6.11 us -> 9.99 us  [send(): return lax.ppermute(value, CHAN, route(dx, other))]
    ppermute x13, starting transfers between devices: 16.1 us -> 12.9 us  [send(): return lax.ppermute(value, CHAN, route(dx, other))]
    pallas_call x14, Pallas kernels: 18.8 us -> 15.8 us  [call(): pl.pallas_call(kernel, out_shape=[jax.ShapeDtypeStruct(shape, dtype) for...]
  transfers between devices with their start and end apart: 17 -> 17, of which waited for: 7 -> 9; matrix products, arithmetic and copies ran while one was open for 3% -> 3% of each run, Pallas kernels for 10% -> 8%
where the time goes in v11:
time: 83.3 us; the launch traced here: 82.8 us
  blocking collectives  26.6 us (32%)
  starting transfers between devices  18.8 us (23%)
  waiting for transfers between devices  16.2 us (19%)
  Pallas kernels  15.8 us (19%)
  local copies, waits for them, and re-layouts  2.82 us (3%)
  other arithmetic  1.76 us (2%)
    pallas_call x14, Pallas kernels, call(): pl.pallas_call(kernel, out_shape=[jax.ShapeDtypeStruct(shape, dtype) for...  15.8 us
    all_to_all x1, blocking collectives, shards(): lax.all_to_all(packed, 'z_hi', 0, 0)  15.7 us
    ppermute x13, starting transfers between devices, send(): return lax.ppermute(value, CHAN, route(dx, other))  12.9 us
    all_to_all x1, blocking collectives, shards(): parts = lax.all_to_all(image_part.reshape(16, 8, LANES), CHAN, 0, 0)  11 us
    ppermute x13, waiting for transfers between devices, send(): return lax.ppermute(value, CHAN, route(dx, other))  9.99 us
    ppermute x3, waiting for transfers between devices, shards(): lax.ppermute(value, 'y', [(y, (y + step) % 4) for y in range(4)])  5.25 us
    ppermute x1, starting transfers between devices, shards(): lax.ppermute(tile, STRIPS + CHAN, seams())  3.13 us
    unnamed x5, local copies, waits for them, and re-layouts  2.82 us
  transfers between devices with their start and end apart: 17, of which 9 were waited for; matrix products, arithmetic and copies ran while one was open for 3% of the time, Pallas kernels for 8%

profile of v11, /device:TPU:24, one launch (start us, length us, event | category | flops | bytes accessed | tf_op | source)
XLA Modules:
  0.0 82.8 jit_solution(18222369066246996320)
XLA Ops:
  0.6 1.0 %copy-done = bf16[64,16,256]{2,1,0:T(8,128)(2,1)S(1)} copy-done((bf16[64,16,256]{2,1,0:T(8,128)(2,1)S(1)}, bf16[64,16,256]{2,1,0:T(8,128)(2,1)}, u32[]{:S(2)}) %copy-start) | copy-done | bytes 524312
  1.7 0.7 copy-done.1
  2.4 1.0 %shard_map.76 = (bf16[64,1152]{1,0:T(8,128)(2,1)S(1)}, bf16[64,1152]{1,0:T(8,128)(2,1)S(1)}, bf16[64,1152]{1,0:T(8,128)(2,1)S(1)}, bf16[64,1152]{1,0:T(8,128)(2,1)S(1)}) custom-call(bf16[64,16,256]{2,1,0:T(8,128)(2,1)S(1)} %copy-done, bf16[64,75]{1,0:T(8,128)(2,1)S(1)} %copy-done.1), custom_call_target="tpu_custom_call" | custom-call | flops 1000000 | bytes 1123712 | tf_op jit(solution)/shard_map/pallas_call | solution.py:456
  3.4 1.5 %collective-permute-start.2 = (bf16[64,1152]{1,0:T(8,128)(2,1)S(1)}, bf16[64,1152]{1,0:T(8,128)(2,1)S(1)}, u32[]{:S(2)}, u32[]{:S(2)}) collective-permute-start(bf16[64,1152]{1,0:T(8,128)(2,1)S(1)} %get-tuple-element.38.refs_0_.after), channel_id=1, source_target_pairs={{0,3},{1,2},{2,1},{3,0},{4,7},{5,6},{6,5},{7,4},{8,11},{9,10},{10,... | collective-permute-start | bytes 442376 | tf_op jit(solution)/shard_map/ppermute | solution.py:470
  4.8 0.7 collective-permute-start
  5.6 0.8 %convert_bitcast_fusion = bf16[1,32,512]{2,1,0:T(8,128)(2,1)S(1)} fusion(s32[32,512]{1,0:T(8,128)} %param.6), kind=kLoop, calls=%fused_computation.1 | loop fusion | flops 16384 | bytes 98304 | tf_op jit(solution)/shard_map/broadcast_in_dim | solution.py:481
  6.5 1.1 %copy.9.whiten = bf16[1024,64]{1,0:T(8,128)(2,1)S(1)} copy(bf16[1024,64]{0,1:T(8,128)(2,1)} %param.8) | data formatting | bytes 262144 | tf_op args[3]
  7.5 0.9 %pad_maximum_fusion.stacked = bf16[4,32,512]{2,1,0:T(8,128)(2,1)S(1)} fusion(bf16[1,32,512]{2,1,0:T(8,128)(2,1)S(1)} %convert_bitcast_fusion, bf16[3,32,512]{2,1,0:T(8,128)(2,1)} %param.5), kind=kLoop, calls=%fused_computation | loop fusion | flops 65536 | bytes 262144 | tf_op jit(solution)/shard_map/concatenate | solution.py:481
  9.2 3.6 %collective-permute-done.1.refs_2_ = bf16[64,1152]{1,0:T(8,128)(2,1)S(1)} collective-permute-done((bf16[64,1152]{1,0:T(8,128)(2,1)S(1)}, bf16[64,1152]{1,0:T(8,128)(2,1)S(1)}, u32[]{:S(2)}, u32[]{:S(2)}) %collective-permute-start.1) | collective-permute-done | bytes 147488 | tf_op jit(solution)/shard_map/ppermute | solution.py:470
  12.8 1.6 %collective-permute-start.3 = (bf16[256,1024]{1,0:T(8,128)(2,1)S(1)}, bf16[256,1024]{1,0:T(8,128)(2,1)S(1)}, u32[]{:S(2)}, u32[]{:S(2)}) collective-permute-start(bf16[256,1024]{1,0:T(8,128)(2,1)S(1)} %shard_map.79.refs_1_.refs_0_), channel_id=1, source_target_pairs={{0,4},{1,5},{2,6},{3,7},{4,8},{5,9},{6,10},{7,11},{8,12},{9,13},{1... | collective-permute-start | bytes 1572872 | tf_op jit(solution)/shard_map/ppermute | solution.py:470
  14.4 1.7 %collective-permute-start.4 = (bf16[256,1024]{1,0:T(8,128)(2,1)S(1)}, bf16[256,1024]{1,0:T(8,128)(2,1)S(1)}, u32[]{:S(2)}, u32[]{:S(2)}) collective-permute-start(bf16[256,1024]{1,0:T(8,128)(2,1)S(1)} %shard_map.79.refs_1_.refs_0_), channel_id=1, source_target_pairs={{0,12},{1,13},{2,14},{3,15},{4,0},{5,1},{6,2},{7,3},{8,4},{9,5},{1... | collective-permute-start | bytes 1572872 | tf_op jit(solution)/shard_map/ppermute | solution.py:470
  16.1 3.1 %collective-permute-start.5 = (bf16[4,32,128]{2,1,0:T(8,128)(2,1)S(1)}, bf16[4,32,128]{2,1,0:T(8,128)(2,1)S(1)}, u32[]{:S(2)}, u32[]{:S(2)}) collective-permute-start(bf16[4,32,128]{2,1,0:T(8,128)(2,1)S(1)} %shard_map.77.refs_4_), channel_id=1, source_target_pairs={{16,3},{20,7},{24,11},{28,15},{32,19},{36,23},{40,27},{44,31},{48,... | collective-permute-start | bytes 98312 | tf_op jit(solution)/shard_map/ppermute | solution.py:513
  19.3 2.1 %collective-permute-start.10 = (bf16[512,128]{1,0:T(8,128)(2,1)S(1)}, bf16[512,128]{1,0:T(8,128)(2,1)S(1)}, u32[]{:S(2)}, u32[]{:S(2)}) collective-permute-start(bf16[512,128]{1,0:T(8,128)(2,1)S(1)} %shard_map.83.refs_0_), channel_id=1, source_target_pairs={{0,3},{1,2},{2,1},{3,0},{4,7},{5,6},{6,5},{7,4},{8,11},{9,10},{10,... | collective-permute-start | bytes 393224 | tf_op jit(solution)/shard_map/ppermute | solution.py:470
  21.3 0.9 %collective-permute-done.5.beyond = bf16[4,32,128]{2,1,0:T(8,128)(2,1)S(1)} collective-permute-done((bf16[4,32,128]{2,1,0:T(8,128)(2,1)S(1)}, bf16[4,32,128]{2,1,0:T(8,128)(2,1)S(1)}, u32[]{:S(2)}, u32[]{:S(2)}) %collective-permute-start.5) | collective-permute-done | bytes 32800 | tf_op jit(solution)/shard_map/ppermute | solution.py:513
  22.3 1.2 %shard_map.80 = (bf16[576,256]{1,0:T(8,128)(2,1)S(1)}, f32[32,256]{1,0:T(8,128)S(1)}, f32[32,256]{1,0:T(8,128)S(1)}, f32[32,256]{1,0:T(8,128)S(1)}, f32[32,256]{...) custom-call(bf16[4,32,512]{2,1,0:T(8,128)(2,1)S(1)} %pad_maximum_fusion.stacked, ...), custom_call_target="tpu_custom_call" | custom-call | flops 1000000000 | bytes 1265664 | tf_op jit(solution)/shard_map/pallas_call | solution.py:456
  23.4 3.6 %shard_map.81 = (bf16[32,256,256]{2,1,0:T(8,128)(2,1)S(1)}, bf16[256,1024]{1,0:T(8,128)(2,1)S(1)}) custom-call(bf16[576,256]{1,0:T(8,128)(2,1)S(1)} %get-tuple-element.39.patches, f32[32,256]{1,0:T(8,128)S(1)} %get-tuple-element.40.tissue, f32[32,256]{1,0:T(8,128)S(1)} %get-tuple-element.41.scale, f32[32,256]{1,0:T(8,128)S(1)} %get-tuple-element.42.norm, ...), custom_call_target="tpu_custom_call" | custom-call | flops 3000000000 | bytes 5156864 | tf_op jit(solution)/shard_map/pallas_call | solution.py:456
  27.0 0.6 collective-permute-done.3.first.refs_2_
  27.7 1.6 %collective-permute-start.6 = (bf16[128,1024]{1,0:T(8,128)(2,1)S(1)}, bf16[128,1024]{1,0:T(8,128)(2,1)S(1)}, u32[]{:S(2)}, u32[]{:S(2)}) collective-permute-start(bf16[128,1024]{1,0:T(8,128)(2,1)S(1)} %get-tuple-element.46), channel_id=1, source_target_pairs={{0,4},{1,5},{2,6},{3,7},{4,8},{5,9},{6,10},{7,11},{8,12},{9,13},{1... | collective-permute-start | bytes 786440 | tf_op jit(solution)/shard_map/ppermute | solution.py:470
  29.2 1.7 %collective-permute-start.7 = (bf16[128,1024]{1,0:T(8,128)(2,1)S(1)}, bf16[128,1024]{1,0:T(8,128)(2,1)S(1)}, u32[]{:S(2)}, u32[]{:S(2)}) collective-permute-start(bf16[128,1024]{1,0:T(8,128)(2,1)S(1)} %get-tuple-element.47), channel_id=1, source_target_pairs={{0,12},{1,13},{2,14},{3,15},{4,0},{5,1},{6,2},{7,3},{8,4},{9,5},{1... | collective-permute-start | bytes 786440 | tf_op jit(solution)/shard_map/ppermute | solution.py:470
  31.0 0.7 shard_map.84.refs_3_.wturned
  31.7 1.1 %shard_map.85 = (f32[256,1024]{1,0:T(8,128)S(1)}, bf16[512,128]{1,0:T(8,128)(2,1)S(1)}, bf16[512,128]{1,0:T(8,128)(2,1)S(1)}, bf16[512,128]{1,0:T(8,128)(2,1)S(1)}, bf16[512,128]{1,0:T(8,128)(2,1)S(1)}) custom-call(bf16[256,1024]{1,0:T(8,128)(2,1)S(1)} %shard_map.79.refs_1_.refs_0_, bf16[256,1024]{1,0:T(8,128)(2,1)S(1)} %collective-permute-done.4.second.refs_1_, ...), custom_call_target="tpu_custom_call" | custom-call | flops 2000000000 | bytes 4194304 | tf_op jit(solution)/shard_map/pallas_call | solution.py:456
  32.7 4.6 %collective-permute-done.6.first.refs_0_ = bf16[128,1024]{1,0:T(8,128)(2,1)S(1)} collective-permute-done((bf16[128,1024]{1,0:T(8,128)(2,1)S(1)}, bf16[128,1024]{1,0:T(8,128)(2,1)S(1)}, u32[]{:S(2)}, u32[]{:S(2)}) %collective-permute-start.6) | collective-permute-done | bytes 262176 | tf_op jit(solution)/shard_map/ppermute | solution.py:470
  37.4 0.6 collective-permute-done.7.second.refs_1_
  38.0 6.5 %shard_map.86 = (f32[80,256]{1,0:T(8,128)S(1)}, bf16[128,256]{1,0:T(8,128)(2,1)S(1)}) custom-call(bf16[128,1024]{1,0:T(8,128)(2,1)S(1)} %collective-permute-done.6.first.refs_0_, bf16[128,1024]{1,0:T(8,128)(2,1)S(1)} %collective-permute-done.7.second.refs_1_, f32[256,1024]{1,0:T(8,128)S(1)} %get-tuple-element.48.partial, ...), custom_call_target="tpu_custom_call" | custom-call | flops 5000000000 | bytes 6811648 | tf_op jit(solution)/shard_map/pallas_call | solution.py:456
  45.1 1.3 %collective-permute-start.12 = (bf16[560,128]{1,0:T(8,128)(2,1)S(1)}, bf16[560,128]{1,0:T(8,128)(2,1)S(1)}, u32[]{:S(2)}, u32[]{:S(2)}) collective-permute-start(bf16[560,128]{1,0:T(8,128)(2,1)S(1)} %get-tuple-element.60), channel_id=1, source_target_pairs={{0,2},{1,3},{2,0},{3,1},{4,6},{5,7},{6,4},{7,5},{8,10},{9,11},{10,... | collective-permute-start | bytes 430088 | tf_op jit(solution)/shard_map/ppermute | solution.py:470
  46.9 11.0 %all_to_all.10.parts = bf16[16,8,256]{2,1,0:T(8,128)(2,1)S(1)} all-to-all(bf16[16,8,256]{2,1,0:T(8,128)(2,1)S(1)} %bitcast.3), channel_id=1, replica_groups=mesh['z_hi'=4,'y'=4,'x'=4,'z_lo'=2,'core'=2] {'x','z_lo','core'}, dimensions={0} | all-to-all | bytes 131072 | tf_op jit(solution)/shard_map/all_to_all | solution.py:548
  58.2 2.7 %collective-permute-start.15 = (bf16[176,128]{1,0:T(8,128)(2,1)S(1)}, bf16[176,128]{1,0:T(8,128)(2,1)S(1)}, u32[]{:S(2)}, u32[]{:S(2)}) collective-permute-start(bf16[176,128]{1,0:T(8,128)(2,1)S(1)} %get-tuple-element.64), channel_id=1, source_target_pairs={{0,32},{16,48},{32,0},{48,16},{1,33},{17,49},{33,1},{49,17},{2,34}... | collective-permute-start | bytes 135176 | tf_op jit(solution)/shard_map/ppermute | solution.py:567
  60.9 1.4 %collective-permute-done.14.one = bf16[176,128]{1,0:T(8,128)(2,1)S(1)} collective-permute-done((bf16[176,128]{1,0:T(8,128)(2,1)S(1)}, bf16[176,128]{1,0:T(8,128)(2,1)S(1)}, u32[]{:S(2)}, u32[]{:S(2)}) %collective-permute-start.14) | collective-permute-done | bytes 45088 | tf_op jit(solution)/shard_map/ppermute | solution.py:567
  62.3 1.5 %collective-permute-done.15.two = bf16[176,128]{1,0:T(8,128)(2,1)S(1)} collective-permute-done((bf16[176,128]{1,0:T(8,128)(2,1)S(1)}, bf16[176,128]{1,0:T(8,128)(2,1)S(1)}, u32[]{:S(2)}, u32[]{:S(2)}) %collective-permute-start.15) | collective-permute-done | bytes 45088 | tf_op jit(solution)/shard_map/ppermute | solution.py:567
  63.8 2.3 %collective-permute-done.16.three = bf16[176,128]{1,0:T(8,128)(2,1)S(1)} collective-permute-done((bf16[176,128]{1,0:T(8,128)(2,1)S(1)}, bf16[176,128]{1,0:T(8,128)(2,1)S(1)}, u32[]{:S(2)}, u32[]{:S(2)}) %collective-permute-start.16) | collective-permute-done | bytes 45088 | tf_op jit(solution)/shard_map/ppermute | solution.py:567
  66.2 15.7 %all_to_all.11.received = bf16[4,80,128]{2,1,0:T(8,128)(2,1)S(1)} all-to-all(bf16[4,80,128]{2,1,0:T(8,128)(2,1)S(1)} %shard_map.89), channel_id=1, replica_groups=mesh['z_hi'=4,'y'=4,'x'=4,'z_lo'=2,'core'=2] {'z_hi'}, dimensions={0} | all-to-all | bytes 163840 | tf_op jit(solution)/shard_map/all_to_all | solution.py:580
  81.9 0.9 %shard_map.90 = (f32[64,75]{1,0:T(8,128)}, f32[64,64]{1,0:T(8,128)}, f32[3,2,512]{2,1,0:T(2,128)}) custom-call(bf16[4,80,128]{2,1,0:T(8,128)(2,1)S(1)} %all_to_all.11.received, f32[8,512]{1,0:T(8,128)S(1)} %get-tuple-element.66.middle), custom_call_target="tpu_custom_call" | custom-call | flops 1000000 | bytes 146176 | tf_op jit(solution)/shard_map/pallas_call | solution.py:456
  (26 shorter events, 2.4 us)
Async XLA Ops:
  0.6 1.0 %copy-start = (bf16[64,16,256]{2,1,0:T(8,128)(2,1)S(1)}, bf16[64,16,256]{2,1,0:T(8,128)(2,1)}, u32[]{:S(2)}) copy-start(bf16[64,16,256]{2,1,0:T(8,128)(2,1)} %cotangent.1) | copy-start | bytes 1572868
  1.7 0.7 copy-start.1
  3.4 5.8 %collective-permute-start.2 = (bf16[64,1152]{1,0:T(8,128)(2,1)S(1)}, bf16[64,1152]{1,0:T(8,128)(2,1)S(1)}, u32[]{:S(2)}, u32[]{:S(2)}) collective-permute-start(bf16[64,1152]{1,0:T(8,128)(2,1)S(1)} %get-tuple-element.38.refs_0_.after), channel_id=1, source_target_pairs={{0,3},{1,2},{2,1},{3,0},{4,7},{5,6},{6,5},{7,4},{8,11},{9,10},{10,... | collective-permute-start | bytes 442376 | tf_op jit(solution)/shard_map/ppermute | solution.py:470
  4.8 4.4 %collective-permute-start = (bf16[64,1152]{1,0:T(8,128)(2,1)S(1)}, bf16[64,1152]{1,0:T(8,128)(2,1)S(1)}, u32[]{:S(2)}, u32[]{:S(2)}) collective-permute-start(bf16[64,1152]{1,0:T(8,128)(2,1)S(1)} %get-tuple-element.36), channel_id=1, source_target_pairs={{0,1},{1,0},{2,3},{3,2},{4,5},{5,4},{6,7},{7,6},{8,9},{9,8},{10,11... | collective-permute-start | bytes 442376 | tf_op jit(solution)/shard_map/ppermute | solution.py:470
  5.5 7.3 %collective-permute-start.1 = (bf16[64,1152]{1,0:T(8,128)(2,1)S(1)}, bf16[64,1152]{1,0:T(8,128)(2,1)S(1)}, u32[]{:S(2)}, u32[]{:S(2)}) collective-permute-start(bf16[64,1152]{1,0:T(8,128)(2,1)S(1)} %get-tuple-element.37), channel_id=1, source_target_pairs={{0,2},{1,3},{2,0},{3,1},{4,6},{5,7},{6,4},{7,5},{8,10},{9,11},{10,... | collective-permute-start | bytes 442376 | tf_op jit(solution)/shard_map/ppermute | solution.py:470
  12.8 14.8 %collective-permute-start.3 = (bf16[256,1024]{1,0:T(8,128)(2,1)S(1)}, bf16[256,1024]{1,0:T(8,128)(2,1)S(1)}, u32[]{:S(2)}, u32[]{:S(2)}) collective-permute-start(bf16[256,1024]{1,0:T(8,128)(2,1)S(1)} %shard_map.79.refs_1_.refs_0_), channel_id=1, source_target_pairs={{0,4},{1,5},{2,6},{3,7},{4,8},{5,9},{6,10},{7,11},{8,12},{9,13},{1... | collective-permute-start | bytes 1572872 | tf_op jit(solution)/shard_map/ppermute | solution.py:470
  14.4 13.3 %collective-permute-start.4 = (bf16[256,1024]{1,0:T(8,128)(2,1)S(1)}, bf16[256,1024]{1,0:T(8,128)(2,1)S(1)}, u32[]{:S(2)}, u32[]{:S(2)}) collective-permute-start(bf16[256,1024]{1,0:T(8,128)(2,1)S(1)} %shard_map.79.refs_1_.refs_0_), channel_id=1, source_target_pairs={{0,12},{1,13},{2,14},{3,15},{4,0},{5,1},{6,2},{7,3},{8,4},{9,5},{1... | collective-permute-start | bytes 1572872 | tf_op jit(solution)/shard_map/ppermute | solution.py:470
  16.1 6.2 %collective-permute-start.5 = (bf16[4,32,128]{2,1,0:T(8,128)(2,1)S(1)}, bf16[4,32,128]{2,1,0:T(8,128)(2,1)S(1)}, u32[]{:S(2)}, u32[]{:S(2)}) collective-permute-start(bf16[4,32,128]{2,1,0:T(8,128)(2,1)S(1)} %shard_map.77.refs_4_), channel_id=1, source_target_pairs={{16,3},{20,7},{24,11},{28,15},{32,19},{36,23},{40,27},{44,31},{48,... | collective-permute-start | bytes 98312 | tf_op jit(solution)/shard_map/ppermute | solution.py:513
  19.3 11.7 %collective-permute-start.10 = (bf16[512,128]{1,0:T(8,128)(2,1)S(1)}, bf16[512,128]{1,0:T(8,128)(2,1)S(1)}, u32[]{:S(2)}, u32[]{:S(2)}) collective-permute-start(bf16[512,128]{1,0:T(8,128)(2,1)S(1)} %shard_map.83.refs_0_), channel_id=1, source_target_pairs={{0,3},{1,2},{2,1},{3,0},{4,7},{5,6},{6,5},{7,4},{8,11},{9,10},{10,... | collective-permute-start | bytes 393224 | tf_op jit(solution)/shard_map/ppermute | solution.py:470
  21.3 9.7 %collective-permute-start.8 = (bf16[512,128]{1,0:T(8,128)(2,1)S(1)}, bf16[512,128]{1,0:T(8,128)(2,1)S(1)}, u32[]{:S(2)}, u32[]{:S(2)}) collective-permute-start(bf16[512,128]{1,0:T(8,128)(2,1)S(1)} %shard_map.83.refs_0_), channel_id=1, source_target_pairs={{0,1},{1,0},{2,3},{3,2},{4,5},{5,4},{6,7},{7,6},{8,9},{9,8},{10,11... | collective-permute-start | bytes 393224 | tf_op jit(solution)/shard_map/ppermute | solution.py:470
  22.3 8.7 %collective-permute-start.9 = (bf16[512,128]{1,0:T(8,128)(2,1)S(1)}, bf16[512,128]{1,0:T(8,128)(2,1)S(1)}, u32[]{:S(2)}, u32[]{:S(2)}) collective-permute-start(bf16[512,128]{1,0:T(8,128)(2,1)S(1)} %shard_map.83.refs_0_), channel_id=1, source_target_pairs={{0,2},{1,3},{2,0},{3,1},{4,6},{5,7},{6,4},{7,5},{8,10},{9,11},{10,... | collective-permute-start | bytes 393224 | tf_op jit(solution)/shard_map/ppermute | solution.py:470
  27.7 9.7 %collective-permute-start.6 = (bf16[128,1024]{1,0:T(8,128)(2,1)S(1)}, bf16[128,1024]{1,0:T(8,128)(2,1)S(1)}, u32[]{:S(2)}, u32[]{:S(2)}) collective-permute-start(bf16[128,1024]{1,0:T(8,128)(2,1)S(1)} %get-tuple-element.46), channel_id=1, source_target_pairs={{0,4},{1,5},{2,6},{3,7},{4,8},{5,9},{6,10},{7,11},{8,12},{9,13},{1... | collective-permute-start | bytes 786440 | tf_op jit(solution)/shard_map/ppermute | solution.py:470
  29.2 8.8 %collective-permute-start.7 = (bf16[128,1024]{1,0:T(8,128)(2,1)S(1)}, bf16[128,1024]{1,0:T(8,128)(2,1)S(1)}, u32[]{:S(2)}, u32[]{:S(2)}) collective-permute-start(bf16[128,1024]{1,0:T(8,128)(2,1)S(1)} %get-tuple-element.47), channel_id=1, source_target_pairs={{0,12},{1,13},{2,14},{3,15},{4,0},{5,1},{6,2},{7,3},{8,4},{9,5},{1... | collective-permute-start | bytes 786440 | tf_op jit(solution)/shard_map/ppermute | solution.py:470
  45.0 12.9 %collective-permute-start.11 = (bf16[560,128]{1,0:T(8,128)(2,1)S(1)}, bf16[560,128]{1,0:T(8,128)(2,1)S(1)}, u32[]{:S(2)}, u32[]{:S(2)}) collective-permute-start(bf16[560,128]{1,0:T(8,128)(2,1)S(1)} %get-tuple-element.59), channel_id=1, source_target_pairs={{0,1},{1,0},{2,3},{3,2},{4,5},{5,4},{6,7},{7,6},{8,9},{9,8},{10,11... | collective-permute-start | bytes 430088 | tf_op jit(solution)/shard_map/ppermute | solution.py:470
  45.1 12.8 %collective-permute-start.12 = (bf16[560,128]{1,0:T(8,128)(2,1)S(1)}, bf16[560,128]{1,0:T(8,128)(2,1)S(1)}, u32[]{:S(2)}, u32[]{:S(2)}) collective-permute-start(bf16[560,128]{1,0:T(8,128)(2,1)S(1)} %get-tuple-element.60), channel_id=1, source_target_pairs={{0,2},{1,3},{2,0},{3,1},{4,6},{5,7},{6,4},{7,5},{8,10},{9,11},{10,... | collective-permute-start | bytes 430088 | tf_op jit(solution)/shard_map/ppermute | solution.py:470
  46.4 11.5 %collective-permute-start.13 = (bf16[560,128]{1,0:T(8,128)(2,1)S(1)}, bf16[560,128]{1,0:T(8,128)(2,1)S(1)}, u32[]{:S(2)}, u32[]{:S(2)}) collective-permute-start(bf16[560,128]{1,0:T(8,128)(2,1)S(1)} %get-tuple-element.61), channel_id=1, source_target_pairs={{0,3},{1,2},{2,1},{3,0},{4,7},{5,6},{6,5},{7,4},{8,11},{9,10},{10,... | collective-permute-start | bytes 430088 | tf_op jit(solution)/shard_map/ppermute | solution.py:470
  58.1 4.2 %collective-permute-start.14 = (bf16[176,128]{1,0:T(8,128)(2,1)S(1)}, bf16[176,128]{1,0:T(8,128)(2,1)S(1)}, u32[]{:S(2)}, u32[]{:S(2)}) collective-permute-start(bf16[176,128]{1,0:T(8,128)(2,1)S(1)} %get-tuple-element.63), channel_id=1, source_target_pairs={{0,16},{16,32},{32,48},{48,0},{1,17},{17,33},{33,49},{49,1},{2,18}... | collective-permute-start | bytes 135176 | tf_op jit(solution)/shard_map/ppermute | solution.py:567
  58.2 5.6 %collective-permute-start.15 = (bf16[176,128]{1,0:T(8,128)(2,1)S(1)}, bf16[176,128]{1,0:T(8,128)(2,1)S(1)}, u32[]{:S(2)}, u32[]{:S(2)}) collective-permute-start(bf16[176,128]{1,0:T(8,128)(2,1)S(1)} %get-tuple-element.64), channel_id=1, source_target_pairs={{0,32},{16,48},{32,0},{48,16},{1,33},{17,49},{33,1},{49,17},{2,34}... | collective-permute-start | bytes 135176 | tf_op jit(solution)/shard_map/ppermute | solution.py:567
  60.9 5.3 %collective-permute-start.16 = (bf16[176,128]{1,0:T(8,128)(2,1)S(1)}, bf16[176,128]{1,0:T(8,128)(2,1)S(1)}, u32[]{:S(2)}, u32[]{:S(2)}) collective-permute-start(bf16[176,128]{1,0:T(8,128)(2,1)S(1)} %get-tuple-element.65), channel_id=1, source_target_pairs={{0,48},{16,0},{32,16},{48,32},{1,49},{17,1},{33,17},{49,33},{2,50}... | collective-permute-start | bytes 135176 | tf_op jit(solution)/shard_map/ppermute | solution.py:567

commit v12 on v11

--- a/solution.py
+++ b/solution.py
@@ -141,24 +141,15 @@
         part[:, FLAT : FLAT + 75] = anchors[...]
 
 
-def join_kernel(*refs):
-    *parts, _, _, joined = refs
-    start = 0
-    for ref in parts:
-        joined[start : start + ref.shape[0]] = ref[:, :FLAT]
-        start += ref.shape[0]
+def join_kernel(upper, lower, *refs):
+    refs[-1][:OWN] = upper[:, :FLAT]
+    refs[-1][OWN:] = lower[:, :FLAT]
 
 
 def bundle_kernel(whiten, after, bundle):
     del after
     bundle[:, :OWN] = whiten[0:512, :]
     bundle[:, OWN:] = whiten[512:1024, :]
-
-
-def halve_kernel(first, second, after, upper, lower):
-    del after
-    upper[...] = first[: KEPT // 2]
-    lower[...] = second[KEPT // 2 :]
 
 
 def rim_kernel(stacked, *refs):
@@ -290,7 +281,7 @@
 
 
 def early_kernel(*refs):
-    blocks, (wturned, whitened, partial, *sums) = refs[:3], refs[3:]
+    blocks, (wturned, whitened, partial, *sums) = refs[:6], refs[6:]
     for ref in sums:
         ref[...] = jnp.zeros_like(ref)
     for cols, stack in stacks(blocks):
@@ -482,17 +473,23 @@
     (tile,) = call(
         rim_kernel, [((4, ROWS, 128), bf16)], [], 1_000_000, 4, stacked, away[2], loose=1
     )
-    (block,) = call(
+    pair = [((2 * OWN, FLAT), bf16)]
+    (near,) = call(join_kernel, pair, [], 1_000_000, 4, *quarters[:2])
+    last, following = [send(near, 1, 0)], [send(near, 3, 0)]
+    (across,) = call(
         join_kernel,
-        [((KEPT, FLAT), bf16)],
+        pair,
         [],
         1_000_000,
         4,
-        *quarters, tile, bundle,
-        loose=2,
-    )
-    last, following = send(block, 1, 0), send(block, 3, 0)
-    bundle = hold(bundle, block)
+        *quarters[2:], tile, bundle, last[0], following[0],
+        loose=4,
+    )
+    last.append(send(across, 1, 0))
+    following.append(send(across, 3, 0))
+    first_blocks = (near, across, *following, *last)
+    last_blocks = (send(last[0], 1, 0), send(following[1], 3, 0))
+    bundle = hold(bundle, last[1])
     shared = [bundle] + [send(bundle, 0, other) for other in (1, 2, 3)]
     plane = ((ROWS, LANES), f32)
     patches, tissue, scale, norm, inv_square, inv_density, anch, anch_t = call(
@@ -521,12 +518,6 @@
         18,
         patches, tissue, scale, norm, inv_density, anch,
     )
-    half = ((KEPT // 2, FLAT), bf16)
-    upper, lower = call(
-        halve_kernel, [half, half], [], 1_000_000, 4, last, following, whitened, loose=1
-    )
-    first_blocks = (block, following, last)
-    last_blocks = (send(upper, 1, 0), send(lower, 3, 0))
     rows = ((512, 128), bf16)
     partial, *early = call(
         early_kernel,

time: 83.3 us -> 84.1 us (level)
  waiting for transfers between devices: 16.2 us -> 13.1 us
  starting transfers between devices: 18.8 us -> 21.1 us
  blocking collectives: 26.6 us -> 28.1 us
    ppermute x13 -> x15, waiting for transfers between devices: 9.99 us -> 3.6 us  [send(): return lax.ppermute(value, CHAN, route(dx, other))]
    ppermute x13 -> x15, starting transfers between devices: 12.9 us -> 16.3 us  [send(): return lax.ppermute(value, CHAN, route(dx, other))]
    ppermute x1, waiting for transfers between devices: 0.94 us -> 4.2 us  [shards(): lax.ppermute(tile, STRIPS + CHAN, seams())]
    ppermute x1, starting transfers between devices: 3.13 us -> 1.91 us  [shards(): lax.ppermute(tile, STRIPS + CHAN, seams())]
    all_to_all x1, blocking collectives: 15.7 us -> 16.8 us  [shards(): lax.all_to_all(packed, 'z_hi', 0, 0)]
  transfers between devices with their start and end apart: 17 -> 19, of which waited for: 9 -> 7; matrix products, arithmetic and copies ran while one was open for 3% -> 3% of each run, Pallas kernels for 8% -> 8%
where the time goes in v12:
time: 84.1 us; the launch traced here: 83.3 us
  blocking collectives  28.1 us (33%)
  starting transfers between devices  21.1 us (25%)
  Pallas kernels  15.8 us (19%)
  waiting for transfers between devices  13.1 us (16%)
  local copies, waits for them, and re-layouts  2.82 us (3%)
  other arithmetic  1.76 us (2%)
    all_to_all x1, blocking collectives, shards(): lax.all_to_all(packed, 'z_hi', 0, 0)  16.8 us
    ppermute x15, starting transfers between devices, send(): return lax.ppermute(value, CHAN, route(dx, other))  16.3 us
    pallas_call x14, Pallas kernels, call(): pl.pallas_call(kernel, out_shape=[jax.ShapeDtypeStruct(shape, dtype) for...  15.8 us
    all_to_all x1, blocking collectives, shards(): parts = lax.all_to_all(image_part.reshape(16, 8, LANES), CHAN, 0, 0)  11.2 us
    ppermute x3, waiting for transfers between devices, shards(): lax.ppermute(value, 'y', [(y, (y + step) % 4) for y in range(4)])  5.25 us
    ppermute x1, waiting for transfers between devices, shards(): lax.ppermute(tile, STRIPS + CHAN, seams())  4.2 us
    ppermute x15, waiting for transfers between devices, send(): return lax.ppermute(value, CHAN, route(dx, other))  3.6 us
    ppermute x3, starting transfers between devices, shards(): lax.ppermute(value, 'y', [(y, (y + step) % 4) for y in range(4)])  2.88 us
  transfers between devices with their start and end apart: 19, of which 7 were waited for; matrix products, arithmetic and copies ran while one was open for 3% of the time, Pallas kernels for 8%

profile of v12, /device:TPU:24, one launch (start us, length us, event | category | flops | bytes accessed | tf_op | source)
XLA Modules:
  0.0 83.3 jit_solution(9735940693167339029)
XLA Ops:
  0.6 1.0 %copy-done = bf16[64,16,256]{2,1,0:T(8,128)(2,1)S(1)} copy-done((bf16[64,16,256]{2,1,0:T(8,128)(2,1)S(1)}, bf16[64,16,256]{2,1,0:T(8,128)(2,1)}, u32[]{:S(2)}) %copy-start) | copy-done | bytes 524312
  1.7 0.7 copy-done.1
  2.4 1.0 %shard_map.76 = (bf16[64,1152]{1,0:T(8,128)(2,1)S(1)}, bf16[64,1152]{1,0:T(8,128)(2,1)S(1)}, bf16[64,1152]{1,0:T(8,128)(2,1)S(1)}, bf16[64,1152]{1,0:T(8,128)(2,1)S(1)}) custom-call(bf16[64,16,256]{2,1,0:T(8,128)(2,1)S(1)} %copy-done, bf16[64,75]{1,0:T(8,128)(2,1)S(1)} %copy-done.1), custom_call_target="tpu_custom_call" | custom-call | flops 1000000 | bytes 1123712 | tf_op jit(solution)/shard_map/pallas_call | solution.py:447
  3.5 2.0 %collective-permute-start.4 = (bf16[64,1152]{1,0:T(8,128)(2,1)S(1)}, bf16[64,1152]{1,0:T(8,128)(2,1)S(1)}, u32[]{:S(2)}, u32[]{:S(2)}) collective-permute-start(bf16[64,1152]{1,0:T(8,128)(2,1)S(1)} %get-tuple-element.36.refs_0_.after), channel_id=1, source_target_pairs={{0,3},{1,2},{2,1},{3,0},{4,7},{5,6},{6,5},{7,4},{8,11},{9,10},{10,... | collective-permute-start | bytes 442376 | tf_op jit(solution)/shard_map/ppermute | solution.py:461
  5.6 1.6 %collective-permute-start.1 = (bf16[128,1024]{1,0:T(8,128)(2,1)S(1)}, bf16[128,1024]{1,0:T(8,128)(2,1)S(1)}, u32[]{:S(2)}, u32[]{:S(2)}) collective-permute-start(bf16[128,1024]{1,0:T(8,128)(2,1)S(1)} %shard_map.77.refs_0_), channel_id=1, source_target_pairs={{0,4},{1,5},{2,6},{3,7},{4,8},{5,9},{6,10},{7,11},{8,12},{9,13},{1... | collective-permute-start | bytes 786440 | tf_op jit(solution)/shard_map/ppermute | solution.py:461
  7.2 1.7 %collective-permute-start.5 = (bf16[128,1024]{1,0:T(8,128)(2,1)S(1)}, bf16[128,1024]{1,0:T(8,128)(2,1)S(1)}, u32[]{:S(2)}, u32[]{:S(2)}) collective-permute-start(bf16[128,1024]{1,0:T(8,128)(2,1)S(1)} %shard_map.77.refs_0_), channel_id=1, source_target_pairs={{0,12},{1,13},{2,14},{3,15},{4,0},{5,1},{6,2},{7,3},{8,4},{9,5},{1... | collective-permute-start | bytes 786440 | tf_op jit(solution)/shard_map/ppermute | solution.py:461
  8.9 0.8 %convert_bitcast_fusion = bf16[1,32,512]{2,1,0:T(8,128)(2,1)S(1)} fusion(s32[32,512]{1,0:T(8,128)} %param.6), kind=kLoop, calls=%fused_computation.1 | loop fusion | flops 16384 | bytes 98304 | tf_op jit(solution)/shard_map/broadcast_in_dim | solution.py:472
  9.8 1.1 %copy.9.whiten = bf16[1024,64]{1,0:T(8,128)(2,1)S(1)} copy(bf16[1024,64]{0,1:T(8,128)(2,1)} %param.8) | data formatting | bytes 262144 | tf_op args[3]
  10.9 0.9 %pad_maximum_fusion.stacked = bf16[4,32,512]{2,1,0:T(8,128)(2,1)S(1)} fusion(bf16[1,32,512]{2,1,0:T(8,128)(2,1)S(1)} %convert_bitcast_fusion, bf16[3,32,512]{2,1,0:T(8,128)(2,1)} %param.5), kind=kLoop, calls=%fused_computation | loop fusion | flops 65536 | bytes 262144 | tf_op jit(solution)/shard_map/concatenate | solution.py:472
  11.9 1.1 %collective-permute-done.3.upper.refs_2_ = bf16[64,1152]{1,0:T(8,128)(2,1)S(1)} collective-permute-done((bf16[64,1152]{1,0:T(8,128)(2,1)S(1)}, bf16[64,1152]{1,0:T(8,128)(2,1)S(1)}, u32[]{:S(2)}, u32[]{:S(2)}) %collective-permute-start.3) | collective-permute-done | bytes 147488 | tf_op jit(solution)/shard_map/ppermute | solution.py:461
  13.0 2.1 %collective-permute-done.1.refs_2_.refs_4_ = bf16[128,1024]{1,0:T(8,128)(2,1)S(1)} collective-permute-done((bf16[128,1024]{1,0:T(8,128)(2,1)S(1)}, bf16[128,1024]{1,0:T(8,128)(2,1)S(1)}, u32[]{:S(2)}, u32[]{:S(2)}) %collective-permute-start.1) | collective-permute-done | bytes 262176 | tf_op jit(solution)/shard_map/ppermute | solution.py:461
  15.2 1.6 %collective-permute-start.8 = (bf16[128,1024]{1,0:T(8,128)(2,1)S(1)}, bf16[128,1024]{1,0:T(8,128)(2,1)S(1)}, u32[]{:S(2)}, u32[]{:S(2)}) collective-permute-start(bf16[128,1024]{1,0:T(8,128)(2,1)S(1)} %shard_map.80.refs_1_), channel_id=1, source_target_pairs={{0,4},{1,5},{2,6},{3,7},{4,8},{5,9},{6,10},{7,11},{8,12},{9,13},{1... | collective-permute-start | bytes 786440 | tf_op jit(solution)/shard_map/ppermute | solution.py:461
  16.8 1.7 %collective-permute-start.6 = (bf16[128,1024]{1,0:T(8,128)(2,1)S(1)}, bf16[128,1024]{1,0:T(8,128)(2,1)S(1)}, u32[]{:S(2)}, u32[]{:S(2)}) collective-permute-start(bf16[128,1024]{1,0:T(8,128)(2,1)S(1)} %shard_map.80.refs_1_), channel_id=1, source_target_pairs={{0,12},{1,13},{2,14},{3,15},{4,0},{5,1},{6,2},{7,3},{8,4},{9,5},{1... | collective-permute-start | bytes 786440 | tf_op jit(solution)/shard_map/ppermute | solution.py:461
  18.5 1.9 %collective-permute-start.12 = (bf16[4,32,128]{2,1,0:T(8,128)(2,1)S(1)}, bf16[4,32,128]{2,1,0:T(8,128)(2,1)S(1)}, u32[]{:S(2)}, u32[]{:S(2)}) collective-permute-start(bf16[4,32,128]{2,1,0:T(8,128)(2,1)S(1)} %shard_map.78.refs_0_), channel_id=1, source_target_pairs={{16,3},{20,7},{24,11},{28,15},{32,19},{36,23},{40,27},{44,31},{48,... | collective-permute-start | bytes 98312 | tf_op jit(solution)/shard_map/ppermute | solution.py:510
  20.4 4.2 %collective-permute-done.12.beyond = bf16[4,32,128]{2,1,0:T(8,128)(2,1)S(1)} collective-permute-done((bf16[4,32,128]{2,1,0:T(8,128)(2,1)S(1)}, bf16[4,32,128]{2,1,0:T(8,128)(2,1)S(1)}, u32[]{:S(2)}, u32[]{:S(2)}) %collective-permute-start.12) | collective-permute-done | bytes 32800 | tf_op jit(solution)/shard_map/ppermute | solution.py:510
  24.6 1.2 %shard_map.83 = (bf16[576,256]{1,0:T(8,128)(2,1)S(1)}, f32[32,256]{1,0:T(8,128)S(1)}, f32[32,256]{1,0:T(8,128)S(1)}, f32[32,256]{1,0:T(8,128)S(1)}, f32[32,256]{...) custom-call(bf16[4,32,512]{2,1,0:T(8,128)(2,1)S(1)} %pad_maximum_fusion.stacked, ...), custom_call_target="tpu_custom_call" | custom-call | flops 1000000000 | bytes 1265664 | tf_op jit(solution)/shard_map/pallas_call | solution.py:447
  26.2 0.8 collective-permute-start.11
  27.0 1.3 %collective-permute-start.9 = (bf16[512,128]{1,0:T(8,128)(2,1)S(1)}, bf16[512,128]{1,0:T(8,128)(2,1)S(1)}, u32[]{:S(2)}, u32[]{:S(2)}) collective-permute-start(bf16[512,128]{1,0:T(8,128)(2,1)S(1)} %shard_map.81.refs_0_), channel_id=1, source_target_pairs={{0,1},{1,0},{2,3},{3,2},{4,5},{5,4},{6,7},{7,6},{8,9},{9,8},{10,11... | collective-permute-start | bytes 393224 | tf_op jit(solution)/shard_map/ppermute | solution.py:461
  28.3 3.0 %collective-permute-start.7 = (bf16[128,1024]{1,0:T(8,128)(2,1)S(1)}, bf16[128,1024]{1,0:T(8,128)(2,1)S(1)}, u32[]{:S(2)}, u32[]{:S(2)}) collective-permute-start(bf16[128,1024]{1,0:T(8,128)(2,1)S(1)} %collective-permute-done.6.refs_3_), channel_id=1, source_target_pairs={{0,12},{1,13},{2,14},{3,15},{4,0},{5,1},{6,2},{7,3},{8,4},{9,5},{1... | collective-permute-start | bytes 786440 | tf_op jit(solution)/shard_map/ppermute | solution.py:461
  31.3 3.6 %shard_map.84 = (bf16[32,256,256]{2,1,0:T(8,128)(2,1)S(1)}, bf16[256,1024]{1,0:T(8,128)(2,1)S(1)}) custom-call(bf16[576,256]{1,0:T(8,128)(2,1)S(1)} %get-tuple-element.37.patches, f32[32,256]{1,0:T(8,128)S(1)} %get-tuple-element.38.tissue, f32[32,256]{1,0:T(8,128)S(1)} %get-tuple-element.39.scale, f32[32,256]{1,0:T(8,128)S(1)} %get-tuple-element.40.norm, ...), custom_call_target="tpu_custom_call" | custom-call | flops 3000000000 | bytes 5156864 | tf_op jit(solution)/shard_map/pallas_call | solution.py:447
  34.9 0.7 shard_map.82.refs_6_.wturned
  35.6 1.1 %shard_map.85 = (f32[256,1024]{1,0:T(8,128)S(1)}, bf16[512,128]{1,0:T(8,128)(2,1)S(1)}, bf16[512,128]{1,0:T(8,128)(2,1)S(1)}, bf16[512,128]{1,0:T(8,128)(2,1)S(1)}, bf16[512,128]{1,0:T(8,128)(2,1)S(1)}) custom-call(bf16[128,1024]{1,0:T(8,128)(2,1)S(1)} %shard_map.77.refs_0_, bf16[128,1024]{1,0:T(8,128)(2,1)S(1)} %shard_map.80.refs_1_, ...), custom_call_target="tpu_custom_call" | custom-call | flops 2000000000 | bytes 4194304 | tf_op jit(solution)/shard_map/pallas_call | solution.py:447
  37.0 6.5 %shard_map.86 = (f32[80,256]{1,0:T(8,128)S(1)}, bf16[128,256]{1,0:T(8,128)(2,1)S(1)}) custom-call(bf16[128,1024]{1,0:T(8,128)(2,1)S(1)} %collective-permute-done.2.first.refs_0_, bf16[128,1024]{1,0:T(8,128)(2,1)S(1)} %collective-permute-done.7.second.refs_1_, f32[256,1024]{1,0:T(8,128)S(1)} %get-tuple-element.44.partial, ...), custom_call_target="tpu_custom_call" | custom-call | flops 5000000000 | bytes 6811648 | tf_op jit(solution)/shard_map/pallas_call | solution.py:447
  44.1 0.8 collective-permute-start.14
  44.9 1.1 %collective-permute-start.15 = (bf16[560,128]{1,0:T(8,128)(2,1)S(1)}, bf16[560,128]{1,0:T(8,128)(2,1)S(1)}, u32[]{:S(2)}, u32[]{:S(2)}) collective-permute-start(bf16[560,128]{1,0:T(8,128)(2,1)S(1)} %get-tuple-element.57), channel_id=1, source_target_pairs={{0,3},{1,2},{2,1},{3,0},{4,7},{5,6},{6,5},{7,4},{8,11},{9,10},{10,... | collective-permute-start | bytes 430088 | tf_op jit(solution)/shard_map/ppermute | solution.py:461
  45.9 11.2 %all_to_all.10.parts = bf16[16,8,256]{2,1,0:T(8,128)(2,1)S(1)} all-to-all(bf16[16,8,256]{2,1,0:T(8,128)(2,1)S(1)} %bitcast.3), channel_id=1, replica_groups=mesh['z_hi'=4,'y'=4,'x'=4,'z_lo'=2,'core'=2] {'x','z_lo','core'}, dimensions={0} | all-to-all | bytes 131072 | tf_op jit(solution)/shard_map/all_to_all | solution.py:539
  57.4 2.8 %collective-permute-start.17 = (bf16[176,128]{1,0:T(8,128)(2,1)S(1)}, bf16[176,128]{1,0:T(8,128)(2,1)S(1)}, u32[]{:S(2)}, u32[]{:S(2)}) collective-permute-start(bf16[176,128]{1,0:T(8,128)(2,1)S(1)} %get-tuple-element.60), channel_id=1, source_target_pairs={{0,32},{16,48},{32,0},{48,16},{1,33},{17,49},{33,1},{49,17},{2,34}... | collective-permute-start | bytes 135176 | tf_op jit(solution)/shard_map/ppermute | solution.py:558
  60.2 1.3 %collective-permute-done.16.one = bf16[176,128]{1,0:T(8,128)(2,1)S(1)} collective-permute-done((bf16[176,128]{1,0:T(8,128)(2,1)S(1)}, bf16[176,128]{1,0:T(8,128)(2,1)S(1)}, u32[]{:S(2)}, u32[]{:S(2)}) %collective-permute-start.16) | collective-permute-done | bytes 45088 | tf_op jit(solution)/shard_map/ppermute | solution.py:558
  61.5 1.6 %collective-permute-done.17.two = bf16[176,128]{1,0:T(8,128)(2,1)S(1)} collective-permute-done((bf16[176,128]{1,0:T(8,128)(2,1)S(1)}, bf16[176,128]{1,0:T(8,128)(2,1)S(1)}, u32[]{:S(2)}, u32[]{:S(2)}) %collective-permute-start.17) | collective-permute-done | bytes 45088 | tf_op jit(solution)/shard_map/ppermute | solution.py:558
  63.1 2.4 %collective-permute-done.18.three = bf16[176,128]{1,0:T(8,128)(2,1)S(1)} collective-permute-done((bf16[176,128]{1,0:T(8,128)(2,1)S(1)}, bf16[176,128]{1,0:T(8,128)(2,1)S(1)}, u32[]{:S(2)}, u32[]{:S(2)}) %collective-permute-start.18) | collective-permute-done | bytes 45088 | tf_op jit(solution)/shard_map/ppermute | solution.py:558
  65.6 16.8 %all_to_all.11.received = bf16[4,80,128]{2,1,0:T(8,128)(2,1)S(1)} all-to-all(bf16[4,80,128]{2,1,0:T(8,128)(2,1)S(1)} %shard_map.89), channel_id=1, replica_groups=mesh['z_hi'=4,'y'=4,'x'=4,'z_lo'=2,'core'=2] {'z_hi'}, dimensions={0} | all-to-all | bytes 163840 | tf_op jit(solution)/shard_map/all_to_all | solution.py:571
  82.4 0.9 %shard_map.90 = (f32[64,75]{1,0:T(8,128)}, f32[64,64]{1,0:T(8,128)}, f32[3,2,512]{2,1,0:T(2,128)}) custom-call(bf16[4,80,128]{2,1,0:T(8,128)(2,1)S(1)} %all_to_all.11.received, f32[8,512]{1,0:T(8,128)S(1)} %get-tuple-element.62.middle), custom_call_target="tpu_custom_call" | custom-call | flops 1000000 | bytes 146176 | tf_op jit(solution)/shard_map/pallas_call | solution.py:447
  (30 shorter events, 2.0 us)
Async XLA Ops:
  0.6 1.0 %copy-start = (bf16[64,16,256]{2,1,0:T(8,128)(2,1)S(1)}, bf16[64,16,256]{2,1,0:T(8,128)(2,1)}, u32[]{:S(2)}) copy-start(bf16[64,16,256]{2,1,0:T(8,128)(2,1)} %cotangent.1) | copy-start | bytes 1572868
  1.7 0.7 copy-start.1
  3.4 2.3 %collective-permute-start = (bf16[64,1152]{1,0:T(8,128)(2,1)S(1)}, bf16[64,1152]{1,0:T(8,128)(2,1)S(1)}, u32[]{:S(2)}, u32[]{:S(2)}) collective-permute-start(bf16[64,1152]{1,0:T(8,128)(2,1)S(1)} %get-tuple-element.34), channel_id=1, source_target_pairs={{0,1},{1,0},{2,3},{3,2},{4,5},{5,4},{6,7},{7,6},{8,9},{9,8},{10,11... | collective-permute-start | bytes 442376 | tf_op jit(solution)/shard_map/ppermute | solution.py:461
  3.5 8.5 %collective-permute-start.4 = (bf16[64,1152]{1,0:T(8,128)(2,1)S(1)}, bf16[64,1152]{1,0:T(8,128)(2,1)S(1)}, u32[]{:S(2)}, u32[]{:S(2)}) collective-permute-start(bf16[64,1152]{1,0:T(8,128)(2,1)S(1)} %get-tuple-element.36.refs_0_.after), channel_id=1, source_target_pairs={{0,3},{1,2},{2,1},{3,0},{4,7},{5,6},{6,5},{7,4},{8,11},{9,10},{10,... | collective-permute-start | bytes 442376 | tf_op jit(solution)/shard_map/ppermute | solution.py:461
  5.5 7.5 %collective-permute-start.3 = (bf16[64,1152]{1,0:T(8,128)(2,1)S(1)}, bf16[64,1152]{1,0:T(8,128)(2,1)S(1)}, u32[]{:S(2)}, u32[]{:S(2)}) collective-permute-start(bf16[64,1152]{1,0:T(8,128)(2,1)S(1)} %get-tuple-element.35), channel_id=1, source_target_pairs={{0,2},{1,3},{2,0},{3,1},{4,6},{5,7},{6,4},{7,5},{8,10},{9,11},{10,... | collective-permute-start | bytes 442376 | tf_op jit(solution)/shard_map/ppermute | solution.py:461
  5.6 9.5 %collective-permute-start.1 = (bf16[128,1024]{1,0:T(8,128)(2,1)S(1)}, bf16[128,1024]{1,0:T(8,128)(2,1)S(1)}, u32[]{:S(2)}, u32[]{:S(2)}) collective-permute-start(bf16[128,1024]{1,0:T(8,128)(2,1)S(1)} %shard_map.77.refs_0_), channel_id=1, source_target_pairs={{0,4},{1,5},{2,6},{3,7},{4,8},{5,9},{6,10},{7,11},{8,12},{9,13},{1... | collective-permute-start | bytes 786440 | tf_op jit(solution)/shard_map/ppermute | solution.py:461
  7.2 8.0 %collective-permute-start.5 = (bf16[128,1024]{1,0:T(8,128)(2,1)S(1)}, bf16[128,1024]{1,0:T(8,128)(2,1)S(1)}, u32[]{:S(2)}, u32[]{:S(2)}) collective-permute-start(bf16[128,1024]{1,0:T(8,128)(2,1)S(1)} %shard_map.77.refs_0_), channel_id=1, source_target_pairs={{0,12},{1,13},{2,14},{3,15},{4,0},{5,1},{6,2},{7,3},{8,4},{9,5},{1... | collective-permute-start | bytes 786440 | tf_op jit(solution)/shard_map/ppermute | solution.py:461
  15.2 11.0 %collective-permute-start.8 = (bf16[128,1024]{1,0:T(8,128)(2,1)S(1)}, bf16[128,1024]{1,0:T(8,128)(2,1)S(1)}, u32[]{:S(2)}, u32[]{:S(2)}) collective-permute-start(bf16[128,1024]{1,0:T(8,128)(2,1)S(1)} %shard_map.80.refs_1_), channel_id=1, source_target_pairs={{0,4},{1,5},{2,6},{3,7},{4,8},{5,9},{6,10},{7,11},{8,12},{9,13},{1... | collective-permute-start | bytes 786440 | tf_op jit(solution)/shard_map/ppermute | solution.py:461
  16.8 11.5 %collective-permute-start.6 = (bf16[128,1024]{1,0:T(8,128)(2,1)S(1)}, bf16[128,1024]{1,0:T(8,128)(2,1)S(1)}, u32[]{:S(2)}, u32[]{:S(2)}) collective-permute-start(bf16[128,1024]{1,0:T(8,128)(2,1)S(1)} %shard_map.80.refs_1_), channel_id=1, source_target_pairs={{0,12},{1,13},{2,14},{3,15},{4,0},{5,1},{6,2},{7,3},{8,4},{9,5},{1... | collective-permute-start | bytes 786440 | tf_op jit(solution)/shard_map/ppermute | solution.py:461
  18.5 6.1 %collective-permute-start.12 = (bf16[4,32,128]{2,1,0:T(8,128)(2,1)S(1)}, bf16[4,32,128]{2,1,0:T(8,128)(2,1)S(1)}, u32[]{:S(2)}, u32[]{:S(2)}) collective-permute-start(bf16[4,32,128]{2,1,0:T(8,128)(2,1)S(1)} %shard_map.78.refs_0_), channel_id=1, source_target_pairs={{16,3},{20,7},{24,11},{28,15},{32,19},{36,23},{40,27},{44,31},{48,... | collective-permute-start | bytes 98312 | tf_op jit(solution)/shard_map/ppermute | solution.py:510
  25.8 10.8 %collective-permute-start.2 = (bf16[128,1024]{1,0:T(8,128)(2,1)S(1)}, bf16[128,1024]{1,0:T(8,128)(2,1)S(1)}, u32[]{:S(2)}, u32[]{:S(2)}) collective-permute-start(bf16[128,1024]{1,0:T(8,128)(2,1)S(1)} %collective-permute-done.1.refs_2_.refs_4_), channel_id=1, source_target_pairs={{0,4},{1,5},{2,6},{3,7},{4,8},{5,9},{6,10},{7,11},{8,12},{9,13},{1... | collective-permute-start | bytes 786440 | tf_op jit(solution)/shard_map/ppermute | solution.py:461
  26.2 8.7 %collective-permute-start.10 = (bf16[512,128]{1,0:T(8,128)(2,1)S(1)}, bf16[512,128]{1,0:T(8,128)(2,1)S(1)}, u32[]{:S(2)}, u32[]{:S(2)}) collective-permute-start(bf16[512,128]{1,0:T(8,128)(2,1)S(1)} %shard_map.81.refs_0_), channel_id=1, source_target_pairs={{0,2},{1,3},{2,0},{3,1},{4,6},{5,7},{6,4},{7,5},{8,10},{9,11},{10,... | collective-permute-start | bytes 393224 | tf_op jit(solution)/shard_map/ppermute | solution.py:461
  26.2 8.7 %collective-permute-start.11 = (bf16[512,128]{1,0:T(8,128)(2,1)S(1)}, bf16[512,128]{1,0:T(8,128)(2,1)S(1)}, u32[]{:S(2)}, u32[]{:S(2)}) collective-permute-start(bf16[512,128]{1,0:T(8,128)(2,1)S(1)} %shard_map.81.refs_0_), channel_id=1, source_target_pairs={{0,3},{1,2},{2,1},{3,0},{4,7},{5,6},{6,5},{7,4},{8,11},{9,10},{10,... | collective-permute-start | bytes 393224 | tf_op jit(solution)/shard_map/ppermute | solution.py:461
  27.0 7.9 %collective-permute-start.9 = (bf16[512,128]{1,0:T(8,128)(2,1)S(1)}, bf16[512,128]{1,0:T(8,128)(2,1)S(1)}, u32[]{:S(2)}, u32[]{:S(2)}) collective-permute-start(bf16[512,128]{1,0:T(8,128)(2,1)S(1)} %shard_map.81.refs_0_), channel_id=1, source_target_pairs={{0,1},{1,0},{2,3},{3,2},{4,5},{5,4},{6,7},{7,6},{8,9},{9,8},{10,11... | collective-permute-start | bytes 393224 | tf_op jit(solution)/shard_map/ppermute | solution.py:461
  28.3 8.7 %collective-permute-start.7 = (bf16[128,1024]{1,0:T(8,128)(2,1)S(1)}, bf16[128,1024]{1,0:T(8,128)(2,1)S(1)}, u32[]{:S(2)}, u32[]{:S(2)}) collective-permute-start(bf16[128,1024]{1,0:T(8,128)(2,1)S(1)} %collective-permute-done.6.refs_3_), channel_id=1, source_target_pairs={{0,12},{1,13},{2,14},{3,15},{4,0},{5,1},{6,2},{7,3},{8,4},{9,5},{1... | collective-permute-start | bytes 786440 | tf_op jit(solution)/shard_map/ppermute | solution.py:461
  44.0 13.2 %collective-permute-start.13 = (bf16[560,128]{1,0:T(8,128)(2,1)S(1)}, bf16[560,128]{1,0:T(8,128)(2,1)S(1)}, u32[]{:S(2)}, u32[]{:S(2)}) collective-permute-start(bf16[560,128]{1,0:T(8,128)(2,1)S(1)} %get-tuple-element.55), channel_id=1, source_target_pairs={{0,1},{1,0},{2,3},{3,2},{4,5},{5,4},{6,7},{7,6},{8,9},{9,8},{10,11... | collective-permute-start | bytes 430088 | tf_op jit(solution)/shard_map/ppermute | solution.py:461
  44.1 13.1 %collective-permute-start.14 = (bf16[560,128]{1,0:T(8,128)(2,1)S(1)}, bf16[560,128]{1,0:T(8,128)(2,1)S(1)}, u32[]{:S(2)}, u32[]{:S(2)}) collective-permute-start(bf16[560,128]{1,0:T(8,128)(2,1)S(1)} %get-tuple-element.56), channel_id=1, source_target_pairs={{0,2},{1,3},{2,0},{3,1},{4,6},{5,7},{6,4},{7,5},{8,10},{9,11},{10,... | collective-permute-start | bytes 430088 | tf_op jit(solution)/shard_map/ppermute | solution.py:461
  44.9 12.3 %collective-permute-start.15 = (bf16[560,128]{1,0:T(8,128)(2,1)S(1)}, bf16[560,128]{1,0:T(8,128)(2,1)S(1)}, u32[]{:S(2)}, u32[]{:S(2)}) collective-permute-start(bf16[560,128]{1,0:T(8,128)(2,1)S(1)} %get-tuple-element.57), channel_id=1, source_target_pairs={{0,3},{1,2},{2,1},{3,0},{4,7},{5,6},{6,5},{7,4},{8,11},{9,10},{10,... | collective-permute-start | bytes 430088 | tf_op jit(solution)/shard_map/ppermute | solution.py:461
  57.3 4.2 %collective-permute-start.16 = (bf16[176,128]{1,0:T(8,128)(2,1)S(1)}, bf16[176,128]{1,0:T(8,128)(2,1)S(1)}, u32[]{:S(2)}, u32[]{:S(2)}) collective-permute-start(bf16[176,128]{1,0:T(8,128)(2,1)S(1)} %get-tuple-element.59), channel_id=1, source_target_pairs={{0,16},{16,32},{32,48},{48,0},{1,17},{17,33},{33,49},{49,1},{2,18}... | collective-permute-start | bytes 135176 | tf_op jit(solution)/shard_map/ppermute | solution.py:558
  57.4 5.6 %collective-permute-start.17 = (bf16[176,128]{1,0:T(8,128)(2,1)S(1)}, bf16[176,128]{1,0:T(8,128)(2,1)S(1)}, u32[]{:S(2)}, u32[]{:S(2)}) collective-permute-start(bf16[176,128]{1,0:T(8,128)(2,1)S(1)} %get-tuple-element.60), channel_id=1, source_target_pairs={{0,32},{16,48},{32,0},{48,16},{1,33},{17,49},{33,1},{49,17},{2,34}... | collective-permute-start | bytes 135176 | tf_op jit(solution)/shard_map/ppermute | solution.py:558
  60.2 5.3 %collective-permute-start.18 = (bf16[176,128]{1,0:T(8,128)(2,1)S(1)}, bf16[176,128]{1,0:T(8,128)(2,1)S(1)}, u32[]{:S(2)}, u32[]{:S(2)}) collective-permute-start(bf16[176,128]{1,0:T(8,128)(2,1)S(1)} %get-tuple-element.61), channel_id=1, source_target_pairs={{0,48},{16,0},{32,16},{48,32},{1,49},{17,1},{33,17},{49,33},{2,50}... | collective-permute-start | bytes 135176 | tf_op jit(solution)/shard_map/ppermute | solution.py:558

commit v13 on v11

--- a/solution.py
+++ b/solution.py
@@ -17,7 +17,7 @@
 GROUP = 16
 OWN = 64
 KEPT = 4 * OWN
-STEP = 16
+STEP = 32
 EARLY = 12
 MIB = 1024 * 1024
 

time: 83.3 us -> 81.4 us (0.977)
  Pallas kernels: 15.8 us -> 13.9 us
    pallas_call x14, Pallas kernels: 15.8 us -> 13.9 us  [call(): pl.pallas_call(kernel, out_shape=[jax.ShapeDtypeStruct(shape, dtype) for...]
  transfers between devices with their start and end apart: 17 -> 17, of which waited for: 9 -> 8; matrix products, arithmetic and copies ran while one was open for 3% -> 3% of each run, Pallas kernels for 8% -> 8%
where the time goes in v13:
time: 81.4 us; the launch traced here: 81 us
  blocking collectives  26.6 us (33%)
  starting transfers between devices  18.6 us (23%)
  waiting for transfers between devices  16.5 us (20%)
  Pallas kernels  13.9 us (17%)
  local copies, waits for them, and re-layouts  2.82 us (3%)
  other arithmetic  1.76 us (2%)
    all_to_all x1, blocking collectives, shards(): lax.all_to_all(packed, 'z_hi', 0, 0)  15.7 us
    pallas_call x14, Pallas kernels, call(): pl.pallas_call(kernel, out_shape=[jax.ShapeDtypeStruct(shape, dtype) for...  13.9 us
    ppermute x13, starting transfers between devices, send(): return lax.ppermute(value, CHAN, route(dx, other))  12.9 us
    all_to_all x1, blocking collectives, shards(): parts = lax.all_to_all(image_part.reshape(16, 8, LANES), CHAN, 0, 0)  10.9 us
    ppermute x13, waiting for transfers between devices, send(): return lax.ppermute(value, CHAN, route(dx, other))  10.3 us
    ppermute x3, waiting for transfers between devices, shards(): lax.ppermute(value, 'y', [(y, (y + step) % 4) for y in range(4)])  5.25 us
    ppermute x1, starting transfers between devices, shards(): lax.ppermute(tile, STRIPS + CHAN, seams())  3.13 us
    unnamed x5, local copies, waits for them, and re-layouts  2.82 us
  transfers between devices with their start and end apart: 17, of which 8 were waited for; matrix products, arithmetic and copies ran while one was open for 3% of the time, Pallas kernels for 8%

profile of v13, /device:TPU:24, one launch (start us, length us, event | category | flops | bytes accessed | tf_op | source)
XLA Modules:
  0.0 81.0 jit_solution(6831471352275473240)
XLA Ops:
  0.6 1.0 %copy-done = bf16[64,16,256]{2,1,0:T(8,128)(2,1)S(1)} copy-done((bf16[64,16,256]{2,1,0:T(8,128)(2,1)S(1)}, bf16[64,16,256]{2,1,0:T(8,128)(2,1)}, u32[]{:S(2)}) %copy-start) | copy-done | bytes 524312
  1.7 0.7 copy-done.1
  2.4 1.0 %shard_map.76 = (bf16[64,1152]{1,0:T(8,128)(2,1)S(1)}, bf16[64,1152]{1,0:T(8,128)(2,1)S(1)}, bf16[64,1152]{1,0:T(8,128)(2,1)S(1)}, bf16[64,1152]{1,0:T(8,128)(2,1)S(1)}) custom-call(bf16[64,16,256]{2,1,0:T(8,128)(2,1)S(1)} %copy-done, bf16[64,75]{1,0:T(8,128)(2,1)S(1)} %copy-done.1), custom_call_target="tpu_custom_call" | custom-call | flops 1000000 | bytes 1123712 | tf_op jit(solution)/shard_map/pallas_call | solution.py:456
  3.4 1.5 %collective-permute-start.2 = (bf16[64,1152]{1,0:T(8,128)(2,1)S(1)}, bf16[64,1152]{1,0:T(8,128)(2,1)S(1)}, u32[]{:S(2)}, u32[]{:S(2)}) collective-permute-start(bf16[64,1152]{1,0:T(8,128)(2,1)S(1)} %get-tuple-element.38.refs_0_.after), channel_id=1, source_target_pairs={{0,3},{1,2},{2,1},{3,0},{4,7},{5,6},{6,5},{7,4},{8,11},{9,10},{10,... | collective-permute-start | bytes 442376 | tf_op jit(solution)/shard_map/ppermute | solution.py:470
  4.8 0.7 collective-permute-start
  5.6 0.8 %convert_bitcast_fusion = bf16[1,32,512]{2,1,0:T(8,128)(2,1)S(1)} fusion(s32[32,512]{1,0:T(8,128)} %param.6), kind=kLoop, calls=%fused_computation.1 | loop fusion | flops 16384 | bytes 98304 | tf_op jit(solution)/shard_map/broadcast_in_dim | solution.py:481
  6.5 1.1 %copy.9.whiten = bf16[1024,64]{1,0:T(8,128)(2,1)S(1)} copy(bf16[1024,64]{0,1:T(8,128)(2,1)} %param.8) | data formatting | bytes 262144 | tf_op args[3]
  7.5 0.9 %pad_maximum_fusion.stacked = bf16[4,32,512]{2,1,0:T(8,128)(2,1)S(1)} fusion(bf16[1,32,512]{2,1,0:T(8,128)(2,1)S(1)} %convert_bitcast_fusion, bf16[3,32,512]{2,1,0:T(8,128)(2,1)} %param.5), kind=kLoop, calls=%fused_computation | loop fusion | flops 65536 | bytes 262144 | tf_op jit(solution)/shard_map/concatenate | solution.py:481
  9.2 3.6 %collective-permute-done.1.refs_2_ = bf16[64,1152]{1,0:T(8,128)(2,1)S(1)} collective-permute-done((bf16[64,1152]{1,0:T(8,128)(2,1)S(1)}, bf16[64,1152]{1,0:T(8,128)(2,1)S(1)}, u32[]{:S(2)}, u32[]{:S(2)}) %collective-permute-start.1) | collective-permute-done | bytes 147488 | tf_op jit(solution)/shard_map/ppermute | solution.py:470
  12.8 1.6 %collective-permute-start.3 = (bf16[256,1024]{1,0:T(8,128)(2,1)S(1)}, bf16[256,1024]{1,0:T(8,128)(2,1)S(1)}, u32[]{:S(2)}, u32[]{:S(2)}) collective-permute-start(bf16[256,1024]{1,0:T(8,128)(2,1)S(1)} %shard_map.79.refs_1_.refs_0_), channel_id=1, source_target_pairs={{0,4},{1,5},{2,6},{3,7},{4,8},{5,9},{6,10},{7,11},{8,12},{9,13},{1... | collective-permute-start | bytes 1572872 | tf_op jit(solution)/shard_map/ppermute | solution.py:470
  14.4 1.7 %collective-permute-start.4 = (bf16[256,1024]{1,0:T(8,128)(2,1)S(1)}, bf16[256,1024]{1,0:T(8,128)(2,1)S(1)}, u32[]{:S(2)}, u32[]{:S(2)}) collective-permute-start(bf16[256,1024]{1,0:T(8,128)(2,1)S(1)} %shard_map.79.refs_1_.refs_0_), channel_id=1, source_target_pairs={{0,12},{1,13},{2,14},{3,15},{4,0},{5,1},{6,2},{7,3},{8,4},{9,5},{1... | collective-permute-start | bytes 1572872 | tf_op jit(solution)/shard_map/ppermute | solution.py:470
  16.1 3.1 %collective-permute-start.5 = (bf16[4,32,128]{2,1,0:T(8,128)(2,1)S(1)}, bf16[4,32,128]{2,1,0:T(8,128)(2,1)S(1)}, u32[]{:S(2)}, u32[]{:S(2)}) collective-permute-start(bf16[4,32,128]{2,1,0:T(8,128)(2,1)S(1)} %shard_map.77.refs_4_), channel_id=1, source_target_pairs={{16,3},{20,7},{24,11},{28,15},{32,19},{36,23},{40,27},{44,31},{48,... | collective-permute-start | bytes 98312 | tf_op jit(solution)/shard_map/ppermute | solution.py:513
  19.3 2.1 %collective-permute-start.10 = (bf16[512,128]{1,0:T(8,128)(2,1)S(1)}, bf16[512,128]{1,0:T(8,128)(2,1)S(1)}, u32[]{:S(2)}, u32[]{:S(2)}) collective-permute-start(bf16[512,128]{1,0:T(8,128)(2,1)S(1)} %shard_map.83.refs_0_), channel_id=1, source_target_pairs={{0,3},{1,2},{2,1},{3,0},{4,7},{5,6},{6,5},{7,4},{8,11},{9,10},{10,... | collective-permute-start | bytes 393224 | tf_op jit(solution)/shard_map/ppermute | solution.py:470
  21.3 0.9 %collective-permute-done.5.beyond = bf16[4,32,128]{2,1,0:T(8,128)(2,1)S(1)} collective-permute-done((bf16[4,32,128]{2,1,0:T(8,128)(2,1)S(1)}, bf16[4,32,128]{2,1,0:T(8,128)(2,1)S(1)}, u32[]{:S(2)}, u32[]{:S(2)}) %collective-permute-start.5) | collective-permute-done | bytes 32800 | tf_op jit(solution)/shard_map/ppermute | solution.py:513
  22.3 1.2 %shard_map.80 = (bf16[576,256]{1,0:T(8,128)(2,1)S(1)}, f32[32,256]{1,0:T(8,128)S(1)}, f32[32,256]{1,0:T(8,128)S(1)}, f32[32,256]{1,0:T(8,128)S(1)}, f32[32,256]{...) custom-call(bf16[4,32,512]{2,1,0:T(8,128)(2,1)S(1)} %pad_maximum_fusion.stacked, ...), custom_call_target="tpu_custom_call" | custom-call | flops 1000000000 | bytes 1265664 | tf_op jit(solution)/shard_map/pallas_call | solution.py:456
  23.4 3.1 %shard_map.81 = (bf16[32,256,256]{2,1,0:T(8,128)(2,1)S(1)}, bf16[256,1024]{1,0:T(8,128)(2,1)S(1)}) custom-call(bf16[576,256]{1,0:T(8,128)(2,1)S(1)} %get-tuple-element.39.patches, f32[32,256]{1,0:T(8,128)S(1)} %get-tuple-element.40.tissue, f32[32,256]{1,0:T(8,128)S(1)} %get-tuple-element.41.scale, f32[32,256]{1,0:T(8,128)S(1)} %get-tuple-element.42.norm, ...), custom_call_target="tpu_custom_call" | custom-call | flops 3000000000 | bytes 5156864 | tf_op jit(solution)/shard_map/pallas_call | solution.py:456
  26.6 1.0 %collective-permute-done.3.first.refs_2_ = bf16[256,1024]{1,0:T(8,128)(2,1)S(1)} collective-permute-done((bf16[256,1024]{1,0:T(8,128)(2,1)S(1)}, bf16[256,1024]{1,0:T(8,128)(2,1)S(1)}, u32[]{:S(2)}, u32[]{:S(2)}) %collective-permute-start.3) | collective-permute-done | bytes 524320 | tf_op jit(solution)/shard_map/ppermute | solution.py:470
  27.7 1.6 %collective-permute-start.6 = (bf16[128,1024]{1,0:T(8,128)(2,1)S(1)}, bf16[128,1024]{1,0:T(8,128)(2,1)S(1)}, u32[]{:S(2)}, u32[]{:S(2)}) collective-permute-start(bf16[128,1024]{1,0:T(8,128)(2,1)S(1)} %get-tuple-element.46), channel_id=1, source_target_pairs={{0,4},{1,5},{2,6},{3,7},{4,8},{5,9},{6,10},{7,11},{8,12},{9,13},{1... | collective-permute-start | bytes 786440 | tf_op jit(solution)/shard_map/ppermute | solution.py:470
  29.2 1.7 %collective-permute-start.7 = (bf16[128,1024]{1,0:T(8,128)(2,1)S(1)}, bf16[128,1024]{1,0:T(8,128)(2,1)S(1)}, u32[]{:S(2)}, u32[]{:S(2)}) collective-permute-start(bf16[128,1024]{1,0:T(8,128)(2,1)S(1)} %get-tuple-element.47), channel_id=1, source_target_pairs={{0,12},{1,13},{2,14},{3,15},{4,0},{5,1},{6,2},{7,3},{8,4},{9,5},{1... | collective-permute-start | bytes 786440 | tf_op jit(solution)/shard_map/ppermute | solution.py:470
  31.0 0.7 shard_map.84.refs_3_.wturned
  31.7 1.1 %shard_map.85 = (f32[256,1024]{1,0:T(8,128)S(1)}, bf16[512,128]{1,0:T(8,128)(2,1)S(1)}, bf16[512,128]{1,0:T(8,128)(2,1)S(1)}, bf16[512,128]{1,0:T(8,128)(2,1)S(1)}, bf16[512,128]{1,0:T(8,128)(2,1)S(1)}) custom-call(bf16[256,1024]{1,0:T(8,128)(2,1)S(1)} %shard_map.79.refs_1_.refs_0_, bf16[256,1024]{1,0:T(8,128)(2,1)S(1)} %collective-permute-done.4.second.refs_1_, ...), custom_call_target="tpu_custom_call" | custom-call | flops 2000000000 | bytes 4194304 | tf_op jit(solution)/shard_map/pallas_call | solution.py:456
  32.7 5.1 %collective-permute-done.6.first.refs_0_ = bf16[128,1024]{1,0:T(8,128)(2,1)S(1)} collective-permute-done((bf16[128,1024]{1,0:T(8,128)(2,1)S(1)}, bf16[128,1024]{1,0:T(8,128)(2,1)S(1)}, u32[]{:S(2)}, u32[]{:S(2)}) %collective-permute-start.6) | collective-permute-done | bytes 262176 | tf_op jit(solution)/shard_map/ppermute | solution.py:470
  37.9 5.1 %shard_map.86 = (f32[80,256]{1,0:T(8,128)S(1)}, bf16[128,256]{1,0:T(8,128)(2,1)S(1)}) custom-call(bf16[128,1024]{1,0:T(8,128)(2,1)S(1)} %collective-permute-done.6.first.refs_0_, bf16[128,1024]{1,0:T(8,128)(2,1)S(1)} %collective-permute-done.7.second.refs_1_, f32[256,1024]{1,0:T(8,128)S(1)} %get-tuple-element.48.partial, ...), custom_call_target="tpu_custom_call" | custom-call | flops 5000000000 | bytes 6811648 | tf_op jit(solution)/shard_map/pallas_call | solution.py:456
  43.6 0.9 %collective-permute-start.12 = (bf16[560,128]{1,0:T(8,128)(2,1)S(1)}, bf16[560,128]{1,0:T(8,128)(2,1)S(1)}, u32[]{:S(2)}, u32[]{:S(2)}) collective-permute-start(bf16[560,128]{1,0:T(8,128)(2,1)S(1)} %get-tuple-element.60), channel_id=1, source_target_pairs={{0,2},{1,3},{2,0},{3,1},{4,6},{5,7},{6,4},{7,5},{8,10},{9,11},{10,... | collective-permute-start | bytes 430088 | tf_op jit(solution)/shard_map/ppermute | solution.py:470
  44.5 0.9 %collective-permute-start.13 = (bf16[560,128]{1,0:T(8,128)(2,1)S(1)}, bf16[560,128]{1,0:T(8,128)(2,1)S(1)}, u32[]{:S(2)}, u32[]{:S(2)}) collective-permute-start(bf16[560,128]{1,0:T(8,128)(2,1)S(1)} %get-tuple-element.61), channel_id=1, source_target_pairs={{0,3},{1,2},{2,1},{3,0},{4,7},{5,6},{6,5},{7,4},{8,11},{9,10},{10,... | collective-permute-start | bytes 430088 | tf_op jit(solution)/shard_map/ppermute | solution.py:470
  45.4 10.9 %all_to_all.10.parts = bf16[16,8,256]{2,1,0:T(8,128)(2,1)S(1)} all-to-all(bf16[16,8,256]{2,1,0:T(8,128)(2,1)S(1)} %bitcast.3), channel_id=1, replica_groups=mesh['z_hi'=4,'y'=4,'x'=4,'z_lo'=2,'core'=2] {'x','z_lo','core'}, dimensions={0} | all-to-all | bytes 131072 | tf_op jit(solution)/shard_map/all_to_all | solution.py:548
  56.6 2.4 %collective-permute-start.15 = (bf16[176,128]{1,0:T(8,128)(2,1)S(1)}, bf16[176,128]{1,0:T(8,128)(2,1)S(1)}, u32[]{:S(2)}, u32[]{:S(2)}) collective-permute-start(bf16[176,128]{1,0:T(8,128)(2,1)S(1)} %get-tuple-element.64), channel_id=1, source_target_pairs={{0,32},{16,48},{32,0},{48,16},{1,33},{17,49},{33,1},{49,17},{2,34}... | collective-permute-start | bytes 135176 | tf_op jit(solution)/shard_map/ppermute | solution.py:567
  59.0 1.6 %collective-permute-done.14.one = bf16[176,128]{1,0:T(8,128)(2,1)S(1)} collective-permute-done((bf16[176,128]{1,0:T(8,128)(2,1)S(1)}, bf16[176,128]{1,0:T(8,128)(2,1)S(1)}, u32[]{:S(2)}, u32[]{:S(2)}) %collective-permute-start.14) | collective-permute-done | bytes 45088 | tf_op jit(solution)/shard_map/ppermute | solution.py:567
  60.6 1.6 %collective-permute-done.15.two = bf16[176,128]{1,0:T(8,128)(2,1)S(1)} collective-permute-done((bf16[176,128]{1,0:T(8,128)(2,1)S(1)}, bf16[176,128]{1,0:T(8,128)(2,1)S(1)}, u32[]{:S(2)}, u32[]{:S(2)}) %collective-permute-start.15) | collective-permute-done | bytes 45088 | tf_op jit(solution)/shard_map/ppermute | solution.py:567
  62.2 2.0 %collective-permute-done.16.three = bf16[176,128]{1,0:T(8,128)(2,1)S(1)} collective-permute-done((bf16[176,128]{1,0:T(8,128)(2,1)S(1)}, bf16[176,128]{1,0:T(8,128)(2,1)S(1)}, u32[]{:S(2)}, u32[]{:S(2)}) %collective-permute-start.16) | collective-permute-done | bytes 45088 | tf_op jit(solution)/shard_map/ppermute | solution.py:567
  64.4 15.7 %all_to_all.11.received = bf16[4,80,128]{2,1,0:T(8,128)(2,1)S(1)} all-to-all(bf16[4,80,128]{2,1,0:T(8,128)(2,1)S(1)} %shard_map.89), channel_id=1, replica_groups=mesh['z_hi'=4,'y'=4,'x'=4,'z_lo'=2,'core'=2] {'z_hi'}, dimensions={0} | all-to-all | bytes 163840 | tf_op jit(solution)/shard_map/all_to_all | solution.py:580
  80.1 0.9 %shard_map.90 = (f32[64,75]{1,0:T(8,128)}, f32[64,64]{1,0:T(8,128)}, f32[3,2,512]{2,1,0:T(2,128)}) custom-call(bf16[4,80,128]{2,1,0:T(8,128)(2,1)S(1)} %all_to_all.11.received, f32[8,512]{1,0:T(8,128)S(1)} %get-tuple-element.66.middle), custom_call_target="tpu_custom_call" | custom-call | flops 1000000 | bytes 146176 | tf_op jit(solution)/shard_map/pallas_call | solution.py:456
  (26 shorter events, 1.9 us)
Async XLA Ops:
  0.6 1.0 %copy-start = (bf16[64,16,256]{2,1,0:T(8,128)(2,1)S(1)}, bf16[64,16,256]{2,1,0:T(8,128)(2,1)}, u32[]{:S(2)}) copy-start(bf16[64,16,256]{2,1,0:T(8,128)(2,1)} %cotangent.1) | copy-start | bytes 1572868
  1.7 0.7 copy-start.1
  3.4 5.8 %collective-permute-start.2 = (bf16[64,1152]{1,0:T(8,128)(2,1)S(1)}, bf16[64,1152]{1,0:T(8,128)(2,1)S(1)}, u32[]{:S(2)}, u32[]{:S(2)}) collective-permute-start(bf16[64,1152]{1,0:T(8,128)(2,1)S(1)} %get-tuple-element.38.refs_0_.after), channel_id=1, source_target_pairs={{0,3},{1,2},{2,1},{3,0},{4,7},{5,6},{6,5},{7,4},{8,11},{9,10},{10,... | collective-permute-start | bytes 442376 | tf_op jit(solution)/shard_map/ppermute | solution.py:470
  4.8 4.4 %collective-permute-start = (bf16[64,1152]{1,0:T(8,128)(2,1)S(1)}, bf16[64,1152]{1,0:T(8,128)(2,1)S(1)}, u32[]{:S(2)}, u32[]{:S(2)}) collective-permute-start(bf16[64,1152]{1,0:T(8,128)(2,1)S(1)} %get-tuple-element.36), channel_id=1, source_target_pairs={{0,1},{1,0},{2,3},{3,2},{4,5},{5,4},{6,7},{7,6},{8,9},{9,8},{10,11... | collective-permute-start | bytes 442376 | tf_op jit(solution)/shard_map/ppermute | solution.py:470
  5.5 7.3 %collective-permute-start.1 = (bf16[64,1152]{1,0:T(8,128)(2,1)S(1)}, bf16[64,1152]{1,0:T(8,128)(2,1)S(1)}, u32[]{:S(2)}, u32[]{:S(2)}) collective-permute-start(bf16[64,1152]{1,0:T(8,128)(2,1)S(1)} %get-tuple-element.37), channel_id=1, source_target_pairs={{0,2},{1,3},{2,0},{3,1},{4,6},{5,7},{6,4},{7,5},{8,10},{9,11},{10,... | collective-permute-start | bytes 442376 | tf_op jit(solution)/shard_map/ppermute | solution.py:470
  12.8 14.8 %collective-permute-start.3 = (bf16[256,1024]{1,0:T(8,128)(2,1)S(1)}, bf16[256,1024]{1,0:T(8,128)(2,1)S(1)}, u32[]{:S(2)}, u32[]{:S(2)}) collective-permute-start(bf16[256,1024]{1,0:T(8,128)(2,1)S(1)} %shard_map.79.refs_1_.refs_0_), channel_id=1, source_target_pairs={{0,4},{1,5},{2,6},{3,7},{4,8},{5,9},{6,10},{7,11},{8,12},{9,13},{1... | collective-permute-start | bytes 1572872 | tf_op jit(solution)/shard_map/ppermute | solution.py:470
  14.4 13.3 %collective-permute-start.4 = (bf16[256,1024]{1,0:T(8,128)(2,1)S(1)}, bf16[256,1024]{1,0:T(8,128)(2,1)S(1)}, u32[]{:S(2)}, u32[]{:S(2)}) collective-permute-start(bf16[256,1024]{1,0:T(8,128)(2,1)S(1)} %shard_map.79.refs_1_.refs_0_), channel_id=1, source_target_pairs={{0,12},{1,13},{2,14},{3,15},{4,0},{5,1},{6,2},{7,3},{8,4},{9,5},{1... | collective-permute-start | bytes 1572872 | tf_op jit(solution)/shard_map/ppermute | solution.py:470
  16.1 6.2 %collective-permute-start.5 = (bf16[4,32,128]{2,1,0:T(8,128)(2,1)S(1)}, bf16[4,32,128]{2,1,0:T(8,128)(2,1)S(1)}, u32[]{:S(2)}, u32[]{:S(2)}) collective-permute-start(bf16[4,32,128]{2,1,0:T(8,128)(2,1)S(1)} %shard_map.77.refs_4_), channel_id=1, source_target_pairs={{16,3},{20,7},{24,11},{28,15},{32,19},{36,23},{40,27},{44,31},{48,... | collective-permute-start | bytes 98312 | tf_op jit(solution)/shard_map/ppermute | solution.py:513
  19.3 11.7 %collective-permute-start.10 = (bf16[512,128]{1,0:T(8,128)(2,1)S(1)}, bf16[512,128]{1,0:T(8,128)(2,1)S(1)}, u32[]{:S(2)}, u32[]{:S(2)}) collective-permute-start(bf16[512,128]{1,0:T(8,128)(2,1)S(1)} %shard_map.83.refs_0_), channel_id=1, source_target_pairs={{0,3},{1,2},{2,1},{3,0},{4,7},{5,6},{6,5},{7,4},{8,11},{9,10},{10,... | collective-permute-start | bytes 393224 | tf_op jit(solution)/shard_map/ppermute | solution.py:470
  21.3 9.7 %collective-permute-start.8 = (bf16[512,128]{1,0:T(8,128)(2,1)S(1)}, bf16[512,128]{1,0:T(8,128)(2,1)S(1)}, u32[]{:S(2)}, u32[]{:S(2)}) collective-permute-start(bf16[512,128]{1,0:T(8,128)(2,1)S(1)} %shard_map.83.refs_0_), channel_id=1, source_target_pairs={{0,1},{1,0},{2,3},{3,2},{4,5},{5,4},{6,7},{7,6},{8,9},{9,8},{10,11... | collective-permute-start | bytes 393224 | tf_op jit(solution)/shard_map/ppermute | solution.py:470
  22.3 8.7 %collective-permute-start.9 = (bf16[512,128]{1,0:T(8,128)(2,1)S(1)}, bf16[512,128]{1,0:T(8,128)(2,1)S(1)}, u32[]{:S(2)}, u32[]{:S(2)}) collective-permute-start(bf16[512,128]{1,0:T(8,128)(2,1)S(1)} %shard_map.83.refs_0_), channel_id=1, source_target_pairs={{0,2},{1,3},{2,0},{3,1},{4,6},{5,7},{6,4},{7,5},{8,10},{9,11},{10,... | collective-permute-start | bytes 393224 | tf_op jit(solution)/shard_map/ppermute | solution.py:470
  27.7 10.2 %collective-permute-start.6 = (bf16[128,1024]{1,0:T(8,128)(2,1)S(1)}, bf16[128,1024]{1,0:T(8,128)(2,1)S(1)}, u32[]{:S(2)}, u32[]{:S(2)}) collective-permute-start(bf16[128,1024]{1,0:T(8,128)(2,1)S(1)} %get-tuple-element.46), channel_id=1, source_target_pairs={{0,4},{1,5},{2,6},{3,7},{4,8},{5,9},{6,10},{7,11},{8,12},{9,13},{1... | collective-permute-start | bytes 786440 | tf_op jit(solution)/shard_map/ppermute | solution.py:470
  29.2 8.6 %collective-permute-start.7 = (bf16[128,1024]{1,0:T(8,128)(2,1)S(1)}, bf16[128,1024]{1,0:T(8,128)(2,1)S(1)}, u32[]{:S(2)}, u32[]{:S(2)}) collective-permute-start(bf16[128,1024]{1,0:T(8,128)(2,1)S(1)} %get-tuple-element.47), channel_id=1, source_target_pairs={{0,12},{1,13},{2,14},{3,15},{4,0},{5,1},{6,2},{7,3},{8,4},{9,5},{1... | collective-permute-start | bytes 786440 | tf_op jit(solution)/shard_map/ppermute | solution.py:470
  43.4 12.9 %collective-permute-start.11 = (bf16[560,128]{1,0:T(8,128)(2,1)S(1)}, bf16[560,128]{1,0:T(8,128)(2,1)S(1)}, u32[]{:S(2)}, u32[]{:S(2)}) collective-permute-start(bf16[560,128]{1,0:T(8,128)(2,1)S(1)} %get-tuple-element.59), channel_id=1, source_target_pairs={{0,1},{1,0},{2,3},{3,2},{4,5},{5,4},{6,7},{7,6},{8,9},{9,8},{10,11... | collective-permute-start | bytes 430088 | tf_op jit(solution)/shard_map/ppermute | solution.py:470
  43.6 12.7 %collective-permute-start.12 = (bf16[560,128]{1,0:T(8,128)(2,1)S(1)}, bf16[560,128]{1,0:T(8,128)(2,1)S(1)}, u32[]{:S(2)}, u32[]{:S(2)}) collective-permute-start(bf16[560,128]{1,0:T(8,128)(2,1)S(1)} %get-tuple-element.60), channel_id=1, source_target_pairs={{0,2},{1,3},{2,0},{3,1},{4,6},{5,7},{6,4},{7,5},{8,10},{9,11},{10,... | collective-permute-start | bytes 430088 | tf_op jit(solution)/shard_map/ppermute | solution.py:470
  44.5 11.8 %collective-permute-start.13 = (bf16[560,128]{1,0:T(8,128)(2,1)S(1)}, bf16[560,128]{1,0:T(8,128)(2,1)S(1)}, u32[]{:S(2)}, u32[]{:S(2)}) collective-permute-start(bf16[560,128]{1,0:T(8,128)(2,1)S(1)} %get-tuple-element.61), channel_id=1, source_target_pairs={{0,3},{1,2},{2,1},{3,0},{4,7},{5,6},{6,5},{7,4},{8,11},{9,10},{10,... | collective-permute-start | bytes 430088 | tf_op jit(solution)/shard_map/ppermute | solution.py:470
  56.5 4.1 %collective-permute-start.14 = (bf16[176,128]{1,0:T(8,128)(2,1)S(1)}, bf16[176,128]{1,0:T(8,128)(2,1)S(1)}, u32[]{:S(2)}, u32[]{:S(2)}) collective-permute-start(bf16[176,128]{1,0:T(8,128)(2,1)S(1)} %get-tuple-element.63), channel_id=1, source_target_pairs={{0,16},{16,32},{32,48},{48,0},{1,17},{17,33},{33,49},{49,1},{2,18}... | collective-permute-start | bytes 135176 | tf_op jit(solution)/shard_map/ppermute | solution.py:567
  56.6 5.6 %collective-permute-start.15 = (bf16[176,128]{1,0:T(8,128)(2,1)S(1)}, bf16[176,128]{1,0:T(8,128)(2,1)S(1)}, u32[]{:S(2)}, u32[]{:S(2)}) collective-permute-start(bf16[176,128]{1,0:T(8,128)(2,1)S(1)} %get-tuple-element.64), channel_id=1, source_target_pairs={{0,32},{16,48},{32,0},{48,16},{1,33},{17,49},{33,1},{49,17},{2,34}... | collective-permute-start | bytes 135176 | tf_op jit(solution)/shard_map/ppermute | solution.py:567
  59.0 5.3 %collective-permute-start.16 = (bf16[176,128]{1,0:T(8,128)(2,1)S(1)}, bf16[176,128]{1,0:T(8,128)(2,1)S(1)}, u32[]{:S(2)}, u32[]{:S(2)}) collective-permute-start(bf16[176,128]{1,0:T(8,128)(2,1)S(1)} %get-tuple-element.65), channel_id=1, source_target_pairs={{0,48},{16,0},{32,16},{48,32},{1,49},{17,1},{33,17},{49,33},{2,50}... | collective-permute-start | bytes 135176 | tf_op jit(solution)/shard_map/ppermute | solution.py:567
